TPU v7x, 32 devices: a whole 2x2x4 slice. The times are simulated.
32 devices in a mesh: shard: 4 (over x, core), ctx: 4 (over z), tp: 2 (over y).
Axes of the slice: x: 2, y: 2, z: 4, core: 2. Of those that a mesh axis runs over, the one named last changes fastest.
Arguments:
- tokens: bfloat16 [8, 2048, 1280], P('shard', 'ctx'), may hold values from -6 to 6
- cotangent: bfloat16 [8, 2048, 1280], P('shard', 'ctx'), may hold values from -6 to 6
- doc_lengths: int32 [8, 4], P('shard'), may hold values from 1 to 2045, as said below
- norm_gains: bfloat16 [2, 2, 1280], P(None, None, 'shard'), may hold values from 0.099609375 to 1.8984375
- norm_biases: bfloat16 [2, 4, 1280], P(None, None, 'shard'), may hold values from -1.796875 to 1.796875
- qkv_weight: bfloat16 [2, 3, 1280, 1280], P(None, None, 'shard', 'tp'), may hold values from -0.15625 to 0.15625
- qv_bias: bfloat16 [2, 2, 1280], P(None, None, 'tp'), may hold values from -1.796875 to 1.796875
- proj_weight: bfloat16 [2, 1280, 1280], P(None, 'tp', 'shard'), may hold values from -0.625 to 0.625
- fc_weight: bfloat16 [2, 1280, 5120], P(None, 'shard', 'tp'), may hold values from -0.15625 to 0.15625
- fc_bias: bfloat16 [2, 5120], P(None, 'tp'), may hold values from -1.796875 to 1.796875
- out_weight: bfloat16 [2, 5120, 1280], P(None, 'tp', 'shard'), may hold values from -0.078125 to 0.078125
Outputs:
- output: bfloat16 [8, 2048, 1280], P('shard', 'ctx')
- token_grad: float32 [8, 2048, 1280], P('shard', 'ctx')
- norm_gains_grad: float32 [2, 2, 1280], P(None, None, 'shard')
- norm_biases_grad: float32 [2, 4, 1280], P(None, None, 'shard')
- qkv_weight_grad: float32 [2, 3, 1280, 1280], P(None, None, 'shard', 'tp')
- qv_bias_grad: float32 [2, 2, 1280], P(None, None, 'tp')
- proj_weight_grad: float32 [2, 1280, 1280], P(None, 'tp', 'shard')
- fc_weight_grad: float32 [2, 1280, 5120], P(None, 'shard', 'tp')
- fc_bias_grad: float32 [2, 5120], P(None, 'tp')
- out_weight_grad: float32 [2, 5120, 1280], P(None, 'tp', 'shard')
Inputs may be any that keep to these rules, and one draw needn't show every extreme that they name: `doc_lengths`: each row sums to 2048. Among the 2 sequences of each index of shard, one document starts within the first 512 positions of its sequence and ends within the last 512.
All inputs are finite; a program needn't handle non-finite values.
Results may differ from a plain program's by a relative error of at most 0.018.
Values may be sent and summed in bfloat16 or wider, within the bound.
No kernel may reach another device: no remote copies, remote signals or barrier semaphores. Data moves between devices by JAX's collectives and lax.ppermute only.
A program may use at most 320 MiB of HBM per device.

v0:
```python
import jax
import jax.numpy as jnp
from jax import lax
from jax.sharding import PartitionSpec as P

HD = 64
WINDOW = 1024


norm_eps = 1e-05
masked_score = -1e30


def from_behind(value, axis, steps):
    count = lax.axis_size(axis)
    first, last = (max(0, -steps), min(count, count - steps))
    return lax.ppermute(value, axis, [(source, source + steps) for source in range(first, last)])


def dot_f32(left_side, right_side):
    return jnp.dot(left_side, right_side, preferred_element_type=jnp.float32)


def dot_first(left_side, right_side):
    return lax.dot_general(
        left_side, right_side, (((0,), (0,)), ((), ())), preferred_element_type=jnp.float32
    )


def dot_second(left_side, right_side):
    return lax.dot_general(
        left_side, right_side, (((1,), (1,)), ((), ())), preferred_element_type=jnp.float32
    )


def norm_forward(hidden, norm_gain, norm_shift):
    row_mean = jnp.mean(hidden, axis=-1, keepdims=True)
    centred = hidden - row_mean
    variance = jnp.mean(centred * centred, axis=-1, keepdims=True)
    inv_std = lax.rsqrt(variance + norm_eps)
    norm_hat = centred * inv_std
    return (norm_hat * norm_gain + norm_shift, norm_hat, inv_std)


def norm_backward(grad_out, norm_hat, inv_std, norm_gain):
    scaled = grad_out * norm_gain
    mean_one = jnp.mean(scaled, axis=-1, keepdims=True)
    mean_two = jnp.mean(scaled * norm_hat, axis=-1, keepdims=True)
    grad_input = inv_std * (scaled - mean_one - norm_hat * mean_two)
    return (grad_input, jnp.sum(grad_out * norm_hat, axis=0), jnp.sum(grad_out, axis=0))


def visible(doc_lengths, block_len, reach_blocks):
    doc_ends = jnp.cumsum(doc_lengths, axis=1)
    start_pos = lax.axis_index("ctx") * block_len
    query_pos = start_pos + jnp.arange(block_len, dtype=jnp.int32)
    key_pos = (
        start_pos
        - reach_blocks * block_len
        + jnp.arange((reach_blocks + 1) * block_len, dtype=jnp.int32)
    )
    query_doc = jnp.sum(
        (doc_ends[:, None, :] <= query_pos[None, :, None]).astype(jnp.int32), axis=-1
    )
    key_doc = jnp.sum((doc_ends[:, None, :] <= key_pos[None, :, None]).astype(jnp.int32), axis=-1)
    distance = query_pos[:, None] - key_pos[None, :]
    inside = (distance >= 0) & (distance < WINDOW) & (key_pos >= 0)[None, :]
    return (query_doc[:, :, None] == key_doc[:, None, :]) & inside[None, :, :]


def head_forward(allowed, score_scale):

    def run_head(pieces):
        q_head, k_head, v_head = pieces
        scores = (
            jnp.einsum("sqd,skd->sqk", q_head, k_head, preferred_element_type=jnp.float32)
            * score_scale
        )
        scores = jnp.where(allowed, scores, masked_score)
        top_score = jnp.max(scores, axis=-1, keepdims=True)
        weights = jnp.exp(scores - top_score)
        row_total = jnp.sum(weights, axis=-1, keepdims=True)
        probs_low = (weights / row_total).astype(jnp.bfloat16)
        attn_mixed = jnp.einsum(
            "sqk,skd->sqd", probs_low, v_head, preferred_element_type=jnp.float32
        )
        return (attn_mixed, top_score + jnp.log(row_total))

    return run_head


def head_backward(allowed, score_scale):

    def run_head(pieces):
        q_head, k_head, v_head, grad_head, log_total = pieces
        scores = (
            jnp.einsum("sqd,skd->sqk", q_head, k_head, preferred_element_type=jnp.float32)
            * score_scale
        )
        scores = jnp.where(allowed, scores, masked_score)
        attn_probs = jnp.exp(scores - log_total)
        grad_probs = jnp.einsum(
            "sqd,skd->sqk", grad_head, v_head, preferred_element_type=jnp.float32
        )
        grad_values = jnp.einsum(
            "sqk,sqd->skd",
            attn_probs.astype(jnp.bfloat16),
            grad_head,
            preferred_element_type=jnp.float32,
        )
        delta_rows = jnp.sum(grad_probs * attn_probs, axis=-1, keepdims=True)
        grad_scores = (attn_probs * (grad_probs - delta_rows)).astype(jnp.bfloat16)
        grad_queries = (
            jnp.einsum("sqk,skd->sqd", grad_scores, k_head, preferred_element_type=jnp.float32)
            * score_scale
        )
        grad_keys = (
            jnp.einsum("sqk,sqd->skd", grad_scores, q_head, preferred_element_type=jnp.float32)
            * score_scale
        )
        return (grad_queries, grad_keys, grad_values)

    return run_head


def split_heads(tensor, heads_here):
    return tensor.reshape(tensor.shape[0], tensor.shape[1], heads_here, HD).transpose(2, 0, 1, 3)


def join_heads(tensor):
    return tensor.transpose(1, 2, 0, 3).reshape(
        tensor.shape[1], tensor.shape[2], tensor.shape[0] * tensor.shape[3]
    )


def branch_total(partial_value):
    return lax.psum(partial_value.astype(jnp.bfloat16), "tp").astype(jnp.float32)


def feature_total(partial_value):
    return lax.psum(partial_value.astype(jnp.bfloat16), "tp").astype(jnp.float32)


def fetch_layer(
    layer_index, qkv_weight, proj_weight, fc_weight, out_weight, norm_gains, norm_biases
):
    return (
        lax.all_gather(qkv_weight[layer_index], "shard", axis=1, tiled=True),
        lax.all_gather(proj_weight[layer_index], "shard", axis=1, tiled=True),
        lax.all_gather(fc_weight[layer_index], "shard", axis=0, tiled=True),
        lax.all_gather(out_weight[layer_index], "shard", axis=1, tiled=True),
        lax.all_gather(norm_gains[layer_index], "shard", axis=1, tiled=True),
        lax.all_gather(norm_biases[layer_index], "shard", axis=1, tiled=True),
    )


def per_device(
    tokens,
    cotangent,
    doc_lengths,
    norm_gains,
    norm_biases,
    qkv_weight,
    qv_bias,
    proj_weight,
    fc_weight,
    fc_bias,
    out_weight,
):
    seqs_here, block_len, model_width = tokens.shape
    row_count = seqs_here * block_len
    reach_blocks = WINDOW // block_len
    heads_here = qkv_weight.shape[3] // HD
    score_scale = HD ** (-0.5)
    layer_count = qkv_weight.shape[0]
    allowed = visible(doc_lengths, block_len, reach_blocks)
    hidden = tokens.reshape(row_count, model_width).astype(jnp.float32)
    stash_list = []
    fetched_list = []
    for layer_index in range(layer_count):
        fetched = fetch_layer(
            layer_index, qkv_weight, proj_weight, fc_weight, out_weight, norm_gains, norm_biases
        )
        fetched_list.append(fetched)
        w_qkv, w_proj, w_fc, w_out, layer_gains, layer_shifts = fetched
        layer_gains = layer_gains.astype(jnp.float32)
        layer_shifts = layer_shifts.astype(jnp.float32)
        normed_attn, hat_attn, inv_attn = norm_forward(hidden, layer_gains[0], layer_shifts[0])
        attn_in = normed_attn.astype(jnp.bfloat16)
        bias_pair = qv_bias[layer_index].astype(jnp.float32)
        query_rows = (dot_f32(attn_in, w_qkv[0]) + bias_pair[0]).astype(jnp.bfloat16)
        key_rows = dot_f32(attn_in, w_qkv[1]).astype(jnp.bfloat16)
        value_rows = (dot_f32(attn_in, w_qkv[2]) + bias_pair[1]).astype(jnp.bfloat16)
        query_seq = query_rows.reshape(seqs_here, block_len, -1)
        key_seq = key_rows.reshape(seqs_here, block_len, -1)
        value_seq = value_rows.reshape(seqs_here, block_len, -1)
        key_parts = []
        value_parts = []
        for steps_back in range(reach_blocks, 0, -1):
            far_key, far_value = from_behind((key_seq, value_seq), "ctx", steps_back)
            key_parts.append(far_key)
            value_parts.append(far_value)
        all_keys = jnp.concatenate(key_parts + [key_seq], axis=1)
        all_values = jnp.concatenate(value_parts + [value_seq], axis=1)
        query_heads = split_heads(query_seq, heads_here)
        key_heads = split_heads(all_keys, heads_here)
        value_heads = split_heads(all_values, heads_here)
        mixed_heads, log_total = lax.map(
            head_forward(allowed, score_scale), (query_heads, key_heads, value_heads)
        )
        attn_mixed = join_heads(mixed_heads).reshape(row_count, -1).astype(jnp.bfloat16)
        middle = hidden + branch_total(dot_f32(attn_mixed, w_proj)) + layer_shifts[1]
        normed_mlp, hat_mlp, inv_mlp = norm_forward(middle, layer_gains[1], layer_shifts[2])
        mlp_in = normed_mlp.astype(jnp.bfloat16)
        pre_act = dot_f32(mlp_in, w_fc) + fc_bias[layer_index].astype(jnp.float32)
        activated = jax.nn.gelu(pre_act, approximate=True).astype(jnp.bfloat16)
        hidden = middle + branch_total(dot_f32(activated, w_out)) + layer_shifts[3]
        stash_list.append(
            (
                attn_in,
                hat_attn,
                inv_attn,
                query_heads,
                key_heads,
                value_heads,
                log_total,
                attn_mixed,
                hat_mlp,
                inv_mlp,
                mlp_in,
                pre_act,
                activated,
            )
        )
    output = hidden.astype(jnp.bfloat16).reshape(seqs_here, block_len, model_width)
    grad_hidden = cotangent.reshape(row_count, model_width).astype(jnp.float32)
    layer_grads = [None] * layer_count
    for layer_index in reversed(range(layer_count)):
        (
            attn_in,
            hat_attn,
            inv_attn,
            query_heads,
            key_heads,
            value_heads,
            log_total,
            attn_mixed,
            hat_mlp,
            inv_mlp,
            mlp_in,
            pre_act,
            activated,
        ) = stash_list[layer_index]
        fetched = fetch_layer(
            layer_index, qkv_weight, proj_weight, fc_weight, out_weight, norm_gains, norm_biases
        )
        w_qkv, w_proj, w_fc, w_out, layer_gains, layer_shifts = fetched
        layer_gains = layer_gains.astype(jnp.float32)
        grad_out_bias = jnp.sum(grad_hidden, axis=0)
        grad_low = grad_hidden.astype(jnp.bfloat16)
        grad_out_w = dot_first(activated, grad_low)
        grad_act = dot_second(grad_low, w_out)
        gelu_value, gelu_pullback = jax.vjp(
            lambda values: jax.nn.gelu(values, approximate=True), pre_act
        )
        grad_pre = gelu_pullback(grad_act)[0].astype(jnp.bfloat16)
        grad_fc_bias = jnp.sum(grad_pre.astype(jnp.float32), axis=0)
        grad_fc_w = dot_first(mlp_in, grad_pre)
        grad_norm_in = feature_total(dot_second(grad_pre, w_fc))
        grad_from_mlp, grad_gain_mlp, grad_shift_mlp = norm_backward(
            grad_norm_in, hat_mlp, inv_mlp, layer_gains[1]
        )
        grad_middle = grad_hidden + grad_from_mlp
        grad_proj_bias = jnp.sum(grad_middle, axis=0)
        grad_low = grad_middle.astype(jnp.bfloat16)
        grad_proj_w = dot_first(attn_mixed, grad_low)
        grad_mixed = dot_second(grad_low, w_proj).astype(jnp.bfloat16)
        grad_mixed_heads = split_heads(grad_mixed.reshape(seqs_here, block_len, -1), heads_here)
        grad_q_heads, grad_k_heads, grad_v_heads = lax.map(
            head_backward(allowed, score_scale),
            (query_heads, key_heads, value_heads, grad_mixed_heads, log_total),
        )
        key_grad_all = join_heads(grad_k_heads)
        value_grad_all = join_heads(grad_v_heads)
        own_keys = key_grad_all[:, reach_blocks * block_len :]
        own_values = value_grad_all[:, reach_blocks * block_len :]
        for steps_back in range(1, reach_blocks + 1):
            start_row = (reach_blocks - steps_back) * block_len
            back_key, back_value = (
                from_behind(
                    key_grad_all[:, start_row : start_row + block_len].astype(jnp.bfloat16),
                    "ctx",
                    -steps_back,
                ).astype(jnp.float32),
                from_behind(
                    value_grad_all[:, start_row : start_row + block_len].astype(jnp.bfloat16),
                    "ctx",
                    -steps_back,
                ).astype(jnp.float32),
            )
            own_keys = own_keys + back_key
            own_values = own_values + back_value
        grad_queries = join_heads(grad_q_heads).reshape(row_count, -1).astype(jnp.bfloat16)
        grad_keys = own_keys.reshape(row_count, -1).astype(jnp.bfloat16)
        grad_values = own_values.reshape(row_count, -1).astype(jnp.bfloat16)
        grad_qv_bias = jnp.stack(
            [
                jnp.sum(grad_queries.astype(jnp.float32), axis=0),
                jnp.sum(grad_values.astype(jnp.float32), axis=0),
            ]
        )
        grad_qkv_w = jnp.stack(
            [
                dot_first(attn_in, grad_queries),
                dot_first(attn_in, grad_keys),
                dot_first(attn_in, grad_values),
            ]
        )
        grad_attn_in = feature_total(
            dot_second(grad_queries, w_qkv[0])
            + dot_second(grad_keys, w_qkv[1])
            + dot_second(grad_values, w_qkv[2])
        )
        grad_from_attn, grad_gain_attn, grad_shift_attn = norm_backward(
            grad_attn_in, hat_attn, inv_attn, layer_gains[0]
        )
        grad_hidden = grad_middle + grad_from_attn
        grad_gains = jnp.stack([grad_gain_attn, grad_gain_mlp])
        grad_shifts = jnp.stack([grad_shift_attn, grad_proj_bias, grad_shift_mlp, grad_out_bias])
        matrices = (grad_qkv_w, grad_proj_w, grad_fc_w, grad_out_w, grad_gains, grad_shifts)
        owned = (
            lax.psum_scatter(
                matrices[0].astype(jnp.bfloat16), "shard", scatter_dimension=1, tiled=True
            ).astype(jnp.float32),
            lax.psum_scatter(
                matrices[1].astype(jnp.bfloat16), "shard", scatter_dimension=1, tiled=True
            ).astype(jnp.float32),
            lax.psum_scatter(
                matrices[2].astype(jnp.bfloat16), "shard", scatter_dimension=0, tiled=True
            ).astype(jnp.float32),
            lax.psum_scatter(
                matrices[3].astype(jnp.bfloat16), "shard", scatter_dimension=1, tiled=True
            ).astype(jnp.float32),
            lax.psum_scatter(
                matrices[4].astype(jnp.bfloat16), "shard", scatter_dimension=1, tiled=True
            ).astype(jnp.float32),
            lax.psum_scatter(
                matrices[5].astype(jnp.bfloat16), "shard", scatter_dimension=1, tiled=True
            ).astype(jnp.float32),
        )
        owned = (
            lax.psum(owned[0].astype(jnp.bfloat16), "ctx").astype(jnp.float32),
            lax.psum(owned[1].astype(jnp.bfloat16), "ctx").astype(jnp.float32),
            lax.psum(owned[2].astype(jnp.bfloat16), "ctx").astype(jnp.float32),
            lax.psum(owned[3].astype(jnp.bfloat16), "ctx").astype(jnp.float32),
            lax.psum(owned[4].astype(jnp.bfloat16), "ctx").astype(jnp.float32),
            lax.psum(owned[5].astype(jnp.bfloat16), "ctx").astype(jnp.float32),
        )
        vector_sums = lax.psum((grad_qv_bias, grad_fc_bias), ("shard", "ctx"))
        layer_grads[layer_index] = (owned, vector_sums)
    token_grad = grad_hidden.reshape(seqs_here, block_len, model_width)
    norm_gains_grad = jnp.stack([entry[0][4] for entry in layer_grads])
    norm_biases_grad = jnp.stack([entry[0][5] for entry in layer_grads])
    qkv_weight_grad = jnp.stack([entry[0][0] for entry in layer_grads])
    qv_bias_grad = jnp.stack([entry[1][0] for entry in layer_grads])
    proj_weight_grad = jnp.stack([entry[0][1] for entry in layer_grads])
    fc_weight_grad = jnp.stack([entry[0][2] for entry in layer_grads])
    fc_bias_grad = jnp.stack([entry[1][1] for entry in layer_grads])
    out_weight_grad = jnp.stack([entry[0][3] for entry in layer_grads])
    return (
        output,
        token_grad,
        norm_gains_grad,
        norm_biases_grad,
        qkv_weight_grad,
        qv_bias_grad,
        proj_weight_grad,
        fc_weight_grad,
        fc_bias_grad,
        out_weight_grad,
    )


def solution(mesh):
    placed = (
        P("shard", "ctx", None),
        P("shard", "ctx", None),
        P("shard", None),
        P(None, None, "shard"),
        P(None, None, "shard"),
        P(None, None, "shard", "tp"),
        P(None, None, "tp"),
        P(None, "tp", "shard"),
        P(None, "shard", "tp"),
        P(None, "tp"),
        P(None, "tp", "shard"),
    )
    return jax.shard_map(
        per_device,
        mesh=mesh,
        in_specs=placed,
        out_specs=(
            P("shard", "ctx", None),
            P("shard", "ctx", None),
            P(None, None, "shard"),
            P(None, None, "shard"),
            P(None, None, "shard", "tp"),
            P(None, None, "tp"),
            P(None, "tp", "shard"),
            P(None, "shard", "tp"),
            P(None, "tp"),
            P(None, "tp", "shard"),
        ),
        check_vma=False,
    )
```

profile of v0, /device:TPU:0, one launch (start us, length us, event | category | flops | bytes accessed | tf_op | source)
XLA Modules:
  0.0 3109.1 jit_solution(6782965835897767985)
XLA Ops:
  22.2 27.0 slice_reduce_fusion.6
  58.4 20.7 slice_reduce_fusion.11
  159.1 23.4 collective-permute-done
  182.5 27.5 collective-permute-done.1
  215.4 76.0 %while.56 = (s32[]{:T(128)}, bf16[10,2,512,64]{2,3,1,0:T(8,128)(2,1)}, f32[10,2,512,1]{2,1,3,0:T(2,128)S(1)}, bf16[10,2,512,64]{2,3,1,0:T(8,128)(2,1)}, bf16[10,...) while((s32[]{:T(128)}, ...), condition=%wide.region_8.9_spmd.clone, body=%wide.region_5.8_spmd.clone.sunk | while | flops 418380800 | bytes 20891752 | solution.py:208
  309.9 122.7 %all-reduce.13.cloned.1.call-done = bf16[1024,1280]{1,0:T(8,128)(2,1)} async-done(((bf16[1024,1280]{1,0:T(8,128)(2,1)}), bf16[1024,1280]{1,0:T(8,128)(2,1)}) %all-reduce.13.cloned.1.call-update) | async-done | bytes 2621456 | tf_op jit(solution)/shard_map/psum | solution.py:137
  440.1 42.6 %all-gather.25.cloned.1.call-done = bf16[1,1280,2560]{2,1,0:T(8,128)(2,1)} async-done(((bf16[1,320,2560]{2,1,0:T(8,128)(2,1)}), bf16[1,1280,2560]{2,1,0:T(8,128)(2,1)}) %all-gather.25.cloned.1.call-update) | async-done | bytes 6553616 | tf_op jit(solution)/shard_map/all_gather | solution.py:150
  482.7 13.3 fusion.114
  495.9 36.7 %all-gather.27.cloned.1.call-done = bf16[1,2560,1280]{1,2,0:T(8,128)(2,1)} async-done(((bf16[1,2560,320]{1,2,0:T(8,128)(2,1)}), bf16[1,2560,1280]{1,2,0:T(8,128)(2,1)}) %all-gather.27.cloned.1.call-update) | async-done | bytes 6553616 | tf_op jit(solution)/shard_map/all_gather | solution.py:151
  532.6 14.9 fusion.164
  566.0 21.0 slice_reduce_fusion.2
  587.0 27.9 slice_reduce_fusion
  630.8 31.4 %all-gather.29.cloned.1.call-done = bf16[1,3,1280,640]{3,2,1,0:T(8,128)(2,1)} async-done(((bf16[1,3,320,640]{3,2,1,0:T(8,128)(2,1)}), bf16[1,3,1280,640]{3,2,1,0:T(8,128)(2,1)}) %all-gather.29.cloned.1.call-update) | async-done | bytes 4915216 | tf_op jit(solution)/shard_map/all_gather | solution.py:148
  706.0 24.1 collective-permute-done.7
  734.6 23.6 collective-permute-done.4
  758.2 27.4 collective-permute-done.5
  790.0 70.0 %while.57 = (s32[]{:T(128)}, bf16[10,2,512,64]{2,3,1,0:T(8,128)(2,1)S(1)}, f32[10,2,512,1]{2,1,3,0:T(2,128)S(1)}, bf16[10,2,512,64]{2,3,1,0:T(8,128)(2,1)}, bf16...) while((s32[]{:T(128)}, ...), condition=%wide.region_18.19_spmd.clone, body=%wide.region_15.18_spmd.clone.sunk | while | flops 418380800 | bytes 20891752 | solution.py:208
  868.7 129.3 %all-reduce.17.cloned.1.call-done = bf16[1024,1280]{1,0:T(8,128)(2,1)} async-done(((bf16[1024,1280]{1,0:T(8,128)(2,1)}), bf16[1024,1280]{1,0:T(8,128)(2,1)}) %all-reduce.17.cloned.1.call-update) | async-done | bytes 2621456 | tf_op jit(solution)/shard_map/psum | solution.py:137
  1005.1 42.4 %all-gather.33.cloned.1.call-done = bf16[1,1280,2560]{2,1,0:T(8,128)(2,1)} async-done(((bf16[1,320,2560]{2,1,0:T(8,128)(2,1)}), bf16[1,1280,2560]{2,1,0:T(8,128)(2,1)}) %all-gather.33.cloned.1.call-update) | async-done | bytes 6553616 | tf_op jit(solution)/shard_map/all_gather | solution.py:150
  1047.4 14.0 fusion.106
  1061.5 36.1 %all-gather.35.cloned.1.call-done = bf16[1,2560,1280]{1,2,0:T(8,128)(2,1)} async-done(((bf16[1,2560,320]{1,2,0:T(8,128)(2,1)}), bf16[1,2560,1280]{1,2,0:T(8,128)(2,1)}) %all-gather.35.cloned.1.call-update) | async-done | bytes 6553616 | tf_op jit(solution)/shard_map/all_gather | solution.py:151
  1097.6 16.7 convert_reduce_fusion
  1124.8 74.5 %all-reduce.19.cloned.1.call-done = bf16[1024,1280]{1,0:T(8,128)(2,1)} async-done(((bf16[1024,1280]{1,0:T(8,128)(2,1)}), bf16[1024,1280]{1,0:T(8,128)(2,1)}) %all-reduce.19.cloned.1.call-update) | async-done | bytes 2621456 | tf_op jit(solution)/shard_map/psum | solution.py:141
  1225.0 136.4 %while.58 = (s32[]{:T(128)}, bf16[10,2,512,64]{2,3,1,0:T(8,128)(2,1)S(1)}, f32[10,2,1536,64]{2,3,0,1:T(8,128)}, f32[10,2,1536,64]{2,3,0,1:T(8,128)}, bf16[10,2,5...) while((s32[]{:T(128)}, ...), condition=%wide.region_28.29_spmd.clone, body=%wide.region_26.28_spmd.clone.sunk | while | flops 1024195584 | bytes 51814532 | solution.py:279
  1381.7 18.7 collective-permute-done.10
  1400.4 84.4 %collective-permute-done.11 = bf16[2,512,640]{1,2,0:T(8,128)(2,1)S(1)} collective-permute-done((bf16[2,512,640]{1,2,0:T(8,128)(2,1)S(1)}, bf16[2,512,640]{1,2,0:T(8,128)(2,1)S(1)}, u32[]{:S(2)}, u32[]{:S(2)}) %collective-permute-start.11) | collective-permute-done | bytes 1310752 | tf_op jit(solution)/shard_map/ppermute | solution.py:17
  1489.2 50.8 %collective-permute-done.9 = bf16[2,512,640]{1,2,0:T(8,128)(2,1)} collective-permute-done((bf16[2,512,640]{1,2,0:T(8,128)(2,1)}, bf16[2,512,640]{1,2,0:T(8,128)(2,1)}, u32[]{:S(2)}, u32[]{:S(2)}) %collective-permute-start.9) | collective-permute-done | bytes 1310752 | tf_op jit(solution)/shard_map/ppermute | solution.py:17
  1554.3 71.7 %all-reduce.21.cloned.1.call-done = bf16[1024,1280]{1,0:T(8,128)(2,1)} async-done(((bf16[1024,1280]{1,0:T(8,128)(2,1)}), bf16[1024,1280]{1,0:T(8,128)(2,1)}) %all-reduce.21.cloned.1.call-update) | async-done | bytes 2621456 | tf_op jit(solution)/shard_map/psum | solution.py:141
  1637.2 18.3 convert_reduce_fusion.1
  1665.8 74.4 %all-reduce.23.cloned.1.call-done = bf16[1024,1280]{1,0:T(8,128)(2,1)} async-done(((bf16[1024,1280]{1,0:T(8,128)(2,1)}), bf16[1024,1280]{1,0:T(8,128)(2,1)}) %all-reduce.23.cloned.1.call-update) | async-done | bytes 2621456 | tf_op jit(solution)/shard_map/psum | solution.py:141
  1767.4 141.7 %while.59 = (s32[]{:T(128)}, bf16[10,2,512,64]{2,3,1,0:T(8,128)(2,1)S(1)}, f32[10,2,1536,64]{2,3,0,1:T(8,128)}, f32[10,2,1536,64]{2,3,0,1:T(8,128)}, bf16[10,2,5...) while((s32[]{:T(128)}, ...), condition=%wide.region_37.38_spmd.clone, body=%wide.region_35.37_spmd.clone.sunk | while | flops 1024195584 | bytes 54960296 | solution.py:279
  1921.6 13.1 fusion.170
  1948.2 84.4 %collective-permute-done.15 = bf16[2,512,640]{1,2,0:T(8,128)(2,1)S(1)} collective-permute-done((bf16[2,512,640]{1,2,0:T(8,128)(2,1)S(1)}, bf16[2,512,640]{1,2,0:T(8,128)(2,1)S(1)}, u32[]{:S(2)}, u32[]{:S(2)}) %collective-permute-start.15) | collective-permute-done | bytes 1310752 | tf_op jit(solution)/shard_map/ppermute | solution.py:17
  2036.4 51.4 %collective-permute-done.13 = bf16[2,512,640]{1,2,0:T(8,128)(2,1)} collective-permute-done((bf16[2,512,640]{1,2,0:T(8,128)(2,1)}, bf16[2,512,640]{1,2,0:T(8,128)(2,1)}, u32[]{:S(2)}, u32[]{:S(2)}) %collective-permute-start.13) | collective-permute-done | bytes 1310752 | tf_op jit(solution)/shard_map/ppermute | solution.py:17
  2156.5 13.8 convolution_convert_fusion.1
  2205.0 25.6 all-reduce.27.cloned.1.call-done
  2239.1 23.3 reduce-scatter.27.cloned.1.call-done
  2262.4 31.0 reduce-scatter.25.cloned.1.call-done
  2293.4 63.3 %reduce-scatter.31.cloned.1.call-done = bf16[320,2560]{1,0:T(8,128)(2,1)} async-done(((bf16[1280,2560]{1,0:T(8,128)(2,1)}), bf16[320,2560]{1,0:T(8,128)(2,1)}) %reduce-scatter.31.cloned.1.call-update) | async-done | bytes 1638416 | tf_op jit(solution)/shard_map/reduce_scatter | solution.py:338
  2356.7 62.7 %reduce-scatter.35.cloned.1.call-done = bf16[2560,320]{0,1:T(8,128)(2,1)} async-done(((bf16[2560,1280]{0,1:T(8,128)(2,1)}), bf16[2560,320]{0,1:T(8,128)(2,1)}) %reduce-scatter.35.cloned.1.call-update) | async-done | bytes 1638416 | tf_op jit(solution)/shard_map/reduce_scatter | solution.py:341
  2419.4 52.4 %reduce-scatter.23.cloned.1.call-done = bf16[3,320,640]{2,1,0:T(8,128)(2,1)} async-done(((bf16[3,1280,640]{2,1,0:T(8,128)(2,1)}), bf16[3,320,640]{2,1,0:T(8,128)(2,1)}) %reduce-scatter.23.cloned.1.call-update) | async-done | bytes 1228816 | tf_op jit(solution)/shard_map/reduce_scatter | solution.py:332
  2471.8 62.7 %reduce-scatter.33.cloned.1.call-done = bf16[2560,320]{0,1:T(8,128)(2,1)} async-done(((bf16[2560,1280]{0,1:T(8,128)(2,1)}), bf16[2560,320]{0,1:T(8,128)(2,1)}) %reduce-scatter.33.cloned.1.call-update) | async-done | bytes 1638416 | tf_op jit(solution)/shard_map/reduce_scatter | solution.py:341
  2534.5 63.4 %reduce-scatter.29.cloned.1.call-done = bf16[320,2560]{1,0:T(8,128)(2,1)} async-done(((bf16[1280,2560]{1,0:T(8,128)(2,1)}), bf16[320,2560]{1,0:T(8,128)(2,1)}) %reduce-scatter.29.cloned.1.call-update) | async-done | bytes 1638416 | tf_op jit(solution)/shard_map/reduce_scatter | solution.py:338
  2598.0 52.4 %reduce-scatter.21.cloned.1.call-done = bf16[3,320,640]{2,1,0:T(8,128)(2,1)} async-done(((bf16[3,1280,640]{2,1,0:T(8,128)(2,1)}), bf16[3,320,640]{2,1,0:T(8,128)(2,1)}) %reduce-scatter.21.cloned.1.call-update) | async-done | bytes 1228816 | tf_op jit(solution)/shard_map/reduce_scatter | solution.py:332
  2652.8 21.2 reduce-scatter.39.cloned.1.call-done
  2674.9 22.0 reduce-scatter.43.cloned.1.call-done
  2699.6 61.1 %all-reduce = (f32[1,2,640]{2,1,0:T(2,128)S(1)}, f32[1,2,640]{2,1,0:T(2,128)S(1)}, f32[1,2560]{1,0:T(1,128)S(1)}, f32[1,2560]{1,0:T(1,128)S(1)}) all-reduce(f32[1,2,640]{2,1,0:T(2,128)S(1)} %maximum_bitcast_fusion.5, f32[1,2,640]{2,1,0:T(2,128)S(1)} %maximum_bitcast_fusion.4, ...), channel_id=1, replica_groups=mesh['shard'=4,'ctx'=4,'tp'=2] {'shard','ctx'}, use_global_device_ids=true, to_apply=%region_70.71 | all-reduce | flops 7680 | bytes 61440 | tf_op jit(solution)/shard_map/psum | solution.py:359
  2785.5 304.1 %all-reduce.25.cloned.1.call-done = (bf16[1,3,320,640]{3,2,1,0:T(8,128)(2,1)}, bf16[1,3,320,640]{3,2,1,0:T(8,128)(2,1)}, bf16[1,640,320]{1,2,0:T(8,128)(2,1)}, b...) async-done(((bf16[1,3,320,640]{3,2,1,0:T(8,128)(2,1)}, ...) | async-done | bytes 9830416 | tf_op jit(solution)/shard_map/psum | solution.py:352
  (784 shorter events, 967.5 us)
Async XLA Ops:
  7.2 77.2 %all-gather.21.cloned.1.call-start = ((), (), s32[]{:S(2)}) async-start(), calls=%async_computation.26 | async-start | bytes 6144000 | tf_op jit(solution)/shard_map/all_gather | solution.py:148
  10.6 285.2 %all-gather.23.cloned.1.call-start = ((), (), s32[]{:S(2)}) async-start(), calls=%async_computation.27 | async-start | bytes 2048000 | tf_op jit(solution)/shard_map/all_gather | solution.py:149
  11.7 421.0 %all-reduce.13.cloned.1.call-start = ((), (), s32[]{:S(2)}) async-start(), calls=%async_computation.12 | async-start | bytes 5242880 | tf_op jit(solution)/shard_map/psum | solution.py:137
  49.2 572.8 %copy-start.46 = (f32[1280]{0:T(1024)}, f32[1280]{0:T(1024)S(1)}, u32[]{:S(2)}) copy-start(f32[1280]{0:T(1024)S(1)} %get-tuple-element.538) | copy-start | bytes 15364
  79.0 357.8 %copy-start.48 = (f32[1280]{0:T(1024)}, f32[1280]{0:T(1024)S(1)}, u32[]{:S(2)}) copy-start(f32[1280]{0:T(1024)S(1)} %get-tuple-element.541) | copy-start | bytes 15364
  92.3 57.9 %collective-permute-start.2 = (bf16[2,512,640]{1,2,0:T(8,128)(2,1)}, bf16[2,512,640]{1,2,0:T(8,128)(2,1)}, u32[]{:S(2)}, u32[]{:S(2)}) collective-permute-start(bf16[2,512,640]{1,2,0:T(8,128)(2,1)} %copy.242), channel_id=1, source_target_pairs={{0,4},{2,6},{1,5},{3,7},{8,12},{10,14},{9,13},{11,15},{16,20},{18,... | collective-permute-start | bytes 3932168 | tf_op jit(solution)/shard_map/ppermute | solution.py:17
  98.3 56.1 %collective-permute-start.3 = (bf16[2,512,640]{1,2,0:T(8,128)(2,1)}, bf16[2,512,640]{1,2,0:T(8,128)(2,1)}, u32[]{:S(2)}, u32[]{:S(2)}) collective-permute-start(bf16[2,512,640]{1,2,0:T(8,128)(2,1)} %copy.242), channel_id=1, source_target_pairs={{0,2},{2,4},{4,6},{1,3},{3,5},{5,7},{8,10},{10,12},{12,14},{9,11},... | collective-permute-start | bytes 3932168 | tf_op jit(solution)/shard_map/ppermute | solution.py:17
  110.8 71.7 %collective-permute-start = (bf16[2,512,640]{1,2,0:T(8,128)(2,1)}, bf16[2,512,640]{1,2,0:T(8,128)(2,1)}, u32[]{:S(2)}, u32[]{:S(2)}) collective-permute-start(bf16[2,512,640]{1,2,0:T(8,128)(2,1)} %copy.238), channel_id=1, source_target_pairs={{0,4},{2,6},{1,5},{3,7},{8,12},{10,14},{9,13},{11,15},{16,20},{18,... | collective-permute-start | bytes 3932168 | tf_op jit(solution)/shard_map/ppermute | solution.py:17
  113.2 96.9 %collective-permute-start.1 = (bf16[2,512,640]{1,2,0:T(8,128)(2,1)}, bf16[2,512,640]{1,2,0:T(8,128)(2,1)}, u32[]{:S(2)}, u32[]{:S(2)}) collective-permute-start(bf16[2,512,640]{1,2,0:T(8,128)(2,1)} %copy.238), channel_id=1, source_target_pairs={{0,2},{2,4},{4,6},{1,3},{3,5},{5,7},{8,10},{10,12},{12,14},{9,11},... | collective-permute-start | bytes 3932168 | tf_op jit(solution)/shard_map/ppermute | solution.py:17
  301.4 181.2 %all-gather.25.cloned.1.call-start = ((), (), s32[]{:S(2)}) async-start(), calls=%async_computation.28 | async-start | bytes 8192000 | tf_op jit(solution)/shard_map/all_gather | solution.py:150
  305.3 227.3 %all-gather.27.cloned.1.call-start = ((), (), s32[]{:S(2)}) async-start(), calls=%async_computation.29 | async-start | bytes 8192000 | tf_op jit(solution)/shard_map/all_gather | solution.py:151
  309.2 312.8 %all-reduce.15.cloned.1.call-start = ((), (), s32[]{:S(2)}) async-start(), calls=%async_computation.13 | async-start | bytes 5242880 | tf_op jit(solution)/shard_map/psum | solution.py:137
  547.5 114.7 %all-gather.29.cloned.1.call-start = ((), (), s32[]{:S(2)}) async-start(), calls=%async_computation.30 | async-start | bytes 6144000 | tf_op jit(solution)/shard_map/all_gather | solution.py:148
  548.3 313.4 %all-gather.31.cloned.1.call-start = ((), (), s32[]{:S(2)}) async-start(), calls=%async_computation.31 | async-start | bytes 2048000 | tf_op jit(solution)/shard_map/all_gather | solution.py:149
  587.0 617.9 %copy-start.59 = (f32[1280]{0:T(1024)}, f32[1280]{0:T(1024)S(1)}, u32[]{:S(2)}) copy-start(f32[1280]{0:T(1024)S(1)} %get-tuple-element.534) | copy-start | bytes 15364
  614.9 432.6 %copy-start.87 = (f32[1280]{0:T(1024)}, f32[1280]{0:T(1024)S(1)}, u32[]{:S(2)}) copy-start(f32[1280]{0:T(1024)S(1)} %get-tuple-element.531) | copy-start | bytes 15364
  668.2 37.8 %collective-permute-start.6 = (bf16[2,512,640]{1,2,0:T(8,128)(2,1)}, bf16[2,512,640]{1,2,0:T(8,128)(2,1)}, u32[]{:S(2)}, u32[]{:S(2)}) collective-permute-start(bf16[2,512,640]{1,2,0:T(8,128)(2,1)} %copy.257), channel_id=1, source_target_pairs={{0,4},{2,6},{1,5},{3,7},{8,12},{10,14},{9,13},{11,15},{16,20},{18,... | collective-permute-start | bytes 3932168 | tf_op jit(solution)/shard_map/ppermute | solution.py:17
  674.0 56.1 %collective-permute-start.7 = (bf16[2,512,640]{1,2,0:T(8,128)(2,1)}, bf16[2,512,640]{1,2,0:T(8,128)(2,1)}, u32[]{:S(2)}, u32[]{:S(2)}) collective-permute-start(bf16[2,512,640]{1,2,0:T(8,128)(2,1)} %copy.257), channel_id=1, source_target_pairs={{0,2},{2,4},{4,6},{1,3},{3,5},{5,7},{8,10},{10,12},{12,14},{9,11},... | collective-permute-start | bytes 3932168 | tf_op jit(solution)/shard_map/ppermute | solution.py:17
  684.4 73.8 %collective-permute-start.4 = (bf16[2,512,640]{1,2,0:T(8,128)(2,1)}, bf16[2,512,640]{1,2,0:T(8,128)(2,1)}, u32[]{:S(2)}, u32[]{:S(2)}) collective-permute-start(bf16[2,512,640]{1,2,0:T(8,128)(2,1)} %copy.253), channel_id=1, source_target_pairs={{0,4},{2,6},{1,5},{3,7},{8,12},{10,14},{9,13},{11,15},{16,20},{18,... | collective-permute-start | bytes 3932168 | tf_op jit(solution)/shard_map/ppermute | solution.py:17
  686.7 98.9 %collective-permute-start.5 = (bf16[2,512,640]{1,2,0:T(8,128)(2,1)}, bf16[2,512,640]{1,2,0:T(8,128)(2,1)}, u32[]{:S(2)}, u32[]{:S(2)}) collective-permute-start(bf16[2,512,640]{1,2,0:T(8,128)(2,1)} %copy.253), channel_id=1, source_target_pairs={{0,2},{2,4},{4,6},{1,3},{3,5},{5,7},{8,10},{10,12},{12,14},{9,11},... | collective-permute-start | bytes 3932168 | tf_op jit(solution)/shard_map/ppermute | solution.py:17
  689.1 308.9 %all-reduce.17.cloned.1.call-start = ((), (), s32[]{:S(2)}) async-start(), calls=%async_computation.14 | async-start | bytes 5242880 | tf_op jit(solution)/shard_map/psum | solution.py:137
  867.3 180.1 %all-gather.33.cloned.1.call-start = ((), (), s32[]{:S(2)}) async-start(), calls=%async_computation.32 | async-start | bytes 8192000 | tf_op jit(solution)/shard_map/all_gather | solution.py:150
  867.9 229.6 %all-gather.35.cloned.1.call-start = ((), (), s32[]{:S(2)}) async-start(), calls=%async_computation.33 | async-start | bytes 8192000 | tf_op jit(solution)/shard_map/all_gather | solution.py:151
  868.7 330.6 %all-reduce.19.cloned.1.call-start = ((), (), s32[]{:S(2)}) async-start(), calls=%async_computation.15 | async-start | bytes 5242880 | tf_op jit(solution)/shard_map/psum | solution.py:141
  1124.8 501.2 %all-reduce.21.cloned.1.call-start = ((), (), s32[]{:S(2)}) async-start(), calls=%async_computation.16 | async-start | bytes 5242880 | tf_op jit(solution)/shard_map/psum | solution.py:141
  1365.9 34.5 %collective-permute-start.10 = (bf16[2,512,640]{1,2,0:T(8,128)(2,1)S(1)}, bf16[2,512,640]{1,2,0:T(8,128)(2,1)S(1)}, u32[]{:S(2)}, u32[]{:S(2)}) collective-permute-start(bf16[2,512,640]{1,2,0:T(8,128)(2,1)S(1)} %get-tuple-element.676), channel_id=1, source_target_pairs={{2,0},{4,2},{6,4},{3,1},{5,3},{7,5},{10,8},{12,10},{14,12},{11,9},... | collective-permute-start | bytes 3932168 | tf_op jit(solution)/shard_map/ppermute | solution.py:17
  1367.4 117.5 %collective-permute-start.11 = (bf16[2,512,640]{1,2,0:T(8,128)(2,1)S(1)}, bf16[2,512,640]{1,2,0:T(8,128)(2,1)S(1)}, u32[]{:S(2)}, u32[]{:S(2)}) collective-permute-start(bf16[2,512,640]{1,2,0:T(8,128)(2,1)S(1)} %get-tuple-element.677), channel_id=1, source_target_pairs={{4,0},{6,2},{5,1},{7,3},{12,8},{14,10},{13,9},{15,11},{20,16},{22,... | collective-permute-start | bytes 3932168 | tf_op jit(solution)/shard_map/ppermute | solution.py:17
  1370.9 118.3 %collective-permute-start.8 = (bf16[2,512,640]{1,2,0:T(8,128)(2,1)}, bf16[2,512,640]{1,2,0:T(8,128)(2,1)}, u32[]{:S(2)}, u32[]{:S(2)}) collective-permute-start(bf16[2,512,640]{1,2,0:T(8,128)(2,1)} %get-tuple-element.678), channel_id=1, source_target_pairs={{2,0},{4,2},{6,4},{3,1},{5,3},{7,5},{10,8},{12,10},{14,12},{11,9},... | collective-permute-start | bytes 3932168 | tf_op jit(solution)/shard_map/ppermute | solution.py:17
  1372.2 167.8 %collective-permute-start.9 = (bf16[2,512,640]{1,2,0:T(8,128)(2,1)}, bf16[2,512,640]{1,2,0:T(8,128)(2,1)}, u32[]{:S(2)}, u32[]{:S(2)}) collective-permute-start(bf16[2,512,640]{1,2,0:T(8,128)(2,1)} %get-tuple-element.679), channel_id=1, source_target_pairs={{4,0},{6,2},{5,1},{7,3},{12,8},{14,10},{13,9},{15,11},{20,16},{22,... | collective-permute-start | bytes 3932168 | tf_op jit(solution)/shard_map/ppermute | solution.py:17
  1554.2 186.0 %all-reduce.23.cloned.1.call-start = ((), (), s32[]{:S(2)}) async-start(), calls=%async_computation.17 | async-start | bytes 5242880 | tf_op jit(solution)/shard_map/psum | solution.py:141
  1665.8 564.9 %all-reduce.27.cloned.1.call-start = ((), (), s32[]{:S(2)}) async-start(), calls=%async_computation.39 | async-start | bytes 10485760 | tf_op jit(solution)/shard_map/psum | solution.py:137
  1913.6 34.6 %collective-permute-start.14 = (bf16[2,512,640]{1,2,0:T(8,128)(2,1)S(1)}, bf16[2,512,640]{1,2,0:T(8,128)(2,1)S(1)}, u32[]{:S(2)}, u32[]{:S(2)}) collective-permute-start(bf16[2,512,640]{1,2,0:T(8,128)(2,1)S(1)} %get-tuple-element.672), channel_id=1, source_target_pairs={{2,0},{4,2},{6,4},{3,1},{5,3},{7,5},{10,8},{12,10},{14,12},{11,9},... | collective-permute-start | bytes 3932168 | tf_op jit(solution)/shard_map/ppermute | solution.py:17
  1915.2 117.4 %collective-permute-start.15 = (bf16[2,512,640]{1,2,0:T(8,128)(2,1)S(1)}, bf16[2,512,640]{1,2,0:T(8,128)(2,1)S(1)}, u32[]{:S(2)}, u32[]{:S(2)}) collective-permute-start(bf16[2,512,640]{1,2,0:T(8,128)(2,1)S(1)} %get-tuple-element.673), channel_id=1, source_target_pairs={{4,0},{6,2},{5,1},{7,3},{12,8},{14,10},{13,9},{15,11},{20,16},{22,... | collective-permute-start | bytes 3932168 | tf_op jit(solution)/shard_map/ppermute | solution.py:17
  1919.0 117.4 %collective-permute-start.12 = (bf16[2,512,640]{1,2,0:T(8,128)(2,1)}, bf16[2,512,640]{1,2,0:T(8,128)(2,1)}, u32[]{:S(2)}, u32[]{:S(2)}) collective-permute-start(bf16[2,512,640]{1,2,0:T(8,128)(2,1)} %get-tuple-element.674), channel_id=1, source_target_pairs={{2,0},{4,2},{6,4},{3,1},{5,3},{7,5},{10,8},{12,10},{14,12},{11,9},... | collective-permute-start | bytes 3932168 | tf_op jit(solution)/shard_map/ppermute | solution.py:17
  1920.3 167.5 %collective-permute-start.13 = (bf16[2,512,640]{1,2,0:T(8,128)(2,1)}, bf16[2,512,640]{1,2,0:T(8,128)(2,1)}, u32[]{:S(2)}, u32[]{:S(2)}) collective-permute-start(bf16[2,512,640]{1,2,0:T(8,128)(2,1)} %get-tuple-element.675), channel_id=1, source_target_pairs={{4,0},{6,2},{5,1},{7,3},{12,8},{14,10},{13,9},{15,11},{20,16},{22,... | collective-permute-start | bytes 3932168 | tf_op jit(solution)/shard_map/ppermute | solution.py:17
  2102.4 160.0 %reduce-scatter.27.cloned.1.call-start = ((), (), s32[]{:S(2)}) async-start(), calls=%async_computation.21 | async-start | bytes 2048000 | tf_op jit(solution)/shard_map/reduce_scatter | solution.py:335
  2110.5 182.9 %reduce-scatter.25.cloned.1.call-start = ((), (), s32[]{:S(2)}) async-start(), calls=%async_computation.20 | async-start | bytes 2048000 | tf_op jit(solution)/shard_map/reduce_scatter | solution.py:335
  2116.5 240.2 %reduce-scatter.31.cloned.1.call-start = ((), (), s32[]{:S(2)}) async-start(), calls=%async_computation.23 | async-start | bytes 8192000 | tf_op jit(solution)/shard_map/reduce_scatter | solution.py:338
  2129.3 290.1 %reduce-scatter.35.cloned.1.call-start = ((), (), s32[]{:S(2)}) async-start(), calls=%async_computation.25 | async-start | bytes 8192000 | tf_op jit(solution)/shard_map/reduce_scatter | solution.py:341
  2143.7 328.1 %reduce-scatter.23.cloned.1.call-start = ((), (), s32[]{:S(2)}) async-start(), calls=%async_computation.19 | async-start | bytes 6144000 | tf_op jit(solution)/shard_map/reduce_scatter | solution.py:332
  2155.8 378.7 %reduce-scatter.33.cloned.1.call-start = ((), (), s32[]{:S(2)}) async-start(), calls=%async_computation.24 | async-start | bytes 8192000 | tf_op jit(solution)/shard_map/reduce_scatter | solution.py:341
  2170.3 427.7 %reduce-scatter.29.cloned.1.call-start = ((), (), s32[]{:S(2)}) async-start(), calls=%async_computation.22 | async-start | bytes 8192000 | tf_op jit(solution)/shard_map/reduce_scatter | solution.py:338
  2183.0 467.4 %reduce-scatter.21.cloned.1.call-start = ((), (), s32[]{:S(2)}) async-start(), calls=%async_computation.18 | async-start | bytes 6144000 | tf_op jit(solution)/shard_map/reduce_scatter | solution.py:332
  2195.3 478.6 %reduce-scatter.39.cloned.1.call-start = ((), (), s32[]{:S(2)}) async-start(), calls=%async_computation.35 | async-start | bytes 409600
  2201.6 495.4 %reduce-scatter.43.cloned.1.call-start = ((), (), s32[]{:S(2)}) async-start(), calls=%async_computation.37 | async-start | bytes 409600
  2202.7 570.2 %reduce-scatter.37.cloned.1.call-start = ((), (), s32[]{:S(2)}) async-start(), calls=%async_computation.34 | async-start | bytes 409600
  2237.8 536.0 %reduce-scatter.41.cloned.1.call-start = ((), (), s32[]{:S(2)}) async-start(), calls=%async_computation.36 | async-start | bytes 409600
  2238.8 850.8 %all-reduce.25.cloned.1.call-start = ((), (), s32[]{:S(2)}) async-start(), calls=%async_computation.38 | async-start | bytes 19660800 | tf_op jit(solution)/shard_map/psum | solution.py:352
  (116 other events, 2510.6 us)
Sparse Core Ops, SparseCore 0:
  10.8 41.2 all-gather.20
  53.6 20.0 all-gather.22
  301.5 131.1 all-reduce.12
  434.8 47.8 all-gather.24
  484.7 47.8 all-gather.26
  547.6 74.3 all-reduce.14
  623.6 38.5 all-gather.28
  689.3 17.2 all-gather.30
  867.5 130.5 all-reduce.16
  999.5 47.8 all-gather.32
  1049.6 47.8 all-gather.34
  1124.9 74.3 all-reduce.18
  1554.3 71.5 all-reduce.20
  1665.9 74.3 all-reduce.22
  2102.5 128.1 all-reduce.26
  2233.8 28.5 reduce-scatter.26
  2264.8 28.5 reduce-scatter.24
  2296.6 60.1 reduce-scatter.30
  2359.3 60.1 reduce-scatter.34
  2422.6 49.1 reduce-scatter.22
  2474.4 60.1 reduce-scatter.32
  2537.8 60.1 reduce-scatter.28
  2601.1 49.1 reduce-scatter.20
  2653.4 20.4 reduce-scatter.38
  2676.5 20.4 reduce-scatter.42
  2699.4 20.4 reduce-scatter.36
  2722.3 20.4 reduce-scatter.40
  2746.7 342.8 all-reduce.24
where the time goes:
time: 3120 us; the launch traced here: 3110 us
  waiting for transfers between devices  1880 us (60%)
  matrix products  631 us (20%)
  local copies, waits for them, and re-layouts  260 us (8%)
  other arithmetic  172 us (6%)
  blocking collectives  104 us (3%)
  starting transfers between devices  42.9 us (1%)
    ppermute x16, waiting for transfers between devices, from_behind(): lax.ppermute(value, axis, [(source, source + steps) for source in range(f...  425 us
    psum x1, waiting for transfers between devices, per_device(): lax.psum(owned[0].astype(jnp.bfloat16), 'ctx').astype(jnp.float32)  304 us
    psum x4, waiting for transfers between devices, branch_total(): lax.psum(partial_value.astype(jnp.bfloat16), 'tp').astype(jnp.float32)  285 us
    psum x3, waiting for transfers between devices, feature_total(): lax.psum(partial_value.astype(jnp.bfloat16), 'tp').astype(jnp.float32)  221 us
    dot_general x40, matrix products, run_head(): jnp.einsum('sqd,skd->sqk', q_head, k_head, preferred_element_type=jnp.flo...  135 us
    reduce_scatter x2, waiting for transfers between devices, per_device(): lax.psum_scatter(matrices[2].astype(jnp.bfloat16), 'shard', scatter_dimen...  127 us
    reduce_scatter x2, waiting for transfers between devices, per_device(): lax.psum_scatter(matrices[3].astype(jnp.bfloat16), 'shard', scatter_dimen...  125 us
    reduce_scatter x2, waiting for transfers between devices, per_device(): lax.psum_scatter(matrices[0].astype(jnp.bfloat16), 'shard', scatter_dimen...  105 us
  transfers between devices with their start and end apart: 44, of which 35 were waited for; matrix products, arithmetic and copies ran while one was open for 18% of the time, Pallas kernels for 0%

commit v1 on v0

v1 whole, which is shorter than its diff:
```python
import jax
import jax.numpy as jnp
from jax import lax
from jax.experimental import pallas as pl
from jax.experimental.pallas import tpu as pltpu
from jax.sharding import PartitionSpec as P

HD = 64
WINDOW = 1024
TILE = 256
masked_score = -1e30


def contract(left_side, right_side, left_dim, right_dim):
    return lax.dot_general(
        left_side, right_side, (((left_dim,), (right_dim,)), ((), ())),
        preferred_element_type=jnp.float32,
    )


def half_mask(shape, half):
    lane = lax.broadcasted_iota(jnp.int32, shape, 1)
    return (lane < HD) if half == 0 else (lane >= HD)


def forward_kernel(q_ref, k_ref, v_ref, low_ref, mixed_ref, total_ref):
    block_len = q_ref.shape[1]
    span = WINDOW + TILE
    eye = lax.broadcasted_iota(jnp.int32, (TILE, TILE), 0) == lax.broadcasted_iota(
        jnp.int32, (TILE, TILE), 1
    )
    for block in range(block_len // TILE):
        rows = pl.ds(block * TILE, TILE)
        window = pl.ds(block * TILE, span)
        queries = q_ref[0, rows, :] * jnp.asarray(HD ** (-0.5), jnp.bfloat16)
        keys = k_ref[0, window, :]
        values = v_ref[0, window, :]
        low_pos = low_ref[0, rows, :] - block * TILE
        key_pos = lax.broadcasted_iota(jnp.int32, (TILE, span), 1)
        query_pos = lax.broadcasted_iota(jnp.int32, (TILE, TILE), 0) + WINDOW
        allowed = key_pos >= low_pos
        causal = key_pos[:, WINDOW:] <= query_pos
        mixed = jnp.zeros((TILE, 2 * HD), jnp.float32)
        for half in range(2):
            scores = contract(
                jnp.where(half_mask(queries.shape, half), queries, 0), keys, 1, 1
            )
            early = jnp.where(allowed[:, :WINDOW], scores[:, :WINDOW], masked_score)
            late = jnp.where(allowed[:, WINDOW:] & causal, scores[:, WINDOW:], masked_score)
            top_score = jnp.maximum(
                jnp.max(early, axis=1, keepdims=True), jnp.max(late, axis=1, keepdims=True)
            )
            early = jnp.exp(early - top_score)
            late = jnp.exp(late - top_score)
            row_total = jnp.sum(early, axis=1, keepdims=True) + jnp.sum(
                late, axis=1, keepdims=True
            )
            part = contract(early.astype(jnp.bfloat16), values[:WINDOW], 1, 0) + contract(
                late.astype(jnp.bfloat16), values[WINDOW:], 1, 0
            )
            part = part * (1.0 / row_total)
            mixed = jnp.where(half_mask(mixed.shape, half), part, mixed)
            log_total = top_score + jnp.log(row_total)
            total_ref[0, 0, half : half + 1, rows] = jnp.sum(
                jnp.where(eye, log_total, 0.0), axis=0, keepdims=True
            )
        mixed_ref[0, rows, :] = mixed.astype(jnp.bfloat16)


def attention_forward(queries, keys, values, low_pos):
    groups, block_len, width = queries.shape
    key_len = keys.shape[1]
    pairs = width // (2 * HD)
    pick = lambda seq, pair: (seq, 0, pair)
    return pl.pallas_call(
        forward_kernel,
        grid=(groups, pairs),
        in_specs=[
            pl.BlockSpec((1, block_len, 2 * HD), pick),
            pl.BlockSpec((1, key_len, 2 * HD), pick),
            pl.BlockSpec((1, key_len, 2 * HD), pick),
            pl.BlockSpec((1, block_len, 1), lambda seq, pair: (seq, 0, 0)),
        ],
        out_specs=[
            pl.BlockSpec((1, block_len, 2 * HD), pick),
            pl.BlockSpec((1, 1, 2, block_len), lambda seq, pair: (seq, pair, 0, 0)),
        ],
        out_shape=[
            jax.ShapeDtypeStruct((groups, block_len, width), jnp.bfloat16),
            jax.ShapeDtypeStruct((groups, pairs, 2, block_len), jnp.float32),
        ],
        compiler_params=pltpu.CompilerParams(vmem_limit_bytes=40 << 20),
        cost_estimate=pl.CostEstimate(
            flops=16 * groups * pairs * block_len * (WINDOW + TILE) * HD,
            bytes_accessed=4 * groups * width * (block_len + key_len),
            transcendentals=2 * groups * pairs * block_len * (WINDOW + TILE),
        ),
    )(queries, keys, values, low_pos[:, :, None])


def backward_kernel(
    q_ref, k_ref, v_ref, mixed_ref, grad_ref, total_ref, low_ref,
    gq_ref, gk_ref, gv_ref, gk_sum, gv_sum,
):
    block_len = q_ref.shape[1]
    span = WINDOW + TILE
    scale = HD ** (-0.5)
    gk_sum[...] = jnp.zeros_like(gk_sum)
    gv_sum[...] = jnp.zeros_like(gv_sum)
    eye = lax.broadcasted_iota(jnp.int32, (TILE, TILE), 0) == lax.broadcasted_iota(
        jnp.int32, (TILE, TILE), 1
    )
    for block in range(block_len // TILE):
        rows = pl.ds(block * TILE, TILE)
        window = pl.ds(block * TILE, span)
        queries = q_ref[0, rows, :] * jnp.asarray(scale, jnp.bfloat16)
        keys = k_ref[0, window, :]
        values = v_ref[0, window, :]
        grads = grad_ref[0, rows, :]
        product = grads.astype(jnp.float32) * mixed_ref[0, rows, :].astype(jnp.float32)
        low_pos = low_ref[0, :, rows] - block * TILE
        key_pos = lax.broadcasted_iota(jnp.int32, (span, TILE), 0)
        query_pos = lax.broadcasted_iota(jnp.int32, (TILE, TILE), 1) + WINDOW
        allowed = key_pos >= low_pos
        late_allowed = allowed[WINDOW:] & (key_pos[WINDOW:] <= query_pos)
        keys_t = jnp.transpose(keys)
        gq_parts = []
        for half in range(2):
            mask = half_mask(queries.shape, half)
            q_half = jnp.where(mask, queries, 0)
            g_half = jnp.where(mask, grads, 0)
            delta = jnp.sum(jnp.where(mask, product, 0.0), axis=1, keepdims=True)
            delta = jnp.sum(jnp.where(eye, delta, 0.0), axis=0, keepdims=True)
            log_total = total_ref[0, 0, half : half + 1, rows]
            scores = contract(keys, q_half, 1, 1)
            probs = jnp.concatenate(
                [
                    jnp.where(allowed[:WINDOW], jnp.exp(scores[:WINDOW] - log_total), 0.0),
                    jnp.where(late_allowed, jnp.exp(scores[WINDOW:] - log_total), 0.0),
                ]
            )
            grad_probs = contract(values, g_half, 1, 1)
            grad_scores = (probs * (grad_probs - delta)).astype(jnp.bfloat16)
            gv_sum[window, :] += contract(probs.astype(jnp.bfloat16), g_half, 1, 0)
            gk_sum[window, :] += contract(grad_scores, q_half, 1, 0)
            gq_parts.append(contract(keys_t[half * HD : (half + 1) * HD], grad_scores, 1, 0))
        gq = jnp.transpose(jnp.concatenate(gq_parts)) * scale
        gq_ref[0, rows, :] = gq.astype(jnp.bfloat16)
    gk_ref[0] = gk_sum[...].astype(jnp.bfloat16)
    gv_ref[0] = gv_sum[...].astype(jnp.bfloat16)


def attention_backward(queries, keys, values, mixed, grads, log_total, low_pos):
    groups, block_len, width = queries.shape
    key_len = keys.shape[1]
    pairs = width // (2 * HD)
    pick = lambda seq, pair: (seq, 0, pair)
    q_spec = pl.BlockSpec((1, block_len, 2 * HD), pick)
    k_spec = pl.BlockSpec((1, key_len, 2 * HD), pick)
    return pl.pallas_call(
        backward_kernel,
        grid=(groups, pairs),
        in_specs=[
            q_spec, k_spec, k_spec, q_spec, q_spec,
            pl.BlockSpec((1, 1, 2, block_len), lambda seq, pair: (seq, pair, 0, 0)),
            pl.BlockSpec((1, 1, block_len), lambda seq, pair: (seq, 0, 0)),
        ],
        out_specs=[q_spec, k_spec, k_spec],
        out_shape=[
            jax.ShapeDtypeStruct(queries.shape, jnp.bfloat16),
            jax.ShapeDtypeStruct(keys.shape, jnp.bfloat16),
            jax.ShapeDtypeStruct(keys.shape, jnp.bfloat16),
        ],
        scratch_shapes=[
            pltpu.VMEM((key_len, 2 * HD), jnp.float32),
            pltpu.VMEM((key_len, 2 * HD), jnp.float32),
        ],
        compiler_params=pltpu.CompilerParams(vmem_limit_bytes=40 << 20),
        cost_estimate=pl.CostEstimate(
            flops=40 * groups * pairs * block_len * (WINDOW + TILE) * HD,
            bytes_accessed=8 * groups * width * (block_len + key_len),
            transcendentals=2 * groups * pairs * block_len * (WINDOW + TILE),
        ),
    )(queries, keys, values, mixed, grads, log_total, low_pos[:, None, :])


norm_eps = 1e-05


def mate(value):
    count = lax.axis_size("shard")
    return lax.ppermute(value, "shard", [(i, i ^ 1) for i in range(count)])


def chip_shift(value, steps, half_only=False):
    count = lax.axis_size("shard")
    if not half_only:
        return lax.ppermute(value, "shard", [(i, (i + 2 * steps) % count) for i in range(count)])
    tp_count = lax.axis_size("tp")
    pairs = [
        (i * tp_count + i % 2, ((i + 2 * steps) % count) * tp_count + i % 2) for i in range(count)
    ]
    return lax.ppermute(value, ("shard", "tp"), pairs)


def cross_out(value):
    pairs = [(i * 2 + i % 2, i * 2 + 1 - i % 2) for i in range(lax.axis_size("shard"))]
    return lax.ppermute(value, ("shard", "tp"), pairs)


def cross_home(value):
    pairs = [(i * 2 + 1 - i % 2, i * 2 + i % 2) for i in range(lax.axis_size("shard"))]
    return lax.ppermute(value, ("shard", "tp"), pairs)


def other_tp(value):
    return lax.ppermute(value, "tp", [(0, 1), (1, 0)])


def onward(value):
    count = lax.axis_size("ctx")
    return lax.ppermute(value, "ctx", [(i, i + 1) for i in range(count - 1)])


def backward_step(value):
    count = lax.axis_size("ctx")
    return lax.ppermute(value, "ctx", [(i + 1, i) for i in range(count - 1)])


def tie(first, second):
    return lax.optimization_barrier((first, second))


def ordered(own, others, chip):
    if len(others) == 1:
        return jnp.where(
            chip == 0, jnp.stack([own, others[0]]), jnp.stack([others[0], own])
        )
    count = len(others) + 1
    whole = jnp.stack([own] + others)
    return jnp.take(whole, (chip - jnp.arange(count)) % count, axis=0)


class Place:
    def __init__(self):
        shard = lax.axis_index("shard")
        self.chips = lax.axis_size("shard") // 2
        self.chip = shard // 2
        self.core = shard % 2
        self.tp = lax.axis_index("tp")
        self.ctx = lax.axis_index("ctx")
        self.home = self.core == self.tp


def gather_core_first(piece, place):
    both = ordered(piece, [mate(piece)], place.core)
    across = cross_out(both)
    yield across
    pair = jnp.where(place.home, both, across)
    others = [chip_shift(pair, steps) for steps in range(1, place.chips)]
    yield tuple(others)
    whole = ordered(pair, others, place.chip)
    yield whole.reshape(-1, piece.shape[1])


def gather_chip_first(piece, place):
    others = [chip_shift(piece, steps) for steps in range(1, place.chips)]
    yield tuple(others)
    own = ordered(piece, others, place.chip)
    both = ordered(own, [mate(own)], place.core)
    across = cross_out(both)
    yield across
    whole = jnp.where(place.home, both, across)
    yield jnp.swapaxes(whole, 0, 1).reshape(-1, piece.shape[1])


def dot_f32(left_side, right_side):
    return jnp.dot(left_side, right_side, preferred_element_type=jnp.float32)


def dot_first(left_side, right_side):
    return contract(left_side, right_side, 0, 0)


def dot_second(left_side, right_side):
    return contract(left_side, right_side, 1, 1)


def norm_forward(hidden, norm_gain, norm_shift):
    row_mean = jnp.mean(hidden, axis=-1, keepdims=True)
    centred = hidden - row_mean
    variance = jnp.mean(centred * centred, axis=-1, keepdims=True)
    inv_std = lax.rsqrt(variance + norm_eps)
    norm_hat = centred * inv_std
    return ((norm_hat * norm_gain + norm_shift).astype(jnp.bfloat16), norm_hat, inv_std)


def norm_backward(grad_out, norm_hat, inv_std, norm_gain):
    scaled = grad_out * norm_gain
    mean_one = jnp.mean(scaled, axis=-1, keepdims=True)
    mean_two = jnp.mean(scaled * norm_hat, axis=-1, keepdims=True)
    grad_input = inv_std * (scaled - mean_one - norm_hat * mean_two)
    return (grad_input, jnp.sum(grad_out * norm_hat, axis=0), jnp.sum(grad_out, axis=0))


def scatter_chip_first(left_side, right_side, place):
    features = left_side.shape[1] // place.chips

    def part(steps):
        start = ((place.chip + steps) % place.chips) * features
        columns = lax.dynamic_slice_in_dim(left_side, start, features, 1)
        return dot_first(columns, right_side).astype(jnp.bfloat16)

    total = None
    sent = [chip_shift(part(steps), steps) for steps in range(1, place.chips)]
    own = part(0)
    total = own.astype(jnp.float32)
    for piece in sent:
        total = total + piece.astype(jnp.float32)
    total = total.astype(jnp.bfloat16)
    total = add_low(total, cross_home(total))
    return share_rows(total, place)


def scatter_tp_first(left_side, right_side, place):
    whole = dot_first(left_side, right_side).astype(jnp.bfloat16)
    whole = add_low(whole, cross_home(whole))
    whole = whole.reshape(place.chips, -1, whole.shape[1])

    def part(steps):
        return lax.dynamic_index_in_dim(whole, (place.chip + steps) % place.chips, 0, False)

    sent = [chip_shift(part(steps), steps, True) for steps in range(1, place.chips)]
    total = part(0)
    for piece in sent:
        total = add_low(total, piece)
    return share_rows(total, place)


def add_low(first, second):
    return (first.astype(jnp.float32) + second.astype(jnp.float32)).astype(jnp.bfloat16)


def share_rows(total, place):
    total = total.reshape(2, -1, total.shape[1])
    own = lax.dynamic_index_in_dim(total, place.core, 0, False)
    other = lax.dynamic_index_in_dim(total, 1 - place.core, 0, False)
    share = jnp.where(place.home, own, mate(other))
    return ctx_total(share, place)


def ctx_total(share, place):
    if lax.axis_size("ctx") != 4:
        return lax.psum(share, "ctx")
    outer = (place.ctx == 0) | (place.ctx == 3)
    inner = add_low(share, lax.ppermute(share, "ctx", [(0, 1), (3, 2)]))
    total = add_low(inner, lax.ppermute(inner, "ctx", [(1, 2), (2, 1)]))
    back = lax.ppermute(total, "ctx", [(1, 0), (2, 3)])
    return jnp.where(outer, back, total)


def core_sum(own_part, mate_part):
    return own_part + mate(mate_part.astype(jnp.bfloat16)).astype(jnp.float32)


def gelu_slope(pre_act, grad_act):
    pullback = jax.vjp(lambda values: jax.nn.gelu(values, approximate=True), pre_act)[1]
    return pullback(grad_act)[0]


def per_device(
    tokens,
    cotangent,
    doc_lengths,
    norm_gains,
    norm_biases,
    qkv_weight,
    qv_bias,
    proj_weight,
    fc_weight,
    fc_bias,
    out_weight,
):
    place = Place()
    block_len, model_width = tokens.shape[1:]
    shard_rows = qkv_weight.shape[2]
    half_width = qkv_weight.shape[3]
    half_hidden = fc_weight.shape[2]
    layer_count = qkv_weight.shape[0]
    reach = WINDOW // block_len
    key_len = (reach + 1) * block_len

    def my_seq(value):
        return lax.dynamic_index_in_dim(value, place.tp, 0, False)

    own_tokens = my_seq(tokens)
    halo = []
    step_value = own_tokens
    for _ in range(reach):
        step_value = onward(step_value)
        halo.insert(0, step_value)
    vectors = jnp.concatenate([norm_gains, norm_biases], axis=1)
    vectors = lax.all_gather(
        vectors.reshape(-1, vectors.shape[2]), "shard", axis=1, tiled=True
    ).astype(jnp.float32)
    vectors = vectors.reshape(layer_count, 6, model_width)

    def half_of(value, axis):
        other = other_tp(value)
        return jnp.where(place.home, value, other).astype(jnp.float32)

    qv_half = half_of(qv_bias, 2)
    fc_half = half_of(fc_bias, 1)

    def packed(layer):
        return (
            jnp.concatenate([qkv_weight[layer, 0], qkv_weight[layer, 1]], axis=1),
            jnp.concatenate(
                [qkv_weight[layer, 2], jnp.transpose(proj_weight[layer])], axis=1
            ),
            fc_weight[layer],
            jnp.transpose(out_weight[layer]),
        )

    weights = []
    gate = None
    for layer in range(layer_count):
        row = []
        pieces = packed(layer)
        for pair in range(2):
            first, second = pieces[2 * pair], pieces[2 * pair + 1]
            if gate is not None:
                (first, second), _ = tie((first, second), gate)
            one = gather_core_first(first, place)
            two = gather_chip_first(second, place)
            next(one), next(two)
            gate = (next(one), next(two))
            row += [next(one), next(two)]
        weights.append(row)

    lengths = my_seq(doc_lengths)
    lengths = jnp.stack([lengths, mate(lengths)])
    doc_ends = jnp.cumsum(lengths, axis=1)
    first_pos = place.ctx * block_len
    query_pos = first_pos + jnp.arange(block_len, dtype=jnp.int32)
    started = doc_ends[:, None, :] <= query_pos[None, :, None]
    doc_start = jnp.max(jnp.where(started, doc_ends[:, None, :], 0), axis=-1)
    low_pos = jnp.maximum(doc_start, query_pos[None, :] - (WINDOW - 1))
    low_pos = (low_pos - first_pos + reach * block_len).astype(jnp.int32)

    hidden = own_tokens.astype(jnp.float32)
    stash = []
    for layer in range(layer_count):
        gains, shifts = vectors[layer, :2], vectors[layer, 2:]
        w_qk, w_vp, w_fc, w_out_t = weights[layer]
        w_q, w_k = w_qk[:, :half_width], w_qk[:, half_width:]
        w_v, w_proj_t = w_vp[:, :half_width], w_vp[:, half_width:]
        attn_in, hat_attn, inv_attn = norm_forward(hidden, gains[0], shifts[0])
        own_near = [attn_in]
        if layer == 0:
            for part in reversed(halo):
                own_near.insert(
                    0, norm_forward(part.astype(jnp.float32), gains[0], shifts[0])[0]
                )
        else:
            step_value = attn_in
            for _ in range(reach):
                step_value = onward(step_value)
                own_near.insert(0, step_value)
        mate_near = [mate(part) for part in own_near]
        near = jnp.concatenate(own_near + mate_near)
        pair_in = jnp.concatenate([own_near[-1], mate_near[-1]])
        queries = (dot_f32(pair_in, w_q) + qv_half[layer, 0]).astype(jnp.bfloat16)
        keys = dot_f32(near, w_k).astype(jnp.bfloat16)
        values = (dot_f32(near, w_v) + qv_half[layer, 1]).astype(jnp.bfloat16)
        queries = queries.reshape(2, block_len, half_width)
        keys = keys.reshape(2, key_len, half_width)
        values = values.reshape(2, key_len, half_width)
        mixed, log_total = attention_forward(queries, keys, values, low_pos)
        mate_part = dot_second(mixed[1], w_proj_t)
        own_part = dot_second(mixed[0], w_proj_t)
        middle = hidden + core_sum(own_part, mate_part) + shifts[1]
        mlp_own, hat_mlp, inv_mlp = norm_forward(middle, gains[1], shifts[2])
        mlp_in = jnp.concatenate([mlp_own, mate(mlp_own)])
        pre_act = dot_f32(mlp_in, w_fc) + fc_half[layer]
        activated = jax.nn.gelu(pre_act, approximate=True).astype(jnp.bfloat16)
        mate_part = dot_second(activated[block_len:], w_out_t)
        own_part = dot_second(activated[:block_len], w_out_t)
        hidden = middle + core_sum(own_part, mate_part) + shifts[3]
        stash.append(
            (
                near, pair_in, hat_attn, inv_attn, queries, keys, values, mixed, log_total,
                hat_mlp, inv_mlp, mlp_in, pre_act, activated,
            )
        )

    own_output = hidden.astype(jnp.bfloat16)
    far_output = other_tp(own_output)

    def both_seqs(own, other):
        return jnp.where(place.tp == 0, jnp.stack([own, other]), jnp.stack([other, own]))

    output = both_seqs(own_output, far_output)

    grad_hidden = my_seq(cotangent).astype(jnp.float32)
    layer_grads = [None] * layer_count
    for layer in reversed(range(layer_count)):
        (
            near, pair_in, hat_attn, inv_attn, queries, keys, values, mixed, log_total,
            hat_mlp, inv_mlp, mlp_in, pre_act, activated,
        ) = stash[layer]
        gains = vectors[layer, :2]
        w_qk, w_vp, w_fc, w_out_t = weights[layer]
        w_q, w_k = w_qk[:, :half_width], w_qk[:, half_width:]
        w_v, w_proj_t = w_vp[:, :half_width], w_vp[:, half_width:]
        grad_out_bias = jnp.sum(grad_hidden, axis=0)
        grad_low = grad_hidden.astype(jnp.bfloat16)
        grad_low = jnp.concatenate([grad_low, mate(grad_low)])
        out_share = scatter_tp_first(grad_low, activated, place)
        grad_pre = gelu_slope(pre_act, dot_f32(grad_low, w_out_t)).astype(jnp.bfloat16)
        grad_fc_bias = jnp.sum(grad_pre.astype(jnp.float32), axis=0)
        fc_share = scatter_chip_first(mlp_in, grad_pre, place)
        mate_part = dot_second(grad_pre[block_len:], w_fc)
        own_part = dot_second(grad_pre[:block_len], w_fc)
        grad_norm_in = core_sum(own_part, mate_part)
        grad_from_mlp, grad_gain_mlp, grad_shift_mlp = norm_backward(
            grad_norm_in, hat_mlp, inv_mlp, gains[1]
        )
        grad_middle = grad_hidden + grad_from_mlp
        grad_proj_bias = jnp.sum(grad_middle, axis=0)
        grad_low = grad_middle.astype(jnp.bfloat16)
        grad_low = jnp.concatenate([grad_low, mate(grad_low)])
        mixed_rows = mixed.reshape(2 * block_len, half_width)
        grad_mixed = dot_f32(grad_low, w_proj_t).astype(jnp.bfloat16)
        grad_q, grad_k, grad_v = attention_backward(
            queries, keys, values, mixed, grad_mixed.reshape(queries.shape), log_total, low_pos
        )
        grad_qv_bias = jnp.stack(
            [
                jnp.sum(grad_q.astype(jnp.float32), axis=(0, 1)),
                jnp.sum(grad_v.astype(jnp.float32), axis=(0, 1)),
            ]
        )
        near_part = [
            dot_second(grad_k[seq], w_k) + dot_second(grad_v[seq], w_v) for seq in range(2)
        ]
        query_part = [dot_second(grad_q[seq], w_q) for seq in range(2)]
        last = reach * block_len
        far_total = core_sum(near_part[0][:last], near_part[1][:last])
        grad_attn_in = core_sum(
            near_part[0][last:] + query_part[0], near_part[1][last:] + query_part[1]
        )
        carried = far_total[:block_len].astype(jnp.bfloat16)
        for step in range(1, reach + 1):
            arrived = backward_step(carried).astype(jnp.float32)
            if step < reach:
                section = far_total[step * block_len : (step + 1) * block_len]
                carried = (arrived + section).astype(jnp.bfloat16)
            else:
                grad_attn_in = grad_attn_in + arrived
        grad_k = grad_k.reshape(2 * key_len, half_width)
        grad_v = grad_v.reshape(2 * key_len, half_width)
        grad_q = grad_q.reshape(2 * block_len, half_width)
        grad_from_attn, grad_gain_attn, grad_shift_attn = norm_backward(
            grad_attn_in, hat_attn, inv_attn, gains[0]
        )
        proj_share = scatter_tp_first(grad_low, mixed_rows, place)
        v_share = scatter_tp_first(near, grad_v, place)
        q_share = scatter_chip_first(pair_in, grad_q, place)
        k_share = scatter_chip_first(near, grad_k, place)
        grad_hidden = grad_middle + grad_from_attn
        halves = jnp.concatenate([grad_qv_bias.reshape(-1), grad_fc_bias])
        empty = jnp.zeros_like(halves)
        small = jnp.concatenate(
            [
                grad_gain_attn, grad_gain_mlp,
                grad_shift_attn, grad_proj_bias, grad_shift_mlp, grad_out_bias,
                jnp.where(place.core == 0, halves, empty),
                jnp.where(place.core == 1, halves, empty),
            ]
        )
        small = lax.psum(small, ("shard", "ctx", "tp"))
        layer_grads[layer] = (q_share, k_share, v_share, proj_share, fc_share, out_share, small)

    own_grad = grad_hidden.astype(jnp.bfloat16)
    far_grad = other_tp(own_grad).astype(jnp.float32)
    token_grad = both_seqs(grad_hidden, far_grad)

    def entries(pick):
        return jnp.stack([pick(entry) for entry in layer_grads])

    def full(value):
        return value.astype(jnp.float32)

    small = entries(lambda entry: entry[6])
    split = 6 * model_width
    norms = small[:, :split].reshape(layer_count, 6, model_width)
    shard = lax.axis_index("shard")
    norms = lax.dynamic_slice_in_dim(norms, shard * shard_rows, shard_rows, 2)
    halves = small[:, split:].reshape(layer_count, 2, -1)
    halves = lax.dynamic_index_in_dim(halves, place.tp, 1, False)
    return (
        output,
        token_grad,
        norms[:, :2],
        norms[:, 2:],
        entries(lambda entry: jnp.stack([full(entry[0]), full(entry[1]), full(entry[2])])),
        halves[:, : 2 * half_width].reshape(layer_count, 2, half_width),
        entries(lambda entry: jnp.transpose(full(entry[3]))),
        entries(lambda entry: full(entry[4])),
        halves[:, 2 * half_width :],
        entries(lambda entry: jnp.transpose(full(entry[5]))),
    )


def solution(mesh):
    placed = (
        P("shard", "ctx", None),
        P("shard", "ctx", None),
        P("shard", None),
        P(None, None, "shard"),
        P(None, None, "shard"),
        P(None, None, "shard", "tp"),
        P(None, None, "tp"),
        P(None, "tp", "shard"),
        P(None, "shard", "tp"),
        P(None, "tp"),
        P(None, "tp", "shard"),
    )
    return jax.shard_map(
        per_device,
        mesh=mesh,
        in_specs=placed,
        out_specs=(
            P("shard", "ctx", None),
            P("shard", "ctx", None),
            P(None, None, "shard"),
            P(None, None, "shard"),
            P(None, None, "shard", "tp"),
            P(None, None, "tp"),
            P(None, "tp", "shard"),
            P(None, "shard", "tp"),
            P(None, "tp"),
            P(None, "tp", "shard"),
        ),
        check_vma=False,
    )
```

time: 3120 us -> 1670 us (0.54)
  waiting for transfers between devices: 1880 us -> 657 us
  matrix products: 631 us -> 330 us
  starting transfers between devices: 42.9 us -> 268 us
  local copies, waits for them, and re-layouts: 260 us -> 51.1 us
  Pallas kernels: 0 us -> 143 us
  blocking collectives: 104 us -> 20.4 us
    psum x8 -> x1, waiting for transfers between devices: 809 us -> 83.4 us  [per_device(): small = lax.psum(small, ('shard', 'ctx', 'tp'))]
    reduce_scatter x8 -> x0, waiting for transfers between devices: 411 us -> none  [the longest x2 127 us: per_device(): lax.psum_scatter(matrices[2].astype(jnp.bfloat16), 'shard', scatter_dimen...]
    dot_general x164 -> x42, matrix products: 535 us -> 226 us  [contract(): lax.dot_general(left_side, right_side, (((left_dim,), (right_dim,)), ((),...]
    ppermute x16 -> x131, starting transfers between devices: 41.3 us -> 268 us  [the longest x12 103 us: ctx_total(): inner = add_low(share, lax.ppermute(share, 'ctx', [(0, 1), (3, 2)]))]
    all_gather x8 -> x0, waiting for transfers between devices: 189 us -> none  [the longest x2 84.9 us: fetch_layer(): lax.all_gather(fc_weight[layer_index], 'shard', axis=0, tiled=True)]
    ppermute x16 -> x131, waiting for transfers between devices: 425 us -> 574 us  [the longest x14 164 us: chip_shift(): lax.ppermute(value, 'shard', [(i, (i + 2 * steps) % count) for i in range...]
    pallas_call x0 -> x4, Pallas kernels: none -> 143 us  [the longest x2 80.4 us: attention_backward(): pl.pallas_call(backward_kernel, grid=(groups, pairs), in_specs=[q_spec, k...]
    slice x16 -> x11, local copies, waits for them, and re-layouts: 113 us -> 8.84 us  [the longest x2 3.49 us: per_device(): far_total = core_sum(near_part[0][:last], near_part[1][:last])]
  transfers between devices with their start and end apart: 44 -> 132, of which waited for: 35 -> 44; matrix products, arithmetic and copies ran while one was open for 18% -> 32% of each run, Pallas kernels for 0% -> 9%
where the time goes in v1:
time: 1670 us; the launch traced here: 1660 us
  waiting for transfers between devices  657 us (39%)
  matrix products  330 us (20%)
  starting transfers between devices  268 us (16%)
  other arithmetic  174 us (10%)
  Pallas kernels  143 us (9%)
  local copies, waits for them, and re-layouts  51.1 us (3%)
  blocking collectives  20.4 us (1%)
  between operations  18.3 us (1%)
    dot_general x42, matrix products, contract(): lax.dot_general(left_side, right_side, (((left_dim,), (right_dim,)), ((),...  226 us
    ppermute x14, waiting for transfers between devices, chip_shift(): lax.ppermute(value, 'shard', [(i, (i + 2 * steps) % count) for i in range...  164 us
    ppermute x12, waiting for transfers between devices, ctx_total(): back = lax.ppermute(total, 'ctx', [(1, 0), (2, 3)])  135 us
    dot_general x12, matrix products, dot_f32(): return jnp.dot(left_side, right_side, preferred_element_type=jnp.float32)  104 us
    ppermute x12, starting transfers between devices, ctx_total(): inner = add_low(share, lax.ppermute(share, 'ctx', [(0, 1), (3, 2)]))  103 us
    psum x1, waiting for transfers between devices, per_device(): small = lax.psum(small, ('shard', 'ctx', 'tp'))  83.4 us
    ppermute x4, waiting for transfers between devices, backward_step(): return lax.ppermute(value, 'ctx', [(i + 1, i) for i in range(count - 1)])  82.1 us
    pallas_call x2, Pallas kernels, attention_backward(): pl.pallas_call(backward_kernel, grid=(groups, pairs), in_specs=[q_spec, k...  80.4 us
  transfers between devices with their start and end apart: 132, of which 44 were waited for; matrix products, arithmetic and copies ran while one was open for 32% of the time, Pallas kernels for 9%

profile of v1, /device:TPU:0, one launch (start us, length us, event | category | flops | bytes accessed | tf_op | source)
XLA Modules:
  0.0 1662.3 jit_solution(7695741102337250177)
XLA Ops:
  23.6 20.4 %all-gather = bf16[4,320,12]{1,2,0:T(8,128)(2,1)S(1)} all-gather(bf16[1,320,12]{1,2,0:T(8,128)(2,1)S(1)} %bitcast.537), channel_id=1, replica_groups=mesh['shard'=4,'ctx'=4,'tp'=2] {'shard'}, dimensions={0}, use_global_device_ids=true | all-gather | bytes 38400 | tf_op jit(solution)/shard_map/all_gather | solution.py:403
  66.3 8.8 collective-permute-done.2
  83.7 8.1 collective-permute-done.6
  106.5 9.1 collective-permute-done.3
  119.6 8.7 convolution_convert_fusion.3
  140.4 26.2 %collective-permute-done.19 = bf16[320,2560]{1,0:T(8,128)(2,1)S(1)} collective-permute-done((bf16[320,2560]{1,0:T(8,128)(2,1)S(1)}, bf16[320,2560]{1,0:T(8,128)(2,1)S(1)}, u32[]{:S(2)}, u32[]{:S(2)}) %collective-permute-start.19) | collective-permute-done | bytes 1638432 | tf_op jit(solution)/shard_map/ppermute | solution.py:198
  175.3 31.4 %shard_map.186 = (bf16[2,512,640]{2,1,0:T(8,128)(2,1)S(1)}, f32[2,5,2,512]{3,2,1,0:T(2,128)S(1)}) custom-call(bf16[2,512,640]{2,1,0:T(8,128)(2,1)S(1)} %bitcast.398, bf16[2,1536,640]{2,1,0:T(8,128)(2,1)S(1)} %bitcast.385, bf16[2,1536,640]{2,1,0:T(8,128)(2,1)S(1)} %bitcast.387, s32[2,512,1]{2,1,0:T(8,128)S(1)} %subtract_add_fusion.low_ref), custom_call_target="tpu_custom_call" | custom-call | flops 6710886400 | bytes 10485760 | tf_op jit(solution)/shard_map/pallas_call | solution.py:75
  215.9 8.9 collective-permute-start.21
  228.7 56.7 %collective-permute-done.17 = bf16[2,320,2560]{2,1,0:T(8,128)(2,1)S(1)} collective-permute-done((bf16[2,320,2560]{2,1,0:T(8,128)(2,1)S(1)}, bf16[2,320,2560]{2,1,0:T(8,128)(2,1)S(1)}, u32[]{:S(2)}, u32[]{:S(2)}) %collective-permute-start.17) | collective-permute-done | bytes 3276832 | tf_op jit(solution)/shard_map/ppermute | solution.py:198
  288.7 15.4 multiply_convert_fusion.1
  334.8 20.9 %collective-permute-done.27 = bf16[512,1280]{1,0:T(8,128)(2,1)S(1)} collective-permute-done((bf16[512,1280]{1,0:T(8,128)(2,1)S(1)}, bf16[512,1280]{1,0:T(8,128)(2,1)S(1)}, u32[]{:S(2)}, u32[]{:S(2)}) %collective-permute-start.27) | collective-permute-done | bytes 1310752 | tf_op jit(solution)/shard_map/ppermute | solution.py:222
  366.6 18.4 %collective-permute-done.28 = bf16[512,1280]{1,0:T(8,128)(2,1)S(1)} collective-permute-done((bf16[512,1280]{1,0:T(8,128)(2,1)S(1)}, bf16[512,1280]{1,0:T(8,128)(2,1)S(1)}, u32[]{:S(2)}, u32[]{:S(2)}) %collective-permute-start.28) | collective-permute-done | bytes 1310752 | tf_op jit(solution)/shard_map/ppermute | solution.py:222
  385.6 9.0 collective-permute-done.26
  428.6 31.4 %shard_map.187 = (bf16[2,512,640]{2,1,0:T(8,128)(2,1)S(1)}, f32[2,5,2,512]{3,2,1,0:T(2,128)S(1)}) custom-call(bf16[2,512,640]{2,1,0:T(8,128)(2,1)S(1)} %bitcast.400, bf16[2,1536,640]{2,1,0:T(8,128)(2,1)S(1)} %bitcast.389, bf16[2,1536,640]{2,1,0:T(8,128)(2,1)S(1)} %bitcast.391, s32[2,512,1]{2,1,0:T(8,128)S(1)} %subtract_add_fusion.low_ref), custom_call_target="tpu_custom_call" | custom-call | flops 6710886400 | bytes 10485760 | tf_op jit(solution)/shard_map/pallas_call | solution.py:75
  489.0 56.8 %collective-permute-done.38 = bf16[2,320,2560]{2,1,0:T(8,128)(2,1)S(1)} collective-permute-done((bf16[2,320,2560]{2,1,0:T(8,128)(2,1)S(1)}, bf16[2,320,2560]{2,1,0:T(8,128)(2,1)S(1)}, u32[]{:S(2)}, u32[]{:S(2)}) %collective-permute-start.38) | collective-permute-done | bytes 3276832 | tf_op jit(solution)/shard_map/ppermute | solution.py:198
  546.9 12.0 multiply_convert_fusion
  559.0 11.6 convolution_convert_fusion
  580.3 19.8 %convert_reduce_fusion = (f32[2560]{0:T(1024)}, bf16[1024,2560]{1,0:T(8,128)(2,1)}) fusion(f32[1024,2560]{1,0:T(8,128)} %get-tuple-element.124, f32[2560]{0:T(1024)S(1)} %get-tuple-element.70, bf16[1280,2560]{1,0:T(8,128)(2,1)} %bitcast.473, bf16[512,1280]{1,0:T(8,128)(2,1)} %collective-permute-done.44, bf16[512,1280]{1,0:T(8,128)(2,1)S(1)} %get-tuple-element.79), kind=kOutput, calls=%fused_computation.22 | convolution fusion | flops 6776419840 | bytes 24924160 | tf_op jit(solution)/shard_map/dot_general | solution.py:278
  635.0 8.9 convolution_convert_fusion.5
  655.4 40.4 %shard_map.188 = (bf16[2,512,640]{2,1,0:T(8,128)(2,1)S(1)}, bf16[2,1536,640]{2,1,0:T(8,128)(2,1)S(1)}, bf16[2,1536,640]{2,1,0:T(8,128)(2,1)S(1)}) custom-call(bf16[2,512,640]{2,1,0:T(8,128)(2,1)S(1)} %bitcast.401, bf16[2,1536,640]{2,1,0:T(8,128)(2,1)} %bitcast.390, bf16[2,1536,640]{2,1,0:T(8,128)(2,1)} %bitcast.392, ...), custom_call_target="tpu_custom_call" | custom-call | flops 16777216000 | bytes 20971520 | tf_op jit(solution)/shard_map/pallas_call | solution.py:160
  711.6 9.6 convolution_convert_fusion.10
  760.9 9.3 add_convert_fusion
  780.5 12.4 collective-permute-done.84
  793.2 8.4 collective-permute-done.78
  846.0 11.3 collective-permute-start.92
  857.3 11.3 collective-permute-start.104
  899.8 25.6 %collective-permute-done.49 = bf16[512,1280]{1,0:T(8,128)(2,1)} collective-permute-done((bf16[512,1280]{1,0:T(8,128)(2,1)}, bf16[512,1280]{1,0:T(8,128)(2,1)}, u32[]{:S(2)}, u32[]{:S(2)}) %collective-permute-start.49) | collective-permute-done | bytes 1310752 | tf_op jit(solution)/shard_map/ppermute | solution.py:227
  943.8 24.7 %collective-permute-done.50 = bf16[512,1280]{1,0:T(8,128)(2,1)} collective-permute-done((bf16[512,1280]{1,0:T(8,128)(2,1)}, bf16[512,1280]{1,0:T(8,128)(2,1)}, u32[]{:S(2)}, u32[]{:S(2)}) %collective-permute-start.50) | collective-permute-done | bytes 1310752 | tf_op jit(solution)/shard_map/ppermute | solution.py:227
  979.9 19.9 %convert_reduce_fusion.1 = (f32[2560]{0:T(1024)}, bf16[1024,2560]{1,0:T(8,128)(2,1)}) fusion(f32[1024,2560]{1,0:T(8,128)} %get-tuple-element.118, f32[2560]{0:T(1024)S(1)} %copy-done.132, bf16[1280,2560]{1,0:T(8,128)(2,1)} %bitcast.472, bf16[512,1280]{1,0:T(8,128)(2,1)} %copy-done.143, bf16[512,1280]{1,0:T(8,128)(2,1)S(1)} %convert_element_type.740), kind=kOutput, calls=%fused_computation.23 | convolution fusion | flops 6776419840 | bytes 24924160 | tf_op jit(solution)/shard_map/dot_general | solution.py:278
  1015.3 11.8 convolution_convert_fusion.1
  1037.6 10.1 collective-permute-done.128
  1064.5 40.0 %shard_map.189 = (bf16[2,512,640]{2,1,0:T(8,128)(2,1)S(1)}, bf16[2,1536,640]{2,1,0:T(8,128)(2,1)S(1)}, bf16[2,1536,640]{2,1,0:T(8,128)(2,1)S(1)}) custom-call(bf16[2,512,640]{2,1,0:T(8,128)(2,1)S(1)} %bitcast.399, bf16[2,1536,640]{2,1,0:T(8,128)(2,1)} %bitcast.386, bf16[2,1536,640]{2,1,0:T(8,128)(2,1)} %bitcast.388, bf16[2,512,640]{2,1,0:T(8,128)(2,1)S(1)} %copy-done.15, ...), custom_call_target="tpu_custom_call" | custom-call | flops 16777216000 | bytes 20971520 | tf_op jit(solution)/shard_map/pallas_call | solution.py:160
  1152.9 12.2 convolution_convert_fusion.11
  1191.3 15.8 collective-permute-done.95
  1216.4 8.3 collective-permute-done.60
  1227.8 25.5 %collective-permute-done.130 = bf16[320,2560]{1,0:T(8,128)(2,1)S(1)} collective-permute-done((bf16[320,2560]{1,0:T(8,128)(2,1)S(1)}, bf16[320,2560]{1,0:T(8,128)(2,1)S(1)}, u32[]{:S(2)}, u32[]{:S(2)}) %collective-permute-start.130) | collective-permute-done | bytes 1638432 | tf_op jit(solution)/shard_map/ppermute | solution.py:358
  1259.3 32.0 %collective-permute-start.68 = (bf16[320,640]{1,0:T(8,128)(2,1)S(1)}, bf16[320,640]{1,0:T(8,128)(2,1)S(1)}, u32[]{:S(2)}, u32[]{:S(2)}) collective-permute-start(bf16[320,640]{1,0:T(8,128)(2,1)S(1)} %bitcast_select_fusion.12), channel_id=1, source_target_pairs={{0,2},{6,4},{1,3},{7,5},{8,10},{14,12},{9,11},{15,13},{16,18},{22,... | collective-permute-start | bytes 1228808 | tf_op jit(solution)/shard_map/ppermute | solution.py:356
  1291.6 8.5 collective-permute-start.62
  1309.7 17.1 %collective-permute-start.74 = (bf16[320,640]{1,0:T(8,128)(2,1)S(1)}, bf16[320,640]{1,0:T(8,128)(2,1)S(1)}, u32[]{:S(2)}, u32[]{:S(2)}) collective-permute-start(bf16[320,640]{1,0:T(8,128)(2,1)S(1)} %bitcast_select_fusion.11), channel_id=1, source_target_pairs={{0,2},{6,4},{1,3},{7,5},{8,10},{14,12},{9,11},{15,13},{16,18},{22,... | collective-permute-start | bytes 1228808 | tf_op jit(solution)/shard_map/ppermute | solution.py:356
  1326.9 7.9 collective-permute-start.98
  1360.8 9.3 add_convert_fusion.1
  1379.4 11.3 collective-permute-done.56
  1399.5 8.6 collective-permute-done.100
  1413.4 20.4 %collective-permute-done.57 = bf16[512,1280]{1,0:T(8,128)(2,1)S(1)} collective-permute-done((bf16[512,1280]{1,0:T(8,128)(2,1)S(1)}, bf16[512,1280]{1,0:T(8,128)(2,1)S(1)}, u32[]{:S(2)}, u32[]{:S(2)}) %collective-permute-start.57) | collective-permute-done | bytes 1310752 | tf_op jit(solution)/shard_map/ppermute | solution.py:227
  1451.9 31.3 %collective-permute-done.110 = bf16[320,2560]{1,0:T(8,128)(2,1)} collective-permute-done((bf16[320,2560]{1,0:T(8,128)(2,1)}, bf16[320,2560]{1,0:T(8,128)(2,1)}, u32[]{:S(2)}, u32[]{:S(2)}) %collective-permute-start.110) | collective-permute-done | bytes 1638432 | tf_op jit(solution)/shard_map/ppermute | solution.py:356
  1486.2 83.4 %all-reduce.3.cloned.1.call-done = (f32[1,15360]{1,0:T(1,128)}, f32[1,15360]{1,0:T(1,128)}) async-done(((f32[1,15360]{1,0:T(1,128)}, f32[1,15360]{1,0:T(1,128)}), (f32[1,15360]{1,0:T(1,128)}, f32[1,15360]{1,0:T(1,128)})) %all-reduce.3.cloned.1.call-update) | async-done | bytes 122896 | tf_op jit(solution)/shard_map/psum | solution.py:582
  1584.3 34.8 %collective-permute-done.112 = bf16[320,2560]{1,0:T(8,128)(2,1)S(1)} collective-permute-done((bf16[320,2560]{1,0:T(8,128)(2,1)S(1)}, bf16[320,2560]{1,0:T(8,128)(2,1)S(1)}, u32[]{:S(2)}, u32[]{:S(2)}) %collective-permute-start.112) | collective-permute-done | bytes 1638432 | tf_op jit(solution)/shard_map/ppermute | solution.py:358
  1622.5 29.3 %collective-permute-done.124 = bf16[320,2560]{1,0:T(8,128)(2,1)S(1)} collective-permute-done((bf16[320,2560]{1,0:T(8,128)(2,1)S(1)}, bf16[320,2560]{1,0:T(8,128)(2,1)S(1)}, u32[]{:S(2)}, u32[]{:S(2)}) %collective-permute-start.124) | collective-permute-done | bytes 1638432 | tf_op jit(solution)/shard_map/ppermute | solution.py:358
  (879 shorter events, 671.0 us)
Async XLA Ops:
  7.2 1562.4 %all-reduce.3.cloned.1.call-start = ((), (), s32[]{:S(2)}) async-start(), calls=%async_computation | async-start | bytes 245760 | tf_op jit(solution)/shard_map/psum | solution.py:582
  7.9 43.1 %collective-permute-start.12 = (s32[4]{0:T(128)S(1)}, s32[4]{0:T(128)S(1)}, u32[]{:S(2)}, u32[]{:S(2)}) collective-permute-start(s32[4]{0:T(128)S(1)} %fusion.276), channel_id=1, source_target_pairs={{0,8},{8,0},{16,24},{24,16},{1,9},{9,1},{17,25},{25,17},{2,10},{10... | collective-permute-start | bytes 56 | tf_op jit(solution)/shard_map/ppermute | solution.py:192
  8.3 87.9 %collective-permute-start.4 = (bf16[2,2,640]{2,1,0:T(2,128)(2,1)}, bf16[2,2,640]{2,1,0:T(2,128)(2,1)}, u32[]{:S(2)}, u32[]{:S(2)}) collective-permute-start(bf16[2,2,640]{2,1,0:T(2,128)(2,1)} %param.17), channel_id=1, source_target_pairs={{0,1},{1,0},{2,3},{3,2},{4,5},{5,4},{6,7},{7,6},{8,9},{9,8},{10,11... | collective-permute-start | bytes 15368 | tf_op jit(solution)/shard_map/ppermute | solution.py:217
  12.5 47.9 %collective-permute-start.5 = (bf16[512,1280]{1,0:T(8,128)(2,1)S(1)}, bf16[512,1280]{1,0:T(8,128)(2,1)}, u32[]{:S(2)}, u32[]{:S(2)}) collective-permute-start(bf16[512,1280]{1,0:T(8,128)(2,1)S(1)} %get-tuple-element.95), channel_id=1, source_target_pairs={{0,2},{2,4},{4,6},{1,3},{3,5},{5,7},{8,10},{10,12},{12,14},{9,11},... | collective-permute-start | bytes 3932168 | tf_op jit(solution)/shard_map/ppermute | solution.py:222
  101.2 123.6 %collective-permute-start.18 = (bf16[2,2560]{1,0:T(2,128)(2,1)S(1)}, bf16[2,2560]{1,0:T(2,128)(2,1)S(1)}, u32[]{:S(2)}, u32[]{:S(2)}) collective-permute-start(bf16[2,2560]{1,0:T(2,128)(2,1)S(1)} %copy-done.133), channel_id=1, source_target_pairs={{0,1},{1,0},{2,3},{3,2},{4,5},{5,4},{6,7},{7,6},{8,9},{9,8},{10,11... | collective-permute-start | bytes 30728 | tf_op jit(solution)/shard_map/ppermute | solution.py:217
  133.9 77.1 %collective-permute-start.16 = (bf16[2,320,2560]{2,1,0:T(8,128)(2,1)}, bf16[2,320,2560]{2,1,0:T(8,128)(2,1)}, u32[]{:S(2)}, u32[]{:S(2)}) collective-permute-start(bf16[2,320,2560]{2,1,0:T(8,128)(2,1)} %maximum_select_fusion.7), channel_id=1, source_target_pairs={{0,1},{9,8},{16,17},{25,24},{2,3},{11,10},{18,19},{27,26},{4,5},{1... | collective-permute-start | bytes 9830408 | tf_op jit(solution)/shard_map/ppermute | solution.py:208
  168.6 43.9 %collective-permute-start.20 = (bf16[2,320,2560]{2,1,0:T(8,128)(2,1)}, bf16[2,320,2560]{2,1,0:T(8,128)(2,1)S(1)}, u32[]{:S(2)}, u32[]{:S(2)}) collective-permute-start(bf16[2,320,2560]{2,1,0:T(8,128)(2,1)} %maximum_select_fusion.8), channel_id=1, source_target_pairs={{0,8},{8,0},{16,24},{24,16},{1,9},{9,1},{17,25},{25,17},{2,10},{10... | collective-permute-start | bytes 9830408 | tf_op jit(solution)/shard_map/ppermute | solution.py:192
  211.9 73.4 %collective-permute-start.17 = (bf16[2,320,2560]{2,1,0:T(8,128)(2,1)S(1)}, bf16[2,320,2560]{2,1,0:T(8,128)(2,1)S(1)}, u32[]{:S(2)}, u32[]{:S(2)}) collective-permute-start(bf16[2,320,2560]{2,1,0:T(8,128)(2,1)S(1)} %broadcast_select_fusion.3), channel_id=1, source_target_pairs={{0,16},{8,24},{16,0},{24,8},{1,17},{9,25},{17,1},{25,9},{2,18},{10... | collective-permute-start | bytes 9830408 | tf_op jit(solution)/shard_map/ppermute | solution.py:198
  215.9 88.2 %collective-permute-start.21 = (bf16[2,2,320,2560]{3,2,0,1:T(8,128)(2,1)}, bf16[2,2,320,2560]{3,2,0,1:T(8,128)(2,1)}, u32[]{:S(2)}, u32[]{:S(2)}) collective-permute-start(bf16[2,2,320,2560]{3,2,0,1:T(8,128)(2,1)} %maximum_select_fusion.1), channel_id=1, source_target_pairs={{0,1},{9,8},{16,17},{25,24},{2,3},{11,10},{18,19},{27,26},{4,5},{1... | collective-permute-start | bytes 19660808 | tf_op jit(solution)/shard_map/ppermute | solution.py:208
  227.7 61.0 %collective-permute-start.14 = (bf16[512,1280]{1,0:T(8,128)(2,1)S(1)}, bf16[512,1280]{1,0:T(8,128)(2,1)S(1)}, u32[]{:S(2)}, u32[]{:S(2)}) collective-permute-start(bf16[512,1280]{1,0:T(8,128)(2,1)S(1)} %add_convert_fusion.23), channel_id=1, source_target_pairs={{0,8},{8,0},{16,24},{24,16},{1,9},{9,1},{17,25},{25,17},{2,10},{10... | collective-permute-start | bytes 3932168 | tf_op jit(solution)/shard_map/ppermute | solution.py:192
  316.9 43.3 %collective-permute-start.25 = (bf16[2,320,1280]{2,1,0:T(8,128)(2,1)S(1)}, bf16[2,320,1280]{2,1,0:T(8,128)(2,1)S(1)}, u32[]{:S(2)}, u32[]{:S(2)}) collective-permute-start(bf16[2,320,1280]{2,1,0:T(8,128)(2,1)S(1)} %maximum_select_fusion.17), channel_id=1, source_target_pairs={{0,1},{9,8},{16,17},{25,24},{2,3},{11,10},{18,19},{27,26},{4,5},{1... | collective-permute-start | bytes 4915208 | tf_op jit(solution)/shard_map/ppermute | solution.py:208
  334.3 60.9 %collective-permute-start.23 = (bf16[512,1280]{1,0:T(8,128)(2,1)S(1)}, bf16[512,1280]{1,0:T(8,128)(2,1)S(1)}, u32[]{:S(2)}, u32[]{:S(2)}) collective-permute-start(bf16[512,1280]{1,0:T(8,128)(2,1)S(1)} %add_convert_fusion.22), channel_id=1, source_target_pairs={{0,8},{8,0},{16,24},{24,16},{1,9},{9,1},{17,25},{25,17},{2,10},{10... | collective-permute-start | bytes 3932168 | tf_op jit(solution)/shard_map/ppermute | solution.py:192
  411.5 50.8 %collective-permute-start.39 = (bf16[320,2560]{1,0:T(8,128)(2,1)S(1)}, bf16[320,2560]{1,0:T(8,128)(2,1)S(1)}, u32[]{:S(2)}, u32[]{:S(2)}) collective-permute-start(bf16[320,2560]{1,0:T(8,128)(2,1)S(1)} %copy-done.38), channel_id=1, source_target_pairs={{0,16},{8,24},{16,0},{24,8},{1,17},{9,25},{17,1},{25,9},{2,18},{10... | collective-permute-start | bytes 4915208 | tf_op jit(solution)/shard_map/ppermute | solution.py:198
  415.2 56.2 %collective-permute-start.37 = (bf16[2,320,2560]{2,1,0:T(8,128)(2,1)}, bf16[2,320,2560]{2,1,0:T(8,128)(2,1)}, u32[]{:S(2)}, u32[]{:S(2)}) collective-permute-start(bf16[2,320,2560]{2,1,0:T(8,128)(2,1)} %maximum_select_fusion.11), channel_id=1, source_target_pairs={{0,1},{9,8},{16,17},{25,24},{2,3},{11,10},{18,19},{27,26},{4,5},{1... | collective-permute-start | bytes 9830408 | tf_op jit(solution)/shard_map/ppermute | solution.py:208
  466.7 92.3 %collective-permute-start.44 = (bf16[512,1280]{1,0:T(8,128)(2,1)S(1)}, bf16[512,1280]{1,0:T(8,128)(2,1)}, u32[]{:S(2)}, u32[]{:S(2)}) collective-permute-start(bf16[512,1280]{1,0:T(8,128)(2,1)S(1)} %get-tuple-element.79), channel_id=1, source_target_pairs={{0,8},{8,0},{16,24},{24,16},{1,9},{9,1},{17,25},{25,17},{2,10},{10... | collective-permute-start | bytes 3932168 | tf_op jit(solution)/shard_map/ppermute | solution.py:192
  472.5 73.4 %collective-permute-start.38 = (bf16[2,320,2560]{2,1,0:T(8,128)(2,1)S(1)}, bf16[2,320,2560]{2,1,0:T(8,128)(2,1)S(1)}, u32[]{:S(2)}, u32[]{:S(2)}) collective-permute-start(bf16[2,320,2560]{2,1,0:T(8,128)(2,1)S(1)} %broadcast_select_fusion.2), channel_id=1, source_target_pairs={{0,16},{8,24},{16,0},{24,8},{1,17},{9,25},{17,1},{25,9},{2,18},{10... | collective-permute-start | bytes 9830408 | tf_op jit(solution)/shard_map/ppermute | solution.py:198
  481.8 90.3 %collective-permute-start.41 = (bf16[2,2,320,2560]{3,2,1,0:T(8,128)(2,1)}, bf16[2,2,320,2560]{3,2,1,0:T(8,128)(2,1)}, u32[]{:S(2)}, u32[]{:S(2)}) collective-permute-start(bf16[2,2,320,2560]{3,2,1,0:T(8,128)(2,1)} %maximum_select_fusion.3), channel_id=1, source_target_pairs={{0,1},{9,8},{16,17},{25,24},{2,3},{11,10},{18,19},{27,26},{4,5},{1... | collective-permute-start | bytes 19660808 | tf_op jit(solution)/shard_map/ppermute | solution.py:208
  487.9 59.0 %collective-permute-start.35 = (bf16[512,1280]{1,0:T(8,128)(2,1)S(1)}, bf16[512,1280]{1,0:T(8,128)(2,1)S(1)}, u32[]{:S(2)}, u32[]{:S(2)}) collective-permute-start(bf16[512,1280]{1,0:T(8,128)(2,1)S(1)} %add_convert_fusion.20), channel_id=1, source_target_pairs={{0,8},{8,0},{16,24},{24,16},{1,9},{9,1},{17,25},{25,17},{2,10},{10... | collective-permute-start | bytes 3932168 | tf_op jit(solution)/shard_map/ppermute | solution.py:192
  570.6 189.0 %collective-permute-start.125 = (bf16[1280,2560]{1,0:T(8,128)(2,1)}, bf16[1280,2560]{1,0:T(8,128)(2,1)}, u32[]{:S(2)}, u32[]{:S(2)}) collective-permute-start(bf16[1280,2560]{1,0:T(8,128)(2,1)} %convolution_convert_fusion), channel_id=1, source_target_pairs={{1,0},{8,9},{17,16},{24,25},{3,2},{10,11},{19,18},{26,27},{5,4},{1... | collective-permute-start | bytes 19660808 | tf_op jit(solution)/shard_map/ppermute | solution.py:213
  624.4 152.0 %collective-permute-start.113 = (bf16[640,2560]{1,0:T(8,128)(2,1)}, bf16[640,2560]{1,0:T(8,128)(2,1)}, u32[]{:S(2)}, u32[]{:S(2)}) collective-permute-start(bf16[640,2560]{1,0:T(8,128)(2,1)} %convolution_convert_fusion.4), channel_id=1, source_target_pairs={{0,16},{8,24},{16,0},{24,8},{1,17},{9,25},{17,1},{25,9},{2,18},{10... | collective-permute-start | bytes 9830408 | tf_op jit(solution)/shard_map/ppermute | solution.py:198
  650.5 70.6 %collective-permute-start.43 = (bf16[512,1280]{1,0:T(8,128)(2,1)}, bf16[512,1280]{1,0:T(8,128)(2,1)}, u32[]{:S(2)}, u32[]{:S(2)}) collective-permute-start(bf16[512,1280]{1,0:T(8,128)(2,1)} %fusion.39), channel_id=1, source_target_pairs={{0,1},{1,0},{2,3},{3,2},{4,5},{5,4},{6,7},{7,6},{8,9},{9,8},{10,11... | collective-permute-start | bytes 3932168 | tf_op jit(solution)/shard_map/ppermute | solution.py:217
  707.4 62.9 %collective-permute-start.83 = (bf16[640,640]{1,0:T(8,128)(2,1)}, bf16[640,640]{1,0:T(8,128)(2,1)}, u32[]{:S(2)}, u32[]{:S(2)}) collective-permute-start(bf16[640,640]{1,0:T(8,128)(2,1)} %fusion.123), channel_id=1, source_target_pairs={{0,16},{8,24},{16,0},{24,8},{1,17},{9,25},{17,1},{25,9},{2,18},{10... | collective-permute-start | bytes 2457608 | tf_op jit(solution)/shard_map/ppermute | solution.py:198
  710.3 63.3 %collective-permute-start.77 = (bf16[640,640]{1,0:T(8,128)(2,1)}, bf16[640,640]{1,0:T(8,128)(2,1)S(1)}, u32[]{:S(2)}, u32[]{:S(2)}) collective-permute-start(bf16[640,640]{1,0:T(8,128)(2,1)} %convolution_convert_fusion.18), channel_id=1, source_target_pairs={{0,16},{8,24},{16,0},{24,8},{1,17},{9,25},{17,1},{25,9},{2,18},{10... | collective-permute-start | bytes 2457608 | tf_op jit(solution)/shard_map/ppermute | solution.py:198
  721.1 80.8 %collective-permute-start.89 = (bf16[1280,640]{1,0:T(8,128)(2,1)}, bf16[1280,640]{1,0:T(8,128)(2,1)}, u32[]{:S(2)}, u32[]{:S(2)}) collective-permute-start(bf16[1280,640]{1,0:T(8,128)(2,1)} %convolution_convert_fusion.10), channel_id=1, source_target_pairs={{1,0},{8,9},{17,16},{24,25},{3,2},{10,11},{19,18},{26,27},{5,4},{1... | collective-permute-start | bytes 4915208 | tf_op jit(solution)/shard_map/ppermute | solution.py:213
  759.7 47.7 %collective-permute-start.101 = (bf16[1280,640]{1,0:T(8,128)(2,1)}, bf16[1280,640]{1,0:T(8,128)(2,1)}, u32[]{:S(2)}, u32[]{:S(2)}) collective-permute-start(bf16[1280,640]{1,0:T(8,128)(2,1)} %convolution_convert_fusion.8), channel_id=1, source_target_pairs={{1,0},{8,9},{17,16},{24,25},{3,2},{10,11},{19,18},{26,27},{5,4},{1... | collective-permute-start | bytes 4915208 | tf_op jit(solution)/shard_map/ppermute | solution.py:213
  770.3 69.7 %collective-permute-start.48 = (bf16[1024,1280]{1,0:T(8,128)(2,1)}, bf16[1024,1280]{1,0:T(8,128)(2,1)}, u32[]{:S(2)}, u32[]{:S(2)}) collective-permute-start(bf16[1024,1280]{1,0:T(8,128)(2,1)} %slice.621), channel_id=1, source_target_pairs={{0,8},{8,0},{16,24},{24,16},{1,9},{9,1},{17,25},{25,17},{2,10},{10... | collective-permute-start | bytes 7864328 | tf_op jit(solution)/shard_map/ppermute | solution.py:192
  815.0 128.8 %collective-permute-start.47 = (bf16[512,1280]{1,0:T(8,128)(2,1)}, bf16[512,1280]{1,0:T(8,128)(2,1)}, u32[]{:S(2)}, u32[]{:S(2)}) collective-permute-start(bf16[512,1280]{1,0:T(8,128)(2,1)} %fusion.40), channel_id=1, source_target_pairs={{0,8},{8,0},{16,24},{24,16},{1,9},{9,1},{17,25},{25,17},{2,10},{10... | collective-permute-start | bytes 3932168 | tf_op jit(solution)/shard_map/ppermute | solution.py:192
  815.0 78.9 %collective-permute-start.114 = (bf16[640,2560]{1,0:T(8,128)(2,1)S(1)}, bf16[640,2560]{1,0:T(8,128)(2,1)S(1)}, u32[]{:S(2)}, u32[]{:S(2)}) collective-permute-start(bf16[640,2560]{1,0:T(8,128)(2,1)S(1)} %add_convert_fusion.5), channel_id=1, source_target_pairs={{1,0},{8,9},{17,16},{24,25},{3,2},{10,11},{19,18},{26,27},{5,4},{1... | collective-permute-start | bytes 9830408 | tf_op jit(solution)/shard_map/ppermute | solution.py:213
  832.9 95.3 %collective-permute-start.126 = (bf16[640,2560]{1,0:T(8,128)(2,1)}, bf16[640,2560]{1,0:T(8,128)(2,1)}, u32[]{:S(2)}, u32[]{:S(2)}) collective-permute-start(bf16[640,2560]{1,0:T(8,128)(2,1)} %dynamic-slice_bitcast_fusion), channel_id=1, source_target_pairs={{0,16},{9,25},{16,0},{25,9},{2,18},{11,27},{18,2},{27,11},{4,20},{... | collective-permute-start | bytes 9830408 | tf_op jit(solution)/shard_map/ppermute | solution.py:203
  895.6 47.3 %collective-permute-start.106 = (bf16[320,640]{1,0:T(8,128)(2,1)S(1)}, bf16[320,640]{1,0:T(8,128)(2,1)S(1)}, u32[]{:S(2)}, u32[]{:S(2)}) collective-permute-start(bf16[320,640]{1,0:T(8,128)(2,1)S(1)} %add_convert_fusion.33), channel_id=1, source_target_pairs={{2,0},{4,6},{3,1},{5,7},{10,8},{12,14},{11,9},{13,15},{18,16},{20,... | collective-permute-start | bytes 1228808 | tf_op jit(solution)/shard_map/ppermute | solution.py:358
  925.5 49.6 %collective-permute-start.115 = (bf16[320,2560]{1,0:T(8,128)(2,1)S(1)}, bf16[320,2560]{1,0:T(8,128)(2,1)}, u32[]{:S(2)}, u32[]{:S(2)}) collective-permute-start(bf16[320,2560]{1,0:T(8,128)(2,1)S(1)} %dynamic-slice_bitcast_fusion.4), channel_id=1, source_target_pairs={{0,8},{8,0},{16,24},{24,16},{1,9},{9,1},{17,25},{25,17},{2,10},{10... | collective-permute-start | bytes 4915208 | tf_op jit(solution)/shard_map/ppermute | solution.py:192
  975.3 61.0 %collective-permute-start.116 = (bf16[320,2560]{1,0:T(8,128)(2,1)S(1)}, bf16[320,2560]{1,0:T(8,128)(2,1)S(1)}, u32[]{:S(2)}, u32[]{:S(2)}) collective-permute-start(bf16[320,2560]{1,0:T(8,128)(2,1)S(1)} %bitcast_select_fusion.4), channel_id=1, source_target_pairs={{0,2},{6,4},{1,3},{7,5},{8,10},{14,12},{9,11},{15,13},{16,18},{22,... | collective-permute-start | bytes 4915208 | tf_op jit(solution)/shard_map/ppermute | solution.py:356
  977.2 70.5 %collective-permute-start.128 = (bf16[320,2560]{1,0:T(8,128)(2,1)S(1)}, bf16[320,2560]{1,0:T(8,128)(2,1)S(1)}, u32[]{:S(2)}, u32[]{:S(2)}) collective-permute-start(bf16[320,2560]{1,0:T(8,128)(2,1)S(1)} %bitcast_select_fusion.2), channel_id=1, source_target_pairs={{0,2},{6,4},{1,3},{7,5},{8,10},{14,12},{9,11},{15,13},{16,18},{22,... | collective-permute-start | bytes 4915208 | tf_op jit(solution)/shard_map/ppermute | solution.py:356
  1005.3 43.6 %collective-permute-start.52 = (bf16[512,1280]{1,0:T(8,128)(2,1)S(1)}, bf16[512,1280]{1,0:T(8,128)(2,1)}, u32[]{:S(2)}, u32[]{:S(2)}) collective-permute-start(bf16[512,1280]{1,0:T(8,128)(2,1)S(1)} %convolution_convert_fusion.14), channel_id=1, source_target_pairs={{0,8},{8,0},{16,24},{24,16},{1,9},{9,1},{17,25},{25,17},{2,10},{10... | collective-permute-start | bytes 3932168 | tf_op jit(solution)/shard_map/ppermute | solution.py:192
  1014.4 152.0 %collective-permute-start.107 = (bf16[640,2560]{1,0:T(8,128)(2,1)}, bf16[640,2560]{1,0:T(8,128)(2,1)}, u32[]{:S(2)}, u32[]{:S(2)}) collective-permute-start(bf16[640,2560]{1,0:T(8,128)(2,1)} %convolution_convert_fusion.6), channel_id=1, source_target_pairs={{0,16},{8,24},{16,0},{24,8},{1,17},{9,25},{17,1},{25,9},{2,18},{10... | collective-permute-start | bytes 9830408 | tf_op jit(solution)/shard_map/ppermute | solution.py:198
  1027.2 332.4 %collective-permute-start.119 = (bf16[1280,2560]{1,0:T(8,128)(2,1)}, bf16[1280,2560]{1,0:T(8,128)(2,1)}, u32[]{:S(2)}, u32[]{:S(2)}) collective-permute-start(bf16[1280,2560]{1,0:T(8,128)(2,1)} %convolution_convert_fusion.1), channel_id=1, source_target_pairs={{1,0},{8,9},{17,16},{24,25},{3,2},{10,11},{19,18},{26,27},{5,4},{1... | collective-permute-start | bytes 19660808 | tf_op jit(solution)/shard_map/ppermute | solution.py:213
  1058.8 122.0 %collective-permute-start.118 = (bf16[320,2560]{1,0:T(8,128)(2,1)}, bf16[320,2560]{1,0:T(8,128)(2,1)}, u32[]{:S(2)}, u32[]{:S(2)}) collective-permute-start(bf16[320,2560]{1,0:T(8,128)(2,1)} %add_convert_fusion.12), channel_id=1, source_target_pairs={{2,0},{4,6},{3,1},{5,7},{10,8},{12,14},{11,9},{13,15},{18,16},{20,... | collective-permute-start | bytes 4915208 | tf_op jit(solution)/shard_map/ppermute | solution.py:358
  1172.4 80.8 %collective-permute-start.130 = (bf16[320,2560]{1,0:T(8,128)(2,1)S(1)}, bf16[320,2560]{1,0:T(8,128)(2,1)S(1)}, u32[]{:S(2)}, u32[]{:S(2)}) collective-permute-start(bf16[320,2560]{1,0:T(8,128)(2,1)S(1)} %copy-done.52), channel_id=1, source_target_pairs={{2,0},{4,6},{3,1},{5,7},{10,8},{12,14},{11,9},{13,15},{18,16},{20,... | collective-permute-start | bytes 4915208 | tf_op jit(solution)/shard_map/ppermute | solution.py:358
  1180.8 124.8 %collective-permute-start.55 = (bf16[1024,1280]{1,0:T(8,128)(2,1)S(1)}, bf16[1024,1280]{1,0:T(8,128)(2,1)S(1)}, u32[]{:S(2)}, u32[]{:S(2)}) collective-permute-start(bf16[1024,1280]{1,0:T(8,128)(2,1)S(1)} %copy-done.69), channel_id=1, source_target_pairs={{0,8},{8,0},{16,24},{24,16},{1,9},{9,1},{17,25},{25,17},{2,10},{10... | collective-permute-start | bytes 7864328 | tf_op jit(solution)/shard_map/ppermute | solution.py:192
  1258.9 154.5 %collective-permute-start.54 = (bf16[512,1280]{1,0:T(8,128)(2,1)}, bf16[512,1280]{1,0:T(8,128)(2,1)}, u32[]{:S(2)}, u32[]{:S(2)}) collective-permute-start(bf16[512,1280]{1,0:T(8,128)(2,1)} %fusion.62), channel_id=1, source_target_pairs={{0,8},{8,0},{16,24},{24,16},{1,9},{9,1},{17,25},{25,17},{2,10},{10... | collective-permute-start | bytes 3932168 | tf_op jit(solution)/shard_map/ppermute | solution.py:192
  1300.5 72.0 %collective-permute-start.108 = (bf16[640,2560]{1,0:T(8,128)(2,1)}, bf16[640,2560]{1,0:T(8,128)(2,1)}, u32[]{:S(2)}, u32[]{:S(2)}) collective-permute-start(bf16[640,2560]{1,0:T(8,128)(2,1)} %add_convert_fusion.7), channel_id=1, source_target_pairs={{1,0},{8,9},{17,16},{24,25},{3,2},{10,11},{19,18},{26,27},{5,4},{1... | collective-permute-start | bytes 9830408 | tf_op jit(solution)/shard_map/ppermute | solution.py:213
  1359.5 48.6 %collective-permute-start.100 = (bf16[320,640]{1,0:T(8,128)(2,1)S(1)}, bf16[320,640]{1,0:T(8,128)(2,1)}, u32[]{:S(2)}, u32[]{:S(2)}) collective-permute-start(bf16[320,640]{1,0:T(8,128)(2,1)S(1)} %add_convert_fusion.35), channel_id=1, source_target_pairs={{2,0},{4,6},{3,1},{5,7},{10,8},{12,14},{11,9},{13,15},{18,16},{20,... | collective-permute-start | bytes 1228808 | tf_op jit(solution)/shard_map/ppermute | solution.py:358
  1372.5 68.5 %collective-permute-start.120 = (bf16[640,2560]{1,0:T(8,128)(2,1)S(1)}, bf16[640,2560]{1,0:T(8,128)(2,1)S(1)}, u32[]{:S(2)}, u32[]{:S(2)}) collective-permute-start(bf16[640,2560]{1,0:T(8,128)(2,1)S(1)} %dynamic-slice_bitcast_fusion.1), channel_id=1, source_target_pairs={{0,16},{9,25},{16,0},{25,9},{2,18},{11,27},{18,2},{27,11},{4,20},{... | collective-permute-start | bytes 9830408 | tf_op jit(solution)/shard_map/ppermute | solution.py:203
  1399.3 43.9 %collective-permute-start.109 = (bf16[320,2560]{1,0:T(8,128)(2,1)S(1)}, bf16[320,2560]{1,0:T(8,128)(2,1)S(1)}, u32[]{:S(2)}, u32[]{:S(2)}) collective-permute-start(bf16[320,2560]{1,0:T(8,128)(2,1)S(1)} %dynamic-slice_bitcast_fusion.5), channel_id=1, source_target_pairs={{0,8},{8,0},{16,24},{24,16},{1,9},{9,1},{17,25},{25,17},{2,10},{10... | collective-permute-start | bytes 4915208 | tf_op jit(solution)/shard_map/ppermute | solution.py:192
  1440.9 137.3 %collective-permute-start.58 = (bf16[512,1280]{1,0:T(8,128)(2,1)}, bf16[512,1280]{1,0:T(8,128)(2,1)}, u32[]{:S(2)}, u32[]{:S(2)}) collective-permute-start(bf16[512,1280]{1,0:T(8,128)(2,1)} %get-tuple-element.86), channel_id=1, source_target_pairs={{0,1},{1,0},{2,3},{3,2},{4,5},{5,4},{6,7},{7,6},{8,9},{9,8},{10,11... | collective-permute-start | bytes 3932168 | tf_op jit(solution)/shard_map/ppermute | solution.py:217
  1449.4 122.5 %collective-permute-start.122 = (bf16[320,2560]{1,0:T(8,128)(2,1)}, bf16[320,2560]{1,0:T(8,128)(2,1)}, u32[]{:S(2)}, u32[]{:S(2)}) collective-permute-start(bf16[320,2560]{1,0:T(8,128)(2,1)} %bitcast_select_fusion.3), channel_id=1, source_target_pairs={{0,2},{6,4},{1,3},{7,5},{8,10},{14,12},{9,11},{15,13},{16,18},{22,... | collective-permute-start | bytes 4915208 | tf_op jit(solution)/shard_map/ppermute | solution.py:356
  1485.4 91.1 %collective-permute-start.111 = (bf16[320,2560]{1,0:T(8,128)(2,1)S(1)}, bf16[320,2560]{1,0:T(8,128)(2,1)S(1)}, u32[]{:S(2)}, u32[]{:S(2)}) collective-permute-start(bf16[320,2560]{1,0:T(8,128)(2,1)S(1)} %add_convert_fusion.15), channel_id=1, source_target_pairs={{2,4},{4,2},{3,5},{5,3},{10,12},{12,10},{11,13},{13,11},{18,20},{2... | collective-permute-start | bytes 4915208 | tf_op jit(solution)/shard_map/ppermute | solution.py:357
  1580.2 71.7 %collective-permute-start.124 = (bf16[320,2560]{1,0:T(8,128)(2,1)S(1)}, bf16[320,2560]{1,0:T(8,128)(2,1)S(1)}, u32[]{:S(2)}, u32[]{:S(2)}) collective-permute-start(bf16[320,2560]{1,0:T(8,128)(2,1)S(1)} %add_convert_fusion.10), channel_id=1, source_target_pairs={{2,0},{4,6},{3,1},{5,7},{10,8},{12,14},{11,9},{13,15},{18,16},{20,... | collective-permute-start | bytes 4915208 | tf_op jit(solution)/shard_map/ppermute | solution.py:358
  (252 other events, 5263.7 us)
Sparse Core Ops, SparseCore 0:
  1448.1 121.5 all-reduce.2

commit v2 on v1

v2 whole, which is shorter than its diff:
```python
import jax
import jax.numpy as jnp
from jax import lax
from jax.experimental import pallas as pl
from jax.experimental.pallas import tpu as pltpu
from jax.sharding import PartitionSpec as P

HD = 64
WINDOW = 1024
TILE = 256
masked_score = -1e30


def contract(left_side, right_side, left_dim, right_dim):
    return lax.dot_general(
        left_side, right_side, (((left_dim,), (right_dim,)), ((), ())),
        preferred_element_type=jnp.float32,
    )


def half_mask(shape, half):
    lane = lax.broadcasted_iota(jnp.int32, shape, 1)
    return (lane < HD) if half == 0 else (lane >= HD)


PAIR = 2 * HD


def forward_kernel(qkv_ref, low_ref, mixed_ref, total_ref):
    block_len = mixed_ref.shape[1]
    first = qkv_ref.shape[1] - block_len
    span = WINDOW + TILE
    eye = lax.broadcasted_iota(jnp.int32, (TILE, TILE), 0) == lax.broadcasted_iota(
        jnp.int32, (TILE, TILE), 1
    )
    for block in range(block_len // TILE):
        rows = pl.ds(block * TILE, TILE)
        window = pl.ds(block * TILE, span)
        queries = qkv_ref[0, pl.ds(first + block * TILE, TILE), :PAIR]
        queries = queries * jnp.asarray(HD ** (-0.5), jnp.bfloat16)
        keys = qkv_ref[0, window, PAIR : 2 * PAIR]
        values = qkv_ref[0, window, 2 * PAIR :]
        low_pos = low_ref[0, rows, :] - block * TILE
        key_pos = lax.broadcasted_iota(jnp.int32, (TILE, span), 1)
        query_pos = lax.broadcasted_iota(jnp.int32, (TILE, TILE), 0) + WINDOW
        allowed = key_pos >= low_pos
        causal = key_pos[:, WINDOW:] <= query_pos
        mixed = jnp.zeros((TILE, 2 * HD), jnp.float32)
        for half in range(2):
            scores = contract(
                jnp.where(half_mask(queries.shape, half), queries, 0), keys, 1, 1
            )
            early = jnp.where(allowed[:, :WINDOW], scores[:, :WINDOW], masked_score)
            late = jnp.where(allowed[:, WINDOW:] & causal, scores[:, WINDOW:], masked_score)
            top_score = jnp.maximum(
                jnp.max(early, axis=1, keepdims=True), jnp.max(late, axis=1, keepdims=True)
            )
            early = jnp.exp(early - top_score)
            late = jnp.exp(late - top_score)
            row_total = jnp.sum(early, axis=1, keepdims=True) + jnp.sum(
                late, axis=1, keepdims=True
            )
            part = contract(early.astype(jnp.bfloat16), values[:WINDOW], 1, 0) + contract(
                late.astype(jnp.bfloat16), values[WINDOW:], 1, 0
            )
            part = part * (1.0 / row_total)
            mixed = jnp.where(half_mask(mixed.shape, half), part, mixed)
            log_total = top_score + jnp.log(row_total)
            total_ref[0, 0, half : half + 1, rows] = jnp.sum(
                jnp.where(eye, log_total, 0.0), axis=0, keepdims=True
            )
        mixed_ref[0, rows, :] = mixed.astype(jnp.bfloat16)


def attention_forward(packed, low_pos):
    groups, key_len, width = packed.shape
    block_len = low_pos.shape[1]
    pairs = width // (3 * PAIR)
    pick = lambda seq, pair: (seq, 0, pair)
    return pl.pallas_call(
        forward_kernel,
        grid=(groups, pairs),
        in_specs=[
            pl.BlockSpec((1, key_len, 3 * PAIR), pick),
            pl.BlockSpec((1, block_len, 1), lambda seq, pair: (seq, 0, 0)),
        ],
        out_specs=[
            pl.BlockSpec((1, block_len, PAIR), pick),
            pl.BlockSpec((1, 1, 2, block_len), lambda seq, pair: (seq, pair, 0, 0)),
        ],
        out_shape=[
            jax.ShapeDtypeStruct((groups, block_len, pairs * PAIR), jnp.bfloat16),
            jax.ShapeDtypeStruct((groups, pairs, 2, block_len), jnp.float32),
        ],
        compiler_params=pltpu.CompilerParams(vmem_limit_bytes=40 << 20),
        cost_estimate=pl.CostEstimate(
            flops=16 * groups * pairs * block_len * (WINDOW + TILE) * HD,
            bytes_accessed=2 * groups * width * key_len,
            transcendentals=2 * groups * pairs * block_len * (WINDOW + TILE),
        ),
    )(packed, low_pos[:, :, None])


def backward_kernel(qkv_ref, mixed_ref, grad_ref, total_ref, low_ref, out_ref, gk_sum, gv_sum):
    block_len = mixed_ref.shape[1]
    first = qkv_ref.shape[1] - block_len
    span = WINDOW + TILE
    scale = HD ** (-0.5)
    gk_sum[...] = jnp.zeros_like(gk_sum)
    gv_sum[...] = jnp.zeros_like(gv_sum)
    eye = lax.broadcasted_iota(jnp.int32, (TILE, TILE), 0) == lax.broadcasted_iota(
        jnp.int32, (TILE, TILE), 1
    )
    for block in range(block_len // TILE):
        rows = pl.ds(block * TILE, TILE)
        window = pl.ds(block * TILE, span)
        queries = qkv_ref[0, pl.ds(first + block * TILE, TILE), :PAIR]
        queries = queries * jnp.asarray(scale, jnp.bfloat16)
        keys = qkv_ref[0, window, PAIR : 2 * PAIR]
        values = qkv_ref[0, window, 2 * PAIR :]
        grads = grad_ref[0, rows, :]
        product = grads.astype(jnp.float32) * mixed_ref[0, rows, :].astype(jnp.float32)
        low_pos = low_ref[0, :, rows] - block * TILE
        key_pos = lax.broadcasted_iota(jnp.int32, (span, TILE), 0)
        query_pos = lax.broadcasted_iota(jnp.int32, (TILE, TILE), 1) + WINDOW
        allowed = key_pos >= low_pos
        late_allowed = allowed[WINDOW:] & (key_pos[WINDOW:] <= query_pos)
        keys_t = jnp.transpose(keys)
        gq_parts = []
        for half in range(2):
            mask = half_mask(queries.shape, half)
            q_half = jnp.where(mask, queries, 0)
            g_half = jnp.where(mask, grads, 0)
            delta = jnp.sum(jnp.where(mask, product, 0.0), axis=1, keepdims=True)
            delta = jnp.sum(jnp.where(eye, delta, 0.0), axis=0, keepdims=True)
            log_total = total_ref[0, 0, half : half + 1, rows]
            scores = contract(keys, q_half, 1, 1)
            probs = jnp.concatenate(
                [
                    jnp.where(allowed[:WINDOW], jnp.exp(scores[:WINDOW] - log_total), 0.0),
                    jnp.where(late_allowed, jnp.exp(scores[WINDOW:] - log_total), 0.0),
                ]
            )
            grad_probs = contract(values, g_half, 1, 1)
            grad_scores = (probs * (grad_probs - delta)).astype(jnp.bfloat16)
            gv_sum[window, :] += contract(probs.astype(jnp.bfloat16), g_half, 1, 0)
            gk_sum[window, :] += contract(grad_scores, q_half, 1, 0)
            gq_parts.append(contract(keys_t[half * HD : (half + 1) * HD], grad_scores, 1, 0))
        gq = jnp.transpose(jnp.concatenate(gq_parts)) * scale
        out_ref[0, pl.ds(first + block * TILE, TILE), :PAIR] = gq.astype(jnp.bfloat16)
    out_ref[0, :first, :PAIR] = jnp.zeros((first, PAIR), jnp.bfloat16)
    out_ref[0, :, PAIR : 2 * PAIR] = gk_sum[...].astype(jnp.bfloat16)
    out_ref[0, :, 2 * PAIR :] = gv_sum[...].astype(jnp.bfloat16)


def attention_backward(packed, mixed, grads, log_total, low_pos):
    groups, key_len, width = packed.shape
    block_len = mixed.shape[1]
    pairs = width // (3 * PAIR)
    pick = lambda seq, pair: (seq, 0, pair)
    row_spec = pl.BlockSpec((1, block_len, PAIR), pick)
    packed_spec = pl.BlockSpec((1, key_len, 3 * PAIR), pick)
    return pl.pallas_call(
        backward_kernel,
        grid=(groups, pairs),
        in_specs=[
            packed_spec, row_spec, row_spec,
            pl.BlockSpec((1, 1, 2, block_len), lambda seq, pair: (seq, pair, 0, 0)),
            pl.BlockSpec((1, 1, block_len), lambda seq, pair: (seq, 0, 0)),
        ],
        out_specs=packed_spec,
        out_shape=jax.ShapeDtypeStruct(packed.shape, jnp.bfloat16),
        scratch_shapes=[
            pltpu.VMEM((key_len, PAIR), jnp.float32),
            pltpu.VMEM((key_len, PAIR), jnp.float32),
        ],
        compiler_params=pltpu.CompilerParams(vmem_limit_bytes=40 << 20),
        cost_estimate=pl.CostEstimate(
            flops=40 * groups * pairs * block_len * (WINDOW + TILE) * HD,
            bytes_accessed=4 * groups * width * key_len,
            transcendentals=2 * groups * pairs * block_len * (WINDOW + TILE),
        ),
    )(packed, mixed, grads, log_total, low_pos[:, None, :])


norm_eps = 1e-05


def mate(value):
    count = lax.axis_size("shard")
    return lax.ppermute(value, "shard", [(i, i ^ 1) for i in range(count)])


def chip_shift(value, steps, half_only=False):
    count = lax.axis_size("shard")
    if not half_only:
        return lax.ppermute(value, "shard", [(i, (i + 2 * steps) % count) for i in range(count)])
    pairs = [(i * 2 + i % 2, ((i + 2 * steps) % count) * 2 + i % 2) for i in range(count)]
    return lax.ppermute(value, ("shard", "tp"), pairs)


def cross_out(value):
    pairs = [(i * 2 + i % 2, i * 2 + 1 - i % 2) for i in range(lax.axis_size("shard"))]
    return lax.ppermute(value, ("shard", "tp"), pairs)


def cross_home(value):
    pairs = [(i * 2 + 1 - i % 2, i * 2 + i % 2) for i in range(lax.axis_size("shard"))]
    return lax.ppermute(value, ("shard", "tp"), pairs)


def other_tp(value):
    return lax.ppermute(value, "tp", [(0, 1), (1, 0)])


def onward(value):
    count = lax.axis_size("ctx")
    return lax.ppermute(value, "ctx", [(i, i + 1) for i in range(count - 1)])


def backward_step(value):
    count = lax.axis_size("ctx")
    return lax.ppermute(value, "ctx", [(i + 1, i) for i in range(count - 1)])


class Place:
    def __init__(self):
        shard = lax.axis_index("shard")
        self.shard = shard
        self.chips = lax.axis_size("shard") // 2
        self.chip = shard // 2
        self.core = shard % 2
        self.tp = lax.axis_index("tp")
        self.ctx = lax.axis_index("ctx")
        self.home = self.core == self.tp


class Flow:
    def __init__(self, steps):
        self.steps = steps
        self.result = None
        self.pending = next(steps)

    def go_on(self, arrived):
        try:
            self.pending = self.steps.send(arrived)
        except StopIteration as stop:
            self.pending, self.result = None, stop.value


def drain(*flows):
    while any(flow.pending is not None for flow in flows):
        for flow in flows:
            if flow.pending is not None:
                flow.go_on(flow.pending)
    return [flow.result for flow in flows]


def pump(value, *flows):
    flows = [flow for flow in flows if flow is not None and flow.pending is not None]
    value, arrived = lax.optimization_barrier((value, [flow.pending for flow in flows]))
    for flow, piece in zip(flows, arrived):
        flow.go_on(piece)
    return value


def ordered(own, others, position, axis=0):
    if len(others) == 1:
        return jnp.where(
            position == 0,
            jnp.stack([own, others[0]], axis=axis),
            jnp.stack([others[0], own], axis=axis),
        )
    count = len(others) + 1
    whole = jnp.stack([own] + others, axis=axis)
    return jnp.take(whole, (position - jnp.arange(count)) % count, axis=axis)


def gather_core_first(piece, place):
    other = yield mate(piece)
    both = ordered(piece, [other], place.core)
    across = yield cross_out(both)
    pair = jnp.where(place.home, both, across)
    others = yield [chip_shift(pair, steps) for steps in range(1, place.chips)]
    return ordered(pair, others, place.chip).reshape(-1, piece.shape[1])


def gather_chip_first(piece, place):
    others = yield [chip_shift(piece, steps) for steps in range(1, place.chips)]
    own = ordered(piece, others, place.chip)
    other = yield mate(own)
    both = ordered(own, [other], place.core, 1)
    across = yield cross_out(both)
    return jnp.where(place.home, both, across).reshape(-1, piece.shape[1])


def gather_small(value, place):
    if place.chips != 2:
        return lax.all_gather(value, "shard", axis=1, tiled=True)
    near, far, last = [
        lax.ppermute(value, "shard", [(i, i ^ flip) for i in range(4)]) for flip in (1, 2, 3)
    ]
    pair = ordered(value, [near], place.core, 1)
    far_pair = ordered(far, [last], place.core, 1)
    return ordered(pair, [far_pair], place.chip, 1).reshape(value.shape[0], -1)


def dot_f32(left_side, right_side):
    return jnp.dot(left_side, right_side, preferred_element_type=jnp.float32)


def dot_first(left_side, right_side):
    return contract(left_side, right_side, 0, 0)


def dot_second(left_side, right_side):
    return contract(left_side, right_side, 1, 1)


def norm_forward(hidden, norm_gain, norm_shift):
    row_mean = jnp.mean(hidden, axis=-1, keepdims=True)
    centred = hidden - row_mean
    variance = jnp.mean(centred * centred, axis=-1, keepdims=True)
    inv_std = lax.rsqrt(variance + norm_eps)
    norm_hat = centred * inv_std
    return ((norm_hat * norm_gain + norm_shift).astype(jnp.bfloat16), norm_hat, inv_std)


def norm_backward(grad_out, norm_hat, inv_std, norm_gain):
    scaled = grad_out * norm_gain
    mean_one = jnp.mean(scaled, axis=-1, keepdims=True)
    mean_two = jnp.mean(scaled * norm_hat, axis=-1, keepdims=True)
    grad_input = inv_std * (scaled - mean_one - norm_hat * mean_two)
    return (grad_input, jnp.sum(grad_out * norm_hat, axis=0), jnp.sum(grad_out, axis=0))


def wide(value):
    return value.astype(jnp.float32)


def narrow(value):
    return value.astype(jnp.bfloat16)


def pick_block(value, index, count):
    size = value.shape[0] // count
    return lax.dynamic_slice_in_dim(value, index * size, size, 0)


def scatter_chip_first(left_side, right_side, place):
    features = left_side.shape[1] // place.chips

    def part(steps):
        start = ((place.chip + steps) % place.chips) * features
        columns = lax.dynamic_slice_in_dim(left_side, start, features, 1)
        return narrow(dot_first(columns, right_side))

    sent = [chip_shift(part(steps), steps) for steps in range(1, place.chips)]
    own = part(0)
    sent = yield sent
    total = wide(own)
    for piece in sent:
        total = total + wide(piece)
    total = narrow(total)
    across = yield cross_home(total)

    def rows(core):
        return narrow(wide(pick_block(total, core, 2)) + wide(pick_block(across, core, 2)))

    other = yield mate(rows(1 - place.core))
    return jnp.where(place.home, rows(place.core), other)


def scatter_tp_first(left_side, right_side, place):
    whole = narrow(dot_first(left_side, right_side))
    across = yield cross_home(whole)

    def part(steps):
        index = (place.chip + steps) % place.chips
        return wide(pick_block(whole, index, place.chips)) + wide(
            pick_block(across, index, place.chips)
        )

    sent = yield [
        chip_shift(narrow(part(steps)), steps, True) for steps in range(1, place.chips)
    ]

    def rows(core):
        total = pick_block(part(0), core, 2)
        for piece in sent:
            total = total + wide(pick_block(piece, core, 2))
        return narrow(total)

    other = yield mate(rows(1 - place.core))
    return jnp.where(place.home, rows(place.core), other)


def ctx_total(share, place):
    if lax.axis_size("ctx") != 4:
        return (yield lax.psum(share, "ctx"))
    outer = (place.ctx == 0) | (place.ctx == 3)
    kind = share.dtype
    add = lambda first, second: (wide(first) + wide(second)).astype(kind)
    came = yield lax.ppermute(share, "ctx", [(0, 1), (3, 2)])
    inner = add(share, came)
    came = yield lax.ppermute(inner, "ctx", [(1, 2), (2, 1)])
    total = add(inner, came)
    back = yield lax.ppermute(total, "ctx", [(1, 0), (2, 3)])
    return jnp.where(outer, back, total)


def scatter_total(steps, place):
    share = yield from steps
    return (yield from ctx_total(share, place))


def small_total(value, place):
    if place.chips != 2 or lax.axis_size("ctx") != 4:
        return (yield lax.psum(value, ("shard", "ctx", "tp")))
    came = yield mate(value)
    value = value + came
    came = yield chip_shift(value, 1)
    value = value + came
    came = yield other_tp(value)
    return (yield from ctx_total(value + came, place))


def core_sum(own_part, mate_part):
    return own_part + wide(mate(narrow(mate_part)))


def gelu_slope(pre_act, grad_act):
    pullback = jax.vjp(lambda values: jax.nn.gelu(values, approximate=True), pre_act)[1]
    return pullback(grad_act)[0]


def pair_major(value):
    lead = value.shape[1:-1]
    pairs = value.shape[-1] // PAIR
    value = value.reshape((3,) + lead + (pairs, PAIR))
    return jnp.moveaxis(value, 0, -2).reshape(lead + (3 * pairs * PAIR,))


def from_pair_major(value):
    lead = value.shape[:-1]
    pairs = value.shape[-1] // (3 * PAIR)
    value = jnp.moveaxis(value.reshape(lead + (pairs, 3, PAIR)), -2, 0)
    return value.reshape((3,) + lead + (pairs * PAIR,))


def per_device(
    tokens,
    cotangent,
    doc_lengths,
    norm_gains,
    norm_biases,
    qkv_weight,
    qv_bias,
    proj_weight,
    fc_weight,
    fc_bias,
    out_weight,
):
    place = Place()
    block_len, model_width = tokens.shape[1:]
    shard_rows = qkv_weight.shape[2]
    half_width = qkv_weight.shape[3]
    layer_count = qkv_weight.shape[0]
    reach = WINDOW // block_len
    key_len = (reach + 1) * block_len
    last = reach * block_len

    def my_seq(value):
        return lax.dynamic_index_in_dim(value, place.tp, 0, False)

    def both_seqs(own, other):
        return ordered(own, [other], place.tp)

    pieces = [
        (
            pair_major(qkv_weight[layer]),
            jnp.transpose(proj_weight[layer]),
            fc_weight[layer],
            jnp.transpose(out_weight[layer]),
        )
        for layer in range(layer_count)
    ]

    def attn_flows(layer):
        return (
            Flow(gather_core_first(pieces[layer][0], place)),
            Flow(gather_chip_first(pieces[layer][1], place)),
        )

    def mlp_flows(layer):
        return (
            Flow(gather_core_first(pieces[layer][2], place)),
            Flow(gather_chip_first(pieces[layer][3], place)),
        )

    own_tokens = my_seq(tokens)
    flow_qkv, flow_proj = attn_flows(0)
    step_value = own_tokens
    halo = []
    for _ in range(reach):
        step_value = onward(step_value)
        halo.insert(0, step_value)
    vectors = jnp.concatenate([norm_gains, norm_biases], axis=1)
    vectors = wide(gather_small(vectors.reshape(-1, vectors.shape[2]), place))
    vectors = vectors.reshape(layer_count, 6, model_width)
    biases = jnp.concatenate([qv_bias.reshape(layer_count, -1), fc_bias], axis=1)
    biases = wide(jnp.where(place.home, biases, other_tp(biases)))
    lengths = my_seq(doc_lengths)
    lengths = jnp.stack([lengths, mate(lengths)])
    pump((), flow_qkv)
    pump((), flow_proj)
    pieces = pump(pieces, flow_qkv, flow_proj)
    flow_fc, flow_out = mlp_flows(0)
    pump((), flow_fc)

    doc_ends = jnp.cumsum(lengths, axis=1)
    first_pos = place.ctx * block_len
    query_pos = first_pos + jnp.arange(block_len, dtype=jnp.int32)
    started = doc_ends[:, None, :] <= query_pos[None, :, None]
    doc_start = jnp.max(jnp.where(started, doc_ends[:, None, :], 0), axis=-1)
    low_pos = jnp.maximum(doc_start, query_pos[None, :] - (WINDOW - 1))
    low_pos = (low_pos - first_pos + last).astype(jnp.int32)

    hidden = wide(own_tokens)
    stash = []
    weights = []
    for layer in range(layer_count):
        gains, shifts = vectors[layer, :2], vectors[layer, 2:]
        bias_q, bias_v = biases[layer, :half_width], biases[layer, half_width : 2 * half_width]
        bias_qkv = pair_major(jnp.stack([bias_q, jnp.zeros_like(bias_q), bias_v])[:, None])
        bias_fc = biases[layer, 2 * half_width :]
        attn_in, hat_attn, inv_attn = norm_forward(hidden, gains[0], shifts[0])
        own_near = [attn_in]
        if layer == 0:
            for part in reversed(halo):
                own_near.insert(0, norm_forward(wide(part), gains[0], shifts[0])[0])
            own_near = jnp.concatenate(own_near)
            near = jnp.concatenate([own_near, mate(own_near)])
        else:
            step_value = attn_in
            mate_near = [mate(attn_in)]
            for _ in range(reach):
                step_value = onward(step_value)
                own_near.insert(0, step_value)
                mate_near.insert(0, mate(step_value))
            near = jnp.concatenate(own_near + mate_near)
        near = pump(near, flow_qkv, flow_proj)
        w_qkv, w_proj_t = flow_qkv.result, flow_proj.result
        packed = narrow(dot_f32(near, w_qkv) + bias_qkv).reshape(2, key_len, -1)
        packed = pump(packed, flow_fc, flow_out)
        packed = pump(packed, flow_out)
        mixed, log_total = attention_forward(packed, low_pos)
        if layer + 1 < layer_count:
            mixed, pieces = lax.optimization_barrier((mixed, pieces))
            flow_qkv, flow_proj = attn_flows(layer + 1)
        mate_part = dot_second(mixed[1], w_proj_t)
        own_part = dot_second(mixed[0], w_proj_t)
        middle = hidden + core_sum(own_part, mate_part) + shifts[1]
        mlp_own, hat_mlp, inv_mlp = norm_forward(middle, gains[1], shifts[2])
        if layer + 1 < layer_count:
            mlp_own = pump(mlp_own, flow_qkv)
        mlp_in = jnp.concatenate([mlp_own, mate(mlp_own)])
        mlp_in = pump(mlp_in, flow_fc)
        w_fc = flow_fc.result
        pre_act = dot_f32(mlp_in, w_fc) + bias_fc
        activated = narrow(jax.nn.gelu(pre_act, approximate=True))
        activated = pump(activated, flow_out)
        w_out_t = flow_out.result
        if layer + 1 < layer_count:
            activated = pump(activated, flow_qkv, flow_proj)
            activated, pieces = lax.optimization_barrier((activated, pieces))
            flow_fc, flow_out = mlp_flows(layer + 1)
        mate_part = dot_second(activated[block_len:], w_out_t)
        own_part = dot_second(activated[:block_len], w_out_t)
        hidden = middle + core_sum(own_part, mate_part) + shifts[3]
        if layer + 1 < layer_count:
            hidden = pump(hidden, flow_fc, flow_proj)
        weights.append((w_qkv, w_proj_t, w_fc, w_out_t))
        stash.append(
            (near, hat_attn, inv_attn, packed, mixed, log_total, hat_mlp, inv_mlp, mlp_in,
             pre_act, activated)
        )

    own_output = narrow(hidden)
    output = both_seqs(own_output, other_tp(own_output))

    grad_hidden = wide(my_seq(cotangent))
    old = {}
    for layer in reversed(range(layer_count)):
        near, hat_attn, inv_attn, packed, mixed, log_total = stash[layer][:6]
        hat_mlp, inv_mlp, mlp_in, pre_act, activated = stash[layer][6:]
        gains = vectors[layer, :2]
        w_qkv, w_proj_t, w_fc, w_out_t = weights[layer]
        final = layer == 0

        def reduced(steps):
            return Flow(scatter_total(steps, place) if final else steps)

        grad_out_bias = jnp.sum(grad_hidden, axis=0)
        grad_low = narrow(grad_hidden)
        grad_low = jnp.concatenate([grad_low, mate(grad_low)])
        flow_out = reduced(scatter_tp_first(grad_low, activated, place))
        grad_pre = narrow(gelu_slope(pre_act, dot_f32(grad_low, w_out_t)))
        grad_pre = pump(grad_pre, old.get("qkv"))
        grad_fc_bias = jnp.sum(wide(grad_pre), axis=0)
        mate_part = dot_second(grad_pre[block_len:], w_fc)
        own_part = dot_second(grad_pre[:block_len], w_fc)
        flow_fc = reduced(scatter_chip_first(mlp_in, grad_pre, place))
        grad_norm_in = core_sum(own_part, mate_part)
        if final:
            share = jnp.concatenate(drain(old["fc"], old["out"]), axis=1)
            old["mlp_ctx"] = Flow(ctx_total(share, place))
        grad_norm_in = pump(grad_norm_in, old.get("qkv"), old.get("small"))
        grad_from_mlp, grad_gain_mlp, grad_shift_mlp = norm_backward(
            grad_norm_in, hat_mlp, inv_mlp, gains[1]
        )
        grad_middle = grad_hidden + grad_from_mlp
        grad_proj_bias = jnp.sum(grad_middle, axis=0)
        grad_low = narrow(grad_middle)
        grad_low = jnp.concatenate([grad_low, mate(grad_low)])
        grad_low = pump(grad_low, old.get("qkv"), old.get("small"))
        if final:
            share = jnp.concatenate(drain(old["qkv"], old["proj"]), axis=1)
            old["attn_ctx"] = Flow(ctx_total(share, place))
        grad_mixed = narrow(dot_f32(grad_low, w_proj_t)).reshape(mixed.shape)
        flow_proj = reduced(
            scatter_tp_first(grad_low, mixed.reshape(2 * block_len, half_width), place)
        )
        grad_mixed = pump(grad_mixed, flow_out, old.get("small"))
        grad_packed = attention_backward(packed, mixed, grad_mixed, log_total, low_pos)
        grad_packed = pump(
            grad_packed, flow_out, flow_fc, flow_proj, old.get("mlp_ctx"), old.get("small")
        )
        grad_packed = pump(grad_packed, flow_out)
        mate_part = dot_second(grad_packed[1], w_qkv)
        own_part = dot_second(grad_packed[0], w_qkv)
        grad_near = core_sum(own_part, mate_part)
        far_total, grad_attn_in = grad_near[:last], grad_near[last:]
        carried = backward_step(narrow(far_total[:block_len]))
        rows = grad_packed.reshape(2 * key_len, -1)
        third = rows.shape[1] // 3
        if final:
            flows_qkv = [
                reduced(scatter_chip_first(near, rows[:, :third], place)),
                reduced(scatter_tp_first(near, rows[:, third : 2 * third], place)),
                reduced(scatter_chip_first(near, rows[:, 2 * third :], place)),
            ]
        else:
            flows_qkv = [reduced(scatter_chip_first(near, rows, place))]
        for step in range(1, reach + 1):
            if step == 1:
                carried = pump(
                    carried, flow_proj, flow_fc, old.get("attn_ctx"), old.get("small"),
                    *((flow_out,) if final else ()),
                )
            if step == 2:
                carried = pump(
                    carried, flow_fc, flow_proj, old.get("mlp_ctx"),
                    *(flows_qkv if final else ()),
                )
            arrived = wide(carried)
            if step < reach:
                section = far_total[step * block_len : (step + 1) * block_len]
                carried = backward_step(narrow(arrived + section))
            else:
                grad_attn_in = grad_attn_in + arrived
        grad_from_attn, grad_gain_attn, grad_shift_attn = norm_backward(
            grad_attn_in, hat_attn, inv_attn, gains[0]
        )
        grad_hidden = grad_middle + grad_from_attn
        grad_bias = jnp.sum(wide(rows), axis=0).reshape(-1, 3, PAIR)
        halves = jnp.concatenate(
            [grad_bias[:, 0].reshape(-1), grad_bias[:, 2].reshape(-1), grad_fc_bias]
        )
        empty = jnp.zeros_like(halves)
        small = jnp.concatenate(
            [
                grad_gain_attn, grad_gain_mlp,
                grad_shift_attn, grad_proj_bias, grad_shift_mlp, grad_out_bias,
                jnp.where(place.core == 0, halves, empty),
                jnp.where(place.core == 1, halves, empty),
            ]
        )
        flow_small = Flow(small_total(small, place))
        if not final:
            old = {
                "qkv": flows_qkv[0], "proj": flow_proj, "fc": flow_fc, "out": flow_out,
                "small": flow_small,
            }

    far_grad = wide(other_tp(narrow(grad_hidden)))
    token_grad = both_seqs(grad_hidden, far_grad)
    mlp_old, attn_old, small_old, out_new, fc_new, proj_new, small_new, *qkv_new = drain(
        old["mlp_ctx"], old["attn_ctx"], old["small"], flow_out, flow_fc, flow_proj, flow_small,
        *flows_qkv,
    )
    fc_width = fc_weight.shape[2]
    qkv_new = jnp.concatenate(qkv_new, axis=1)
    small = jnp.stack([small_new, small_old])
    split = 6 * model_width
    norms = small[:, :split].reshape(layer_count, 6, model_width)
    norms = lax.dynamic_slice_in_dim(norms, place.shard * shard_rows, shard_rows, 2)
    halves = small[:, split:].reshape(layer_count, 2, -1)
    halves = lax.dynamic_index_in_dim(halves, place.tp, 1, False)
    return (
        output,
        token_grad,
        norms[:, :2],
        norms[:, 2:],
        jnp.stack([from_pair_major(wide(v)) for v in (qkv_new, attn_old[:, : 3 * half_width])]),
        halves[:, : 2 * half_width].reshape(layer_count, 2, half_width),
        jnp.stack([jnp.transpose(wide(v)) for v in (proj_new, attn_old[:, 3 * half_width :])]),
        jnp.stack([wide(v) for v in (fc_new, mlp_old[:, :fc_width])]),
        halves[:, 2 * half_width :],
        jnp.stack([jnp.transpose(wide(v)) for v in (out_new, mlp_old[:, fc_width:])]),
    )


def solution(mesh):
    placed = (
        P("shard", "ctx", None),
        P("shard", "ctx", None),
        P("shard", None),
        P(None, None, "shard"),
        P(None, None, "shard"),
        P(None, None, "shard", "tp"),
        P(None, None, "tp"),
        P(None, "tp", "shard"),
        P(None, "shard", "tp"),
        P(None, "tp"),
        P(None, "tp", "shard"),
    )
    return jax.shard_map(
        per_device,
        mesh=mesh,
        in_specs=placed,
        out_specs=(
            P("shard", "ctx", None),
            P("shard", "ctx", None),
            P(None, None, "shard"),
            P(None, None, "shard"),
            P(None, None, "shard", "tp"),
            P(None, None, "tp"),
            P(None, "tp", "shard"),
            P(None, "shard", "tp"),
            P(None, "tp"),
            P(None, "tp", "shard"),
        ),
        check_vma=False,
    )
```

time: 1670 us -> 1840 us (1.10)
  other arithmetic: 174 us -> 346 us
  local copies, waits for them, and re-layouts: 51.1 us -> 139 us
  waiting for transfers between devices: 657 us -> 602 us
  blocking collectives: 20.4 us -> 0 us
    psum x1 -> x0, waiting for transfers between devices: 83.4 us -> none  [per_device(): small = lax.psum(small, ('shard', 'ctx', 'tp'))]
    select_n x36 -> x47, other arithmetic: 45.6 us -> 122 us  [the longest x26 88.1 us: ordered(): jnp.where(position == 0, jnp.stack([own, others[0]], axis=axis), jnp.stac...]
    ppermute x4, waiting for transfers between devices: 82.1 us -> 37.7 us  [backward_step(): return lax.ppermute(value, 'ctx', [(i + 1, i) for i in range(count - 1)])]
    ppermute x8, waiting for transfers between devices: 16.7 us -> 59.9 us  [cross_out(): return lax.ppermute(value, ('shard', 'tp'), pairs)]
    ppermute x4 -> x5, waiting for transfers between devices: 0.01 us -> 37.5 us  [other_tp(): return lax.ppermute(value, 'tp', [(0, 1), (1, 0)])]
    select_n x0 -> x6, local copies, waits for them, and re-layouts: none -> 34.1 us  [the longest x4 25.2 us: ordered(): jnp.where(position == 0, jnp.stack([own, others[0]], axis=axis), jnp.stac...]
    concatenate x1 -> x9, other arithmetic: 0.12 us -> 28.9 us  [the longest x1 17 us: per_device(): near = jnp.concatenate([own_near, mate(own_near)])]
    optimization_barrier x0 -> x7, local copies, waits for them, and re-layouts: none -> 25 us  [the longest x6 23 us: pump(): lax.optimization_barrier((value, [flow.pending for flow in flows]))]
  transfers between devices with their start and end apart: 132 -> 123, of which waited for: 44 -> 41; matrix products, arithmetic and copies ran while one was open for 32% -> 41% of each run, Pallas kernels for 9% -> 6%
where the time goes in v2:
time: 1840 us; the launch traced here: 1820 us
  waiting for transfers between devices  602 us (33%)
  other arithmetic  346 us (19%)
  matrix products  322 us (18%)
  starting transfers between devices  269 us (15%)
  Pallas kernels  142 us (8%)
  local copies, waits for them, and re-layouts  139 us (8%)
    dot_general x31, matrix products, contract(): lax.dot_general(left_side, right_side, (((left_dim,), (right_dim,)), ((),...  220 us
    ppermute x15, waiting for transfers between devices, chip_shift(): lax.ppermute(value, 'shard', [(i, (i + 2 * steps) % count) for i in range...  155 us
    ppermute x10, waiting for transfers between devices, ctx_total(): back = (yield lax.ppermute(total, 'ctx', [(1, 0), (2, 3)]))  150 us
    dot_general x8, matrix products, dot_f32(): return jnp.dot(left_side, right_side, preferred_element_type=jnp.float32)  103 us
    ppermute x10, starting transfers between devices, ctx_total(): came = (yield lax.ppermute(share, 'ctx', [(0, 1), (3, 2)]))  94.4 us
    select_n x26, other arithmetic, ordered(): jnp.where(position == 0, jnp.stack([own, others[0]], axis=axis), jnp.stac...  88.1 us
    pallas_call x2, Pallas kernels, attention_backward(): pl.pallas_call(backward_kernel, grid=(groups, pairs), in_specs=[packed_sp...  79.3 us
    pallas_call x2, Pallas kernels, attention_forward(): pl.pallas_call(forward_kernel, grid=(groups, pairs), in_specs=[pl.BlockSp...  62.2 us
  transfers between devices with their start and end apart: 123, of which 41 were waited for; matrix products, arithmetic and copies ran while one was open for 41% of the time, Pallas kernels for 6%

profile of v2, /device:TPU:0, one launch (start us, length us, event | category | flops | bytes accessed | tf_op | source)
XLA Modules:
  0.0 1824.1 jit_solution(275422103593397705)
XLA Ops:
  27.0 11.4 collective-permute-done
  126.2 17.0 pad_maximum_fusion
  144.4 17.5 collective-permute-done.10
  183.0 22.0 %add_convert_fusion.1 = bf16[3072,1920]{1,0:T(8,128)(2,1)} fusion(bf16[3072,1280]{1,0:T(8,128)(2,1)} %pad_maximum_fusion, bf16[1280,1920]{1,0:T(8,128)(2,1)} %bitcast.329, f32[1920]{0:T(1024)S(1)} %add.646), kind=kOutput, calls=%fused_computation.3 | convolution fusion | flops 15111290880 | bytes 24583680 | tf_op jit(solution)/shard_map/dot_general | solution.py:309
  226.2 31.2 %shard_map.186 = (bf16[2,512,640]{2,1,0:T(8,128)(2,1)S(1)}, f32[2,5,2,512]{3,2,1,0:T(2,128)S(1)}) custom-call(bf16[2,1536,1920]{2,1,0:T(8,128)(2,1)S(1)} %bitcast.249, s32[2,512,1]{2,1,0:T(8,128)S(1)} %subtract_add_fusion.low_ref), custom_call_target="tpu_custom_call" | custom-call | flops 6710886400 | bytes 11796480 | tf_op jit(solution)/shard_map/pallas_call | solution.py:80
  272.2 8.8 maximum_select_fusion.1
  313.6 25.0 %collective-permute-done.21 = bf16[2,320,2560]{2,1,0:T(8,128)(2,1)} collective-permute-done((bf16[2,320,2560]{2,1,0:T(8,128)(2,1)}, bf16[2,320,2560]{2,1,0:T(8,128)(2,1)}, u32[]{:S(2)}, u32[]{:S(2)}) %collective-permute-start.21) | collective-permute-done | bytes 3276832 | tf_op jit(solution)/shard_map/ppermute | solution.py:197
  343.3 11.0 multiply_convert_fusion.1
  361.5 21.6 %collective-permute-done.23 = bf16[2,320,1920]{2,1,0:T(8,128)(2,1)S(1)} collective-permute-done((bf16[2,320,1920]{2,1,0:T(8,128)(2,1)}, bf16[2,320,1920]{2,1,0:T(8,128)(2,1)S(1)}, u32[]{:S(2)}, u32[]{:S(2)}) %collective-permute-start.23) | collective-permute-done | bytes 2457632 | tf_op jit(solution)/shard_map/ppermute | solution.py:204
  406.6 23.0 %collective-permute-done.28 = bf16[512,1280]{1,0:T(8,128)(2,1)} collective-permute-done((bf16[512,1280]{1,0:T(8,128)(2,1)}, bf16[512,1280]{1,0:T(8,128)(2,1)}, u32[]{:S(2)}, u32[]{:S(2)}) %collective-permute-start.28) | collective-permute-done | bytes 1310752 | tf_op jit(solution)/shard_map/ppermute | solution.py:218
  479.8 21.4 %collective-permute-done.33 = bf16[2,320,1920]{2,1,0:T(8,128)(2,1)} collective-permute-done((bf16[2,320,1920]{2,1,0:T(8,128)(2,1)}, bf16[2,320,1920]{2,1,0:T(8,128)(2,1)}, u32[]{:S(2)}, u32[]{:S(2)}) %collective-permute-start.33) | collective-permute-done | bytes 2457632 | tf_op jit(solution)/shard_map/ppermute | solution.py:197
  505.7 8.5 maximum_select_fusion.5
  522.3 20.0 %add_convert_fusion = bf16[3072,1920]{1,0:T(8,128)(2,1)S(1)} fusion(bf16[3072,1280]{1,0:T(8,128)(2,1)} %copy-done.117, bf16[1280,1920]{1,0:T(8,128)(2,1)} %bitcast.332, f32[1920]{0:T(1024)S(1)} %add.676), kind=kOutput, calls=%fused_computation.2 | convolution fusion | flops 15111290880 | bytes 24583680 | tf_op jit(solution)/shard_map/dot_general | solution.py:309
  559.2 31.0 %shard_map.187 = (bf16[2,512,640]{2,1,0:T(8,128)(2,1)S(1)}, f32[2,5,2,512]{3,2,1,0:T(2,128)S(1)}) custom-call(bf16[2,1536,1920]{2,1,0:T(8,128)(2,1)S(1)} %bitcast.250, s32[2,512,1]{2,1,0:T(8,128)S(1)} %subtract_add_fusion.low_ref), custom_call_target="tpu_custom_call" | custom-call | flops 6710886400 | bytes 11796480 | tf_op jit(solution)/shard_map/pallas_call | solution.py:80
  599.6 9.3 collective-permute-start.41
  630.2 11.5 multiply_convert_fusion
  641.7 35.9 %collective-permute-done.41 = bf16[2,2,320,2560]{3,2,1,0:T(8,128)(2,1)} collective-permute-done((bf16[2,2,320,2560]{3,2,1,0:T(8,128)(2,1)}, bf16[2,2,320,2560]{3,2,1,0:T(8,128)(2,1)}, u32[]{:S(2)}, u32[]{:S(2)}) %collective-permute-start.41) | collective-permute-done | bytes 6553632 | tf_op jit(solution)/shard_map/ppermute | solution.py:204
  680.5 14.1 convolution_convert_fusion.1
  695.9 17.3 fusion.13
  747.0 25.6 %collective-permute-done.47 = bf16[1280,2560]{1,0:T(8,128)(2,1)} collective-permute-done((bf16[1280,2560]{1,0:T(8,128)(2,1)}, bf16[1280,2560]{1,0:T(8,128)(2,1)}, u32[]{:S(2)}, u32[]{:S(2)}) %collective-permute-start.47) | collective-permute-done | bytes 6553632 | tf_op jit(solution)/shard_map/ppermute | solution.py:209
  772.6 10.6 convert_add_fusion.3
  792.0 39.8 %shard_map.188 = bf16[2,1536,1920]{2,1,0:T(8,128)(2,1)S(1)} custom-call(bf16[2,1536,1920]{2,1,0:T(8,128)(2,1)} %bitcast.251, bf16[2,512,640]{2,1,0:T(8,128)(2,1)S(1)} %get-tuple-element.150.mixed_ref, bf16[2,512,640]{2,1,0:T(8,128)(2,1)S(1)} %bitcast.254, f32[2,5,2,512]{3,2,1,0:T(2,128)S(1)} %get-tuple-element.159.total_ref, ...), custom_call_target="tpu_custom_call" | custom-call | flops 16777216000 | bytes 23592960 | tf_op jit(solution)/shard_map/pallas_call | solution.py:163
  831.8 18.6 %collective-permute-done.48 = bf16[640,2560]{1,0:T(8,128)(2,1)} collective-permute-done((bf16[640,2560]{1,0:T(8,128)(2,1)}, bf16[640,2560]{1,0:T(8,128)(2,1)}, u32[]{:S(2)}, u32[]{:S(2)}) %collective-permute-start.48) | collective-permute-done | bytes 3276832 | tf_op jit(solution)/shard_map/ppermute | solution.py:199
  860.4 12.7 convolution_convert_fusion.3
  891.6 19.3 %collective-permute-done.43 = bf16[512,1280]{1,0:T(8,128)(2,1)S(1)} collective-permute-done((bf16[512,1280]{1,0:T(8,128)(2,1)S(1)}, bf16[512,1280]{1,0:T(8,128)(2,1)S(1)}, u32[]{:S(2)}, u32[]{:S(2)}) %collective-permute-start.43) | collective-permute-done | bytes 1310752 | tf_op jit(solution)/shard_map/ppermute | solution.py:213
  923.0 13.5 convert_add_fusion.1
  939.7 12.2 fusion.48
  951.9 10.3 collective-permute-done.55
  962.3 9.5 collective-permute-done.53
  977.9 12.1 fusion.51
  995.6 12.2 collective-permute-done.56
  1033.0 16.6 fusion.6
  1049.6 9.4 convolution_convert_fusion.12
  1063.0 10.9 convolution_convert_fusion
  1113.7 66.4 %collective-permute-done.66 = f32[15360]{0:T(1024)S(1)} collective-permute-done((f32[15360]{0:T(1024)S(1)}, f32[15360]{0:T(1024)S(1)}, u32[]{:S(2)}, u32[]{:S(2)}) %collective-permute-start.66) | collective-permute-done | bytes 61472 | tf_op jit(solution)/shard_map/ppermute | solution.py:197
  1208.2 39.6 %shard_map.189 = bf16[2,1536,1920]{2,1,0:T(8,128)(2,1)S(1)} custom-call(bf16[2,1536,1920]{2,1,0:T(8,128)(2,1)} %bitcast.248, bf16[2,512,640]{2,1,0:T(8,128)(2,1)S(1)} %copy-done.7, bf16[2,512,640]{2,1,0:T(8,128)(2,1)S(1)} %bitcast.253, f32[2,5,2,512]{3,2,1,0:T(2,128)S(1)} %get-tuple-element.178.total_ref, s32[2,1,512]{2,1,0:T(1,128)S(1)} %subtract_add_fusion.1.low_ref), custom_call_target="tpu_custom_call" | custom-call | flops 16777216000 | bytes 23592960 | tf_op jit(solution)/shard_map/pallas_call | solution.py:163
  1275.5 12.2 convolution_convert_fusion.2
  1315.1 11.1 fusion.54
  1326.2 13.5 convert_add_fusion
  1360.4 16.1 collective-permute-done.76
  1397.8 29.6 %collective-permute-done.96 = f32[15360]{0:T(1024)S(1)} collective-permute-done((f32[15360]{0:T(1024)S(1)}, f32[15360]{0:T(1024)S(1)}, u32[]{:S(2)}, u32[]{:S(2)}) %collective-permute-start.96) | collective-permute-done | bytes 61472 | tf_op jit(solution)/shard_map/ppermute | solution.py:408
  1447.7 8.7 collective-permute-done.91
  1457.7 18.1 collective-permute-done.92
  1477.2 71.6 %collective-permute-start.93 = (f32[15360]{0:T(1024)S(1)}, f32[15360]{0:T(1024)S(1)}, u32[]{:S(2)}, u32[]{:S(2)}) collective-permute-start(f32[15360]{0:T(1024)S(1)} %add.749), channel_id=1, source_target_pairs={{0,2},{6,4},{1,3},{7,5},{8,10},{14,12},{9,11},{15,13},{16,18},{22,... | collective-permute-start | bytes 184328 | tf_op jit(solution)/shard_map/ppermute | solution.py:404
  1584.5 12.7 collective-permute-done.116
  1613.0 35.1 %collective-permute-done.109 = bf16[320,640]{1,0:T(8,128)(2,1)S(1)} collective-permute-done((bf16[320,640]{1,0:T(8,128)(2,1)S(1)}, bf16[320,640]{1,0:T(8,128)(2,1)S(1)}, u32[]{:S(2)}, u32[]{:S(2)}) %collective-permute-start.109) | collective-permute-done | bytes 409632 | tf_op jit(solution)/shard_map/ppermute | solution.py:404
  1672.0 59.5 %collective-permute-done.122 = bf16[320,2560]{1,0:T(8,128)(2,1)S(1)} collective-permute-done((bf16[320,2560]{1,0:T(8,128)(2,1)S(1)}, bf16[320,2560]{1,0:T(8,128)(2,1)S(1)}, u32[]{:S(2)}, u32[]{:S(2)}) %collective-permute-start.122) | collective-permute-done | bytes 1638432 | tf_op jit(solution)/shard_map/ppermute | solution.py:408
  1796.1 24.4 %collective-permute-done.119 = bf16[320,2560]{1,0:T(8,128)(2,1)S(1)} collective-permute-done((bf16[320,2560]{1,0:T(8,128)(2,1)S(1)}, bf16[320,2560]{1,0:T(8,128)(2,1)S(1)}, u32[]{:S(2)}, u32[]{:S(2)}) %collective-permute-start.119) | collective-permute-done | bytes 1638432 | tf_op jit(solution)/shard_map/ppermute | solution.py:408
  (872 shorter events, 810.5 us)
Async XLA Ops:
  23.8 63.5 %collective-permute-start.8 = (bf16[320,640]{1,0:T(8,128)(2,1)}, bf16[320,640]{1,0:T(8,128)(2,1)}, u32[]{:S(2)}, u32[]{:S(2)}) collective-permute-start(bf16[320,640]{1,0:T(8,128)(2,1)} %get-tuple-element.333), channel_id=1, source_target_pairs={{0,16},{8,24},{16,0},{24,8},{1,17},{9,25},{17,1},{25,9},{2,18},{10... | collective-permute-start | bytes 1228808 | tf_op jit(solution)/shard_map/ppermute | solution.py:197
  25.4 64.5 %collective-permute-start.12 = (bf16[2,3840]{1,0:T(2,128)(2,1)S(1)}, bf16[2,3840]{1,0:T(2,128)(2,1)S(1)}, u32[]{:S(2)}, u32[]{:S(2)}) collective-permute-start(bf16[2,3840]{1,0:T(2,128)(2,1)S(1)} %constant_dynamic-update-slice_fusion), channel_id=1, source_target_pairs={{0,1},{1,0},{2,3},{3,2},{4,5},{5,4},{6,7},{7,6},{8,9},{9,8},{10,11... | collective-permute-start | bytes 46088 | tf_op jit(solution)/shard_map/ppermute | solution.py:213
  105.6 56.3 %collective-permute-start.10 = (bf16[2,320,1920]{2,1,0:T(8,128)(2,1)}, bf16[2,320,1920]{2,1,0:T(8,128)(2,1)}, u32[]{:S(2)}, u32[]{:S(2)}) collective-permute-start(bf16[2,320,1920]{2,1,0:T(8,128)(2,1)} %copy.188), channel_id=1, source_target_pairs={{0,16},{8,24},{16,0},{24,8},{1,17},{9,25},{17,1},{25,9},{2,18},{10... | collective-permute-start | bytes 7372808 | tf_op jit(solution)/shard_map/ppermute | solution.py:197
  117.8 87.2 %collective-permute-start.15 = (bf16[320,2560]{1,0:T(8,128)(2,1)}, bf16[320,2560]{1,0:T(8,128)(2,1)S(1)}, u32[]{:S(2)}, u32[]{:S(2)}) collective-permute-start(bf16[320,2560]{1,0:T(8,128)(2,1)} %get-tuple-element.113), channel_id=1, source_target_pairs={{0,16},{8,24},{16,0},{24,8},{1,17},{9,25},{17,1},{25,9},{2,18},{10... | collective-permute-start | bytes 4915208 | tf_op jit(solution)/shard_map/ppermute | solution.py:197
  122.8 82.2 %collective-permute-start.14 = (bf16[2,320,2560]{2,1,0:T(8,128)(2,1)}, bf16[2,320,2560]{2,1,0:T(8,128)(2,1)}, u32[]{:S(2)}, u32[]{:S(2)}) collective-permute-start(bf16[2,320,2560]{2,1,0:T(8,128)(2,1)} %maximum_select_fusion.7), channel_id=1, source_target_pairs={{0,1},{9,8},{16,17},{25,24},{2,3},{11,10},{18,19},{27,26},{4,5},{1... | collective-permute-start | bytes 9830408 | tf_op jit(solution)/shard_map/ppermute | solution.py:204
  264.5 74.1 %collective-permute-start.21 = (bf16[2,320,2560]{2,1,0:T(8,128)(2,1)}, bf16[2,320,2560]{2,1,0:T(8,128)(2,1)}, u32[]{:S(2)}, u32[]{:S(2)}) collective-permute-start(bf16[2,320,2560]{2,1,0:T(8,128)(2,1)} %broadcast_select_fusion.4), channel_id=1, source_target_pairs={{0,16},{8,24},{16,0},{24,8},{1,17},{9,25},{17,1},{25,9},{2,18},{10... | collective-permute-start | bytes 9830408 | tf_op jit(solution)/shard_map/ppermute | solution.py:197
  281.0 75.9 %collective-permute-start.22 = (bf16[2,2,320,2560]{3,2,1,0:T(8,128)(2,1)}, bf16[2,2,320,2560]{3,2,1,0:T(8,128)(2,1)}, u32[]{:S(2)}, u32[]{:S(2)}) collective-permute-start(bf16[2,2,320,2560]{3,2,1,0:T(8,128)(2,1)} %maximum_select_fusion.1), channel_id=1, source_target_pairs={{0,1},{9,8},{16,17},{25,24},{2,3},{11,10},{18,19},{27,26},{4,5},{1... | collective-permute-start | bytes 19660808 | tf_op jit(solution)/shard_map/ppermute | solution.py:204
  297.6 64.0 %collective-permute-start.24 = (bf16[320,640]{1,0:T(8,128)(2,1)S(1)}, bf16[320,640]{1,0:T(8,128)(2,1)S(1)}, u32[]{:S(2)}, u32[]{:S(2)}) collective-permute-start(bf16[320,640]{1,0:T(8,128)(2,1)S(1)} %copy-done.61), channel_id=1, source_target_pairs={{0,16},{8,24},{16,0},{24,8},{1,17},{9,25},{17,1},{25,9},{2,18},{10... | collective-permute-start | bytes 1228808 | tf_op jit(solution)/shard_map/ppermute | solution.py:197
  309.2 73.9 %collective-permute-start.23 = (bf16[2,320,1920]{2,1,0:T(8,128)(2,1)}, bf16[2,320,1920]{2,1,0:T(8,128)(2,1)S(1)}, u32[]{:S(2)}, u32[]{:S(2)}) collective-permute-start(bf16[2,320,1920]{2,1,0:T(8,128)(2,1)} %copy.196), channel_id=1, source_target_pairs={{0,1},{9,8},{16,17},{25,24},{2,3},{11,10},{18,19},{27,26},{4,5},{1... | collective-permute-start | bytes 7372808 | tf_op jit(solution)/shard_map/ppermute | solution.py:204
  444.6 56.6 %collective-permute-start.33 = (bf16[2,320,1920]{2,1,0:T(8,128)(2,1)}, bf16[2,320,1920]{2,1,0:T(8,128)(2,1)}, u32[]{:S(2)}, u32[]{:S(2)}) collective-permute-start(bf16[2,320,1920]{2,1,0:T(8,128)(2,1)} %copy.198), channel_id=1, source_target_pairs={{0,16},{8,24},{16,0},{24,8},{1,17},{9,25},{17,1},{25,9},{2,18},{10... | collective-permute-start | bytes 7372808 | tf_op jit(solution)/shard_map/ppermute | solution.py:197
  469.5 72.8 %collective-permute-start.36 = (bf16[320,2560]{1,0:T(8,128)(2,1)}, bf16[320,2560]{1,0:T(8,128)(2,1)S(1)}, u32[]{:S(2)}, u32[]{:S(2)}) collective-permute-start(bf16[320,2560]{1,0:T(8,128)(2,1)} %get-tuple-element.146), channel_id=1, source_target_pairs={{0,16},{8,24},{16,0},{24,8},{1,17},{9,25},{17,1},{25,9},{2,18},{10... | collective-permute-start | bytes 4915208 | tf_op jit(solution)/shard_map/ppermute | solution.py:197
  470.4 71.9 %collective-permute-start.35 = (bf16[2,320,2560]{2,1,0:T(8,128)(2,1)}, bf16[2,320,2560]{2,1,0:T(8,128)(2,1)}, u32[]{:S(2)}, u32[]{:S(2)}) collective-permute-start(bf16[2,320,2560]{2,1,0:T(8,128)(2,1)} %maximum_select_fusion.10), channel_id=1, source_target_pairs={{0,1},{9,8},{16,17},{25,24},{2,3},{11,10},{18,19},{27,26},{4,5},{1... | collective-permute-start | bytes 9830408 | tf_op jit(solution)/shard_map/ppermute | solution.py:204
  552.6 73.1 %collective-permute-start.40 = (bf16[2,320,2560]{2,1,0:T(8,128)(2,1)}, bf16[2,320,2560]{2,1,0:T(8,128)(2,1)}, u32[]{:S(2)}, u32[]{:S(2)}) collective-permute-start(bf16[2,320,2560]{2,1,0:T(8,128)(2,1)} %broadcast_select_fusion.3), channel_id=1, source_target_pairs={{0,16},{8,24},{16,0},{24,8},{1,17},{9,25},{17,1},{25,9},{2,18},{10... | collective-permute-start | bytes 9830408 | tf_op jit(solution)/shard_map/ppermute | solution.py:197
  599.6 77.9 %collective-permute-start.41 = (bf16[2,2,320,2560]{3,2,1,0:T(8,128)(2,1)}, bf16[2,2,320,2560]{3,2,1,0:T(8,128)(2,1)}, u32[]{:S(2)}, u32[]{:S(2)}) collective-permute-start(bf16[2,2,320,2560]{3,2,1,0:T(8,128)(2,1)} %maximum_select_fusion.3), channel_id=1, source_target_pairs={{0,1},{9,8},{16,17},{25,24},{2,3},{11,10},{18,19},{27,26},{4,5},{1... | collective-permute-start | bytes 19660808 | tf_op jit(solution)/shard_map/ppermute | solution.py:204
  614.0 66.5 %collective-permute-start.44 = (bf16[512,1280]{1,0:T(8,128)(2,1)S(1)}, bf16[512,1280]{1,0:T(8,128)(2,1)}, u32[]{:S(2)}, u32[]{:S(2)}) collective-permute-start(bf16[512,1280]{1,0:T(8,128)(2,1)S(1)} %get-tuple-element.307), channel_id=1, source_target_pairs={{0,8},{8,0},{16,24},{24,16},{1,9},{9,1},{17,25},{25,17},{2,10},{10... | collective-permute-start | bytes 3932168 | tf_op jit(solution)/shard_map/ppermute | solution.py:191
  694.6 78.1 %collective-permute-start.47 = (bf16[1280,2560]{1,0:T(8,128)(2,1)}, bf16[1280,2560]{1,0:T(8,128)(2,1)}, u32[]{:S(2)}, u32[]{:S(2)}) collective-permute-start(bf16[1280,2560]{1,0:T(8,128)(2,1)} %convolution_convert_fusion.1), channel_id=1, source_target_pairs={{1,0},{8,9},{17,16},{24,25},{3,2},{10,11},{19,18},{26,27},{5,4},{1... | collective-permute-start | bytes 19660808 | tf_op jit(solution)/shard_map/ppermute | solution.py:209
  742.0 89.8 %collective-permute-start.49 = (bf16[640,2560]{1,0:T(8,128)(2,1)}, bf16[640,2560]{1,0:T(8,128)(2,1)}, u32[]{:S(2)}, u32[]{:S(2)}) collective-permute-start(bf16[640,2560]{1,0:T(8,128)(2,1)} %convolution_convert_fusion.7), channel_id=1, source_target_pairs={{0,16},{8,24},{16,0},{24,8},{1,17},{9,25},{17,1},{25,9},{2,18},{10... | collective-permute-start | bytes 9830408 | tf_op jit(solution)/shard_map/ppermute | solution.py:197
  783.3 67.1 %collective-permute-start.48 = (bf16[640,2560]{1,0:T(8,128)(2,1)}, bf16[640,2560]{1,0:T(8,128)(2,1)}, u32[]{:S(2)}, u32[]{:S(2)}) collective-permute-start(bf16[640,2560]{1,0:T(8,128)(2,1)} %get-tuple-element.315), channel_id=1, source_target_pairs={{0,16},{9,25},{16,0},{25,9},{2,18},{11,27},{18,2},{27,11},{4,20},{... | collective-permute-start | bytes 9830408 | tf_op jit(solution)/shard_map/ppermute | solution.py:199
  873.1 49.9 %collective-permute-start.52 = (bf16[1536,1280]{1,0:T(8,128)(2,1)}, bf16[1536,1280]{1,0:T(8,128)(2,1)}, u32[]{:S(2)}, u32[]{:S(2)}) collective-permute-start(bf16[1536,1280]{1,0:T(8,128)(2,1)} %convolution_convert_fusion.3), channel_id=1, source_target_pairs={{0,8},{8,0},{16,24},{24,16},{1,9},{9,1},{17,25},{25,17},{2,10},{10... | collective-permute-start | bytes 11796488 | tf_op jit(solution)/shard_map/ppermute | solution.py:191
  990.0 59.5 %collective-permute-start.60 = (bf16[640,1920]{1,0:T(8,128)(2,1)}, bf16[640,1920]{1,0:T(8,128)(2,1)}, u32[]{:S(2)}, u32[]{:S(2)}) collective-permute-start(bf16[640,1920]{1,0:T(8,128)(2,1)} %fusion.48), channel_id=1, source_target_pairs={{0,16},{8,24},{16,0},{24,8},{1,17},{9,25},{17,1},{25,9},{2,18},{10... | collective-permute-start | bytes 7372808 | tf_op jit(solution)/shard_map/ppermute | solution.py:197
  1032.5 59.0 %collective-permute-start.63 = (f32[15360]{0:T(1024)}, f32[15360]{0:T(1024)S(1)}, u32[]{:S(2)}, u32[]{:S(2)}) collective-permute-start(f32[15360]{0:T(1024)} %select_dynamic-update-slice_fusion.2), channel_id=1, source_target_pairs={{0,8},{8,0},{16,24},{24,16},{1,9},{9,1},{17,25},{25,17},{2,10},{10... | collective-permute-start | bytes 184328 | tf_op jit(solution)/shard_map/ppermute | solution.py:191
  1074.0 110.4 %collective-permute-start.67 = (bf16[1280,2560]{1,0:T(8,128)(2,1)S(1)}, bf16[1280,2560]{1,0:T(8,128)(2,1)}, u32[]{:S(2)}, u32[]{:S(2)}) collective-permute-start(bf16[1280,2560]{1,0:T(8,128)(2,1)S(1)} %convolution_convert_fusion), channel_id=1, source_target_pairs={{1,0},{8,9},{17,16},{24,25},{3,2},{10,11},{19,18},{26,27},{5,4},{1... | collective-permute-start | bytes 19660808 | tf_op jit(solution)/shard_map/ppermute | solution.py:209
  1079.8 168.0 %collective-permute-start.72 = (bf16[320,5120]{1,0:T(8,128)(2,1)}, bf16[320,5120]{1,0:T(8,128)(2,1)}, u32[]{:S(2)}, u32[]{:S(2)}) collective-permute-start(bf16[320,5120]{1,0:T(8,128)(2,1)} %pad_maximum_fusion.3), channel_id=1, source_target_pairs={{0,2},{6,4},{1,3},{7,5},{8,10},{14,12},{9,11},{15,13},{16,18},{22,... | collective-permute-start | bytes 9830408 | tf_op jit(solution)/shard_map/ppermute | solution.py:404
  1099.3 80.7 %collective-permute-start.65 = (bf16[320,1920]{1,0:T(8,128)(2,1)S(1)}, bf16[320,1920]{1,0:T(8,128)(2,1)S(1)}, u32[]{:S(2)}, u32[]{:S(2)}) collective-permute-start(bf16[320,1920]{1,0:T(8,128)(2,1)S(1)} %add_convert_fusion.27), channel_id=1, source_target_pairs={{0,8},{8,0},{16,24},{24,16},{1,9},{9,1},{17,25},{25,17},{2,10},{10... | collective-permute-start | bytes 3686408 | tf_op jit(solution)/shard_map/ppermute | solution.py:191
  1105.4 145.5 %collective-permute-start.70 = (bf16[640,2560]{1,0:T(8,128)(2,1)}, bf16[640,2560]{1,0:T(8,128)(2,1)}, u32[]{:S(2)}, u32[]{:S(2)}) collective-permute-start(bf16[640,2560]{1,0:T(8,128)(2,1)} %convolution_convert_fusion.5), channel_id=1, source_target_pairs={{0,16},{8,24},{16,0},{24,8},{1,17},{9,25},{17,1},{25,9},{2,18},{10... | collective-permute-start | bytes 9830408 | tf_op jit(solution)/shard_map/ppermute | solution.py:197
  1112.1 67.9 %collective-permute-start.66 = (f32[15360]{0:T(1024)S(1)}, f32[15360]{0:T(1024)S(1)}, u32[]{:S(2)}, u32[]{:S(2)}) collective-permute-start(f32[15360]{0:T(1024)S(1)} %add.724), channel_id=1, source_target_pairs={{0,16},{8,24},{16,0},{24,8},{1,17},{9,25},{17,1},{25,9},{2,18},{10... | collective-permute-start | bytes 184328 | tf_op jit(solution)/shard_map/ppermute | solution.py:197
  1192.6 58.3 %collective-permute-start.69 = (bf16[640,2560]{1,0:T(8,128)(2,1)}, bf16[640,2560]{1,0:T(8,128)(2,1)}, u32[]{:S(2)}, u32[]{:S(2)}) collective-permute-start(bf16[640,2560]{1,0:T(8,128)(2,1)} %get-tuple-element.313), channel_id=1, source_target_pairs={{0,16},{9,25},{16,0},{25,9},{2,18},{11,27},{18,2},{27,11},{4,20},{... | collective-permute-start | bytes 9830408 | tf_op jit(solution)/shard_map/ppermute | solution.py:199
  1247.8 102.8 %collective-permute-start.79 = (bf16[320,2560]{1,0:T(8,128)(2,1)}, bf16[320,2560]{1,0:T(8,128)(2,1)}, u32[]{:S(2)}, u32[]{:S(2)}) collective-permute-start(bf16[320,2560]{1,0:T(8,128)(2,1)} %pad_maximum_fusion.19), channel_id=1, source_target_pairs={{0,2},{6,4},{1,3},{7,5},{8,10},{14,12},{9,11},{15,13},{16,18},{22,... | collective-permute-start | bytes 4915208 | tf_op jit(solution)/shard_map/ppermute | solution.py:404
  1260.4 96.5 %collective-permute-start.77 = (bf16[640,640]{1,0:T(8,128)(2,1)}, bf16[640,640]{1,0:T(8,128)(2,1)}, u32[]{:S(2)}, u32[]{:S(2)}) collective-permute-start(bf16[640,640]{1,0:T(8,128)(2,1)} %get-tuple-element.321), channel_id=1, source_target_pairs={{0,16},{9,25},{16,0},{25,9},{2,18},{11,27},{18,2},{27,11},{4,20},{... | collective-permute-start | bytes 2457608 | tf_op jit(solution)/shard_map/ppermute | solution.py:199
  1269.3 88.4 %collective-permute-start.78 = (bf16[640,2560]{1,0:T(8,128)(2,1)}, bf16[640,2560]{1,0:T(8,128)(2,1)}, u32[]{:S(2)}, u32[]{:S(2)}) collective-permute-start(bf16[640,2560]{1,0:T(8,128)(2,1)} %add_convert_fusion.4), channel_id=1, source_target_pairs={{1,0},{8,9},{17,16},{24,25},{3,2},{10,11},{19,18},{26,27},{5,4},{1... | collective-permute-start | bytes 9830408 | tf_op jit(solution)/shard_map/ppermute | solution.py:209
  1295.6 63.4 %collective-permute-start.81 = (bf16[320,2560]{1,0:T(8,128)(2,1)}, bf16[320,2560]{1,0:T(8,128)(2,1)}, u32[]{:S(2)}, u32[]{:S(2)}) collective-permute-start(bf16[320,2560]{1,0:T(8,128)(2,1)} %fusion.103), channel_id=1, source_target_pairs={{0,2},{6,4},{1,3},{7,5},{8,10},{14,12},{9,11},{15,13},{16,18},{22,... | collective-permute-start | bytes 4915208 | tf_op jit(solution)/shard_map/ppermute | solution.py:404
  1355.6 71.8 %collective-permute-start.85 = (bf16[320,5120]{1,0:T(8,128)(2,1)}, bf16[320,5120]{1,0:T(8,128)(2,1)S(1)}, u32[]{:S(2)}, u32[]{:S(2)}) collective-permute-start(bf16[320,5120]{1,0:T(8,128)(2,1)} %add_convert_fusion.3), channel_id=1, source_target_pairs={{2,4},{4,2},{3,5},{5,3},{10,12},{12,10},{11,13},{13,11},{18,20},{2... | collective-permute-start | bytes 9830408 | tf_op jit(solution)/shard_map/ppermute | solution.py:406
  1357.7 71.7 %collective-permute-start.87 = (bf16[1280,640]{1,0:T(8,128)(2,1)}, bf16[1280,640]{1,0:T(8,128)(2,1)S(1)}, u32[]{:S(2)}, u32[]{:S(2)}) collective-permute-start(bf16[1280,640]{1,0:T(8,128)(2,1)} %fusion.54), channel_id=1, source_target_pairs={{1,0},{8,9},{17,16},{24,25},{3,2},{10,11},{19,18},{26,27},{5,4},{1... | collective-permute-start | bytes 4915208 | tf_op jit(solution)/shard_map/ppermute | solution.py:209
  1378.8 51.4 %collective-permute-start.83 = (bf16[320,2560]{1,0:T(8,128)(2,1)S(1)}, bf16[320,2560]{1,0:T(8,128)(2,1)S(1)}, u32[]{:S(2)}, u32[]{:S(2)}) collective-permute-start(bf16[320,2560]{1,0:T(8,128)(2,1)S(1)} %add_convert_fusion.16), channel_id=1, source_target_pairs={{0,8},{8,0},{16,24},{24,16},{1,9},{9,1},{17,25},{25,17},{2,10},{10... | collective-permute-start | bytes 4915208 | tf_op jit(solution)/shard_map/ppermute | solution.py:191
  1434.3 173.1 %collective-permute-start.89 = (bf16[512,1280]{1,0:T(8,128)(2,1)}, bf16[512,1280]{1,0:T(8,128)(2,1)}, u32[]{:S(2)}, u32[]{:S(2)}) collective-permute-start(bf16[512,1280]{1,0:T(8,128)(2,1)} %get-tuple-element.304), channel_id=1, source_target_pairs={{0,1},{1,0},{2,3},{3,2},{4,5},{5,4},{6,7},{7,6},{8,9},{9,8},{10,11... | collective-permute-start | bytes 3932168 | tf_op jit(solution)/shard_map/ppermute | solution.py:213
  1436.2 141.8 %collective-permute-start.107 = (bf16[640,640]{1,0:T(8,128)(2,1)}, bf16[640,640]{1,0:T(8,128)(2,1)}, u32[]{:S(2)}, u32[]{:S(2)}) collective-permute-start(bf16[640,640]{1,0:T(8,128)(2,1)} %add_convert_fusion.28), channel_id=1, source_target_pairs={{1,0},{8,9},{17,16},{24,25},{3,2},{10,11},{19,18},{26,27},{5,4},{1... | collective-permute-start | bytes 2457608 | tf_op jit(solution)/shard_map/ppermute | solution.py:209
  1440.6 141.5 %collective-permute-start.102 = (bf16[640,640]{1,0:T(8,128)(2,1)}, bf16[640,640]{1,0:T(8,128)(2,1)}, u32[]{:S(2)}, u32[]{:S(2)}) collective-permute-start(bf16[640,640]{1,0:T(8,128)(2,1)} %get-tuple-element.318), channel_id=1, source_target_pairs={{0,16},{9,25},{16,0},{25,9},{2,18},{11,27},{18,2},{27,11},{4,20},{... | collective-permute-start | bytes 2457608 | tf_op jit(solution)/shard_map/ppermute | solution.py:199
  1475.8 104.8 %collective-permute-start.97 = (bf16[640,640]{1,0:T(8,128)(2,1)}, bf16[640,640]{1,0:T(8,128)(2,1)}, u32[]{:S(2)}, u32[]{:S(2)}) collective-permute-start(bf16[640,640]{1,0:T(8,128)(2,1)} %add_convert_fusion.30), channel_id=1, source_target_pairs={{1,0},{8,9},{17,16},{24,25},{3,2},{10,11},{19,18},{26,27},{5,4},{1... | collective-permute-start | bytes 2457608 | tf_op jit(solution)/shard_map/ppermute | solution.py:209
  1477.2 73.5 %collective-permute-start.93 = (f32[15360]{0:T(1024)S(1)}, f32[15360]{0:T(1024)S(1)}, u32[]{:S(2)}, u32[]{:S(2)}) collective-permute-start(f32[15360]{0:T(1024)S(1)} %add.749), channel_id=1, source_target_pairs={{0,2},{6,4},{1,3},{7,5},{8,10},{14,12},{9,11},{15,13},{16,18},{22,... | collective-permute-start | bytes 184328 | tf_op jit(solution)/shard_map/ppermute | solution.py:404
  1578.0 89.4 %collective-permute-start.113 = (bf16[320,2560]{1,0:T(8,128)(2,1)}, bf16[320,2560]{1,0:T(8,128)(2,1)S(1)}, u32[]{:S(2)}, u32[]{:S(2)}) collective-permute-start(bf16[320,2560]{1,0:T(8,128)(2,1)} %add_convert_fusion.14), channel_id=1, source_target_pairs={{2,0},{4,6},{3,1},{5,7},{10,8},{12,14},{11,9},{13,15},{18,16},{20,... | collective-permute-start | bytes 4915208 | tf_op jit(solution)/shard_map/ppermute | solution.py:408
  1582.1 207.0 %collective-permute-start.120 = (bf16[320,5120]{1,0:T(8,128)(2,1)S(1)}, bf16[320,5120]{1,0:T(8,128)(2,1)}, u32[]{:S(2)}, u32[]{:S(2)}) collective-permute-start(bf16[320,5120]{1,0:T(8,128)(2,1)S(1)} %add_convert_fusion.2), channel_id=1, source_target_pairs={{2,0},{4,6},{3,1},{5,7},{10,8},{12,14},{11,9},{13,15},{18,16},{20,... | collective-permute-start | bytes 9830408 | tf_op jit(solution)/shard_map/ppermute | solution.py:408
  1600.9 68.2 %collective-permute-start.117 = (bf16[320,2560]{1,0:T(8,128)(2,1)S(1)}, bf16[320,2560]{1,0:T(8,128)(2,1)S(1)}, u32[]{:S(2)}, u32[]{:S(2)}) collective-permute-start(bf16[320,2560]{1,0:T(8,128)(2,1)S(1)} %copy-done.70), channel_id=1, source_target_pairs={{0,2},{6,4},{1,3},{7,5},{8,10},{14,12},{9,11},{15,13},{16,18},{22,... | collective-permute-start | bytes 4915208 | tf_op jit(solution)/shard_map/ppermute | solution.py:404
  1607.4 49.4 %collective-permute-start.104 = (bf16[320,640]{1,0:T(8,128)(2,1)S(1)}, bf16[320,640]{1,0:T(8,128)(2,1)S(1)}, u32[]{:S(2)}, u32[]{:S(2)}) collective-permute-start(bf16[320,640]{1,0:T(8,128)(2,1)S(1)} %fusion.146), channel_id=1, source_target_pairs={{0,2},{6,4},{1,3},{7,5},{8,10},{14,12},{9,11},{15,13},{16,18},{22,... | collective-permute-start | bytes 1228808 | tf_op jit(solution)/shard_map/ppermute | solution.py:404
  1656.9 74.6 %collective-permute-start.122 = (bf16[320,2560]{1,0:T(8,128)(2,1)S(1)}, bf16[320,2560]{1,0:T(8,128)(2,1)S(1)}, u32[]{:S(2)}, u32[]{:S(2)}) collective-permute-start(bf16[320,2560]{1,0:T(8,128)(2,1)S(1)} %copy-done.69), channel_id=1, source_target_pairs={{2,0},{4,6},{3,1},{5,7},{10,8},{12,14},{11,9},{13,15},{18,16},{20,... | collective-permute-start | bytes 4915208 | tf_op jit(solution)/shard_map/ppermute | solution.py:408
  1665.1 78.2 %collective-permute-start.110 = (bf16[320,640]{1,0:T(8,128)(2,1)}, bf16[320,640]{1,0:T(8,128)(2,1)}, u32[]{:S(2)}, u32[]{:S(2)}) collective-permute-start(bf16[320,640]{1,0:T(8,128)(2,1)} %add_convert_fusion.37), channel_id=1, source_target_pairs={{2,4},{4,2},{3,5},{5,3},{10,12},{12,10},{11,13},{13,11},{18,20},{2... | collective-permute-start | bytes 1228808 | tf_op jit(solution)/shard_map/ppermute | solution.py:406
  1667.4 78.4 %collective-permute-start.105 = (bf16[320,640]{1,0:T(8,128)(2,1)}, bf16[320,640]{1,0:T(8,128)(2,1)}, u32[]{:S(2)}, u32[]{:S(2)}) collective-permute-start(bf16[320,640]{1,0:T(8,128)(2,1)} %add_convert_fusion.41), channel_id=1, source_target_pairs={{2,4},{4,2},{3,5},{5,3},{10,12},{12,10},{11,13},{13,11},{18,20},{2... | collective-permute-start | bytes 1228808 | tf_op jit(solution)/shard_map/ppermute | solution.py:406
  1669.0 79.3 %collective-permute-start.100 = (bf16[320,640]{1,0:T(8,128)(2,1)}, bf16[320,640]{1,0:T(8,128)(2,1)}, u32[]{:S(2)}, u32[]{:S(2)}) collective-permute-start(bf16[320,640]{1,0:T(8,128)(2,1)} %add_convert_fusion.45), channel_id=1, source_target_pairs={{2,4},{4,2},{3,5},{5,3},{10,12},{12,10},{11,13},{13,11},{18,20},{2... | collective-permute-start | bytes 1228808 | tf_op jit(solution)/shard_map/ppermute | solution.py:406
  1731.5 53.9 %collective-permute-start.118 = (bf16[320,2560]{1,0:T(8,128)(2,1)}, bf16[320,2560]{1,0:T(8,128)(2,1)}, u32[]{:S(2)}, u32[]{:S(2)}) collective-permute-start(bf16[320,2560]{1,0:T(8,128)(2,1)} %add_convert_fusion.12), channel_id=1, source_target_pairs={{2,4},{4,2},{3,5},{5,3},{10,12},{12,10},{11,13},{13,11},{18,20},{2... | collective-permute-start | bytes 4915208 | tf_op jit(solution)/shard_map/ppermute | solution.py:406
  (251 other events, 5567.3 us)

commit v3 on v2

v3 whole, which is shorter than its diff:
```python
import jax
import jax.numpy as jnp
from jax import lax
from jax.experimental import pallas as pl
from jax.experimental.pallas import tpu as pltpu
from jax.sharding import PartitionSpec as P

HD = 64
WINDOW = 1024
TILE = 256
masked_score = -1e30


def contract(left_side, right_side, left_dim, right_dim):
    return lax.dot_general(
        left_side, right_side, (((left_dim,), (right_dim,)), ((), ())),
        preferred_element_type=jnp.float32,
    )


def half_mask(shape, half):
    lane = lax.broadcasted_iota(jnp.int32, shape, 1)
    return (lane < HD) if half == 0 else (lane >= HD)


PAIR = 2 * HD


def forward_kernel(qkv_ref, low_ref, mixed_ref, total_ref):
    block_len = mixed_ref.shape[1]
    first = qkv_ref.shape[1] - block_len
    span = WINDOW + TILE
    eye = lax.broadcasted_iota(jnp.int32, (TILE, TILE), 0) == lax.broadcasted_iota(
        jnp.int32, (TILE, TILE), 1
    )
    for block in range(block_len // TILE):
        rows = pl.ds(block * TILE, TILE)
        window = pl.ds(block * TILE, span)
        queries = qkv_ref[0, pl.ds(first + block * TILE, TILE), :PAIR]
        queries = queries * jnp.asarray(HD ** (-0.5), jnp.bfloat16)
        keys = qkv_ref[0, window, PAIR : 2 * PAIR]
        values = qkv_ref[0, window, 2 * PAIR :]
        low_pos = low_ref[0, rows, :] - block * TILE
        key_pos = lax.broadcasted_iota(jnp.int32, (TILE, span), 1)
        query_pos = lax.broadcasted_iota(jnp.int32, (TILE, TILE), 0) + WINDOW
        allowed = key_pos >= low_pos
        causal = key_pos[:, WINDOW:] <= query_pos
        mixed = jnp.zeros((TILE, 2 * HD), jnp.float32)
        for half in range(2):
            scores = contract(
                jnp.where(half_mask(queries.shape, half), queries, 0), keys, 1, 1
            )
            early = jnp.where(allowed[:, :WINDOW], scores[:, :WINDOW], masked_score)
            late = jnp.where(allowed[:, WINDOW:] & causal, scores[:, WINDOW:], masked_score)
            top_score = jnp.maximum(
                jnp.max(early, axis=1, keepdims=True), jnp.max(late, axis=1, keepdims=True)
            )
            early = jnp.exp(early - top_score)
            late = jnp.exp(late - top_score)
            row_total = jnp.sum(early, axis=1, keepdims=True) + jnp.sum(
                late, axis=1, keepdims=True
            )
            part = contract(early.astype(jnp.bfloat16), values[:WINDOW], 1, 0) + contract(
                late.astype(jnp.bfloat16), values[WINDOW:], 1, 0
            )
            part = part * (1.0 / row_total)
            mixed = jnp.where(half_mask(mixed.shape, half), part, mixed)
            log_total = top_score + jnp.log(row_total)
            total_ref[0, 0, half : half + 1, rows] = jnp.sum(
                jnp.where(eye, log_total, 0.0), axis=0, keepdims=True
            )
        mixed_ref[0, rows, :] = mixed.astype(jnp.bfloat16)


def attention_forward(packed, low_pos):
    groups, key_len, width = packed.shape
    block_len = low_pos.shape[1]
    pairs = width // (3 * PAIR)
    pick = lambda seq, pair: (seq, 0, pair)
    return pl.pallas_call(
        forward_kernel,
        grid=(groups, pairs),
        in_specs=[
            pl.BlockSpec((1, key_len, 3 * PAIR), pick),
            pl.BlockSpec((1, block_len, 1), lambda seq, pair: (seq, 0, 0)),
        ],
        out_specs=[
            pl.BlockSpec((1, block_len, PAIR), pick),
            pl.BlockSpec((1, 1, 2, block_len), lambda seq, pair: (seq, pair, 0, 0)),
        ],
        out_shape=[
            jax.ShapeDtypeStruct((groups, block_len, pairs * PAIR), jnp.bfloat16),
            jax.ShapeDtypeStruct((groups, pairs, 2, block_len), jnp.float32),
        ],
        compiler_params=pltpu.CompilerParams(vmem_limit_bytes=40 << 20),
        cost_estimate=pl.CostEstimate(
            flops=16 * groups * pairs * block_len * (WINDOW + TILE) * HD,
            bytes_accessed=2 * groups * width * key_len,
            transcendentals=2 * groups * pairs * block_len * (WINDOW + TILE),
        ),
    )(packed, low_pos[:, :, None])


def backward_kernel(qkv_ref, mixed_ref, grad_ref, total_ref, low_ref, out_ref, gk_sum, gv_sum):
    block_len = mixed_ref.shape[1]
    first = qkv_ref.shape[1] - block_len
    span = WINDOW + TILE
    scale = HD ** (-0.5)
    gk_sum[...] = jnp.zeros_like(gk_sum)
    gv_sum[...] = jnp.zeros_like(gv_sum)
    eye = lax.broadcasted_iota(jnp.int32, (TILE, TILE), 0) == lax.broadcasted_iota(
        jnp.int32, (TILE, TILE), 1
    )
    for block in range(block_len // TILE):
        rows = pl.ds(block * TILE, TILE)
        window = pl.ds(block * TILE, span)
        queries = qkv_ref[0, pl.ds(first + block * TILE, TILE), :PAIR]
        queries = queries * jnp.asarray(scale, jnp.bfloat16)
        keys = qkv_ref[0, window, PAIR : 2 * PAIR]
        values = qkv_ref[0, window, 2 * PAIR :]
        grads = grad_ref[0, rows, :]
        product = grads.astype(jnp.float32) * mixed_ref[0, rows, :].astype(jnp.float32)
        low_pos = low_ref[0, :, rows] - block * TILE
        key_pos = lax.broadcasted_iota(jnp.int32, (span, TILE), 0)
        query_pos = lax.broadcasted_iota(jnp.int32, (TILE, TILE), 1) + WINDOW
        allowed = key_pos >= low_pos
        late_allowed = allowed[WINDOW:] & (key_pos[WINDOW:] <= query_pos)
        keys_t = jnp.transpose(keys)
        gq_parts = []
        for half in range(2):
            mask = half_mask(queries.shape, half)
            q_half = jnp.where(mask, queries, 0)
            g_half = jnp.where(mask, grads, 0)
            delta = jnp.sum(jnp.where(mask, product, 0.0), axis=1, keepdims=True)
            delta = jnp.sum(jnp.where(eye, delta, 0.0), axis=0, keepdims=True)
            log_total = total_ref[0, 0, half : half + 1, rows]
            scores = contract(keys, q_half, 1, 1)
            probs = jnp.concatenate(
                [
                    jnp.where(allowed[:WINDOW], jnp.exp(scores[:WINDOW] - log_total), 0.0),
                    jnp.where(late_allowed, jnp.exp(scores[WINDOW:] - log_total), 0.0),
                ]
            )
            grad_probs = contract(values, g_half, 1, 1)
            grad_scores = (probs * (grad_probs - delta)).astype(jnp.bfloat16)
            gv_sum[window, :] += contract(probs.astype(jnp.bfloat16), g_half, 1, 0)
            gk_sum[window, :] += contract(grad_scores, q_half, 1, 0)
            gq_parts.append(contract(keys_t[half * HD : (half + 1) * HD], grad_scores, 1, 0))
        gq = jnp.transpose(jnp.concatenate(gq_parts)) * scale
        out_ref[0, pl.ds(first + block * TILE, TILE), :PAIR] = gq.astype(jnp.bfloat16)
    out_ref[0, :first, :PAIR] = jnp.zeros((first, PAIR), jnp.bfloat16)
    out_ref[0, :, PAIR : 2 * PAIR] = gk_sum[...].astype(jnp.bfloat16)
    out_ref[0, :, 2 * PAIR :] = gv_sum[...].astype(jnp.bfloat16)


def attention_backward(packed, mixed, grads, log_total, low_pos):
    groups, key_len, width = packed.shape
    block_len = mixed.shape[1]
    pairs = width // (3 * PAIR)
    pick = lambda seq, pair: (seq, 0, pair)
    row_spec = pl.BlockSpec((1, block_len, PAIR), pick)
    packed_spec = pl.BlockSpec((1, key_len, 3 * PAIR), pick)
    return pl.pallas_call(
        backward_kernel,
        grid=(groups, pairs),
        in_specs=[
            packed_spec, row_spec, row_spec,
            pl.BlockSpec((1, 1, 2, block_len), lambda seq, pair: (seq, pair, 0, 0)),
            pl.BlockSpec((1, 1, block_len), lambda seq, pair: (seq, 0, 0)),
        ],
        out_specs=packed_spec,
        out_shape=jax.ShapeDtypeStruct(packed.shape, jnp.bfloat16),
        scratch_shapes=[
            pltpu.VMEM((key_len, PAIR), jnp.float32),
            pltpu.VMEM((key_len, PAIR), jnp.float32),
        ],
        compiler_params=pltpu.CompilerParams(vmem_limit_bytes=40 << 20),
        cost_estimate=pl.CostEstimate(
            flops=40 * groups * pairs * block_len * (WINDOW + TILE) * HD,
            bytes_accessed=4 * groups * width * key_len,
            transcendentals=2 * groups * pairs * block_len * (WINDOW + TILE),
        ),
    )(packed, mixed, grads, log_total, low_pos[:, None, :])


norm_eps = 1e-05


def mate(value):
    return lax.ppermute(value, "core", [(0, 1), (1, 0)])


def other_tp(value):
    return lax.ppermute(value, "tp", [(0, 1), (1, 0)])


def onward(value):
    count = lax.axis_size("ctx")
    return lax.ppermute(value, "ctx", [(i, i + 1) for i in range(count - 1)])


def backward_step(value):
    count = lax.axis_size("ctx")
    return lax.ppermute(value, "ctx", [(i + 1, i) for i in range(count - 1)])


class Place:
    def __init__(self):
        self.chips = lax.axis_size("x")
        self.core = lax.axis_index("core")
        self.shard = lax.axis_index("x") * 2 + self.core
        self.tp = lax.axis_index("tp")
        self.ctx = lax.axis_index("ctx")
        self.home = self.core == self.tp


def tie(*values):
    return lax.optimization_barrier(values)


def ordered(own, other, position, axis=0):
    return jnp.where(
        position == 0,
        jnp.stack([own, other], axis=axis),
        jnp.stack([other, own], axis=axis),
    )


class CoreSwap:
    def __init__(self, blocks, place):
        self.place = place
        self.kept = lax.dynamic_index_in_dim(blocks, place.core, 1, False)
        self.came = mate(lax.dynamic_index_in_dim(blocks, 1 - place.core, 1, False))

    def join(self):
        whole = ordered(self.kept, self.came, self.place.core, 1)
        return whole.reshape(-1, whole.shape[-1])


def gather_blocks(piece, place):
    whole = lax.all_gather(piece, ("x", "tp"), axis=0, tiled=False)
    return whole.reshape((place.chips, 2) + piece.shape)


def scatter_swap(grads, place):
    return CoreSwap(grads.reshape(place.chips, 2, -1, grads.shape[1]), place)


def scatter_sum(blocks):
    return lax.psum_scatter(blocks, ("x", "tp"), scatter_dimension=0, tiled=True)


def dot_f32(left_side, right_side):
    return jnp.dot(left_side, right_side, preferred_element_type=jnp.float32)


def dot_first(left_side, right_side):
    return contract(left_side, right_side, 0, 0)


def dot_second(left_side, right_side):
    return contract(left_side, right_side, 1, 1)


def gather_small(value, place):
    if place.chips != 2:
        return lax.all_gather(value, ("x", "core"), axis=1, tiled=True)
    near = mate(value)
    pair = ordered(value, near, place.core, 1).reshape(value.shape[0], -1)
    far = lax.ppermute(pair, "x", [(0, 1), (1, 0)])
    return ordered(pair, far, lax.axis_index("x"), 1).reshape(value.shape[0], -1)


def norm_forward(hidden, norm_gain, norm_shift):
    row_mean = jnp.mean(hidden, axis=-1, keepdims=True)
    centred = hidden - row_mean
    variance = jnp.mean(centred * centred, axis=-1, keepdims=True)
    inv_std = lax.rsqrt(variance + norm_eps)
    norm_hat = centred * inv_std
    return ((norm_hat * norm_gain + norm_shift).astype(jnp.bfloat16), norm_hat, inv_std)


def norm_backward(grad_out, norm_hat, inv_std, norm_gain):
    scaled = grad_out * norm_gain
    mean_one = jnp.mean(scaled, axis=-1, keepdims=True)
    mean_two = jnp.mean(scaled * norm_hat, axis=-1, keepdims=True)
    grad_input = inv_std * (scaled - mean_one - norm_hat * mean_two)
    return (grad_input, jnp.sum(grad_out * norm_hat, axis=0), jnp.sum(grad_out, axis=0))


def wide(value):
    return value.astype(jnp.float32)


def narrow(value):
    return value.astype(jnp.bfloat16)


def pick_block(value, index, count):
    size = value.shape[0] // count
    return lax.dynamic_slice_in_dim(value, index * size, size, 0)


def core_sum(own_part, mate_part):
    return own_part + wide(mate(narrow(mate_part)))


def gelu_slope(pre_act, grad_act):
    pullback = jax.vjp(lambda values: jax.nn.gelu(values, approximate=True), pre_act)[1]
    return pullback(grad_act)[0]


def pair_major(value):
    width = value.shape[-1]
    return jnp.concatenate(
        [value[kind, ..., at : at + PAIR] for at in range(0, width, PAIR) for kind in range(3)],
        axis=-1,
    )


def from_pair_major(value):
    width = value.shape[-1]
    return jnp.stack(
        [
            jnp.concatenate(
                [value[..., at : at + PAIR] for at in range(kind * PAIR, width, 3 * PAIR)], axis=-1
            )
            for kind in range(3)
        ]
    )


def per_device(
    tokens,
    cotangent,
    doc_lengths,
    norm_gains,
    norm_biases,
    qkv_weight,
    qv_bias,
    proj_weight,
    fc_weight,
    fc_bias,
    out_weight,
):
    place = Place()
    block_len, model_width = tokens.shape[1:]
    shard_rows = qkv_weight.shape[2]
    half_width = qkv_weight.shape[3]
    layer_count = qkv_weight.shape[0]
    reach = WINDOW // block_len
    key_len = (reach + 1) * block_len
    last = reach * block_len

    def my_seq(value):
        return lax.dynamic_index_in_dim(value, place.tp, 0, False)

    def both_seqs(own, other):
        return ordered(own, other, place.tp)

    def attn_piece(layer):
        return jnp.concatenate(
            [pair_major(qkv_weight[layer]), jnp.transpose(proj_weight[layer])], axis=1
        )

    own_tokens = my_seq(tokens)
    attn_blocks = gather_blocks(attn_piece(0), place)
    step_value = own_tokens
    halo = []
    for _ in range(reach):
        step_value = onward(step_value)
        halo.insert(0, step_value)
    vectors = jnp.concatenate([norm_gains, norm_biases], axis=1)
    vectors = gather_small(vectors.reshape(-1, vectors.shape[2]), place)
    vectors = wide(vectors).reshape(layer_count, 6, model_width)
    biases = jnp.concatenate([qv_bias.reshape(layer_count, -1), fc_bias], axis=1)
    biases = wide(jnp.where(place.home, biases, other_tp(biases)))
    lengths = my_seq(doc_lengths)
    lengths = jnp.stack([lengths, mate(lengths)])
    attn_blocks, later = tie(
        attn_blocks,
        (fc_weight[0], jnp.transpose(out_weight[0]), attn_piece(1),
         fc_weight[1], jnp.transpose(out_weight[1])),
    )
    fc_blocks = gather_blocks(later[0], place)
    out_blocks = gather_blocks(later[1], place)

    doc_ends = jnp.cumsum(lengths, axis=1)
    first_pos = place.ctx * block_len
    query_pos = first_pos + jnp.arange(block_len, dtype=jnp.int32)
    started = doc_ends[:, None, :] <= query_pos[None, :, None]
    doc_start = jnp.max(jnp.where(started, doc_ends[:, None, :], 0), axis=-1)
    low_pos = jnp.maximum(doc_start, query_pos[None, :] - (WINDOW - 1))
    low_pos = (low_pos - first_pos + last).astype(jnp.int32)

    hidden = wide(own_tokens)
    stash = []
    weights = []
    for layer in range(layer_count):
        gains, shifts = vectors[layer, :2], vectors[layer, 2:]
        bias_q, bias_v = biases[layer, :half_width], biases[layer, half_width : 2 * half_width]
        bias_qkv = pair_major(jnp.stack([bias_q, jnp.zeros_like(bias_q), bias_v])[:, None])
        bias_fc = biases[layer, 2 * half_width :]
        attn_in, hat_attn, inv_attn = norm_forward(hidden, gains[0], shifts[0])
        own_near = [attn_in]
        mate_near = [mate(attn_in)]
        step_value = attn_in
        for index in range(reach):
            if layer == 0:
                part = norm_forward(wide(halo[reach - 1 - index]), gains[0], shifts[0])[0]
            else:
                step_value = part = onward(step_value)
            own_near.insert(0, part)
            mate_near.insert(0, mate(part))
        near = jnp.concatenate(own_near + mate_near)
        attn_swap = CoreSwap(attn_blocks, place)
        w_attn = attn_swap.join()
        w_qkv, w_proj_t = w_attn[:, : 3 * half_width], w_attn[:, 3 * half_width :]
        packed = narrow(dot_f32(near, w_qkv) + bias_qkv).reshape(2, key_len, -1)
        mixed, log_total = attention_forward(packed, low_pos)
        mate_part = dot_second(mixed[1], w_proj_t)
        own_part = dot_second(mixed[0], w_proj_t)
        middle = hidden + core_sum(own_part, mate_part) + shifts[1]
        mlp_own, hat_mlp, inv_mlp = norm_forward(middle, gains[1], shifts[2])
        mlp_in = jnp.concatenate([mlp_own, mate(mlp_own)])
        mlp_in, fc_blocks = tie(mlp_in, fc_blocks)
        w_fc = CoreSwap(fc_blocks, place).join()
        if layer + 1 < layer_count:
            fc_blocks, piece = tie(fc_blocks, later[2])
            attn_blocks = gather_blocks(piece, place)
        pre_act = dot_f32(mlp_in, w_fc) + bias_fc
        activated = narrow(jax.nn.gelu(pre_act, approximate=True))
        activated, out_blocks = tie(activated, out_blocks)
        w_out_t = CoreSwap(out_blocks, place).join()
        if layer + 1 < layer_count:
            out_blocks, pieces = tie(out_blocks, later[3:])
            fc_blocks = gather_blocks(pieces[0], place)
            out_blocks = gather_blocks(pieces[1], place)
        mate_part = dot_second(activated[block_len:], w_out_t)
        own_part = dot_second(activated[:block_len], w_out_t)
        hidden = middle + core_sum(own_part, mate_part) + shifts[3]
        weights.append((w_qkv, w_proj_t, w_fc, w_out_t))
        stash.append(
            (near, hat_attn, inv_attn, packed, mixed, log_total, hat_mlp, inv_mlp, mlp_in,
             pre_act, activated)
        )

    own_output = narrow(hidden)
    output = both_seqs(own_output, other_tp(own_output))

    grad_hidden = wide(my_seq(cotangent))
    last_sum = None
    sums = {}
    waiting = []
    small_parts = [None] * layer_count

    def advance(value, name):
        nonlocal last_sum
        share = waiting.pop(0)
        assert share[0] == name
        value, share, last_sum = tie(value, share[1], last_sum)
        last_sum = lax.psum(share, "ctx")
        sums[name] = last_sum
        return value

    for layer in reversed(range(layer_count)):
        near, hat_attn, inv_attn, packed, mixed, log_total = stash[layer][:6]
        hat_mlp, inv_mlp, mlp_in, pre_act, activated = stash[layer][6:]
        gains = vectors[layer, :2]
        w_qkv, w_proj_t, w_fc, w_out_t = weights[layer]
        final = layer == 0
        grad_out_bias = jnp.sum(grad_hidden, axis=0)
        grad_low = narrow(grad_hidden)
        grad_low = jnp.concatenate([grad_low, mate(grad_low)])
        out_swap = scatter_swap(narrow(dot_first(grad_low, activated)), place)
        grad_pre = narrow(gelu_slope(pre_act, dot_f32(grad_low, w_out_t)))
        grad_pre, out_swap.came = tie(grad_pre, out_swap.came)
        waiting.append(("out%d" % layer, scatter_sum(out_swap.join())))
        grad_fc_bias = jnp.sum(wide(grad_pre), axis=0)
        mate_part = dot_second(grad_pre[block_len:], w_fc)
        own_part = dot_second(grad_pre[:block_len], w_fc)
        grad_norm_in = core_sum(own_part, mate_part)
        fc_swap = scatter_swap(narrow(dot_first(mlp_in, grad_pre)), place)
        if final:
            grad_norm_in = advance(grad_norm_in, "attn1")
        grad_from_mlp, grad_gain_mlp, grad_shift_mlp = norm_backward(
            grad_norm_in, hat_mlp, inv_mlp, gains[1]
        )
        grad_middle = grad_hidden + grad_from_mlp
        grad_proj_bias = jnp.sum(grad_middle, axis=0)
        grad_low = narrow(grad_middle)
        grad_low, fc_swap.came = tie(grad_low, fc_swap.came)
        waiting.append(("fc%d" % layer, scatter_sum(fc_swap.join())))
        grad_low = jnp.concatenate([grad_low, mate(grad_low)])
        grad_mixed = narrow(dot_f32(grad_low, w_proj_t)).reshape(mixed.shape)
        grad_proj = narrow(dot_first(grad_low, mixed.reshape(2 * block_len, half_width)))
        grad_packed = attention_backward(packed, mixed, grad_mixed, log_total, low_pos)
        grad_packed = advance(grad_packed, "out%d" % layer)
        mate_part = dot_second(grad_packed[1], w_qkv)
        own_part = dot_second(grad_packed[0], w_qkv)
        grad_near = core_sum(own_part, mate_part)
        far_total, grad_attn_in = grad_near[:last], grad_near[last:]
        carried = backward_step(narrow(far_total[:block_len]))
        rows = grad_packed.reshape(2 * key_len, -1)
        grad_attn = jnp.concatenate([narrow(dot_first(near, rows)), grad_proj], axis=1)
        attn_swap = scatter_swap(grad_attn, place)
        for step in range(1, reach + 1):
            if step == 1:
                carried, attn_swap.came = tie(carried, attn_swap.came)
                waiting.append(("attn%d" % layer, scatter_sum(attn_swap.join())))
            if step == 2:
                carried = advance(carried, "fc%d" % layer)
            arrived = wide(carried)
            if step < reach:
                section = far_total[step * block_len : (step + 1) * block_len]
                carried = backward_step(narrow(arrived + section))
            else:
                grad_attn_in = grad_attn_in + arrived
        grad_from_attn, grad_gain_attn, grad_shift_attn = norm_backward(
            grad_attn_in, hat_attn, inv_attn, gains[0]
        )
        grad_hidden = grad_middle + grad_from_attn
        grad_bias = jnp.sum(wide(rows), axis=0).reshape(-1, 3, PAIR)
        halves = jnp.concatenate(
            [grad_bias[:, 0].reshape(-1), grad_bias[:, 2].reshape(-1), grad_fc_bias]
        )
        empty = jnp.zeros_like(halves)
        small_parts[layer] = jnp.concatenate(
            [
                grad_gain_attn, grad_gain_mlp,
                grad_shift_attn, grad_proj_bias, grad_shift_mlp, grad_out_bias,
                jnp.where(place.core == 0, halves, empty),
                jnp.where(place.core == 1, halves, empty),
            ]
        )

    small = lax.psum(jnp.stack(small_parts), ("x", "core", "ctx", "tp"))
    far_grad = wide(other_tp(narrow(grad_hidden)))
    token_grad = both_seqs(grad_hidden, far_grad)
    advance((), "attn0")
    split = 6 * model_width
    norms = small[:, :split].reshape(layer_count, 6, model_width)
    norms = lax.dynamic_slice_in_dim(norms, place.shard * shard_rows, shard_rows, 2)
    halves = small[:, split:].reshape(layer_count, 2, -1)
    halves = lax.dynamic_index_in_dim(halves, place.tp, 1, False)
    packed_width = 3 * half_width
    attn = [sums["attn%d" % layer] for layer in range(layer_count)]
    return (
        output,
        token_grad,
        norms[:, :2],
        norms[:, 2:],
        jnp.stack([from_pair_major(wide(v[:, :packed_width])) for v in attn]),
        halves[:, : 2 * half_width].reshape(layer_count, 2, half_width),
        jnp.stack([jnp.transpose(wide(v[:, packed_width:])) for v in attn]),
        jnp.stack([wide(sums["fc%d" % layer]) for layer in range(layer_count)]),
        halves[:, 2 * half_width :],
        jnp.stack([jnp.transpose(wide(sums["out%d" % layer])) for layer in range(layer_count)]),
    )


def solution(mesh):
    devices = mesh.devices
    devices = devices.reshape((devices.shape[0] // 2, 2) + devices.shape[1:])
    mesh = jax.sharding.Mesh(devices, ("x", "core", "ctx", "tp"))
    placed = (
        P(("x", "core"), "ctx", None),
        P(("x", "core"), "ctx", None),
        P(("x", "core"), None),
        P(None, None, ("x", "core")),
        P(None, None, ("x", "core")),
        P(None, None, ("x", "core"), "tp"),
        P(None, None, "tp"),
        P(None, "tp", ("x", "core")),
        P(None, ("x", "core"), "tp"),
        P(None, "tp"),
        P(None, "tp", ("x", "core")),
    )
    return jax.shard_map(
        per_device,
        mesh=mesh,
        in_specs=placed,
        out_specs=(
            P(("x", "core"), "ctx", None),
            P(("x", "core"), "ctx", None),
            P(None, None, ("x", "core")),
            P(None, None, ("x", "core")),
            P(None, None, ("x", "core"), "tp"),
            P(None, None, "tp"),
            P(None, "tp", ("x", "core")),
            P(None, ("x", "core"), "tp"),
            P(None, "tp"),
            P(None, "tp", ("x", "core")),
        ),
        check_vma=False,
    )
```

time: 1840 us -> 1600 us (0.87)
  starting transfers between devices: 269 us -> 39.6 us
  waiting for transfers between devices: 602 us -> 778 us
  other arithmetic: 346 us -> 175 us
    ppermute x110 -> x35, waiting for transfers between devices: 485 us -> 47.5 us  [the longest x34 47.5 us: mate(): return lax.ppermute(value, 'core', [(0, 1), (1, 0)])]
    reduce_scatter x0 -> x6, waiting for transfers between devices: none -> 262 us  [scatter_sum(): lax.psum_scatter(blocks, ('x', 'tp'), scatter_dimension=0, tiled=True)]
    ppermute x110 -> x35, starting transfers between devices: 235 us -> 8.21 us  [the longest x34 6.86 us: mate(): return lax.ppermute(value, 'core', [(0, 1), (1, 0)])]
    psum x0 -> x7, waiting for transfers between devices: none -> 194 us  [the longest x6 147 us: advance(): last_sum = lax.psum(share, 'ctx')]
    all_gather x0 -> x6, waiting for transfers between devices: none -> 99.8 us  [gather_blocks(): whole = lax.all_gather(piece, ('x', 'tp'), axis=0, tiled=False)]
    select_n x51 -> x15, other arithmetic: 140 us -> 78.6 us  [ordered(): jnp.where(position == 0, jnp.stack([own, other], axis=axis), jnp.stack([o...]
    dynamic_slice x0 -> x12, local copies, waits for them, and re-layouts: none -> 54.6 us  [__init__(): self.kept = lax.dynamic_index_in_dim(blocks, place.core, 1, False)]
    ppermute x4, waiting for transfers between devices: 37.7 us -> 76.4 us  [backward_step(): return lax.ppermute(value, 'ctx', [(i + 1, i) for i in range(count - 1)])]
  transfers between devices with their start and end apart: 123 -> 65, of which waited for: 41 -> 35; matrix products, arithmetic and copies ran while one was open for 41% -> 35% of each run, Pallas kernels for 6% -> 9%
where the time goes in v3:
time: 1600 us; the launch traced here: 1590 us
  waiting for transfers between devices  778 us (49%)
  matrix products  305 us (19%)
  other arithmetic  175 us (11%)
  Pallas kernels  142 us (9%)
  local copies, waits for them, and re-layouts  136 us (8%)
  starting transfers between devices  39.6 us (2%)
  between operations  16.5 us (1%)
    reduce_scatter x6, waiting for transfers between devices, scatter_sum(): lax.psum_scatter(blocks, ('x', 'tp'), scatter_dimension=0, tiled=True)  262 us
    dot_general x24, matrix products, contract(): lax.dot_general(left_side, right_side, (((left_dim,), (right_dim,)), ((),...  198 us
    psum x6, waiting for transfers between devices, advance(): last_sum = lax.psum(share, 'ctx')  147 us
    dot_general x8, matrix products, dot_f32(): return jnp.dot(left_side, right_side, preferred_element_type=jnp.float32)  107 us
    all_gather x6, waiting for transfers between devices, gather_blocks(): whole = lax.all_gather(piece, ('x', 'tp'), axis=0, tiled=False)  99.8 us
    pallas_call x2, Pallas kernels, attention_backward(): pl.pallas_call(backward_kernel, grid=(groups, pairs), in_specs=[packed_sp...  79.5 us
    select_n x15, other arithmetic, ordered(): jnp.where(position == 0, jnp.stack([own, other], axis=axis), jnp.stack([o...  78.6 us
    ppermute x4, waiting for transfers between devices, backward_step(): return lax.ppermute(value, 'ctx', [(i + 1, i) for i in range(count - 1)])  76.4 us
  transfers between devices with their start and end apart: 65, of which 35 were waited for; matrix products, arithmetic and copies ran while one was open for 35% of the time, Pallas kernels for 9%

profile of v3, /device:TPU:0, one launch (start us, length us, event | category | flops | bytes accessed | tf_op | source)
XLA Modules:
  0.0 1591.0 jit_solution(6101436746265111941)
XLA Ops:
  59.1 24.5 %collective-permute-done.1 = bf16[512,1280]{1,0:T(8,128)(2,1)} collective-permute-done((bf16[512,1280]{1,0:T(8,128)(2,1)S(1)}, bf16[512,1280]{1,0:T(8,128)(2,1)}, u32[]{:S(2)}, u32[]{:S(2)}) %collective-permute-start.1) | collective-permute-done | bytes 1310752 | tf_op jit(solution)/shard_map/ppermute | solution.py:199
  87.0 23.8 %all-gather.13.cloned.1.call-done = bf16[1280,2560]{1,0:T(8,128)(2,1)} async-done(((bf16[320,2560]{1,0:T(8,128)(2,1)}), bf16[1280,2560]{1,0:T(8,128)(2,1)}) %all-gather.13.cloned.1.call-update) | async-done | bytes 6553616 | tf_op jit(solution)/shard_map/all_gather | solution.py:241
  137.7 20.0 %add_convert_fusion.1 = bf16[3072,1920]{1,0:T(8,128)(2,1)S(1)} fusion(bf16[3072,1280]{1,0:T(8,128)(2,1)} %constant_dynamic-update-slice_fusion, f32[1920]{0:T(1024)S(1)} %reduce.4, bf16[1280,2560]{1,0:T(8,128)(2,1)S(1)} %bitcast.489), kind=kOutput, calls=%fused_computation.3 | convolution fusion | flops 15111290880 | bytes 24584192 | tf_op jit(solution)/shard_map/dot_general | solution.py:254
  157.7 31.1 %shard_map.186 = (bf16[2,512,640]{2,1,0:T(8,128)(2,1)S(1)}, f32[2,5,2,512]{3,2,1,0:T(2,128)S(1)}) custom-call(bf16[2,1536,1920]{2,1,0:T(8,128)(2,1)S(1)} %bitcast.467, s32[2,512,1]{2,1,0:T(8,128)S(1)} %subtract_add_fusion.low_ref), custom_call_target="tpu_custom_call" | custom-call | flops 6710886400 | bytes 11796480 | tf_op jit(solution)/shard_map/pallas_call | solution.py:80
  217.4 11.2 multiply_convert_fusion.1
  228.7 35.1 %all-gather.17.cloned.1.call-done = bf16[1280,2560]{1,0:T(8,128)(2,1)} async-done(((bf16[320,2560]{1,0:T(8,128)(2,1)}), bf16[1280,2560]{1,0:T(8,128)(2,1)}) %all-gather.17.cloned.1.call-update) | async-done | bytes 6553616 | tf_op jit(solution)/shard_map/all_gather | solution.py:241
  276.1 7.2 maximum_select_fusion.2
  283.4 7.5 convolution_convert_fusion.15
  304.3 27.2 %collective-permute-done.15 = bf16[512,1280]{1,0:T(8,128)(2,1)} collective-permute-done((bf16[512,1280]{1,0:T(8,128)(2,1)S(1)}, bf16[512,1280]{1,0:T(8,128)(2,1)}, u32[]{:S(2)}, u32[]{:S(2)}) %collective-permute-start.15) | collective-permute-done | bytes 1310752 | tf_op jit(solution)/shard_map/ppermute | solution.py:199
  348.7 15.1 collective-permute-done.16
  377.8 20.1 %add_convert_fusion = bf16[3072,1920]{1,0:T(8,128)(2,1)S(1)} fusion(bf16[3072,1280]{1,0:T(8,128)(2,1)} %copy-done.62, f32[1920]{0:T(1024)S(1)} %reduce.12, bf16[1280,2560]{1,0:T(8,128)(2,1)S(1)} %bitcast.483), kind=kOutput, calls=%fused_computation.2 | convolution fusion | flops 15111290880 | bytes 24584192 | tf_op jit(solution)/shard_map/dot_general | solution.py:254
  398.0 31.1 %shard_map.187 = (bf16[2,512,640]{2,1,0:T(8,128)(2,1)S(1)}, f32[2,5,2,512]{3,2,1,0:T(2,128)S(1)}) custom-call(bf16[2,1536,1920]{2,1,0:T(8,128)(2,1)S(1)} %bitcast.469, s32[2,512,1]{2,1,0:T(8,128)S(1)} %subtract_add_fusion.low_ref), custom_call_target="tpu_custom_call" | custom-call | flops 6710886400 | bytes 11796480 | tf_op jit(solution)/shard_map/pallas_call | solution.py:80
  458.3 11.6 multiply_convert_fusion
  469.9 35.6 %all-gather.23.cloned.1.call-done = bf16[1280,2560]{1,0:T(8,128)(2,1)} async-done(((bf16[320,2560]{1,0:T(8,128)(2,1)}), bf16[1280,2560]{1,0:T(8,128)(2,1)}) %all-gather.23.cloned.1.call-update) | async-done | bytes 6553616 | tf_op jit(solution)/shard_map/all_gather | solution.py:241
  510.9 9.0 convolution_convert_fusion.3
  527.1 19.3 %fusion.13 = bf16[1024,2560]{1,0:T(8,128)(2,1)} fusion(f32[1024,2560]{1,0:T(8,128)} %get-tuple-element.229, f32[2560]{0:T(1024)S(1)} %get-tuple-element.126, bf16[1280,2560]{1,0:T(8,128)(2,1)S(1)} %bitcast.495, bf16[512,1280]{1,0:T(8,128)(2,1)} %collective-permute-done.27, bf16[512,1280]{1,0:T(8,128)(2,1)} %get-tuple-element.137), kind=kOutput, calls=%fused_computation.25 | convolution fusion | flops 6771179520 | bytes 24913920 | tf_op jit(solution)/shard_map/dot_general | solution.py:254
  549.9 8.5 convolution_convert_fusion.13
  558.4 10.1 convolution_convert_fusion.2
  589.6 39.9 %shard_map.188 = bf16[2,1536,1920]{2,1,0:T(8,128)(2,1)S(1)} custom-call(bf16[2,1536,1920]{2,1,0:T(8,128)(2,1)} %bitcast.470, bf16[2,512,640]{2,1,0:T(8,128)(2,1)S(1)} %get-tuple-element.64.mixed_ref, bf16[2,512,640]{2,1,0:T(8,128)(2,1)S(1)} %bitcast.473, f32[2,5,2,512]{3,2,1,0:T(2,128)S(1)} %get-tuple-element.75.total_ref, ...), custom_call_target="tpu_custom_call" | custom-call | flops 16777216000 | bytes 23592960 | tf_op jit(solution)/shard_map/pallas_call | solution.py:163
  633.8 9.0 maximum_select_fusion.7
  648.3 13.9 convolution_convert_fusion.7
  662.5 18.8 %convolution_convert_fusion.5 = bf16[1280,1920]{1,0:T(8,128)(2,1)} fusion(bf16[3072,1280]{1,0:T(8,128)(2,1)S(1)} %bitcast.544, bf16[3072,1920]{1,0:T(8,128)(2,1)S(1)} %bitcast.458), kind=kOutput, calls=%fused_computation.33 | convolution fusion | flops 15101952000 | bytes 24576000 | tf_op jit(solution)/shard_map/dot_general | solution.py:15
  694.4 12.3 convert_add_fusion.1
  708.1 31.5 %collective-permute-done.33 = bf16[512,1280]{1,0:T(8,128)(2,1)S(1)} collective-permute-done((bf16[512,1280]{1,0:T(8,128)(2,1)S(1)}, bf16[512,1280]{1,0:T(8,128)(2,1)S(1)}, u32[]{:S(2)}, u32[]{:S(2)}) %collective-permute-start.33) | collective-permute-done | bytes 1310752 | tf_op jit(solution)/shard_map/ppermute | solution.py:204
  741.2 39.2 %reduce-scatter.9.cloned.1.call-done = bf16[320,2560]{1,0:T(8,128)(2,1)} async-done(((bf16[1280,2560]{1,0:T(8,128)(2,1)}), bf16[320,2560]{1,0:T(8,128)(2,1)}) %reduce-scatter.9.cloned.1.call-update) | async-done | bytes 1638416 | tf_op jit(solution)/shard_map/reduce_scatter | solution.py:250
  780.5 8.7 maximum_select_fusion.8
  803.8 7.4 convolution_convert_fusion.1
  815.0 15.8 fusion.6
  842.9 11.2 all-reduce.10.cloned.1.call-done
  854.1 75.0 %reduce-scatter.11.cloned.1.call-done = bf16[320,2560]{1,0:T(8,128)(2,1)} async-done(((bf16[1280,2560]{1,0:T(8,128)(2,1)}), bf16[320,2560]{1,0:T(8,128)(2,1)}) %reduce-scatter.11.cloned.1.call-update) | async-done | bytes 1638416 | tf_op jit(solution)/shard_map/reduce_scatter | solution.py:250
  929.2 8.9 maximum_select_fusion.9
  938.2 10.3 convolution_convert_fusion
  964.4 39.6 %shard_map.189 = bf16[2,1536,1920]{2,1,0:T(8,128)(2,1)S(1)} custom-call(bf16[2,1536,1920]{2,1,0:T(8,128)(2,1)} %bitcast.468, bf16[2,512,640]{2,1,0:T(8,128)(2,1)S(1)} %copy-done.7, bf16[2,512,640]{2,1,0:T(8,128)(2,1)S(1)} %bitcast.472, f32[2,5,2,512]{3,2,1,0:T(2,128)S(1)} %get-tuple-element.87.total_ref, s32[2,1,512]{2,1,0:T(1,128)S(1)} %subtract_add_fusion.1.low_ref), custom_call_target="tpu_custom_call" | custom-call | flops 16777216000 | bytes 23592960 | tf_op jit(solution)/shard_map/pallas_call | solution.py:163
  1008.3 69.8 %reduce-scatter.13.cloned.1.call-done = bf16[320,2560]{1,0:T(8,128)(2,1)} async-done(((bf16[1280,2560]{1,0:T(8,128)(2,1)}), bf16[320,2560]{1,0:T(8,128)(2,1)}) %reduce-scatter.13.cloned.1.call-update) | async-done | bytes 1638416 | tf_op jit(solution)/shard_map/reduce_scatter | solution.py:250
  1078.1 8.7 maximum_select_fusion.10
  1094.0 13.3 convolution_convert_fusion.6
  1107.4 19.1 %convolution_convert_fusion.4 = bf16[1280,1920]{1,0:T(8,128)(2,1)} fusion(bf16[3072,1280]{1,0:T(8,128)(2,1)S(1)} %bitcast.542, bf16[3072,1920]{1,0:T(8,128)(2,1)S(1)} %bitcast.463), kind=kOutput, calls=%fused_computation.32 | convolution fusion | flops 15101952000 | bytes 24576000 | tf_op jit(solution)/shard_map/dot_general | solution.py:15
  1139.8 12.3 convert_add_fusion
  1164.2 24.0 %collective-permute-done.42 = bf16[512,1280]{1,0:T(8,128)(2,1)S(1)} collective-permute-done((bf16[512,1280]{1,0:T(8,128)(2,1)S(1)}, bf16[512,1280]{1,0:T(8,128)(2,1)S(1)}, u32[]{:S(2)}, u32[]{:S(2)}) %collective-permute-start.42) | collective-permute-done | bytes 1310752 | tf_op jit(solution)/shard_map/ppermute | solution.py:204
  1202.6 20.9 %collective-permute-done.44 = bf16[512,1280]{1,0:T(8,128)(2,1)S(1)} collective-permute-done((bf16[512,1280]{1,0:T(8,128)(2,1)}, bf16[512,1280]{1,0:T(8,128)(2,1)S(1)}, u32[]{:S(2)}, u32[]{:S(2)}) %collective-permute-start.44) | collective-permute-done | bytes 1310752 | tf_op jit(solution)/shard_map/ppermute | solution.py:204
  1230.7 8.8 maximum_select_fusion.11
  1239.6 7.4 convolution_convert_fusion.14
  1250.1 8.4 add_convert_fusion.2
  1259.9 30.1 %collective-permute-done.26 = bf16[512,1280]{1,0:T(8,128)(2,1)S(1)} collective-permute-done((bf16[512,1280]{1,0:T(8,128)(2,1)}, bf16[512,1280]{1,0:T(8,128)(2,1)S(1)}, u32[]{:S(2)}, u32[]{:S(2)}) %collective-permute-start.26) | collective-permute-done | bytes 1310752 | tf_op jit(solution)/shard_map/ppermute | solution.py:194
  1306.1 47.4 %all-reduce.16.cloned.1.call-done = f32[2,15360]{1,0:T(2,128)} async-done(((f32[2,15360]{1,0:T(2,128)}), f32[2,15360]{1,0:T(2,128)}) %all-reduce.16.cloned.1.call-update) | async-done | bytes 122896 | tf_op jit(solution)/shard_map/psum | solution.py:537
  1356.3 70.8 %all-reduce.18.cloned.1.call-done = bf16[320,2560]{1,0:T(8,128)(2,1)} async-done(((bf16[320,2560]{1,0:T(8,128)(2,1)}), bf16[320,2560]{1,0:T(8,128)(2,1)}) %all-reduce.18.cloned.1.call-update) | async-done | bytes 1638416 | tf_op jit(solution)/shard_map/psum | solution.py:462
  1427.1 75.2 %reduce-scatter.17.cloned.1.call-done = bf16[320,2560]{1,0:T(8,128)(2,1)} async-done(((bf16[1280,2560]{1,0:T(8,128)(2,1)}), bf16[320,2560]{1,0:T(8,128)(2,1)}) %reduce-scatter.17.cloned.1.call-update) | async-done | bytes 1638416 | tf_op jit(solution)/shard_map/reduce_scatter | solution.py:250
  1511.1 64.9 %all-reduce.20.cloned.1.call-done = bf16[320,2560]{1,0:T(8,128)(2,1)} async-done(((bf16[320,2560]{1,0:T(8,128)(2,1)}), bf16[320,2560]{1,0:T(8,128)(2,1)}) %all-reduce.20.cloned.1.call-update) | async-done | bytes 1638416 | tf_op jit(solution)/shard_map/psum | solution.py:462
  (643 shorter events, 403.9 us)
Async XLA Ops:
  7.2 103.6 %all-gather.13.cloned.1.call-start = ((), (), s32[]{:S(2)}) async-start(), calls=%async_computation.19 | async-start | bytes 8192000 | tf_op jit(solution)/shard_map/all_gather | solution.py:241
  7.9 40.0 %collective-permute-start.9 = (s32[4]{0:T(128)S(1)}, s32[4]{0:T(128)S(1)}, u32[]{:S(2)}, u32[]{:S(2)}) collective-permute-start(s32[4]{0:T(128)S(1)} %fusion.152), channel_id=1, source_target_pairs={{0,8},{8,0},{1,9},{9,1},{2,10},{10,2},{3,11},{11,3},{4,12},{12,4},... | collective-permute-start | bytes 56 | tf_op jit(solution)/shard_map/ppermute | solution.py:190
  9.1 41.9 %collective-permute-start.2 = (bf16[12,320]{1,0:T(8,128)(2,1)S(1)}, bf16[12,320]{1,0:T(8,128)(2,1)S(1)}, u32[]{:S(2)}, u32[]{:S(2)}) collective-permute-start(bf16[12,320]{1,0:T(8,128)(2,1)S(1)} %reshape.399), channel_id=1, source_target_pairs={{0,8},{8,0},{1,9},{9,1},{2,10},{10,2},{3,11},{11,3},{4,12},{12,4},... | collective-permute-start | bytes 23048 | tf_op jit(solution)/shard_map/ppermute | solution.py:190
  10.8 41.8 %collective-permute-start.8 = (bf16[2,3840]{1,0:T(2,128)(2,1)S(1)}, bf16[2,3840]{1,0:T(2,128)(2,1)S(1)}, u32[]{:S(2)}, u32[]{:S(2)}) collective-permute-start(bf16[2,3840]{1,0:T(2,128)(2,1)S(1)} %constant_dynamic-update-slice_fusion.36), channel_id=1, source_target_pairs={{0,1},{1,0},{2,3},{3,2},{4,5},{5,4},{6,7},{7,6},{8,9},{9,8},{10,11... | collective-permute-start | bytes 46088 | tf_op jit(solution)/shard_map/ppermute | solution.py:194
  15.4 37.6 %collective-permute-start = (bf16[512,1280]{1,0:T(8,128)(2,1)S(1)}, bf16[512,1280]{1,0:T(8,128)(2,1)S(1)}, u32[]{:S(2)}, u32[]{:S(2)}) collective-permute-start(bf16[512,1280]{1,0:T(8,128)(2,1)S(1)} %get-tuple-element.145), channel_id=1, source_target_pairs={{0,2},{2,4},{4,6},{1,3},{3,5},{5,7},{8,10},{10,12},{12,14},{9,11},... | collective-permute-start | bytes 3932168 | tf_op jit(solution)/shard_map/ppermute | solution.py:199
  39.1 165.2 %all-gather.15.cloned.1.call-start = ((), (), s32[]{:S(2)}) async-start(), calls=%async_computation.20 | async-start | bytes 8192000 | tf_op jit(solution)/shard_map/all_gather | solution.py:241
  51.2 6.3 collective-permute-start.3
  53.0 30.7 %collective-permute-start.1 = (bf16[512,1280]{1,0:T(8,128)(2,1)S(1)}, bf16[512,1280]{1,0:T(8,128)(2,1)}, u32[]{:S(2)}, u32[]{:S(2)}) collective-permute-start(bf16[512,1280]{1,0:T(8,128)(2,1)S(1)} %collective-permute-done), channel_id=1, source_target_pairs={{0,2},{2,4},{4,6},{1,3},{3,5},{5,7},{8,10},{10,12},{12,14},{9,11},... | collective-permute-start | bytes 3932168 | tf_op jit(solution)/shard_map/ppermute | solution.py:199
  110.8 152.9 %all-gather.17.cloned.1.call-start = ((), (), s32[]{:S(2)}) async-start(), calls=%async_computation.21 | async-start | bytes 8192000 | tf_op jit(solution)/shard_map/all_gather | solution.py:241
  117.5 15.3 collective-permute-start.7
  122.0 8.4 collective-permute-start.5
  191.1 151.5 %all-gather.19.cloned.1.call-start = ((), (), s32[]{:S(2)}) async-start(), calls=%async_computation.22 | async-start | bytes 8192000 | tf_op jit(solution)/shard_map/all_gather | solution.py:241
  269.9 175.2 %all-gather.21.cloned.1.call-start = ((), (), s32[]{:S(2)}) async-start(), calls=%async_computation.23 | async-start | bytes 8192000 | tf_op jit(solution)/shard_map/all_gather | solution.py:241
  299.7 31.8 %collective-permute-start.15 = (bf16[512,1280]{1,0:T(8,128)(2,1)S(1)}, bf16[512,1280]{1,0:T(8,128)(2,1)}, u32[]{:S(2)}, u32[]{:S(2)}) collective-permute-start(bf16[512,1280]{1,0:T(8,128)(2,1)S(1)} %add_convert_fusion.4), channel_id=1, source_target_pairs={{0,2},{2,4},{4,6},{1,3},{3,5},{5,7},{8,10},{10,12},{12,14},{9,11},... | collective-permute-start | bytes 3932168 | tf_op jit(solution)/shard_map/ppermute | solution.py:199
  304.3 201.2 %all-gather.23.cloned.1.call-start = ((), (), s32[]{:S(2)}) async-start(), calls=%async_computation.24 | async-start | bytes 8192000 | tf_op jit(solution)/shard_map/all_gather | solution.py:241
  331.5 32.3 %collective-permute-start.16 = (bf16[512,1280]{1,0:T(8,128)(2,1)}, bf16[512,1280]{1,0:T(8,128)(2,1)}, u32[]{:S(2)}, u32[]{:S(2)}) collective-permute-start(bf16[512,1280]{1,0:T(8,128)(2,1)} %collective-permute-done.15), channel_id=1, source_target_pairs={{0,2},{2,4},{4,6},{1,3},{3,5},{5,7},{8,10},{10,12},{12,14},{9,11},... | collective-permute-start | bytes 3932168 | tf_op jit(solution)/shard_map/ppermute | solution.py:199
  348.7 22.3 %collective-permute-start.20 = (bf16[2,320,2560]{2,1,0:T(8,128)(2,1)}, bf16[2,320,2560]{2,1,0:T(8,128)(2,1)}, u32[]{:S(2)}, u32[]{:S(2)}) collective-permute-start(bf16[2,320,2560]{2,1,0:T(8,128)(2,1)} %get-tuple-element.167), channel_id=1, source_target_pairs={{0,8},{8,0},{1,9},{9,1},{2,10},{10,2},{3,11},{11,3},{4,12},{12,4},... | collective-permute-start | bytes 9830408 | tf_op jit(solution)/shard_map/ppermute | solution.py:190
  363.9 7.0 collective-permute-start.19
  364.5 6.4 collective-permute-start.18
  431.5 202.3 %reduce-scatter.7.cloned.1.call-start = ((), (), s32[]{:S(2)}) async-start(), calls=%async_computation.6 | async-start | bytes 8192000 | tf_op jit(solution)/shard_map/reduce_scatter | solution.py:250
  450.7 60.2 %collective-permute-start.27 = (bf16[512,1280]{1,0:T(8,128)(2,1)}, bf16[512,1280]{1,0:T(8,128)(2,1)}, u32[]{:S(2)}, u32[]{:S(2)}) collective-permute-start(bf16[512,1280]{1,0:T(8,128)(2,1)} %get-tuple-element.137), channel_id=1, source_target_pairs={{0,8},{8,0},{1,9},{9,1},{2,10},{10,2},{3,11},{11,3},{4,12},{12,4},... | collective-permute-start | bytes 3932168 | tf_op jit(solution)/shard_map/ppermute | solution.py:190
  510.9 11.8 collective-permute-start.24
  522.2 24.2 %collective-permute-start.28 = (bf16[2,320,2560]{2,1,0:T(8,128)(2,1)}, bf16[2,320,2560]{2,1,0:T(8,128)(2,1)S(1)}, u32[]{:S(2)}, u32[]{:S(2)}) collective-permute-start(bf16[2,320,2560]{2,1,0:T(8,128)(2,1)} %get-tuple-element.161), channel_id=1, source_target_pairs={{0,8},{8,0},{1,9},{9,1},{2,10},{10,2},{3,11},{11,3},{4,12},{12,4},... | collective-permute-start | bytes 9830408 | tf_op jit(solution)/shard_map/ppermute | solution.py:190
  549.8 191.4 %all-reduce.8.cloned.1.call-start = ((), (), s32[]{:S(2)}) async-start(), calls=%async_computation.8 | async-start | bytes 3276800 | tf_op jit(solution)/shard_map/psum | solution.py:462
  558.4 14.1 collective-permute-start.29
  571.9 9.9 collective-permute-start.30
  633.8 146.7 %reduce-scatter.9.cloned.1.call-start = ((), (), s32[]{:S(2)}) async-start(), calls=%async_computation.7 | async-start | bytes 8192000 | tf_op jit(solution)/shard_map/reduce_scatter | solution.py:250
  642.9 211.2 %all-reduce.10.cloned.1.call-start = ((), (), s32[]{:S(2)}) async-start(), calls=%async_computation.10 | async-start | bytes 3276800 | tf_op jit(solution)/shard_map/psum | solution.py:462
  662.2 32.2 %collective-permute-start.32 = (bf16[1536,1280]{1,0:T(8,128)(2,1)}, bf16[1536,1280]{1,0:T(8,128)(2,1)}, u32[]{:S(2)}, u32[]{:S(2)}) collective-permute-start(bf16[1536,1280]{1,0:T(8,128)(2,1)} %convolution_convert_fusion.7), channel_id=1, source_target_pairs={{0,8},{8,0},{1,9},{9,1},{2,10},{10,2},{3,11},{11,3},{4,12},{12,4},... | collective-permute-start | bytes 11796488 | tf_op jit(solution)/shard_map/ppermute | solution.py:190
  694.1 14.1 collective-permute-start.34
  706.8 32.8 %collective-permute-start.33 = (bf16[512,1280]{1,0:T(8,128)(2,1)S(1)}, bf16[512,1280]{1,0:T(8,128)(2,1)S(1)}, u32[]{:S(2)}, u32[]{:S(2)}) collective-permute-start(bf16[512,1280]{1,0:T(8,128)(2,1)S(1)} %slice.1151), channel_id=1, source_target_pairs={{2,0},{4,2},{6,4},{3,1},{5,3},{7,5},{10,8},{12,10},{14,12},{11,9},... | collective-permute-start | bytes 3932168 | tf_op jit(solution)/shard_map/ppermute | solution.py:204
  739.9 40.6 %collective-permute-start.35 = (bf16[512,1280]{1,0:T(8,128)(2,1)S(1)}, bf16[512,1280]{1,0:T(8,128)(2,1)S(1)}, u32[]{:S(2)}, u32[]{:S(2)}) collective-permute-start(bf16[512,1280]{1,0:T(8,128)(2,1)S(1)} %fusion.62), channel_id=1, source_target_pairs={{2,0},{4,2},{6,4},{3,1},{5,3},{7,5},{10,8},{12,10},{14,12},{11,9},... | collective-permute-start | bytes 3932168 | tf_op jit(solution)/shard_map/ppermute | solution.py:204
  780.5 148.7 %reduce-scatter.11.cloned.1.call-start = ((), (), s32[]{:S(2)}) async-start(), calls=%async_computation.9 | async-start | bytes 8192000 | tf_op jit(solution)/shard_map/reduce_scatter | solution.py:250
  789.3 219.0 %all-reduce.12.cloned.1.call-start = ((), (), s32[]{:S(2)}) async-start(), calls=%async_computation.12 | async-start | bytes 3276800 | tf_op jit(solution)/shard_map/psum | solution.py:462
  814.9 15.9 %collective-permute-start.37 = (bf16[2,320,2560]{2,1,0:T(8,128)(2,1)}, bf16[2,320,2560]{2,1,0:T(8,128)(2,1)}, u32[]{:S(2)}, u32[]{:S(2)}) collective-permute-start(bf16[2,320,2560]{2,1,0:T(8,128)(2,1)} %get-tuple-element.155), channel_id=1, source_target_pairs={{0,8},{8,0},{1,9},{9,1},{2,10},{10,2},{3,11},{11,3},{4,12},{12,4},... | collective-permute-start | bytes 9830408 | tf_op jit(solution)/shard_map/ppermute | solution.py:190
  929.2 148.9 %reduce-scatter.13.cloned.1.call-start = ((), (), s32[]{:S(2)}) async-start(), calls=%async_computation.11 | async-start | bytes 8192000 | tf_op jit(solution)/shard_map/reduce_scatter | solution.py:250
  938.2 264.4 %all-reduce.14.cloned.1.call-start = ((), (), s32[]{:S(2)}) async-start(), calls=%async_computation.14 | async-start | bytes 3276800 | tf_op jit(solution)/shard_map/psum | solution.py:462
  1078.1 147.9 %reduce-scatter.15.cloned.1.call-start = ((), (), s32[]{:S(2)}) async-start(), calls=%async_computation.13 | async-start | bytes 8192000 | tf_op jit(solution)/shard_map/reduce_scatter | solution.py:250
  1086.9 266.5 %all-reduce.16.cloned.1.call-start = ((), (), s32[]{:S(2)}) async-start(), calls=%async_computation.15 | async-start | bytes 245760 | tf_op jit(solution)/shard_map/psum | solution.py:537
  1107.4 32.4 %collective-permute-start.41 = (bf16[1536,1280]{1,0:T(8,128)(2,1)}, bf16[1536,1280]{1,0:T(8,128)(2,1)}, u32[]{:S(2)}, u32[]{:S(2)}) collective-permute-start(bf16[1536,1280]{1,0:T(8,128)(2,1)} %convolution_convert_fusion.6), channel_id=1, source_target_pairs={{0,8},{8,0},{1,9},{9,1},{2,10},{10,2},{3,11},{11,3},{4,12},{12,4},... | collective-permute-start | bytes 11796488 | tf_op jit(solution)/shard_map/ppermute | solution.py:190
  1139.3 24.9 %collective-permute-start.43 = (bf16[2,320,2560]{2,1,0:T(8,128)(2,1)}, bf16[2,320,2560]{2,1,0:T(8,128)(2,1)}, u32[]{:S(2)}, u32[]{:S(2)}) collective-permute-start(bf16[2,320,2560]{2,1,0:T(8,128)(2,1)} %get-tuple-element.151), channel_id=1, source_target_pairs={{0,8},{8,0},{1,9},{9,1},{2,10},{10,2},{3,11},{11,3},{4,12},{12,4},... | collective-permute-start | bytes 9830408 | tf_op jit(solution)/shard_map/ppermute | solution.py:190
  1155.5 32.7 %collective-permute-start.42 = (bf16[512,1280]{1,0:T(8,128)(2,1)S(1)}, bf16[512,1280]{1,0:T(8,128)(2,1)S(1)}, u32[]{:S(2)}, u32[]{:S(2)}) collective-permute-start(bf16[512,1280]{1,0:T(8,128)(2,1)S(1)} %slice.1150), channel_id=1, source_target_pairs={{2,0},{4,2},{6,4},{3,1},{5,3},{7,5},{10,8},{12,10},{14,12},{11,9},... | collective-permute-start | bytes 3932168 | tf_op jit(solution)/shard_map/ppermute | solution.py:204
  1191.4 32.1 %collective-permute-start.44 = (bf16[512,1280]{1,0:T(8,128)(2,1)}, bf16[512,1280]{1,0:T(8,128)(2,1)S(1)}, u32[]{:S(2)}, u32[]{:S(2)}) collective-permute-start(bf16[512,1280]{1,0:T(8,128)(2,1)} %fusion.61), channel_id=1, source_target_pairs={{2,0},{4,2},{6,4},{3,1},{5,3},{7,5},{10,8},{12,10},{14,12},{11,9},... | collective-permute-start | bytes 3932168 | tf_op jit(solution)/shard_map/ppermute | solution.py:204
  1230.1 197.0 %all-reduce.18.cloned.1.call-start = ((), (), s32[]{:S(2)}) async-start(), calls=%async_computation.17 | async-start | bytes 3276800 | tf_op jit(solution)/shard_map/psum | solution.py:462
  1230.7 271.6 %reduce-scatter.17.cloned.1.call-start = ((), (), s32[]{:S(2)}) async-start(), calls=%async_computation.16 | async-start | bytes 8192000 | tf_op jit(solution)/shard_map/reduce_scatter | solution.py:250
  1239.6 336.5 %all-reduce.20.cloned.1.call-start = ((), (), s32[]{:S(2)}) async-start(), calls=%async_computation.18 | async-start | bytes 3276800 | tf_op jit(solution)/shard_map/psum | solution.py:462
  1258.6 31.4 %collective-permute-start.26 = (bf16[512,1280]{1,0:T(8,128)(2,1)}, bf16[512,1280]{1,0:T(8,128)(2,1)S(1)}, u32[]{:S(2)}, u32[]{:S(2)}) collective-permute-start(bf16[512,1280]{1,0:T(8,128)(2,1)} %add_convert_fusion.2), channel_id=1, source_target_pairs={{0,1},{1,0},{2,3},{3,2},{4,5},{5,4},{6,7},{7,6},{8,9},{9,8},{10,11... | collective-permute-start | bytes 3932168 | tf_op jit(solution)/shard_map/ppermute | solution.py:194
  1304.9 198.1 %collective-permute-start.45 = (bf16[512,1280]{1,0:T(8,128)(2,1)}, bf16[512,1280]{1,0:T(8,128)(2,1)}, u32[]{:S(2)}, u32[]{:S(2)}) collective-permute-start(bf16[512,1280]{1,0:T(8,128)(2,1)} %get-tuple-element.140), channel_id=1, source_target_pairs={{0,1},{1,0},{2,3},{3,2},{4,5},{5,4},{6,7},{7,6},{8,9},{9,8},{10,11... | collective-permute-start | bytes 3932168 | tf_op jit(solution)/shard_map/ppermute | solution.py:194
  (143 other events, 2115.0 us)
Sparse Core Ops, SparseCore 0:
  39.2 71.5 all-gather.12
  112.7 72.3 all-gather.14
  191.2 72.5 all-gather.16
  270.1 72.4 all-gather.18
  344.3 72.3 all-gather.20
  431.6 73.8 all-gather.22
  550.0 72.4 reduce-scatter.6
  633.9 71.7 all-reduce.7
  709.0 71.3 reduce-scatter.8
  782.8 71.2 all-reduce.9
  857.7 71.3 reduce-scatter.10
  931.4 71.2 all-reduce.11
  1006.6 71.3 reduce-scatter.12
  1080.4 71.2 all-reduce.13
  1154.6 71.3 reduce-scatter.14
  1231.4 121.9 all-reduce.15
  1355.7 71.3 all-reduce.17
  1430.8 71.3 reduce-scatter.16
  1504.8 71.2 all-reduce.19

commit v4 on v3

--- a/solution.py
+++ b/solution.py
@@ -229,11 +229,15 @@
 class CoreSwap:
     def __init__(self, blocks, place):
         self.place = place
-        self.kept = lax.dynamic_index_in_dim(blocks, place.core, 1, False)
-        self.came = mate(lax.dynamic_index_in_dim(blocks, 1 - place.core, 1, False))
+        self.blocks = blocks
+        self.came = mate(jnp.where(place.core == 0, blocks[:, 1], blocks[:, 0]))
 
     def join(self):
-        whole = ordered(self.kept, self.came, self.place.core, 1)
+        whole = jnp.where(
+            self.place.core == 0,
+            jnp.stack([self.blocks[:, 0], self.came], axis=1),
+            jnp.stack([self.came, self.blocks[:, 1]], axis=1),
+        )
         return whole.reshape(-1, whole.shape[-1])
 
 
@@ -301,6 +305,18 @@
     return lax.dynamic_slice_in_dim(value, index * size, size, 0)
 
 
+def small_total(value, place):
+    if place.chips != 2 or lax.axis_size("ctx") != 4:
+        return lax.psum(value, ("x", "core", "ctx", "tp"))
+    value = value + mate(value)
+    value = value + other_tp(value)
+    value = value + lax.ppermute(value, "x", [(0, 1), (1, 0)])
+    value = value + lax.ppermute(value, "ctx", [(0, 1), (3, 2)])
+    value = value + lax.ppermute(value, "ctx", [(1, 2), (2, 1)])
+    outer = (place.ctx == 0) | (place.ctx == 3)
+    return jnp.where(outer, lax.ppermute(value, "ctx", [(1, 0), (2, 3)]), value)
+
+
 def core_sum(own_part, mate_part):
     return own_part + wide(mate(narrow(mate_part)))
 
@@ -313,21 +329,62 @@
 def pair_major(value):
     width = value.shape[-1]
     return jnp.concatenate(
-        [value[kind, ..., at : at + PAIR] for at in range(0, width, PAIR) for kind in range(3)],
+        [value[kind, :, at : at + PAIR] for at in range(0, width, PAIR) for kind in range(3)],
         axis=-1,
     )
 
 
-def from_pair_major(value):
-    width = value.shape[-1]
-    return jnp.stack(
-        [
-            jnp.concatenate(
-                [value[..., at : at + PAIR] for at in range(kind * PAIR, width, 3 * PAIR)], axis=-1
-            )
-            for kind in range(3)
-        ]
-    )
+def pack_kernel(qkv_ref, proj_ref, out_ref):
+    step = pl.program_id(0)
+    head_steps = pl.num_programs(0) // 4 * 3
+
+    @pl.when(step < head_steps)
+    def _():
+        out_ref[...] = qkv_ref[0, 0]
+
+    @pl.when(step >= head_steps)
+    def _():
+        out_ref[...] = jnp.transpose(proj_ref[0])
+
+
+def attn_piece(layer, qkv_weight, proj_weight):
+    rows, width = qkv_weight.shape[2:]
+    head_steps = 3 * width // PAIR
+
+    def qkv_place(step):
+        step = jnp.minimum(step, head_steps - 1)
+        return (layer, step % 3, 0, step // 3)
+
+    return pl.pallas_call(
+        pack_kernel,
+        grid=(head_steps + width // PAIR,),
+        in_specs=[
+            pl.BlockSpec((1, 1, rows, PAIR), qkv_place),
+            pl.BlockSpec(
+                (1, PAIR, rows), lambda step: (layer, jnp.maximum(step - head_steps, 0), 0)
+            ),
+        ],
+        out_specs=pl.BlockSpec((rows, PAIR), lambda step: (0, step)),
+        out_shape=jax.ShapeDtypeStruct((rows, 4 * width), jnp.bfloat16),
+    )(qkv_weight, proj_weight)
+
+
+def unpack_kernel(first_ref, second_ref, out_ref):
+    out_ref[0, 0] = first_ref[...].astype(jnp.float32)
+    out_ref[1, 0] = second_ref[...].astype(jnp.float32)
+
+
+def unpack_heads(first, second):
+    rows, width = first.shape
+    width = width // 4
+    block = pl.BlockSpec((rows, PAIR), lambda step: (0, step))
+    return pl.pallas_call(
+        unpack_kernel,
+        grid=(3 * width // PAIR,),
+        in_specs=[block, block],
+        out_specs=pl.BlockSpec((2, 1, rows, PAIR), lambda step: (0, step % 3, 0, step // 3)),
+        out_shape=jax.ShapeDtypeStruct((2, 3, rows, width), jnp.float32),
+    )(first, second)
 
 
 def per_device(
@@ -358,18 +415,11 @@
     def both_seqs(own, other):
         return ordered(own, other, place.tp)
 
-    def attn_piece(layer):
-        return jnp.concatenate(
-            [pair_major(qkv_weight[layer]), jnp.transpose(proj_weight[layer])], axis=1
-        )
-
     own_tokens = my_seq(tokens)
-    attn_blocks = gather_blocks(attn_piece(0), place)
-    step_value = own_tokens
-    halo = []
-    for _ in range(reach):
-        step_value = onward(step_value)
-        halo.insert(0, step_value)
+    attn_blocks = gather_blocks(attn_piece(0, qkv_weight, proj_weight), place)
+    halo = [onward(own_tokens)]
+    for _ in range(reach - 1):
+        halo.insert(0, onward(halo[0]))
     vectors = jnp.concatenate([norm_gains, norm_biases], axis=1)
     vectors = gather_small(vectors.reshape(-1, vectors.shape[2]), place)
     vectors = wide(vectors).reshape(layer_count, 6, model_width)
@@ -377,13 +427,14 @@
     biases = wide(jnp.where(place.home, biases, other_tp(biases)))
     lengths = my_seq(doc_lengths)
     lengths = jnp.stack([lengths, mate(lengths)])
-    attn_blocks, later = tie(
-        attn_blocks,
-        (fc_weight[0], jnp.transpose(out_weight[0]), attn_piece(1),
-         fc_weight[1], jnp.transpose(out_weight[1])),
-    )
-    fc_blocks = gather_blocks(later[0], place)
-    out_blocks = gather_blocks(later[1], place)
+    mlp_pieces = [
+        jnp.concatenate([fc_weight[layer], jnp.transpose(out_weight[layer])], axis=1)
+        for layer in range(layer_count)
+    ]
+    attn_later = attn_piece(1, qkv_weight, proj_weight)
+    halo[-1], mlp_pieces, attn_later = tie(halo[-1], mlp_pieces, attn_later)
+    mlp_blocks = gather_blocks(mlp_pieces[0], place)
+    fc_width = fc_weight.shape[2]
 
     doc_ends = jnp.cumsum(lengths, axis=1)
     first_pos = place.ctx * block_len
@@ -418,24 +469,23 @@
         w_qkv, w_proj_t = w_attn[:, : 3 * half_width], w_attn[:, 3 * half_width :]
         packed = narrow(dot_f32(near, w_qkv) + bias_qkv).reshape(2, key_len, -1)
         mixed, log_total = attention_forward(packed, low_pos)
+        if layer + 1 < layer_count:
+            mixed, attn_later = tie(mixed, attn_later)
+            attn_blocks = gather_blocks(attn_later, place)
         mate_part = dot_second(mixed[1], w_proj_t)
         own_part = dot_second(mixed[0], w_proj_t)
         middle = hidden + core_sum(own_part, mate_part) + shifts[1]
         mlp_own, hat_mlp, inv_mlp = norm_forward(middle, gains[1], shifts[2])
         mlp_in = jnp.concatenate([mlp_own, mate(mlp_own)])
-        mlp_in, fc_blocks = tie(mlp_in, fc_blocks)
-        w_fc = CoreSwap(fc_blocks, place).join()
+        mlp_in, mlp_blocks = tie(mlp_in, mlp_blocks)
+        w_fc = CoreSwap(mlp_blocks[..., :fc_width], place).join()
+        out_swap = CoreSwap(mlp_blocks[..., fc_width:], place)
         if layer + 1 < layer_count:
-            fc_blocks, piece = tie(fc_blocks, later[2])
-            attn_blocks = gather_blocks(piece, place)
+            w_fc, piece = tie(w_fc, mlp_pieces[layer + 1])
+            mlp_blocks = gather_blocks(piece, place)
         pre_act = dot_f32(mlp_in, w_fc) + bias_fc
         activated = narrow(jax.nn.gelu(pre_act, approximate=True))
-        activated, out_blocks = tie(activated, out_blocks)
-        w_out_t = CoreSwap(out_blocks, place).join()
-        if layer + 1 < layer_count:
-            out_blocks, pieces = tie(out_blocks, later[3:])
-            fc_blocks = gather_blocks(pieces[0], place)
-            out_blocks = gather_blocks(pieces[1], place)
+        w_out_t = out_swap.join()
         mate_part = dot_second(activated[block_len:], w_out_t)
         own_part = dot_second(activated[:block_len], w_out_t)
         hidden = middle + core_sum(own_part, mate_part) + shifts[3]
@@ -448,10 +498,10 @@
     own_output = narrow(hidden)
     output = both_seqs(own_output, other_tp(own_output))
 
-    grad_hidden = wide(my_seq(cotangent))
+    grad_hidden, _ = tie(wide(my_seq(cotangent)), own_output)
     last_sum = None
     sums = {}
-    waiting = []
+    waiting, latest, first_sum = [], [], []
     small_parts = [None] * layer_count
 
     def advance(value, name):
@@ -459,6 +509,11 @@
         share = waiting.pop(0)
         assert share[0] == name
         value, share, last_sum = tie(value, share[1], last_sum)
+        if latest:
+            sums[latest[0]] = last_sum
+        else:
+            first_sum.append(last_sum)
+        latest[:] = [name]
         last_sum = lax.psum(share, "ctx")
         sums[name] = last_sum
         return value
@@ -470,6 +525,11 @@
         w_qkv, w_proj_t, w_fc, w_out_t = weights[layer]
         final = layer == 0
         grad_out_bias = jnp.sum(grad_hidden, axis=0)
+        if not final:
+            bias_parts = jnp.sum(grad_hidden.reshape(16, -1, model_width), axis=1)
+            grad_hidden, bias_parts = tie(grad_hidden, bias_parts)
+            bias_parts = lax.psum(bias_parts, ("x", "core", "ctx", "tp"))
+            last_sum = bias_parts
         grad_low = narrow(grad_hidden)
         grad_low = jnp.concatenate([grad_low, mate(grad_low)])
         out_swap = scatter_swap(narrow(dot_first(grad_low, activated)), place)
@@ -534,12 +594,13 @@
             ]
         )
 
-    small = lax.psum(jnp.stack(small_parts), ("x", "core", "ctx", "tp"))
+    small = small_total(jnp.stack(small_parts), place)
     far_grad = wide(other_tp(narrow(grad_hidden)))
     token_grad = both_seqs(grad_hidden, far_grad)
     advance((), "attn0")
     split = 6 * model_width
     norms = small[:, :split].reshape(layer_count, 6, model_width)
+    norms = norms.at[1, 5].set(jnp.sum(first_sum[0], axis=0))
     norms = lax.dynamic_slice_in_dim(norms, place.shard * shard_rows, shard_rows, 2)
     halves = small[:, split:].reshape(layer_count, 2, -1)
     halves = lax.dynamic_index_in_dim(halves, place.tp, 1, False)
@@ -550,7 +611,7 @@
         token_grad,
         norms[:, :2],
         norms[:, 2:],
-        jnp.stack([from_pair_major(wide(v[:, :packed_width])) for v in attn]),
+        unpack_heads(*attn),
         halves[:, : 2 * half_width].reshape(layer_count, 2, half_width),
         jnp.stack([jnp.transpose(wide(v[:, packed_width:])) for v in attn]),
         jnp.stack([wide(sums["fc%d" % layer]) for layer in range(layer_count)]),

time: 1600 us -> 1570 us (0.981)
  waiting for transfers between devices: 778 us -> 697 us
  Pallas kernels: 142 us -> 175 us
  other arithmetic: 175 us -> 196 us
    select_n x15 -> x3, other arithmetic: 78.6 us -> 7.01 us  [ordered(): jnp.where(position == 0, jnp.stack([own, other], axis=axis), jnp.stack([o...]
    select_n x0 -> x19, other arithmetic: none -> 62.8 us  [the longest x12 49.4 us: join(): jnp.where(self.place.core == 0, jnp.stack([self.blocks[:, 0], self.came],...]
    dynamic_slice x12 -> x0, local copies, waits for them, and re-layouts: 54.6 us -> none  [__init__(): self.kept = lax.dynamic_index_in_dim(blocks, place.core, 1, False)]
    psum x6, waiting for transfers between devices: 147 us -> 94.2 us  [advance(): last_sum = lax.psum(share, 'ctx')]
    psum x1, waiting for transfers between devices: 47.4 us -> 0.01 us  [per_device(): bias_parts = lax.psum(bias_parts, ('x', 'core', 'ctx', 'tp'))]
    all_gather x6 -> x4, waiting for transfers between devices: 99.8 us -> 57 us  [gather_blocks(): whole = lax.all_gather(piece, ('x', 'tp'), axis=0, tiled=False)]
    reduce_scatter x6, waiting for transfers between devices: 262 us -> 300 us  [scatter_sum(): lax.psum_scatter(blocks, ('x', 'tp'), scatter_dimension=0, tiled=True)]
    pallas_call x0 -> x3, Pallas kernels: none -> 32.6 us  [the longest x2 22.9 us: attn_piece(): pl.pallas_call(pack_kernel, grid=(head_steps + width // PAIR,), in_specs=...]
  transfers between devices with their start and end apart: 65 -> 69, of which waited for: 35 -> 34; matrix products, arithmetic and copies ran while one was open for 35% -> 34% of each run, Pallas kernels for 9% -> 10%
where the time goes in v4:
time: 1570 us; the launch traced here: 1560 us
  waiting for transfers between devices  697 us (44%)
  matrix products  307 us (20%)
  other arithmetic  196 us (12%)
  Pallas kernels  175 us (11%)
  local copies, waits for them, and re-layouts  123 us (8%)
  starting transfers between devices  48.3 us (3%)
  between operations  16.6 us (1%)
    reduce_scatter x6, waiting for transfers between devices, scatter_sum(): lax.psum_scatter(blocks, ('x', 'tp'), scatter_dimension=0, tiled=True)  300 us
    dot_general x24, matrix products, contract(): lax.dot_general(left_side, right_side, (((left_dim,), (right_dim,)), ((),...  197 us
    dot_general x8, matrix products, dot_f32(): return jnp.dot(left_side, right_side, preferred_element_type=jnp.float32)  110 us
    psum x6, waiting for transfers between devices, advance(): last_sum = lax.psum(share, 'ctx')  94.2 us
    ppermute x4, waiting for transfers between devices, onward(): return lax.ppermute(value, 'ctx', [(i, i + 1) for i in range(count - 1)])  82.8 us
    pallas_call x2, Pallas kernels, attention_backward(): pl.pallas_call(backward_kernel, grid=(groups, pairs), in_specs=[packed_sp...  79.8 us
    unnamed x312, local copies, waits for them, and re-layouts  78.9 us
    ppermute x4, waiting for transfers between devices, backward_step(): return lax.ppermute(value, 'ctx', [(i + 1, i) for i in range(count - 1)])  77.6 us
  transfers between devices with their start and end apart: 69, of which 34 were waited for; matrix products, arithmetic and copies ran while one was open for 34% of the time, Pallas kernels for 10%

profile of v4, /device:TPU:0, one launch (start us, length us, event | category | flops | bytes accessed | tf_op | source)
XLA Modules:
  0.0 1562.6 jit_solution(4746144767275287107)
XLA Ops:
  9.5 11.4 shard_map.187
  29.9 11.5 shard_map.186
  48.4 9.3 collective-permute-done
  70.2 23.7 %collective-permute-done.1 = bf16[512,1280]{1,0:T(8,128)(2,1)} collective-permute-done((bf16[512,1280]{1,0:T(8,128)(2,1)S(1)}, bf16[512,1280]{1,0:T(8,128)(2,1)}, u32[]{:S(2)}, u32[]{:S(2)}) %collective-permute-start.1) | collective-permute-done | bytes 1310752 | tf_op jit(solution)/shard_map/ppermute | solution.py:199
  124.5 20.0 %add_convert_fusion.1 = bf16[3072,1920]{1,0:T(8,128)(2,1)S(1)} fusion(bf16[3072,1280]{1,0:T(8,128)(2,1)} %constant_dynamic-update-slice_fusion, f32[1920]{0:T(1024)S(1)} %reduce.6, bf16[1280,2560]{1,0:T(8,128)(2,1)S(1)} %bitcast.481), kind=kOutput, calls=%fused_computation.13 | convolution fusion | flops 15111290880 | bytes 24584192 | tf_op jit(solution)/shard_map/dot_general | solution.py:258
  144.5 31.1 %shard_map.188 = (bf16[2,512,640]{2,1,0:T(8,128)(2,1)S(1)}, f32[2,5,2,512]{3,2,1,0:T(2,128)S(1)}) custom-call(bf16[2,1536,1920]{2,1,0:T(8,128)(2,1)S(1)} %bitcast.427, s32[2,512,1]{2,1,0:T(8,128)S(1)} %subtract_add_fusion.low_ref), custom_call_target="tpu_custom_call" | custom-call | flops 6710886400 | bytes 11796480 | tf_op jit(solution)/shard_map/pallas_call | solution.py:80
  191.1 34.7 %all-gather.11.cloned.1.call-done = bf16[1280,5120]{1,0:T(8,128)(2,1)} async-done(((bf16[320,5120]{1,0:T(8,128)(2,1)}), bf16[1280,5120]{1,0:T(8,128)(2,1)}) %all-gather.11.cloned.1.call-update) | async-done | bytes 13107216 | tf_op jit(solution)/shard_map/all_gather | solution.py:245
  225.8 8.9 fusion.144
  235.3 8.5 collective-permute-done.12
  248.2 15.9 %multiply_convert_fusion.1 = (bf16[1024,2560]{1,0:T(8,128)(2,1)}, f32[1024,2560]{1,0:T(8,128)}) fusion(f32[2560]{0:T(1024)S(1)} %get-tuple-element.147, bf16[1024,1280]{1,0:T(8,128)(2,1)} %pad_maximum_fusion.5, bf16[1280,2560]{1,0:T(8,128)(2,1)} %bitcast.462), kind=kOutput, calls=%fused_computation.39 | convolution fusion | flops 6737100800 | bytes 24913920 | tf_op jit(solution)/shard_map/dot_general | solution.py:258
  269.3 8.3 convolution_convert_fusion.15
  277.8 22.3 %all-gather.13.cloned.1.call-done = bf16[1280,2560]{1,0:T(8,128)(2,1)} async-done(((bf16[320,2560]{1,0:T(8,128)(2,1)}), bf16[1280,2560]{1,0:T(8,128)(2,1)}) %all-gather.13.cloned.1.call-update) | async-done | bytes 6553616 | tf_op jit(solution)/shard_map/all_gather | solution.py:245
  318.3 26.9 %collective-permute-done.15 = bf16[512,1280]{1,0:T(8,128)(2,1)} collective-permute-done((bf16[512,1280]{1,0:T(8,128)(2,1)S(1)}, bf16[512,1280]{1,0:T(8,128)(2,1)}, u32[]{:S(2)}, u32[]{:S(2)}) %collective-permute-start.15) | collective-permute-done | bytes 1310752 | tf_op jit(solution)/shard_map/ppermute | solution.py:199
  354.2 22.9 %collective-permute-done.16 = bf16[512,1280]{1,0:T(8,128)(2,1)} collective-permute-done((bf16[512,1280]{1,0:T(8,128)(2,1)}, bf16[512,1280]{1,0:T(8,128)(2,1)}, u32[]{:S(2)}, u32[]{:S(2)}) %collective-permute-start.16) | collective-permute-done | bytes 1310752 | tf_op jit(solution)/shard_map/ppermute | solution.py:199
  394.8 18.5 %add_convert_fusion = bf16[3072,1920]{1,0:T(8,128)(2,1)S(1)} fusion(bf16[3072,1280]{1,0:T(8,128)(2,1)} %copy-done.62, f32[1920]{0:T(1024)S(1)} %reduce.14, bf16[1280,2560]{1,0:T(8,128)(2,1)S(1)} %bitcast.456), kind=kOutput, calls=%fused_computation.12 | convolution fusion | flops 15111290880 | bytes 24584192 | tf_op jit(solution)/shard_map/dot_general | solution.py:258
  413.4 31.1 %shard_map.189 = (bf16[2,512,640]{2,1,0:T(8,128)(2,1)S(1)}, f32[2,5,2,512]{3,2,1,0:T(2,128)S(1)}) custom-call(bf16[2,1536,1920]{2,1,0:T(8,128)(2,1)S(1)} %bitcast.429, s32[2,512,1]{2,1,0:T(8,128)S(1)} %subtract_add_fusion.low_ref), custom_call_target="tpu_custom_call" | custom-call | flops 6710886400 | bytes 11796480 | tf_op jit(solution)/shard_map/pallas_call | solution.py:80
  457.9 9.0 fusion.143
  467.4 8.6 collective-permute-done.23
  493.5 12.7 multiply_convert_fusion
  528.8 10.3 convolution_convert_fusion.3
  540.1 17.8 %fusion.13 = bf16[1024,2560]{1,0:T(8,128)(2,1)} fusion(f32[1024,2560]{1,0:T(8,128)} %get-tuple-element.219, f32[2560]{0:T(1024)S(1)} %get-tuple-element.146, bf16[1280,2560]{1,0:T(8,128)(2,1)} %bitcast.478, bf16[512,1280]{1,0:T(8,128)(2,1)} %collective-permute-done.27, bf16[512,1280]{1,0:T(8,128)(2,1)} %convert_element_type.225), kind=kOutput, calls=%fused_computation.35 | convolution fusion | flops 6771179520 | bytes 24913920 | tf_op jit(solution)/shard_map/dot_general | solution.py:258
  567.6 8.5 convolution_convert_fusion.13
  576.4 10.2 convolution_convert_fusion.2
  591.1 7.4 multiply_reduce_fusion
  609.7 40.0 %shard_map.190 = bf16[2,1536,1920]{2,1,0:T(8,128)(2,1)S(1)} custom-call(bf16[2,1536,1920]{2,1,0:T(8,128)(2,1)} %bitcast.430, bf16[2,512,640]{2,1,0:T(8,128)(2,1)S(1)} %get-tuple-element.80.mixed_ref, bf16[2,512,640]{2,1,0:T(8,128)(2,1)S(1)} %bitcast.433, f32[2,5,2,512]{3,2,1,0:T(2,128)S(1)} %get-tuple-element.88.total_ref, ...), custom_call_target="tpu_custom_call" | custom-call | flops 16777216000 | bytes 23592960 | tf_op jit(solution)/shard_map/pallas_call | solution.py:163
  654.0 71.7 %reduce-scatter.7.cloned.1.call-done = bf16[320,2560]{1,0:T(8,128)(2,1)} async-done(((bf16[1280,2560]{1,0:T(8,128)(2,1)}), bf16[320,2560]{1,0:T(8,128)(2,1)}) %reduce-scatter.7.cloned.1.call-update) | async-done | bytes 1638416 | tf_op jit(solution)/shard_map/reduce_scatter | solution.py:254
  742.3 13.5 convolution_convert_fusion.7
  755.8 18.8 %convolution_convert_fusion.5 = bf16[1280,1920]{1,0:T(8,128)(2,1)} fusion(bf16[3072,1280]{1,0:T(8,128)(2,1)S(1)} %bitcast.506, bf16[3072,1920]{1,0:T(8,128)(2,1)S(1)} %bitcast.418), kind=kOutput, calls=%fused_computation.43 | convolution fusion | flops 15101952000 | bytes 24576000 | tf_op jit(solution)/shard_map/dot_general | solution.py:15
  786.8 12.3 convert_add_fusion.1
  800.6 31.3 %collective-permute-done.33 = bf16[512,1280]{1,0:T(8,128)(2,1)S(1)} collective-permute-done((bf16[512,1280]{1,0:T(8,128)(2,1)S(1)}, bf16[512,1280]{1,0:T(8,128)(2,1)S(1)}, u32[]{:S(2)}, u32[]{:S(2)}) %collective-permute-start.33) | collective-permute-done | bytes 1310752 | tf_op jit(solution)/shard_map/ppermute | solution.py:204
  833.5 40.7 %reduce-scatter.9.cloned.1.call-done = bf16[320,2560]{1,0:T(8,128)(2,1)} async-done(((bf16[1280,2560]{1,0:T(8,128)(2,1)}), bf16[320,2560]{1,0:T(8,128)(2,1)}) %reduce-scatter.9.cloned.1.call-update) | async-done | bytes 1638416 | tf_op jit(solution)/shard_map/reduce_scatter | solution.py:254
  911.2 15.7 %fusion.6 = bf16[1024,2560]{1,0:T(8,128)(2,1)S(1)} fusion(f32[1024,2560]{1,0:T(8,128)} %get-tuple-element.213, f32[2560]{0:T(1024)S(1)} %copy-done.92, bf16[1280,2560]{1,0:T(8,128)(2,1)S(1)} %bitcast.471, bf16[512,1280]{1,0:T(8,128)(2,1)} %copy-done.100, bf16[512,1280]{1,0:T(8,128)(2,1)S(1)} %convert_element_type.240), kind=kOutput, calls=%fused_computation.28 | convolution fusion | flops 6771179520 | bytes 24913920 | tf_op jit(solution)/shard_map/dot_general | solution.py:258
  939.1 8.9 all-reduce.12.cloned.1.call-done
  948.0 74.3 %reduce-scatter.11.cloned.1.call-done = bf16[320,2560]{1,0:T(8,128)(2,1)} async-done(((bf16[1280,2560]{1,0:T(8,128)(2,1)}), bf16[320,2560]{1,0:T(8,128)(2,1)}) %reduce-scatter.11.cloned.1.call-update) | async-done | bytes 1638416 | tf_op jit(solution)/shard_map/reduce_scatter | solution.py:254
  1033.6 10.1 convolution_convert_fusion
  1055.2 23.2 %collective-permute-done.26 = bf16[512,1280]{1,0:T(8,128)(2,1)} collective-permute-done((bf16[512,1280]{1,0:T(8,128)(2,1)}, bf16[512,1280]{1,0:T(8,128)(2,1)}, u32[]{:S(2)}, u32[]{:S(2)}) %collective-permute-start.26) | collective-permute-done | bytes 1310752 | tf_op jit(solution)/shard_map/ppermute | solution.py:194
  1093.4 39.8 %shard_map.191 = bf16[2,1536,1920]{2,1,0:T(8,128)(2,1)S(1)} custom-call(bf16[2,1536,1920]{2,1,0:T(8,128)(2,1)} %bitcast.428, bf16[2,512,640]{2,1,0:T(8,128)(2,1)S(1)} %copy-done.7, bf16[2,512,640]{2,1,0:T(8,128)(2,1)S(1)} %bitcast.432, f32[2,5,2,512]{3,2,1,0:T(2,128)S(1)} %get-tuple-element.101.total_ref, s32[2,1,512]{2,1,0:T(1,128)S(1)} %subtract_add_fusion.1.low_ref), custom_call_target="tpu_custom_call" | custom-call | flops 16777216000 | bytes 23592960 | tf_op jit(solution)/shard_map/pallas_call | solution.py:163
  1137.5 33.1 %reduce-scatter.13.cloned.1.call-done = bf16[320,2560]{1,0:T(8,128)(2,1)} async-done(((bf16[1280,2560]{1,0:T(8,128)(2,1)}), bf16[320,2560]{1,0:T(8,128)(2,1)}) %reduce-scatter.13.cloned.1.call-update) | async-done | bytes 1638416 | tf_op jit(solution)/shard_map/reduce_scatter | solution.py:254
  1184.3 13.8 convolution_convert_fusion.6
  1198.2 18.6 %convolution_convert_fusion.4 = bf16[1280,1920]{1,0:T(8,128)(2,1)} fusion(bf16[3072,1280]{1,0:T(8,128)(2,1)S(1)} %bitcast.504, bf16[3072,1920]{1,0:T(8,128)(2,1)S(1)} %bitcast.423), kind=kOutput, calls=%fused_computation.42 | convolution fusion | flops 15101952000 | bytes 24576000 | tf_op jit(solution)/shard_map/dot_general | solution.py:15
  1230.5 12.3 convert_add_fusion
  1253.8 25.1 %collective-permute-done.42 = bf16[512,1280]{1,0:T(8,128)(2,1)S(1)} collective-permute-done((bf16[512,1280]{1,0:T(8,128)(2,1)S(1)}, bf16[512,1280]{1,0:T(8,128)(2,1)S(1)}, u32[]{:S(2)}, u32[]{:S(2)}) %collective-permute-start.42) | collective-permute-done | bytes 1310752 | tf_op jit(solution)/shard_map/ppermute | solution.py:204
  1292.9 21.2 %collective-permute-done.44 = bf16[512,1280]{1,0:T(8,128)(2,1)S(1)} collective-permute-done((bf16[512,1280]{1,0:T(8,128)(2,1)}, bf16[512,1280]{1,0:T(8,128)(2,1)S(1)}, u32[]{:S(2)}, u32[]{:S(2)}) %collective-permute-start.44) | collective-permute-done | bytes 1310752 | tf_op jit(solution)/shard_map/ppermute | solution.py:204
  1363.5 8.8 collective-permute-done.51
  1374.5 20.5 %all-reduce.18.cloned.1.call-done = bf16[320,2560]{1,0:T(8,128)(2,1)} async-done(((bf16[320,2560]{1,0:T(8,128)(2,1)}), bf16[320,2560]{1,0:T(8,128)(2,1)}) %all-reduce.18.cloned.1.call-update) | async-done | bytes 1638416 | tf_op jit(solution)/shard_map/psum | solution.py:517
  1395.0 75.2 %reduce-scatter.17.cloned.1.call-done = bf16[320,2560]{1,0:T(8,128)(2,1)} async-done(((bf16[1280,2560]{1,0:T(8,128)(2,1)}), bf16[320,2560]{1,0:T(8,128)(2,1)}) %reduce-scatter.17.cloned.1.call-update) | async-done | bytes 1638416 | tf_op jit(solution)/shard_map/reduce_scatter | solution.py:254
  1479.0 64.8 %all-reduce.20.cloned.1.call-done.first_ref = bf16[320,2560]{1,0:T(8,128)(2,1)} async-done(((bf16[320,2560]{1,0:T(8,128)(2,1)}), bf16[320,2560]{1,0:T(8,128)(2,1)}) %all-reduce.20.cloned.1.call-update) | async-done | bytes 1638416 | tf_op jit(solution)/shard_map/psum | solution.py:517
  1546.1 9.7 shard_map.192
  (638 shorter events, 453.0 us)
Async XLA Ops:
  7.2 90.1 %all-gather.9.cloned.1.call-start = ((), (), s32[]{:S(2)}) async-start(), calls=%async_computation.19 | async-start | bytes 8192000 | tf_op jit(solution)/shard_map/all_gather | solution.py:245
  20.9 205.0 %all-gather.11.cloned.1.call-start = ((), (), s32[]{:S(2)}) async-start(), calls=%async_computation.20 | async-start | bytes 16384000 | tf_op jit(solution)/shard_map/all_gather | solution.py:245
  20.9 37.0 %collective-permute-start.9 = (s32[4]{0:T(128)S(1)}, s32[4]{0:T(128)S(1)}, u32[]{:S(2)}, u32[]{:S(2)}) collective-permute-start(s32[4]{0:T(128)S(1)} %fusion.183), channel_id=1, source_target_pairs={{0,8},{8,0},{1,9},{9,1},{2,10},{10,2},{3,11},{11,3},{4,12},{12,4},... | collective-permute-start | bytes 56 | tf_op jit(solution)/shard_map/ppermute | solution.py:190
  21.5 39.1 %collective-permute-start.2 = (bf16[12,320]{1,0:T(8,128)(2,1)S(1)}, bf16[12,320]{1,0:T(8,128)(2,1)S(1)}, u32[]{:S(2)}, u32[]{:S(2)}) collective-permute-start(bf16[12,320]{1,0:T(8,128)(2,1)S(1)} %reshape.456), channel_id=1, source_target_pairs={{0,8},{8,0},{1,9},{9,1},{2,10},{10,2},{3,11},{11,3},{4,12},{12,4},... | collective-permute-start | bytes 23048 | tf_op jit(solution)/shard_map/ppermute | solution.py:190
  21.7 40.7 %collective-permute-start.8 = (bf16[2,3840]{1,0:T(2,128)(2,1)S(1)}, bf16[2,3840]{1,0:T(2,128)(2,1)S(1)}, u32[]{:S(2)}, u32[]{:S(2)}) collective-permute-start(bf16[2,3840]{1,0:T(2,128)(2,1)S(1)} %constant_dynamic-update-slice_fusion.6), channel_id=1, source_target_pairs={{0,1},{1,0},{2,3},{3,2},{4,5},{5,4},{6,7},{7,6},{8,9},{9,8},{10,11... | collective-permute-start | bytes 46088 | tf_op jit(solution)/shard_map/ppermute | solution.py:194
  26.3 31.4 %collective-permute-start = (bf16[512,1280]{1,0:T(8,128)(2,1)S(1)}, bf16[512,1280]{1,0:T(8,128)(2,1)S(1)}, u32[]{:S(2)}, u32[]{:S(2)}) collective-permute-start(bf16[512,1280]{1,0:T(8,128)(2,1)S(1)} %get-tuple-element.163), channel_id=1, source_target_pairs={{0,2},{2,4},{4,6},{1,3},{3,5},{5,7},{8,10},{10,12},{12,14},{9,11},... | collective-permute-start | bytes 3932168 | tf_op jit(solution)/shard_map/ppermute | solution.py:199
  57.7 242.3 %all-gather.13.cloned.1.call-start = ((), (), s32[]{:S(2)}) async-start(), calls=%async_computation.21 | async-start | bytes 8192000 | tf_op jit(solution)/shard_map/all_gather | solution.py:245
  62.7 31.2 %collective-permute-start.1 = (bf16[512,1280]{1,0:T(8,128)(2,1)S(1)}, bf16[512,1280]{1,0:T(8,128)(2,1)}, u32[]{:S(2)}, u32[]{:S(2)}) collective-permute-start(bf16[512,1280]{1,0:T(8,128)(2,1)S(1)} %collective-permute-done), channel_id=1, source_target_pairs={{0,2},{2,4},{4,6},{1,3},{3,5},{5,7},{8,10},{10,12},{12,14},{9,11},... | collective-permute-start | bytes 3932168 | tf_op jit(solution)/shard_map/ppermute | solution.py:199
  103.2 15.9 %collective-permute-start.7 = (bf16[2,320,2560]{2,1,0:T(8,128)(2,1)}, bf16[2,320,2560]{2,1,0:T(8,128)(2,1)}, u32[]{:S(2)}, u32[]{:S(2)}) collective-permute-start(bf16[2,320,2560]{2,1,0:T(8,128)(2,1)} %get-tuple-element.196), channel_id=1, source_target_pairs={{0,8},{8,0},{1,9},{9,1},{2,10},{10,2},{3,11},{11,3},{4,12},{12,4},... | collective-permute-start | bytes 9830408 | tf_op jit(solution)/shard_map/ppermute | solution.py:190
  178.0 279.9 %all-gather.15.cloned.1.call-start = ((), (), s32[]{:S(2)}) async-start(), calls=%async_computation.22 | async-start | bytes 16384000 | tf_op jit(solution)/shard_map/all_gather | solution.py:245
  234.8 29.4 %collective-permute-start.13 = (bf16[2,320,2560]{2,1,0:T(8,128)(2,1)}, bf16[2,320,2560]{2,1,0:T(8,128)(2,1)}, u32[]{:S(2)}, u32[]{:S(2)}) collective-permute-start(bf16[2,320,2560]{2,1,0:T(8,128)(2,1)} %get-tuple-element.176), channel_id=1, source_target_pairs={{0,8},{8,0},{1,9},{9,1},{2,10},{10,2},{3,11},{11,3},{4,12},{12,4},... | collective-permute-start | bytes 9830408 | tf_op jit(solution)/shard_map/ppermute | solution.py:190
  248.1 405.9 %all-reduce.8.cloned.1.call-start = ((), (), s32[]{:S(2)}) async-start(), calls=%async_computation.7 | async-start | bytes 163840 | tf_op jit(solution)/shard_map/psum | solution.py:531
  277.7 27.5 %collective-permute-start.14 = (bf16[512,1280]{1,0:T(8,128)(2,1)}, bf16[512,1280]{1,0:T(8,128)(2,1)S(1)}, u32[]{:S(2)}, u32[]{:S(2)}) collective-permute-start(bf16[512,1280]{1,0:T(8,128)(2,1)} %convolution_convert_fusion.15), channel_id=1, source_target_pairs={{0,8},{8,0},{1,9},{9,1},{2,10},{10,2},{3,11},{11,3},{4,12},{12,4},... | collective-permute-start | bytes 3932168 | tf_op jit(solution)/shard_map/ppermute | solution.py:190
  305.1 72.0 %collective-permute-start.20 = (bf16[2,320,2560]{2,1,0:T(8,128)(2,1)}, bf16[2,320,2560]{2,1,0:T(8,128)(2,1)}, u32[]{:S(2)}, u32[]{:S(2)}) collective-permute-start(bf16[2,320,2560]{2,1,0:T(8,128)(2,1)} %fusion.36), channel_id=1, source_target_pairs={{0,8},{8,0},{1,9},{9,1},{2,10},{10,2},{3,11},{11,3},{4,12},{12,4},... | collective-permute-start | bytes 9830408 | tf_op jit(solution)/shard_map/ppermute | solution.py:190
  314.1 31.1 %collective-permute-start.15 = (bf16[512,1280]{1,0:T(8,128)(2,1)S(1)}, bf16[512,1280]{1,0:T(8,128)(2,1)}, u32[]{:S(2)}, u32[]{:S(2)}) collective-permute-start(bf16[512,1280]{1,0:T(8,128)(2,1)S(1)} %add_convert_fusion.3), channel_id=1, source_target_pairs={{0,2},{2,4},{4,6},{1,3},{3,5},{5,7},{8,10},{10,12},{12,14},{9,11},... | collective-permute-start | bytes 3932168 | tf_op jit(solution)/shard_map/ppermute | solution.py:199
  345.2 31.9 %collective-permute-start.16 = (bf16[512,1280]{1,0:T(8,128)(2,1)}, bf16[512,1280]{1,0:T(8,128)(2,1)}, u32[]{:S(2)}, u32[]{:S(2)}) collective-permute-start(bf16[512,1280]{1,0:T(8,128)(2,1)} %collective-permute-done.15), channel_id=1, source_target_pairs={{0,2},{2,4},{4,6},{1,3},{3,5},{5,7},{8,10},{10,12},{12,14},{9,11},... | collective-permute-start | bytes 3932168 | tf_op jit(solution)/shard_map/ppermute | solution.py:199
  354.1 36.2 %collective-permute-start.19 = (bf16[512,1280]{1,0:T(8,128)(2,1)S(1)}, bf16[512,1280]{1,0:T(8,128)(2,1)}, u32[]{:S(2)}, u32[]{:S(2)}) collective-permute-start(bf16[512,1280]{1,0:T(8,128)(2,1)S(1)} %add_convert_fusion.3), channel_id=1, source_target_pairs={{0,8},{8,0},{1,9},{9,1},{2,10},{10,2},{3,11},{11,3},{4,12},{12,4},... | collective-permute-start | bytes 3932168 | tf_op jit(solution)/shard_map/ppermute | solution.py:190
  377.1 11.7 collective-permute-start.17
  467.0 16.6 %collective-permute-start.24 = (bf16[2,320,2560]{2,1,0:T(8,128)(2,1)}, bf16[2,320,2560]{2,1,0:T(8,128)(2,1)}, u32[]{:S(2)}, u32[]{:S(2)}) collective-permute-start(bf16[2,320,2560]{2,1,0:T(8,128)(2,1)} %get-tuple-element.170), channel_id=1, source_target_pairs={{0,8},{8,0},{1,9},{9,1},{2,10},{10,2},{3,11},{11,3},{4,12},{12,4},... | collective-permute-start | bytes 9830408 | tf_op jit(solution)/shard_map/ppermute | solution.py:190
  525.6 200.1 %reduce-scatter.7.cloned.1.call-start = ((), (), s32[]{:S(2)}) async-start(), calls=%async_computation.6 | async-start | bytes 8192000 | tf_op jit(solution)/shard_map/reduce_scatter | solution.py:254
  539.9 18.0 %collective-permute-start.28 = (bf16[2,320,2560]{2,1,0:T(8,128)(2,1)S(1)}, bf16[2,320,2560]{2,1,0:T(8,128)(2,1)S(1)}, u32[]{:S(2)}, u32[]{:S(2)}) collective-permute-start(bf16[2,320,2560]{2,1,0:T(8,128)(2,1)S(1)} %fusion.39), channel_id=1, source_target_pairs={{0,8},{8,0},{1,9},{9,1},{2,10},{10,2},{3,11},{11,3},{4,12},{12,4},... | collective-permute-start | bytes 9830408 | tf_op jit(solution)/shard_map/ppermute | solution.py:190
  567.5 265.9 %all-reduce.10.cloned.1.call-start = ((), (), s32[]{:S(2)}) async-start(), calls=%async_computation.9 | async-start | bytes 3276800 | tf_op jit(solution)/shard_map/psum | solution.py:517
  576.1 13.8 collective-permute-start.29
  589.7 12.2 collective-permute-start.30
  725.8 148.4 %reduce-scatter.9.cloned.1.call-start = ((), (), s32[]{:S(2)}) async-start(), calls=%async_computation.8 | async-start | bytes 8192000 | tf_op jit(solution)/shard_map/reduce_scatter | solution.py:254
  736.9 211.1 %all-reduce.12.cloned.1.call-start = ((), (), s32[]{:S(2)}) async-start(), calls=%async_computation.11 | async-start | bytes 3276800 | tf_op jit(solution)/shard_map/psum | solution.py:517
  755.7 31.0 %collective-permute-start.32 = (bf16[1536,1280]{1,0:T(8,128)(2,1)}, bf16[1536,1280]{1,0:T(8,128)(2,1)}, u32[]{:S(2)}, u32[]{:S(2)}) collective-permute-start(bf16[1536,1280]{1,0:T(8,128)(2,1)} %convolution_convert_fusion.7), channel_id=1, source_target_pairs={{0,8},{8,0},{1,9},{9,1},{2,10},{10,2},{3,11},{11,3},{4,12},{12,4},... | collective-permute-start | bytes 11796488 | tf_op jit(solution)/shard_map/ppermute | solution.py:190
  786.3 14.3 collective-permute-start.34
  799.3 32.6 %collective-permute-start.33 = (bf16[512,1280]{1,0:T(8,128)(2,1)S(1)}, bf16[512,1280]{1,0:T(8,128)(2,1)S(1)}, u32[]{:S(2)}, u32[]{:S(2)}) collective-permute-start(bf16[512,1280]{1,0:T(8,128)(2,1)S(1)} %slice.941), channel_id=1, source_target_pairs={{2,0},{4,2},{6,4},{3,1},{5,3},{7,5},{10,8},{12,10},{14,12},{11,9},... | collective-permute-start | bytes 3932168 | tf_op jit(solution)/shard_map/ppermute | solution.py:204
  832.1 42.1 %collective-permute-start.35 = (bf16[512,1280]{1,0:T(8,128)(2,1)S(1)}, bf16[512,1280]{1,0:T(8,128)(2,1)S(1)}, u32[]{:S(2)}, u32[]{:S(2)}) collective-permute-start(bf16[512,1280]{1,0:T(8,128)(2,1)S(1)} %fusion.72), channel_id=1, source_target_pairs={{2,0},{4,2},{6,4},{3,1},{5,3},{7,5},{10,8},{12,10},{14,12},{11,9},... | collective-permute-start | bytes 3932168 | tf_op jit(solution)/shard_map/ppermute | solution.py:204
  874.2 148.1 %reduce-scatter.11.cloned.1.call-start = ((), (), s32[]{:S(2)}) async-start(), calls=%async_computation.10 | async-start | bytes 8192000 | tf_op jit(solution)/shard_map/reduce_scatter | solution.py:254
  885.9 251.5 %all-reduce.14.cloned.1.call-start = ((), (), s32[]{:S(2)}) async-start(), calls=%async_computation.13 | async-start | bytes 3276800 | tf_op jit(solution)/shard_map/psum | solution.py:517
  911.0 15.9 %collective-permute-start.37 = (bf16[2,320,2560]{2,1,0:T(8,128)(2,1)}, bf16[2,320,2560]{2,1,0:T(8,128)(2,1)}, u32[]{:S(2)}, u32[]{:S(2)}) collective-permute-start(bf16[2,320,2560]{2,1,0:T(8,128)(2,1)} %fusion.42), channel_id=1, source_target_pairs={{0,8},{8,0},{1,9},{9,1},{2,10},{10,2},{3,11},{11,3},{4,12},{12,4},... | collective-permute-start | bytes 9830408 | tf_op jit(solution)/shard_map/ppermute | solution.py:190
  1022.3 148.3 %reduce-scatter.13.cloned.1.call-start = ((), (), s32[]{:S(2)}) async-start(), calls=%async_computation.12 | async-start | bytes 8192000 | tf_op jit(solution)/shard_map/reduce_scatter | solution.py:254
  1033.6 259.4 %all-reduce.16.cloned.1.call-start = ((), (), s32[]{:S(2)}) async-start(), calls=%async_computation.15 | async-start | bytes 3276800 | tf_op jit(solution)/shard_map/psum | solution.py:517
  1046.9 31.5 %collective-permute-start.26 = (bf16[512,1280]{1,0:T(8,128)(2,1)}, bf16[512,1280]{1,0:T(8,128)(2,1)}, u32[]{:S(2)}, u32[]{:S(2)}) collective-permute-start(bf16[512,1280]{1,0:T(8,128)(2,1)} %fusion.85), channel_id=1, source_target_pairs={{0,1},{1,0},{2,3},{3,2},{4,5},{5,4},{6,7},{7,6},{8,9},{9,8},{10,11... | collective-permute-start | bytes 3932168 | tf_op jit(solution)/shard_map/ppermute | solution.py:194
  1054.8 32.5 %collective-permute-start.40 = (bf16[512,1280]{1,0:T(8,128)(2,1)}, bf16[512,1280]{1,0:T(8,128)(2,1)}, u32[]{:S(2)}, u32[]{:S(2)}) collective-permute-start(bf16[512,1280]{1,0:T(8,128)(2,1)} %convert_element_type.245), channel_id=1, source_target_pairs={{0,8},{8,0},{1,9},{9,1},{2,10},{10,2},{3,11},{11,3},{4,12},{12,4},... | collective-permute-start | bytes 3932168 | tf_op jit(solution)/shard_map/ppermute | solution.py:190
  1170.7 148.1 %reduce-scatter.15.cloned.1.call-start = ((), (), s32[]{:S(2)}) async-start(), calls=%async_computation.14 | async-start | bytes 8192000 | tf_op jit(solution)/shard_map/reduce_scatter | solution.py:254
  1178.9 216.0 %all-reduce.18.cloned.1.call-start = ((), (), s32[]{:S(2)}) async-start(), calls=%async_computation.17 | async-start | bytes 3276800 | tf_op jit(solution)/shard_map/psum | solution.py:517
  1198.1 32.3 %collective-permute-start.41 = (bf16[1536,1280]{1,0:T(8,128)(2,1)}, bf16[1536,1280]{1,0:T(8,128)(2,1)}, u32[]{:S(2)}, u32[]{:S(2)}) collective-permute-start(bf16[1536,1280]{1,0:T(8,128)(2,1)} %convolution_convert_fusion.6), channel_id=1, source_target_pairs={{0,8},{8,0},{1,9},{9,1},{2,10},{10,2},{3,11},{11,3},{4,12},{12,4},... | collective-permute-start | bytes 11796488 | tf_op jit(solution)/shard_map/ppermute | solution.py:190
  1229.9 23.9 %collective-permute-start.43 = (bf16[2,320,2560]{2,1,0:T(8,128)(2,1)}, bf16[2,320,2560]{2,1,0:T(8,128)(2,1)}, u32[]{:S(2)}, u32[]{:S(2)}) collective-permute-start(bf16[2,320,2560]{2,1,0:T(8,128)(2,1)} %get-tuple-element.181), channel_id=1, source_target_pairs={{0,8},{8,0},{1,9},{9,1},{2,10},{10,2},{3,11},{11,3},{4,12},{12,4},... | collective-permute-start | bytes 9830408 | tf_op jit(solution)/shard_map/ppermute | solution.py:190
  1246.1 32.7 %collective-permute-start.42 = (bf16[512,1280]{1,0:T(8,128)(2,1)S(1)}, bf16[512,1280]{1,0:T(8,128)(2,1)S(1)}, u32[]{:S(2)}, u32[]{:S(2)}) collective-permute-start(bf16[512,1280]{1,0:T(8,128)(2,1)S(1)} %slice.940), channel_id=1, source_target_pairs={{2,0},{4,2},{6,4},{3,1},{5,3},{7,5},{10,8},{12,10},{14,12},{11,9},... | collective-permute-start | bytes 3932168 | tf_op jit(solution)/shard_map/ppermute | solution.py:204
  1282.0 32.1 %collective-permute-start.44 = (bf16[512,1280]{1,0:T(8,128)(2,1)}, bf16[512,1280]{1,0:T(8,128)(2,1)S(1)}, u32[]{:S(2)}, u32[]{:S(2)}) collective-permute-start(bf16[512,1280]{1,0:T(8,128)(2,1)} %fusion.71), channel_id=1, source_target_pairs={{2,0},{4,2},{6,4},{3,1},{5,3},{7,5},{10,8},{12,10},{14,12},{11,9},... | collective-permute-start | bytes 3932168 | tf_op jit(solution)/shard_map/ppermute | solution.py:204
  1318.8 151.4 %reduce-scatter.17.cloned.1.call-start = ((), (), s32[]{:S(2)}) async-start(), calls=%async_computation.16 | async-start | bytes 8192000 | tf_op jit(solution)/shard_map/reduce_scatter | solution.py:254
  1331.4 212.4 %all-reduce.20.cloned.1.call-start = ((), (), s32[]{:S(2)}) async-start(), calls=%async_computation.18 | async-start | bytes 3276800 | tf_op jit(solution)/shard_map/psum | solution.py:517
  1342.6 9.2 collective-permute-start.49
  1357.4 113.5 %collective-permute-start.45 = (bf16[512,1280]{1,0:T(8,128)(2,1)}, bf16[512,1280]{1,0:T(8,128)(2,1)}, u32[]{:S(2)}, u32[]{:S(2)}) collective-permute-start(bf16[512,1280]{1,0:T(8,128)(2,1)} %get-tuple-element.158), channel_id=1, source_target_pairs={{0,1},{1,0},{2,3},{3,2},{4,5},{5,4},{6,7},{7,6},{8,9},{9,8},{10,11... | collective-permute-start | bytes 3932168 | tf_op jit(solution)/shard_map/ppermute | solution.py:194
  1358.9 13.3 collective-permute-start.51
  (149 other events, 2273.9 us)
Sparse Core Ops, SparseCore 0:
  21.0 75.4 all-gather.8
  98.9 126.8 all-gather.10
  227.7 72.3 all-gather.12
  301.7 126.8 all-gather.14
  525.8 122.6 all-reduce.7
  651.4 74.3 reduce-scatter.6
  728.1 71.2 all-reduce.9
  802.7 71.3 reduce-scatter.8
  876.7 71.2 all-reduce.11
  950.9 71.3 reduce-scatter.10
  1024.7 71.2 all-reduce.13
  1099.2 71.3 reduce-scatter.12
  1173.1 71.2 all-reduce.15
  1247.3 71.3 reduce-scatter.14
  1321.0 73.9 all-reduce.17
  1398.7 71.3 reduce-scatter.16
  1472.5 71.2 all-reduce.19

commit v5 on v4

--- a/solution.py
+++ b/solution.py
@@ -226,19 +226,60 @@
     )
 
 
+def join_kernel(core_ref, *refs):
+    out_ref = refs[-1]
+    own = pl.program_id(1) == core_ref[0]
+    at = 0
+    for blocks_ref, came_ref in zip(refs[0:-1:2], refs[1:-1:2]):
+        width = came_ref.shape[2]
+
+        @pl.when(own)
+        def _(at=at, width=width, blocks_ref=blocks_ref):
+            out_ref[:, at : at + width] = blocks_ref[0, 0]
+
+        @pl.when(jnp.logical_not(own))
+        def _(at=at, width=width, came_ref=came_ref):
+            out_ref[:, at : at + width] = came_ref[0]
+
+        at += width
+
+
 class CoreSwap:
-    def __init__(self, blocks, place):
-        self.place = place
-        self.blocks = blocks
-        self.came = mate(jnp.where(place.core == 0, blocks[:, 1], blocks[:, 0]))
-
-    def join(self):
-        whole = jnp.where(
-            self.place.core == 0,
-            jnp.stack([self.blocks[:, 0], self.came], axis=1),
-            jnp.stack([self.came, self.blocks[:, 1]], axis=1),
-        )
-        return whole.reshape(-1, whole.shape[-1])
+    def __init__(self, blocks, place, column=0, width=None):
+        self.place, self.blocks, self.column = place, blocks, column
+        width = blocks.shape[3] if width is None else width
+        other = lax.dynamic_index_in_dim(blocks, 1 - place.core, 1, False)
+        self.came = mate(other[..., column * width : (column + 1) * width])
+
+
+def join(*swaps):
+    chips, rows = swaps[0].came.shape[:2]
+    in_specs, operands, total = [], [], 0
+    for swap in swaps:
+        width = swap.came.shape[2]
+        in_specs += [
+            pl.BlockSpec(
+                (1, 1, rows, width),
+                lambda chip, part, core, column=swap.column: (chip, core[0], 0, column),
+            ),
+            pl.BlockSpec((1, rows, width), lambda chip, part, core: (chip, 0, 0)),
+        ]
+        operands += [swap.blocks, swap.came]
+        total += width
+    return pl.pallas_call(
+        join_kernel,
+        grid_spec=pltpu.PrefetchScalarGridSpec(
+            num_scalar_prefetch=1,
+            grid=(chips, 2),
+            in_specs=in_specs,
+            out_specs=pl.BlockSpec((rows, total), lambda chip, part, core: (chip * 2 + part, 0)),
+        ),
+        out_shape=jax.ShapeDtypeStruct((chips * 2 * rows, total), jnp.bfloat16),
+        compiler_params=pltpu.CompilerParams(vmem_limit_bytes=24 << 20),
+        cost_estimate=pl.CostEstimate(
+            flops=0, bytes_accessed=8 * chips * rows * total, transcendentals=0
+        ),
+    )(swaps[0].place.core.reshape(1).astype(jnp.int32), *operands)
 
 
 def gather_blocks(piece, place):
@@ -335,55 +376,51 @@
 
 
 def pack_kernel(qkv_ref, proj_ref, out_ref):
-    step = pl.program_id(0)
-    head_steps = pl.num_programs(0) // 4 * 3
-
-    @pl.when(step < head_steps)
-    def _():
-        out_ref[...] = qkv_ref[0, 0]
-
-    @pl.when(step >= head_steps)
-    def _():
-        out_ref[...] = jnp.transpose(proj_ref[0])
+    width = qkv_ref.shape[3]
+    for pair in range(width // PAIR):
+        for kind in range(3):
+            at = (3 * pair + kind) * PAIR
+            out_ref[:, at : at + PAIR] = qkv_ref[0, kind, :, pair * PAIR : (pair + 1) * PAIR]
+    out_ref[:, 3 * width :] = jnp.transpose(proj_ref[0])
 
 
 def attn_piece(layer, qkv_weight, proj_weight):
     rows, width = qkv_weight.shape[2:]
-    head_steps = 3 * width // PAIR
-
-    def qkv_place(step):
-        step = jnp.minimum(step, head_steps - 1)
-        return (layer, step % 3, 0, step // 3)
-
     return pl.pallas_call(
         pack_kernel,
-        grid=(head_steps + width // PAIR,),
+        grid=(1,),
         in_specs=[
-            pl.BlockSpec((1, 1, rows, PAIR), qkv_place),
-            pl.BlockSpec(
-                (1, PAIR, rows), lambda step: (layer, jnp.maximum(step - head_steps, 0), 0)
-            ),
+            pl.BlockSpec((1, 3, rows, width), lambda step: (layer, 0, 0, 0)),
+            pl.BlockSpec((1, width, rows), lambda step: (layer, 0, 0)),
         ],
-        out_specs=pl.BlockSpec((rows, PAIR), lambda step: (0, step)),
+        out_specs=pl.BlockSpec((rows, 4 * width), lambda step: (0, 0)),
         out_shape=jax.ShapeDtypeStruct((rows, 4 * width), jnp.bfloat16),
+        compiler_params=pltpu.CompilerParams(vmem_limit_bytes=24 << 20),
     )(qkv_weight, proj_weight)
 
 
 def unpack_kernel(first_ref, second_ref, out_ref):
-    out_ref[0, 0] = first_ref[...].astype(jnp.float32)
-    out_ref[1, 0] = second_ref[...].astype(jnp.float32)
+    kind = pl.program_id(0)
+    width = out_ref.shape[3]
+    for pair in range(width // PAIR):
+        at = pl.multiple_of((3 * pair + kind) * PAIR, PAIR)
+        for layer, ref in enumerate((first_ref, second_ref)):
+            out_ref[layer, 0, :, pair * PAIR : (pair + 1) * PAIR] = ref[
+                :, pl.ds(at, PAIR)
+            ].astype(jnp.float32)
 
 
 def unpack_heads(first, second):
     rows, width = first.shape
     width = width // 4
-    block = pl.BlockSpec((rows, PAIR), lambda step: (0, step))
+    block = pl.BlockSpec((rows, 4 * width), lambda kind: (0, 0))
     return pl.pallas_call(
         unpack_kernel,
-        grid=(3 * width // PAIR,),
+        grid=(3,),
         in_specs=[block, block],
-        out_specs=pl.BlockSpec((2, 1, rows, PAIR), lambda step: (0, step % 3, 0, step // 3)),
+        out_specs=pl.BlockSpec((2, 1, rows, width), lambda kind: (0, kind, 0, 0)),
         out_shape=jax.ShapeDtypeStruct((2, 3, rows, width), jnp.float32),
+        compiler_params=pltpu.CompilerParams(vmem_limit_bytes=24 << 20),
     )(first, second)
 
 
@@ -416,6 +453,9 @@
         return ordered(own, other, place.tp)
 
     own_tokens = my_seq(tokens)
+    grad_hidden = wide(my_seq(cotangent))
+    bias_parts = jnp.sum(grad_hidden.reshape(16, -1, model_width), axis=1)
+    bias_parts = lax.psum(bias_parts, ("x", "core", "ctx", "tp"))
     attn_blocks = gather_blocks(attn_piece(0, qkv_weight, proj_weight), place)
     halo = [onward(own_tokens)]
     for _ in range(reach - 1):
@@ -461,11 +501,17 @@
                 part = norm_forward(wide(halo[reach - 1 - index]), gains[0], shifts[0])[0]
             else:
                 step_value = part = onward(step_value)
+                if index == 0:
+                    step_value, piece = tie(step_value, mlp_pieces[layer])
+                    mlp_blocks = gather_blocks(piece, place)
+                    part = step_value
             own_near.insert(0, part)
             mate_near.insert(0, mate(part))
         near = jnp.concatenate(own_near + mate_near)
+        if layer == 0:
+            near, bias_parts = tie(near, bias_parts)
         attn_swap = CoreSwap(attn_blocks, place)
-        w_attn = attn_swap.join()
+        w_attn = join(attn_swap)
         w_qkv, w_proj_t = w_attn[:, : 3 * half_width], w_attn[:, 3 * half_width :]
         packed = narrow(dot_f32(near, w_qkv) + bias_qkv).reshape(2, key_len, -1)
         mixed, log_total = attention_forward(packed, low_pos)
@@ -478,14 +524,11 @@
         mlp_own, hat_mlp, inv_mlp = norm_forward(middle, gains[1], shifts[2])
         mlp_in = jnp.concatenate([mlp_own, mate(mlp_own)])
         mlp_in, mlp_blocks = tie(mlp_in, mlp_blocks)
-        w_fc = CoreSwap(mlp_blocks[..., :fc_width], place).join()
-        out_swap = CoreSwap(mlp_blocks[..., fc_width:], place)
-        if layer + 1 < layer_count:
-            w_fc, piece = tie(w_fc, mlp_pieces[layer + 1])
-            mlp_blocks = gather_blocks(piece, place)
+        w_fc = join(CoreSwap(mlp_blocks, place, 0, fc_width))
+        out_swap = CoreSwap(mlp_blocks, place, 1, fc_width)
         pre_act = dot_f32(mlp_in, w_fc) + bias_fc
         activated = narrow(jax.nn.gelu(pre_act, approximate=True))
-        w_out_t = out_swap.join()
+        w_out_t = join(out_swap)
         mate_part = dot_second(activated[block_len:], w_out_t)
         own_part = dot_second(activated[:block_len], w_out_t)
         hidden = middle + core_sum(own_part, mate_part) + shifts[3]
@@ -498,7 +541,6 @@
     own_output = narrow(hidden)
     output = both_seqs(own_output, other_tp(own_output))
 
-    grad_hidden, _ = tie(wide(my_seq(cotangent)), own_output)
     last_sum = None
     sums = {}
     waiting, latest, first_sum = [], [], []
@@ -526,23 +568,20 @@
         final = layer == 0
         grad_out_bias = jnp.sum(grad_hidden, axis=0)
         if not final:
-            bias_parts = jnp.sum(grad_hidden.reshape(16, -1, model_width), axis=1)
-            grad_hidden, bias_parts = tie(grad_hidden, bias_parts)
-            bias_parts = lax.psum(bias_parts, ("x", "core", "ctx", "tp"))
             last_sum = bias_parts
         grad_low = narrow(grad_hidden)
         grad_low = jnp.concatenate([grad_low, mate(grad_low)])
         out_swap = scatter_swap(narrow(dot_first(grad_low, activated)), place)
         grad_pre = narrow(gelu_slope(pre_act, dot_f32(grad_low, w_out_t)))
         grad_pre, out_swap.came = tie(grad_pre, out_swap.came)
-        waiting.append(("out%d" % layer, scatter_sum(out_swap.join())))
+        if final:
+            grad_pre = advance(grad_pre, "attn1")
+        waiting.append(("out%d" % layer, scatter_sum(join(out_swap))))
         grad_fc_bias = jnp.sum(wide(grad_pre), axis=0)
         mate_part = dot_second(grad_pre[block_len:], w_fc)
         own_part = dot_second(grad_pre[:block_len], w_fc)
         grad_norm_in = core_sum(own_part, mate_part)
         fc_swap = scatter_swap(narrow(dot_first(mlp_in, grad_pre)), place)
-        if final:
-            grad_norm_in = advance(grad_norm_in, "attn1")
         grad_from_mlp, grad_gain_mlp, grad_shift_mlp = norm_backward(
             grad_norm_in, hat_mlp, inv_mlp, gains[1]
         )
@@ -550,26 +589,28 @@
         grad_proj_bias = jnp.sum(grad_middle, axis=0)
         grad_low = narrow(grad_middle)
         grad_low, fc_swap.came = tie(grad_low, fc_swap.came)
-        waiting.append(("fc%d" % layer, scatter_sum(fc_swap.join())))
+        waiting.append(("fc%d" % layer, scatter_sum(join(fc_swap))))
         grad_low = jnp.concatenate([grad_low, mate(grad_low)])
         grad_mixed = narrow(dot_f32(grad_low, w_proj_t)).reshape(mixed.shape)
-        grad_proj = narrow(dot_first(grad_low, mixed.reshape(2 * block_len, half_width)))
+        proj_swap = scatter_swap(
+            narrow(dot_first(grad_low, mixed.reshape(2 * block_len, half_width))), place
+        )
         grad_packed = attention_backward(packed, mixed, grad_mixed, log_total, low_pos)
         grad_packed = advance(grad_packed, "out%d" % layer)
         mate_part = dot_second(grad_packed[1], w_qkv)
         own_part = dot_second(grad_packed[0], w_qkv)
         grad_near = core_sum(own_part, mate_part)
         far_total, grad_attn_in = grad_near[:last], grad_near[last:]
+        rows = grad_packed.reshape(2 * key_len, -1)
+        grad_near, rows = tie(grad_near, rows)
+        far_total, grad_attn_in = grad_near[:last], grad_near[last:]
         carried = backward_step(narrow(far_total[:block_len]))
-        rows = grad_packed.reshape(2 * key_len, -1)
-        grad_attn = jnp.concatenate([narrow(dot_first(near, rows)), grad_proj], axis=1)
-        attn_swap = scatter_swap(grad_attn, place)
+        attn_swap = scatter_swap(narrow(dot_first(near, rows)), place)
         for step in range(1, reach + 1):
             if step == 1:
                 carried, attn_swap.came = tie(carried, attn_swap.came)
-                waiting.append(("attn%d" % layer, scatter_sum(attn_swap.join())))
-            if step == 2:
                 carried = advance(carried, "fc%d" % layer)
+                waiting.append(("attn%d" % layer, scatter_sum(join(attn_swap, proj_swap))))
             arrived = wide(carried)
             if step < reach:
                 section = far_total[step * block_len : (step + 1) * block_len]

time: 1570 us -> 1380 us (0.88)
  waiting for transfers between devices: 697 us -> 592 us
  other arithmetic: 196 us -> 95.3 us
  local copies, waits for them, and re-layouts: 123 us -> 145 us
  Pallas kernels: 175 us -> 158 us
    reduce_scatter x6, waiting for transfers between devices: 300 us -> 51.2 us  [scatter_sum(): lax.psum_scatter(blocks, ('x', 'tp'), scatter_dimension=0, tiled=True)]
    psum x1, waiting for transfers between devices: 0.01 us -> 152 us  [per_device(): bias_parts = lax.psum(bias_parts, ('x', 'core', 'ctx', 'tp'))]
    ppermute x4, waiting for transfers between devices: 77.6 us -> 162 us  [backward_step(): return lax.ppermute(value, 'ctx', [(i + 1, i) for i in range(count - 1)])]
    select_n x18 -> x0, other arithmetic: 62.7 us -> none  [the longest x12 49.4 us: join(): jnp.where(self.place.core == 0, jnp.stack([self.blocks[:, 0], self.came],...]
    all_gather x4, waiting for transfers between devices: 57 us -> 14.6 us  [gather_blocks(): whole = lax.all_gather(piece, ('x', 'tp'), axis=0, tiled=False)]
    psum x6, waiting for transfers between devices: 94.2 us -> 62.6 us  [advance(): last_sum = lax.psum(share, 'ctx')]
    select_n x11 -> x0, local copies, waits for them, and re-layouts: 30.1 us -> none  [join(): jnp.where(self.place.core == 0, jnp.stack([self.blocks[:, 0], self.came],...]
    ppermute x4, waiting for transfers between devices: 26.4 us -> 4.39 us  [other_tp(): return lax.ppermute(value, 'tp', [(0, 1), (1, 0)])]
  transfers between devices with their start and end apart: 69 -> 71, of which waited for: 34 -> 29; matrix products, arithmetic and copies ran while one was open for 34% -> 33% of each run, Pallas kernels for 10% -> 11%
where the time goes in v5:
time: 1380 us; the launch traced here: 1370 us
  waiting for transfers between devices  592 us (43%)
  matrix products  305 us (22%)
  Pallas kernels  158 us (11%)
  local copies, waits for them, and re-layouts  145 us (11%)
  other arithmetic  95.3 us (7%)
  starting transfers between devices  52.1 us (4%)
  between operations  18.3 us (1%)
    dot_general x24, matrix products, contract(): lax.dot_general(left_side, right_side, (((left_dim,), (right_dim,)), ((),...  200 us
    ppermute x4, waiting for transfers between devices, backward_step(): return lax.ppermute(value, 'ctx', [(i + 1, i) for i in range(count - 1)])  162 us
    psum x1, waiting for transfers between devices, per_device(): bias_parts = lax.psum(bias_parts, ('x', 'core', 'ctx', 'tp'))  152 us
    dot_general x8, matrix products, dot_f32(): return jnp.dot(left_side, right_side, preferred_element_type=jnp.float32)  105 us
    unnamed x340, local copies, waits for them, and re-layouts  97.8 us
    ppermute x4, waiting for transfers between devices, onward(): return lax.ppermute(value, 'ctx', [(i, i + 1) for i in range(count - 1)])  87.5 us
    pallas_call x2, Pallas kernels, attention_backward(): pl.pallas_call(backward_kernel, grid=(groups, pairs), in_specs=[packed_sp...  79.7 us
    psum x6, waiting for transfers between devices, advance(): last_sum = lax.psum(share, 'ctx')  62.6 us
  transfers between devices with their start and end apart: 71, of which 29 were waited for; matrix products, arithmetic and copies ran while one was open for 33% of the time, Pallas kernels for 11%

profile of v5, /device:TPU:0, one launch (start us, length us, event | category | flops | bytes accessed | tf_op | source)
XLA Modules:
  0.0 1366.4 jit_solution(11631330331514182745)
XLA Ops:
  43.1 8.3 collective-permute-done
  60.4 23.1 %collective-permute-done.1 = bf16[512,1280]{1,0:T(8,128)(2,1)S(1)} collective-permute-done((bf16[512,1280]{1,0:T(8,128)(2,1)}, bf16[512,1280]{1,0:T(8,128)(2,1)S(1)}, u32[]{:S(2)}, u32[]{:S(2)}) %collective-permute-start.1) | collective-permute-done | bytes 1310752 | tf_op jit(solution)/shard_map/ppermute | solution.py:199
  113.4 152.1 %all-reduce.8.cloned.1.call-done = f32[16,1280]{1,0:T(8,128)} async-done(((f32[16,1280]{1,0:T(8,128)}), f32[16,1280]{1,0:T(8,128)}) %all-reduce.8.cloned.1.call-update) | async-done | bytes 81936 | tf_op jit(solution)/shard_map/psum | solution.py:458
  269.1 20.0 %add_convert_fusion.1 = bf16[3072,1920]{1,0:T(8,128)(2,1)S(1)} fusion(bf16[3072,1280]{1,0:T(8,128)(2,1)} %constant_dynamic-update-slice_fusion, f32[1920]{0:T(1024)S(1)} %reduce.4, bf16[1280,2560]{1,0:T(8,128)(2,1)S(1)} %shard_map.188), kind=kOutput, calls=%fused_computation.3 | convolution fusion | flops 15111290880 | bytes 24584192 | tf_op jit(solution)/shard_map/dot_general | solution.py:299
  289.2 31.0 %shard_map.189 = (bf16[2,512,640]{2,1,0:T(8,128)(2,1)S(1)}, f32[2,5,2,512]{3,2,1,0:T(2,128)S(1)}) custom-call(bf16[2,1536,1920]{2,1,0:T(8,128)(2,1)S(1)} %bitcast.335, s32[2,512,1]{2,1,0:T(8,128)S(1)} %copy-done.35), custom_call_target="tpu_custom_call" | custom-call | flops 6710886400 | bytes 11796480 | tf_op jit(solution)/shard_map/pallas_call | solution.py:80
  341.0 8.9 collective-permute-done.12.refs_1_
  349.9 5.8 copy-done.2
  363.3 10.9 multiply_convert_fusion.1
  383.2 5.6 fusion.108
  390.4 5.6 collective-permute-start.15
  395.9 28.2 %collective-permute-done.15 = bf16[512,1280]{1,0:T(8,128)(2,1)S(1)} collective-permute-done((bf16[512,1280]{1,0:T(8,128)(2,1)S(1)}, bf16[512,1280]{1,0:T(8,128)(2,1)S(1)}, u32[]{:S(2)}, u32[]{:S(2)}) %collective-permute-start.15) | collective-permute-done | bytes 1310752 | tf_op jit(solution)/shard_map/ppermute | solution.py:199
  429.1 5.5 collective-permute-start.16
  434.6 27.9 %collective-permute-done.16 = bf16[512,1280]{1,0:T(8,128)(2,1)} collective-permute-done((bf16[512,1280]{1,0:T(8,128)(2,1)}, bf16[512,1280]{1,0:T(8,128)(2,1)}, u32[]{:S(2)}, u32[]{:S(2)}) %collective-permute-start.16) | collective-permute-done | bytes 1310752 | tf_op jit(solution)/shard_map/ppermute | solution.py:199
  478.7 19.1 %add_convert_fusion = bf16[3072,1920]{1,0:T(8,128)(2,1)S(1)} fusion(bf16[3072,1280]{1,0:T(8,128)(2,1)} %constant_dynamic-update-slice_fusion.23, f32[1920]{0:T(1024)S(1)} %reduce.12, bf16[1280,2560]{1,0:T(8,128)(2,1)S(1)} %shard_map.192), kind=kOutput, calls=%fused_computation.2 | convolution fusion | flops 15111290880 | bytes 24584192 | tf_op jit(solution)/shard_map/dot_general | solution.py:299
  497.9 31.1 %shard_map.193 = (bf16[2,512,640]{2,1,0:T(8,128)(2,1)S(1)}, f32[2,5,2,512]{3,2,1,0:T(2,128)S(1)}) custom-call(bf16[2,1536,1920]{2,1,0:T(8,128)(2,1)S(1)} %bitcast.337, s32[2,512,1]{2,1,0:T(8,128)S(1)} %copy-done.36), custom_call_target="tpu_custom_call" | custom-call | flops 6710886400 | bytes 11796480 | tf_op jit(solution)/shard_map/pallas_call | solution.py:80
  541.0 10.7 all-gather.15.cloned.1.call-done
  559.4 7.4 collective-permute-done.23.refs_1_
  567.6 11.4 multiply_convert_fusion
  579.0 10.2 convolution_convert_fusion.3
  594.9 17.8 %fusion.13 = bf16[1024,2560]{1,0:T(8,128)(2,1)} fusion(f32[1024,2560]{1,0:T(8,128)} %get-tuple-element.201, f32[2560]{0:T(1024)S(1)} %get-tuple-element.152, bf16[1280,2560]{1,0:T(8,128)(2,1)} %copy-done.28, bf16[512,1280]{1,0:T(8,128)(2,1)} %copy-done.121, bf16[512,1280]{1,0:T(8,128)(2,1)} %bitcast.343), kind=kOutput, calls=%fused_computation.25 | convolution fusion | flops 6771179520 | bytes 24913920 | tf_op jit(solution)/shard_map/dot_general | solution.py:299
  616.4 7.5 convolution_convert_fusion.13
  624.3 10.0 convolution_convert_fusion.2
  638.7 6.2 multiply_reduce_fusion
  656.3 39.9 %shard_map.196 = bf16[2,1536,1920]{2,1,0:T(8,128)(2,1)S(1)} custom-call(bf16[2,1536,1920]{2,1,0:T(8,128)(2,1)} %bitcast.338, bf16[2,512,640]{2,1,0:T(8,128)(2,1)S(1)} %copy-done.38, bf16[2,512,640]{2,1,0:T(8,128)(2,1)S(1)} %bitcast.341, f32[2,5,2,512]{3,2,1,0:T(2,128)S(1)} %get-tuple-element.90.total_ref, s32[2,1,512]{2,1,0:T(1,128)S(1)} %subtract_add_fusion.1.low_ref), custom_call_target="tpu_custom_call" | custom-call | flops 16777216000 | bytes 23592960 | tf_op jit(solution)/shard_map/pallas_call | solution.py:163
  706.7 12.0 convolution_convert_fusion.7
  719.1 6.5 collective-permute-done.32
  725.6 14.2 %convolution_add_fusion.1 = f32[1536,1280]{1,0:T(8,128)} fusion(bf16[1536,1280]{1,0:T(8,128)(2,1)S(1)} %collective-permute-done.32, bf16[2,1536,1920]{2,1,0:T(8,128)(2,1)} %copy-done.18, bf16[1280,2560]{1,0:T(8,128)(2,1)} %copy-done.23), kind=kOutput, calls=%fused_computation.31 | convolution fusion | flops 7553679360 | bytes 22609920 | tf_op jit(solution)/shard_map/dot_general | solution.py:15
  739.8 19.5 %convolution_convert_fusion.5 = bf16[1280,1920]{1,0:T(8,128)(2,1)S(1)} fusion(bf16[3072,1280]{1,0:T(8,128)(2,1)} %constant_dynamic-update-slice_fusion.23, bf16[3072,1920]{1,0:T(8,128)(2,1)S(1)} %bitcast.311), kind=kOutput, calls=%fused_computation.33 | convolution fusion | flops 15101952000 | bytes 24576000 | tf_op jit(solution)/shard_map/dot_general | solution.py:15
  764.3 34.5 %collective-permute-done.33 = bf16[512,1280]{1,0:T(8,128)(2,1)} collective-permute-done((bf16[512,1280]{1,0:T(8,128)(2,1)S(1)}, bf16[512,1280]{1,0:T(8,128)(2,1)}, u32[]{:S(2)}, u32[]{:S(2)}) %collective-permute-start.33) | collective-permute-done | bytes 1310752 | tf_op jit(solution)/shard_map/ppermute | solution.py:204
  813.9 51.6 %collective-permute-done.35 = bf16[512,1280]{1,0:T(8,128)(2,1)S(1)} collective-permute-done((bf16[512,1280]{1,0:T(8,128)(2,1)S(1)}, bf16[512,1280]{1,0:T(8,128)(2,1)S(1)}, u32[]{:S(2)}, u32[]{:S(2)}) %collective-permute-start.35) | collective-permute-done | bytes 1310752 | tf_op jit(solution)/shard_map/ppermute | solution.py:204
  875.8 9.9 convolution_convert_fusion.1
  888.6 16.3 %fusion.6 = bf16[1024,2560]{1,0:T(8,128)(2,1)} fusion(f32[1024,2560]{1,0:T(8,128)} %get-tuple-element.195, f32[2560]{0:T(1024)S(1)} %copy-done.113, bf16[1280,2560]{1,0:T(8,128)(2,1)S(1)} %bitcast.327, bf16[512,1280]{1,0:T(8,128)(2,1)S(1)} %collective-permute-done.36, bf16[512,1280]{1,0:T(8,128)(2,1)S(1)} %convert_element_type.242), kind=kOutput, calls=%fused_computation.18 | convolution fusion | flops 6771179520 | bytes 24913920 | tf_op jit(solution)/shard_map/dot_general | solution.py:299
  911.4 7.4 convolution_convert_fusion.12
  919.3 10.0 convolution_convert_fusion
  933.1 7.4 multiply_reduce_fusion.2
  951.2 39.8 %shard_map.200 = bf16[2,1536,1920]{2,1,0:T(8,128)(2,1)S(1)} custom-call(bf16[2,1536,1920]{2,1,0:T(8,128)(2,1)} %bitcast.336, bf16[2,512,640]{2,1,0:T(8,128)(2,1)S(1)} %copy-done.42, bf16[2,512,640]{2,1,0:T(8,128)(2,1)S(1)} %bitcast.340, f32[2,5,2,512]{3,2,1,0:T(2,128)S(1)} %get-tuple-element.105.total_ref, s32[2,1,512]{2,1,0:T(1,128)S(1)} %subtract_add_fusion.1.low_ref), custom_call_target="tpu_custom_call" | custom-call | flops 16777216000 | bytes 23592960 | tf_op jit(solution)/shard_map/pallas_call | solution.py:163
  1001.6 13.1 convolution_convert_fusion.6
  1014.9 8.8 convolution_convert_fusion.14
  1023.8 14.8 %convolution_add_fusion = f32[1536,1280]{1,0:T(8,128)} fusion(bf16[1536,1280]{1,0:T(8,128)(2,1)} %collective-permute-done.42, bf16[2,1536,1920]{2,1,0:T(8,128)(2,1)} %copy-done.19, bf16[1280,2560]{1,0:T(8,128)(2,1)} %copy-done.26), kind=kOutput, calls=%fused_computation.30 | convolution fusion | flops 7553679360 | bytes 22609920 | tf_op jit(solution)/shard_map/dot_general | solution.py:15
  1038.6 19.8 %convolution_convert_fusion.4 = bf16[1280,1920]{1,0:T(8,128)(2,1)S(1)} fusion(bf16[3072,1280]{1,0:T(8,128)(2,1)} %constant_dynamic-update-slice_fusion, bf16[3072,1920]{1,0:T(8,128)(2,1)S(1)} %bitcast.315), kind=kOutput, calls=%fused_computation.32 | convolution fusion | flops 15101952000 | bytes 24576000 | tf_op jit(solution)/shard_map/dot_general | solution.py:15
  1063.0 7.1 fusion.45
  1072.3 6.1 convert_reduce_fusion
  1085.1 27.9 %collective-permute-done.43 = bf16[512,1280]{1,0:T(8,128)(2,1)} collective-permute-done((bf16[512,1280]{1,0:T(8,128)(2,1)S(1)}, bf16[512,1280]{1,0:T(8,128)(2,1)}, u32[]{:S(2)}, u32[]{:S(2)}) %collective-permute-start.43) | collective-permute-done | bytes 1310752 | tf_op jit(solution)/shard_map/ppermute | solution.py:204
  1121.2 6.0 convert_reduce_fusion.1
  1127.6 48.1 %collective-permute-done.45 = bf16[512,1280]{1,0:T(8,128)(2,1)} collective-permute-done((bf16[512,1280]{1,0:T(8,128)(2,1)}, bf16[512,1280]{1,0:T(8,128)(2,1)}, u32[]{:S(2)}, u32[]{:S(2)}) %collective-permute-start.45) | collective-permute-done | bytes 1310752 | tf_op jit(solution)/shard_map/ppermute | solution.py:204
  1223.5 5.7 collective-permute-done.52
  1231.5 51.2 %reduce-scatter.17.cloned.1.call-done = bf16[320,2560]{1,0:T(8,128)(2,1)} async-done(((bf16[1280,2560]{1,0:T(8,128)(2,1)}), bf16[320,2560]{1,0:T(8,128)(2,1)}) %reduce-scatter.17.cloned.1.call-update) | async-done | bytes 1638416 | tf_op jit(solution)/shard_map/reduce_scatter | solution.py:295
  1291.2 62.6 %all-reduce.20.cloned.1.call-done.first_ref = bf16[320,2560]{1,0:T(8,128)(2,1)} async-done(((bf16[320,2560]{1,0:T(8,128)(2,1)}), bf16[320,2560]{1,0:T(8,128)(2,1)}) %all-reduce.20.cloned.1.call-update) | async-done | bytes 1638416 | tf_op jit(solution)/shard_map/psum | solution.py:559
  (657 shorter events, 343.6 us)
Async XLA Ops:
  8.0 80.1 %all-gather.9.cloned.1.call-start = ((), (), s32[]{:S(2)}) async-start(), calls=%async_computation.19 | async-start | bytes 8192000 | tf_op jit(solution)/shard_map/all_gather | solution.py:286
  12.9 252.6 %all-reduce.8.cloned.1.call-start = ((), (), s32[]{:S(2)}) async-start(), calls=%async_computation.6 | async-start | bytes 163840 | tf_op jit(solution)/shard_map/psum | solution.py:458
  12.9 26.8 %collective-permute-start.9 = (s32[4]{0:T(128)S(1)}, s32[4]{0:T(128)S(1)}, u32[]{:S(2)}, u32[]{:S(2)}) collective-permute-start(s32[4]{0:T(128)S(1)} %fusion.143), channel_id=1, source_target_pairs={{0,8},{8,0},{1,9},{9,1},{2,10},{10,2},{3,11},{11,3},{4,12},{12,4},... | collective-permute-start | bytes 56 | tf_op jit(solution)/shard_map/ppermute | solution.py:190
  13.5 27.7 %collective-permute-start.2 = (bf16[12,320]{1,0:T(8,128)(2,1)S(1)}, bf16[12,320]{1,0:T(8,128)(2,1)S(1)}, u32[]{:S(2)}, u32[]{:S(2)}) collective-permute-start(bf16[12,320]{1,0:T(8,128)(2,1)S(1)} %reshape.391), channel_id=1, source_target_pairs={{0,8},{8,0},{1,9},{9,1},{2,10},{10,2},{3,11},{11,3},{4,12},{12,4},... | collective-permute-start | bytes 23048 | tf_op jit(solution)/shard_map/ppermute | solution.py:190
  13.7 29.3 %collective-permute-start.8 = (bf16[2,3840]{1,0:T(2,128)(2,1)S(1)}, bf16[2,3840]{1,0:T(2,128)(2,1)S(1)}, u32[]{:S(2)}, u32[]{:S(2)}) collective-permute-start(bf16[2,3840]{1,0:T(2,128)(2,1)S(1)} %constant_dynamic-update-slice_fusion.6), channel_id=1, source_target_pairs={{0,1},{1,0},{2,3},{3,2},{4,5},{5,4},{6,7},{7,6},{8,9},{9,8},{10,11... | collective-permute-start | bytes 46088 | tf_op jit(solution)/shard_map/ppermute | solution.py:194
  19.3 32.1 %collective-permute-start = (bf16[512,1280]{1,0:T(8,128)(2,1)}, bf16[512,1280]{1,0:T(8,128)(2,1)}, u32[]{:S(2)}, u32[]{:S(2)}) collective-permute-start(bf16[512,1280]{1,0:T(8,128)(2,1)} %get-tuple-element.171), channel_id=1, source_target_pairs={{0,2},{2,4},{4,6},{1,3},{3,5},{5,7},{8,10},{10,12},{12,14},{9,11},... | collective-permute-start | bytes 3932168 | tf_op jit(solution)/shard_map/ppermute | solution.py:199
  26.8 307.0 %all-gather.11.cloned.1.call-start = ((), (), s32[]{:S(2)}) async-start(), calls=%async_computation.20 | async-start | bytes 16384000 | tf_op jit(solution)/shard_map/all_gather | solution.py:286
  41.4 14.8 %collective-permute-start.3 = (bf16[12,640]{1,0:T(8,128)(2,1)S(1)}, bf16[12,640]{1,0:T(8,128)(2,1)S(1)}, u32[]{:S(2)}, u32[]{:S(2)}) collective-permute-start(bf16[12,640]{1,0:T(8,128)(2,1)S(1)} %select_n.127), channel_id=1, source_target_pairs={{0,16},{16,0},{1,17},{17,1},{2,18},{18,2},{3,19},{19,3},{4,20},{20... | collective-permute-start | bytes 46088 | tf_op jit(solution)/shard_map/ppermute | solution.py:315
  51.4 372.9 %all-gather.13.cloned.1.call-start = ((), (), s32[]{:S(2)}) async-start(), calls=%async_computation.21 | async-start | bytes 8192000 | tf_op jit(solution)/shard_map/all_gather | solution.py:286
  51.7 31.8 %collective-permute-start.1 = (bf16[512,1280]{1,0:T(8,128)(2,1)}, bf16[512,1280]{1,0:T(8,128)(2,1)S(1)}, u32[]{:S(2)}, u32[]{:S(2)}) collective-permute-start(bf16[512,1280]{1,0:T(8,128)(2,1)} %collective-permute-done), channel_id=1, source_target_pairs={{0,2},{2,4},{4,6},{1,3},{3,5},{5,7},{8,10},{10,12},{12,14},{9,11},... | collective-permute-start | bytes 3932168 | tf_op jit(solution)/shard_map/ppermute | solution.py:199
  92.0 173.5 %collective-permute-start.7 = (bf16[2,320,2560]{2,1,0:T(8,128)(2,1)}, bf16[2,320,2560]{2,1,0:T(8,128)(2,1)S(1)}, u32[]{:S(2)}, u32[]{:S(2)}) collective-permute-start(bf16[2,320,2560]{2,1,0:T(8,128)(2,1)} %dynamic-slice_bitcast_fusion.7), channel_id=1, source_target_pairs={{0,8},{8,0},{1,9},{9,1},{2,10},{10,2},{3,11},{11,3},{4,12},{12,4},... | collective-permute-start | bytes 9830408 | tf_op jit(solution)/shard_map/ppermute | solution.py:190
  340.7 18.9 %collective-permute-start.13 = (bf16[2,320,2560]{2,1,0:T(8,128)(2,1)}, bf16[2,320,2560]{2,1,0:T(8,128)(2,1)S(1)}, u32[]{:S(2)}, u32[]{:S(2)}) collective-permute-start(bf16[2,320,2560]{2,1,0:T(8,128)(2,1)} %get-tuple-element.179), channel_id=1, source_target_pairs={{0,8},{8,0},{1,9},{9,1},{2,10},{10,2},{3,11},{11,3},{4,12},{12,4},... | collective-permute-start | bytes 9830408 | tf_op jit(solution)/shard_map/ppermute | solution.py:190
  340.9 210.8 %all-gather.15.cloned.1.call-start = ((), (), s32[]{:S(2)}) async-start(), calls=%async_computation.22 | async-start | bytes 16384000 | tf_op jit(solution)/shard_map/all_gather | solution.py:286
  390.4 33.8 %collective-permute-start.15 = (bf16[512,1280]{1,0:T(8,128)(2,1)S(1)}, bf16[512,1280]{1,0:T(8,128)(2,1)S(1)}, u32[]{:S(2)}, u32[]{:S(2)}) collective-permute-start(bf16[512,1280]{1,0:T(8,128)(2,1)S(1)} %add_convert_fusion.5), channel_id=1, source_target_pairs={{0,2},{2,4},{4,6},{1,3},{3,5},{5,7},{8,10},{10,12},{12,14},{9,11},... | collective-permute-start | bytes 3932168 | tf_op jit(solution)/shard_map/ppermute | solution.py:199
  424.2 276.2 %reduce-scatter.7.cloned.1.call-start = ((), (), s32[]{:S(2)}) async-start(), calls=%async_computation.7 | async-start | bytes 8192000 | tf_op jit(solution)/shard_map/reduce_scatter | solution.py:295
  429.1 34.0 %collective-permute-start.20 = (bf16[2,320,2560]{2,1,0:T(8,128)(2,1)}, bf16[2,320,2560]{2,1,0:T(8,128)(2,1)S(1)}, u32[]{:S(2)}, u32[]{:S(2)}) collective-permute-start(bf16[2,320,2560]{2,1,0:T(8,128)(2,1)} %dynamic-slice_bitcast_fusion.6), channel_id=1, source_target_pairs={{0,8},{8,0},{1,9},{9,1},{2,10},{10,2},{3,11},{11,3},{4,12},{12,4},... | collective-permute-start | bytes 9830408 | tf_op jit(solution)/shard_map/ppermute | solution.py:190
  429.1 33.4 %collective-permute-start.16 = (bf16[512,1280]{1,0:T(8,128)(2,1)}, bf16[512,1280]{1,0:T(8,128)(2,1)}, u32[]{:S(2)}, u32[]{:S(2)}) collective-permute-start(bf16[512,1280]{1,0:T(8,128)(2,1)} %copy-done.75), channel_id=1, source_target_pairs={{0,2},{2,4},{4,6},{1,3},{3,5},{5,7},{8,10},{10,12},{12,14},{9,11},... | collective-permute-start | bytes 3932168 | tf_op jit(solution)/shard_map/ppermute | solution.py:199
  462.5 11.4 collective-permute-start.17
  462.5 15.0 %collective-permute-start.19 = (bf16[512,1280]{1,0:T(8,128)(2,1)}, bf16[512,1280]{1,0:T(8,128)(2,1)S(1)}, u32[]{:S(2)}, u32[]{:S(2)}) collective-permute-start(bf16[512,1280]{1,0:T(8,128)(2,1)} %copy-done.74), channel_id=1, source_target_pairs={{0,8},{8,0},{1,9},{9,1},{2,10},{10,2},{3,11},{11,3},{4,12},{12,4},... | collective-permute-start | bytes 3932168 | tf_op jit(solution)/shard_map/ppermute | solution.py:190
  558.9 20.1 %collective-permute-start.27 = (bf16[512,1280]{1,0:T(8,128)(2,1)S(1)}, bf16[512,1280]{1,0:T(8,128)(2,1)S(1)}, u32[]{:S(2)}, u32[]{:S(2)}) collective-permute-start(bf16[512,1280]{1,0:T(8,128)(2,1)S(1)} %bitcast.344), channel_id=1, source_target_pairs={{0,8},{8,0},{1,9},{9,1},{2,10},{10,2},{3,11},{11,3},{4,12},{12,4},... | collective-permute-start | bytes 3932168 | tf_op jit(solution)/shard_map/ppermute | solution.py:190
  559.4 31.9 %collective-permute-start.24 = (bf16[2,320,2560]{2,1,0:T(8,128)(2,1)}, bf16[2,320,2560]{2,1,0:T(8,128)(2,1)S(1)}, u32[]{:S(2)}, u32[]{:S(2)}) collective-permute-start(bf16[2,320,2560]{2,1,0:T(8,128)(2,1)} %get-tuple-element.177), channel_id=1, source_target_pairs={{0,8},{8,0},{1,9},{9,1},{2,10},{10,2},{3,11},{11,3},{4,12},{12,4},... | collective-permute-start | bytes 9830408 | tf_op jit(solution)/shard_map/ppermute | solution.py:190
  591.2 21.5 %collective-permute-start.28 = (bf16[2,320,2560]{2,1,0:T(8,128)(2,1)}, bf16[2,320,2560]{2,1,0:T(8,128)(2,1)S(1)}, u32[]{:S(2)}, u32[]{:S(2)}) collective-permute-start(bf16[2,320,2560]{2,1,0:T(8,128)(2,1)} %dynamic-slice_bitcast_fusion.5), channel_id=1, source_target_pairs={{0,8},{8,0},{1,9},{9,1},{2,10},{10,2},{3,11},{11,3},{4,12},{12,4},... | collective-permute-start | bytes 9830408 | tf_op jit(solution)/shard_map/ppermute | solution.py:190
  615.9 182.9 %all-reduce.10.cloned.1.call-start = ((), (), s32[]{:S(2)}) async-start(), calls=%async_computation.9 | async-start | bytes 3276800 | tf_op jit(solution)/shard_map/psum | solution.py:559
  623.9 14.7 %collective-permute-start.29 = (bf16[512,1280]{1,0:T(8,128)(2,1)S(1)}, bf16[512,1280]{1,0:T(8,128)(2,1)S(1)}, u32[]{:S(2)}, u32[]{:S(2)}) collective-permute-start(bf16[512,1280]{1,0:T(8,128)(2,1)S(1)} %convolution_convert_fusion.13), channel_id=1, source_target_pairs={{0,8},{8,0},{1,9},{9,1},{2,10},{10,2},{3,11},{11,3},{4,12},{12,4},... | collective-permute-start | bytes 3932168 | tf_op jit(solution)/shard_map/ppermute | solution.py:190
  700.4 98.4 %reduce-scatter.9.cloned.1.call-start = ((), (), s32[]{:S(2)}) async-start(), calls=%async_computation.8 | async-start | bytes 8192000 | tf_op jit(solution)/shard_map/reduce_scatter | solution.py:295
  706.6 198.3 %all-reduce.12.cloned.1.call-start = ((), (), s32[]{:S(2)}) async-start(), calls=%async_computation.11 | async-start | bytes 3276800 | tf_op jit(solution)/shard_map/psum | solution.py:559
  759.5 39.3 %collective-permute-start.34 = (bf16[2,320,1920]{2,1,0:T(8,128)(2,1)S(1)}, bf16[2,320,1920]{2,1,0:T(8,128)(2,1)S(1)}, u32[]{:S(2)}, u32[]{:S(2)}) collective-permute-start(bf16[2,320,1920]{2,1,0:T(8,128)(2,1)S(1)} %dynamic-slice_bitcast_fusion.9), channel_id=1, source_target_pairs={{0,8},{8,0},{1,9},{9,1},{2,10},{10,2},{3,11},{11,3},{4,12},{12,4},... | collective-permute-start | bytes 7372808 | tf_op jit(solution)/shard_map/ppermute | solution.py:190
  763.0 35.8 %collective-permute-start.33 = (bf16[512,1280]{1,0:T(8,128)(2,1)S(1)}, bf16[512,1280]{1,0:T(8,128)(2,1)}, u32[]{:S(2)}, u32[]{:S(2)}) collective-permute-start(bf16[512,1280]{1,0:T(8,128)(2,1)S(1)} %slice.728), channel_id=1, source_target_pairs={{2,0},{4,2},{6,4},{3,1},{5,3},{7,5},{10,8},{12,10},{14,12},{11,9},... | collective-permute-start | bytes 3932168 | tf_op jit(solution)/shard_map/ppermute | solution.py:204
  798.8 106.1 %reduce-scatter.11.cloned.1.call-start = ((), (), s32[]{:S(2)}) async-start(), calls=%async_computation.10 | async-start | bytes 8192000 | tf_op jit(solution)/shard_map/reduce_scatter | solution.py:295
  809.3 186.0 %all-reduce.14.cloned.1.call-start = ((), (), s32[]{:S(2)}) async-start(), calls=%async_computation.13 | async-start | bytes 3276800 | tf_op jit(solution)/shard_map/psum | solution.py:559
  811.9 53.6 %collective-permute-start.35 = (bf16[512,1280]{1,0:T(8,128)(2,1)S(1)}, bf16[512,1280]{1,0:T(8,128)(2,1)S(1)}, u32[]{:S(2)}, u32[]{:S(2)}) collective-permute-start(bf16[512,1280]{1,0:T(8,128)(2,1)S(1)} %add_convert_fusion.3), channel_id=1, source_target_pairs={{2,0},{4,2},{6,4},{3,1},{5,3},{7,5},{10,8},{12,10},{14,12},{11,9},... | collective-permute-start | bytes 3932168 | tf_op jit(solution)/shard_map/ppermute | solution.py:204
  888.5 16.4 %collective-permute-start.37 = (bf16[2,320,2560]{2,1,0:T(8,128)(2,1)S(1)}, bf16[2,320,2560]{2,1,0:T(8,128)(2,1)S(1)}, u32[]{:S(2)}, u32[]{:S(2)}) collective-permute-start(bf16[2,320,2560]{2,1,0:T(8,128)(2,1)S(1)} %dynamic-slice_bitcast_fusion.3), channel_id=1, source_target_pairs={{0,8},{8,0},{1,9},{9,1},{2,10},{10,2},{3,11},{11,3},{4,12},{12,4},... | collective-permute-start | bytes 9830408 | tf_op jit(solution)/shard_map/ppermute | solution.py:190
  905.0 90.3 %reduce-scatter.13.cloned.1.call-start = ((), (), s32[]{:S(2)}) async-start(), calls=%async_computation.12 | async-start | bytes 8192000 | tf_op jit(solution)/shard_map/reduce_scatter | solution.py:295
  911.2 201.9 %all-reduce.16.cloned.1.call-start = ((), (), s32[]{:S(2)}) async-start(), calls=%async_computation.15 | async-start | bytes 3276800 | tf_op jit(solution)/shard_map/psum | solution.py:559
  918.8 13.7 %collective-permute-start.39 = (bf16[512,1280]{1,0:T(8,128)(2,1)S(1)}, bf16[512,1280]{1,0:T(8,128)(2,1)}, u32[]{:S(2)}, u32[]{:S(2)}) collective-permute-start(bf16[512,1280]{1,0:T(8,128)(2,1)S(1)} %convolution_convert_fusion.12), channel_id=1, source_target_pairs={{0,8},{8,0},{1,9},{9,1},{2,10},{10,2},{3,11},{11,3},{4,12},{12,4},... | collective-permute-start | bytes 3932168 | tf_op jit(solution)/shard_map/ppermute | solution.py:190
  995.3 117.7 %reduce-scatter.15.cloned.1.call-start = ((), (), s32[]{:S(2)}) async-start(), calls=%async_computation.14 | async-start | bytes 8192000 | tf_op jit(solution)/shard_map/reduce_scatter | solution.py:295
  1001.6 229.9 %all-reduce.18.cloned.1.call-start = ((), (), s32[]{:S(2)}) async-start(), calls=%async_computation.17 | async-start | bytes 3276800 | tf_op jit(solution)/shard_map/psum | solution.py:559
  1023.6 39.3 %collective-permute-start.25 = (bf16[512,1280]{1,0:T(8,128)(2,1)}, bf16[512,1280]{1,0:T(8,128)(2,1)}, u32[]{:S(2)}, u32[]{:S(2)}) collective-permute-start(bf16[512,1280]{1,0:T(8,128)(2,1)} %convolution_convert_fusion.14), channel_id=1, source_target_pairs={{0,8},{8,0},{1,9},{9,1},{2,10},{10,2},{3,11},{11,3},{4,12},{12,4},... | collective-permute-start | bytes 3932168 | tf_op jit(solution)/shard_map/ppermute | solution.py:190
  1062.6 50.5 %collective-permute-start.44 = (bf16[2,320,1920]{2,1,0:T(8,128)(2,1)}, bf16[2,320,1920]{2,1,0:T(8,128)(2,1)S(1)}, u32[]{:S(2)}, u32[]{:S(2)}) collective-permute-start(bf16[2,320,1920]{2,1,0:T(8,128)(2,1)} %dynamic-slice_bitcast_fusion.8), channel_id=1, source_target_pairs={{0,8},{8,0},{1,9},{9,1},{2,10},{10,2},{3,11},{11,3},{4,12},{12,4},... | collective-permute-start | bytes 7372808 | tf_op jit(solution)/shard_map/ppermute | solution.py:190
  1070.1 110.3 %collective-permute-start.26 = (bf16[512,1280]{1,0:T(8,128)(2,1)}, bf16[512,1280]{1,0:T(8,128)(2,1)}, u32[]{:S(2)}, u32[]{:S(2)}) collective-permute-start(bf16[512,1280]{1,0:T(8,128)(2,1)} %fusion.45), channel_id=1, source_target_pairs={{0,1},{1,0},{2,3},{3,2},{4,5},{5,4},{6,7},{7,6},{8,9},{9,8},{10,11... | collective-permute-start | bytes 3932168 | tf_op jit(solution)/shard_map/ppermute | solution.py:194
  1080.3 32.7 %collective-permute-start.43 = (bf16[512,1280]{1,0:T(8,128)(2,1)S(1)}, bf16[512,1280]{1,0:T(8,128)(2,1)}, u32[]{:S(2)}, u32[]{:S(2)}) collective-permute-start(bf16[512,1280]{1,0:T(8,128)(2,1)S(1)} %slice.727), channel_id=1, source_target_pairs={{2,0},{4,2},{6,4},{3,1},{5,3},{7,5},{10,8},{12,10},{14,12},{11,9},... | collective-permute-start | bytes 3932168 | tf_op jit(solution)/shard_map/ppermute | solution.py:204
  1117.4 58.2 %collective-permute-start.45 = (bf16[512,1280]{1,0:T(8,128)(2,1)}, bf16[512,1280]{1,0:T(8,128)(2,1)}, u32[]{:S(2)}, u32[]{:S(2)}) collective-permute-start(bf16[512,1280]{1,0:T(8,128)(2,1)} %add_convert_fusion.2), channel_id=1, source_target_pairs={{2,0},{4,2},{6,4},{3,1},{5,3},{7,5},{10,8},{12,10},{14,12},{11,9},... | collective-permute-start | bytes 3932168 | tf_op jit(solution)/shard_map/ppermute | solution.py:204
  1121.2 64.3 %collective-permute-start.53 = (bf16[2,320,640]{2,1,0:T(8,128)(2,1)S(1)}, bf16[2,320,640]{2,1,0:T(8,128)(2,1)S(1)}, u32[]{:S(2)}, u32[]{:S(2)}) collective-permute-start(bf16[2,320,640]{2,1,0:T(8,128)(2,1)S(1)} %dynamic-slice_bitcast_fusion.11), channel_id=1, source_target_pairs={{0,8},{8,0},{1,9},{9,1},{2,10},{10,2},{3,11},{11,3},{4,12},{12,4},... | collective-permute-start | bytes 2457608 | tf_op jit(solution)/shard_map/ppermute | solution.py:190
  1127.3 155.4 %reduce-scatter.17.cloned.1.call-start = ((), (), s32[]{:S(2)}) async-start(), calls=%async_computation.16 | async-start | bytes 8192000 | tf_op jit(solution)/shard_map/reduce_scatter | solution.py:295
  1180.4 12.7 collective-permute-start.47
  1193.0 160.8 %all-reduce.20.cloned.1.call-start = ((), (), s32[]{:S(2)}) async-start(), calls=%async_computation.18 | async-start | bytes 3276800 | tf_op jit(solution)/shard_map/psum | solution.py:559
  1216.6 12.6 collective-permute-start.52
  1222.4 61.0 %collective-permute-start.46 = (bf16[512,1280]{1,0:T(8,128)(2,1)}, bf16[512,1280]{1,0:T(8,128)(2,1)S(1)}, u32[]{:S(2)}, u32[]{:S(2)}) collective-permute-start(bf16[512,1280]{1,0:T(8,128)(2,1)} %get-tuple-element.166), channel_id=1, source_target_pairs={{0,1},{1,0},{2,3},{3,2},{4,5},{5,4},{6,7},{7,6},{8,9},{9,8},{10,11... | collective-permute-start | bytes 3932168 | tf_op jit(solution)/shard_map/ppermute | solution.py:194
  (168 other events, 2924.8 us)
Sparse Core Ops, SparseCore 0:
  13.0 75.1 all-gather.8
  90.5 127.0 all-gather.10
  341.0 74.0 all-gather.12
  424.3 127.3 all-gather.14
  616.0 72.4 reduce-scatter.6
  706.8 72.7 reduce-scatter.8
  809.4 72.3 reduce-scatter.10
  911.3 71.3 reduce-scatter.12
  1001.7 71.3 reduce-scatter.14
  1193.1 89.5 reduce-scatter.16
Sparse Core Ops, SparseCore 1:
  26.9 238.5 all-reduce.7
  700.5 72.9 all-reduce.9
  798.9 89.7 all-reduce.11
  905.1 69.9 all-reduce.13
  995.4 69.9 all-reduce.15
  1127.4 84.2 all-reduce.17
  1282.8 70.9 all-reduce.19

commit v6 on v5

--- a/solution.py
+++ b/solution.py
@@ -92,7 +92,7 @@
             jax.ShapeDtypeStruct((groups, block_len, pairs * PAIR), jnp.bfloat16),
             jax.ShapeDtypeStruct((groups, pairs, 2, block_len), jnp.float32),
         ],
-        compiler_params=pltpu.CompilerParams(vmem_limit_bytes=40 << 20),
+        compiler_params=pltpu.CompilerParams(vmem_limit_bytes=56 << 20),
         cost_estimate=pl.CostEstimate(
             flops=16 * groups * pairs * block_len * (WINDOW + TILE) * HD,
             bytes_accessed=2 * groups * width * key_len,
@@ -174,7 +174,7 @@
             pltpu.VMEM((key_len, PAIR), jnp.float32),
             pltpu.VMEM((key_len, PAIR), jnp.float32),
         ],
-        compiler_params=pltpu.CompilerParams(vmem_limit_bytes=40 << 20),
+        compiler_params=pltpu.CompilerParams(vmem_limit_bytes=56 << 20),
         cost_estimate=pl.CostEstimate(
             flops=40 * groups * pairs * block_len * (WINDOW + TILE) * HD,
             bytes_accessed=4 * groups * width * key_len,
@@ -275,7 +275,7 @@
             out_specs=pl.BlockSpec((rows, total), lambda chip, part, core: (chip * 2 + part, 0)),
         ),
         out_shape=jax.ShapeDtypeStruct((chips * 2 * rows, total), jnp.bfloat16),
-        compiler_params=pltpu.CompilerParams(vmem_limit_bytes=24 << 20),
+        compiler_params=pltpu.CompilerParams(vmem_limit_bytes=56 << 20),
         cost_estimate=pl.CostEstimate(
             flops=0, bytes_accessed=8 * chips * rows * total, transcendentals=0
         ),
@@ -395,7 +395,7 @@
         ],
         out_specs=pl.BlockSpec((rows, 4 * width), lambda step: (0, 0)),
         out_shape=jax.ShapeDtypeStruct((rows, 4 * width), jnp.bfloat16),
-        compiler_params=pltpu.CompilerParams(vmem_limit_bytes=24 << 20),
+        compiler_params=pltpu.CompilerParams(vmem_limit_bytes=56 << 20),
     )(qkv_weight, proj_weight)
 
 
@@ -412,15 +412,15 @@
 
 def unpack_heads(first, second):
     rows, width = first.shape
-    width = width // 4
-    block = pl.BlockSpec((rows, 4 * width), lambda kind: (0, 0))
+    width = width // 3
+    block = pl.BlockSpec((rows, 3 * width), lambda kind: (0, 0))
     return pl.pallas_call(
         unpack_kernel,
         grid=(3,),
         in_specs=[block, block],
         out_specs=pl.BlockSpec((2, 1, rows, width), lambda kind: (0, kind, 0, 0)),
         out_shape=jax.ShapeDtypeStruct((2, 3, rows, width), jnp.float32),
-        compiler_params=pltpu.CompilerParams(vmem_limit_bytes=24 << 20),
+        compiler_params=pltpu.CompilerParams(vmem_limit_bytes=56 << 20),
     )(first, second)
 
 
@@ -455,7 +455,7 @@
     own_tokens = my_seq(tokens)
     grad_hidden = wide(my_seq(cotangent))
     bias_parts = jnp.sum(grad_hidden.reshape(16, -1, model_width), axis=1)
-    bias_parts = lax.psum(bias_parts, ("x", "core", "ctx", "tp"))
+    bias_parts = lax.psum(bias_parts, "ctx")
     attn_blocks = gather_blocks(attn_piece(0, qkv_weight, proj_weight), place)
     halo = [onward(own_tokens)]
     for _ in range(reach - 1):
@@ -588,15 +588,17 @@
         grad_middle = grad_hidden + grad_from_mlp
         grad_proj_bias = jnp.sum(grad_middle, axis=0)
         grad_low = narrow(grad_middle)
-        grad_low, fc_swap.came = tie(grad_low, fc_swap.came)
-        waiting.append(("fc%d" % layer, scatter_sum(join(fc_swap))))
         grad_low = jnp.concatenate([grad_low, mate(grad_low)])
         grad_mixed = narrow(dot_f32(grad_low, w_proj_t)).reshape(mixed.shape)
         proj_swap = scatter_swap(
             narrow(dot_first(grad_low, mixed.reshape(2 * block_len, half_width))), place
         )
+        grad_mixed, fc_swap.came, proj_swap.came = tie(grad_mixed, fc_swap.came, proj_swap.came)
+        grad_fc = join(fc_swap, proj_swap)
         grad_packed = attention_backward(packed, mixed, grad_mixed, log_total, low_pos)
         grad_packed = advance(grad_packed, "out%d" % layer)
+        grad_packed, grad_fc = tie(grad_packed, grad_fc)
+        waiting.append(("fc%d" % layer, scatter_sum(grad_fc)))
         mate_part = dot_second(grad_packed[1], w_qkv)
         own_part = dot_second(grad_packed[0], w_qkv)
         grad_near = core_sum(own_part, mate_part)
@@ -608,9 +610,15 @@
         attn_swap = scatter_swap(narrow(dot_first(near, rows)), place)
         for step in range(1, reach + 1):
             if step == 1:
-                carried, attn_swap.came = tie(carried, attn_swap.came)
+                carried, grad_attn = tie(carried, join(attn_swap))
+                if final:
+                    carried = advance(carried, "fc%d" % layer)
+                else:
+                    carried, grad_attn, waiting[0] = tie(carried, grad_attn, waiting[0][1])
+                    waiting[0] = ("fc%d" % layer, waiting[0])
+                waiting.append(("attn%d" % layer, scatter_sum(grad_attn)))
+            if step == 2 and not final:
                 carried = advance(carried, "fc%d" % layer)
-                waiting.append(("attn%d" % layer, scatter_sum(join(attn_swap, proj_swap))))
             arrived = wide(carried)
             if step < reach:
                 section = far_total[step * block_len : (step + 1) * block_len]
@@ -626,6 +634,8 @@
             [grad_bias[:, 0].reshape(-1), grad_bias[:, 2].reshape(-1), grad_fc_bias]
         )
         empty = jnp.zeros_like(halves)
+        if not final:
+            grad_out_bias = jnp.where(place.ctx == 0, jnp.sum(first_sum[0], axis=0), 0.0)
         small_parts[layer] = jnp.concatenate(
             [
                 grad_gain_attn, grad_gain_mlp,
@@ -641,12 +651,11 @@
     advance((), "attn0")
     split = 6 * model_width
     norms = small[:, :split].reshape(layer_count, 6, model_width)
-    norms = norms.at[1, 5].set(jnp.sum(first_sum[0], axis=0))
     norms = lax.dynamic_slice_in_dim(norms, place.shard * shard_rows, shard_rows, 2)
     halves = small[:, split:].reshape(layer_count, 2, -1)
     halves = lax.dynamic_index_in_dim(halves, place.tp, 1, False)
-    packed_width = 3 * half_width
     attn = [sums["attn%d" % layer] for layer in range(layer_count)]
+    fc_proj = [sums["fc%d" % layer] for layer in range(layer_count)]
     return (
         output,
         token_grad,
@@ -654,8 +663,8 @@
         norms[:, 2:],
         unpack_heads(*attn),
         halves[:, : 2 * half_width].reshape(layer_count, 2, half_width),
-        jnp.stack([jnp.transpose(wide(v[:, packed_width:])) for v in attn]),
-        jnp.stack([wide(sums["fc%d" % layer]) for layer in range(layer_count)]),
+        jnp.stack([jnp.transpose(wide(v[:, fc_width:])) for v in fc_proj]),
+        jnp.stack([wide(v[:, :fc_width]) for v in fc_proj]),
         halves[:, 2 * half_width :],
         jnp.stack([jnp.transpose(wide(sums["out%d" % layer])) for layer in range(layer_count)]),
     )

time: 1380 us -> 1340 us (0.971)
  Pallas kernels: 158 us -> 240 us
  waiting for transfers between devices: 592 us -> 530 us
  local copies, waits for them, and re-layouts: 145 us -> 88.4 us
    psum x1, waiting for transfers between devices: 152 us -> 0.01 us  [per_device(): bias_parts = lax.psum(bias_parts, 'ctx')]
    psum x6, waiting for transfers between devices: 62.6 us -> 185 us  [advance(): last_sum = lax.psum(share, 'ctx')]
    pallas_call x12, Pallas kernels: 10.8 us -> 85.3 us  [join(): pl.pallas_call(join_kernel, grid_spec=pltpu.PrefetchScalarGridSpec(num_sc...]
    ppermute x4, waiting for transfers between devices: 162 us -> 96.5 us  [backward_step(): return lax.ppermute(value, 'ctx', [(i + 1, i) for i in range(count - 1)])]
    unnamed x340 -> x261, local copies, waits for them, and re-layouts: 97.8 us -> 38.9 us
    reduce_scatter x6, waiting for transfers between devices: 51.2 us -> 0.07 us  [scatter_sum(): lax.psum_scatter(blocks, ('x', 'tp'), scatter_dimension=0, tiled=True)]
    ppermute x4, waiting for transfers between devices: 4.39 us -> 52.2 us  [other_tp(): return lax.ppermute(value, 'tp', [(0, 1), (1, 0)])]
    all_gather x4, waiting for transfers between devices: 14.6 us -> 43.3 us  [gather_blocks(): whole = lax.all_gather(piece, ('x', 'tp'), axis=0, tiled=False)]
  transfers between devices with their start and end apart: 71 -> 71, of which waited for: 29 -> 33; matrix products, arithmetic and copies ran while one was open for 33% -> 34% of each run, Pallas kernels for 11% -> 17%
where the time goes in v6:
time: 1340 us; the launch traced here: 1330 us
  waiting for transfers between devices  530 us (40%)
  matrix products  312 us (23%)
  Pallas kernels  240 us (18%)
  other arithmetic  94.1 us (7%)
  local copies, waits for them, and re-layouts  88.4 us (7%)
  starting transfers between devices  49.2 us (4%)
  between operations  17.9 us (1%)
    dot_general x24, matrix products, contract(): lax.dot_general(left_side, right_side, (((left_dim,), (right_dim,)), ((),...  199 us
    psum x6, waiting for transfers between devices, advance(): last_sum = lax.psum(share, 'ctx')  185 us
    dot_general x8, matrix products, dot_f32(): return jnp.dot(left_side, right_side, preferred_element_type=jnp.float32)  113 us
    ppermute x4, waiting for transfers between devices, backward_step(): return lax.ppermute(value, 'ctx', [(i + 1, i) for i in range(count - 1)])  96.5 us
    ppermute x4, waiting for transfers between devices, onward(): return lax.ppermute(value, 'ctx', [(i, i + 1) for i in range(count - 1)])  89 us
    pallas_call x12, Pallas kernels, join(): pl.pallas_call(join_kernel, grid_spec=pltpu.PrefetchScalarGridSpec(num_sc...  85.3 us
    pallas_call x2, Pallas kernels, attention_backward(): pl.pallas_call(backward_kernel, grid=(groups, pairs), in_specs=[packed_sp...  80.8 us
    pallas_call x2, Pallas kernels, attention_forward(): pl.pallas_call(forward_kernel, grid=(groups, pairs), in_specs=[pl.BlockSp...  63.6 us
  transfers between devices with their start and end apart: 71, of which 33 were waited for; matrix products, arithmetic and copies ran while one was open for 34% of the time, Pallas kernels for 17%

profile of v6, /device:TPU:0, one launch (start us, length us, event | category | flops | bytes accessed | tf_op | source)
XLA Modules:
  0.0 1331.0 jit_solution(10968880633133994927)
XLA Ops:
  43.0 9.3 collective-permute-done
  59.7 24.5 %collective-permute-done.1 = bf16[512,1280]{1,0:T(8,128)(2,1)} collective-permute-done((bf16[512,1280]{1,0:T(8,128)(2,1)S(1)}, bf16[512,1280]{1,0:T(8,128)(2,1)}, u32[]{:S(2)}, u32[]{:S(2)}) %collective-permute-start.1) | collective-permute-done | bytes 1310752 | tf_op jit(solution)/shard_map/ppermute | solution.py:199
  109.8 7.5 shard_map.188
  117.3 21.9 %add_convert_fusion.1 = bf16[3072,1920]{1,0:T(8,128)(2,1)} fusion(bf16[3072,1280]{1,0:T(8,128)(2,1)} %constant_dynamic-update-slice_fusion, f32[1920]{0:T(1024)S(1)} %reduce.2, bf16[1280,2560]{1,0:T(8,128)(2,1)} %shard_map.188), kind=kOutput, calls=%fused_computation.3 | convolution fusion | flops 15111290880 | bytes 24583680 | tf_op jit(solution)/shard_map/dot_general | solution.py:299
  139.2 31.8 %shard_map.189 = (bf16[2,512,640]{2,1,0:T(8,128)(2,1)}, f32[2,5,2,512]{3,2,1,0:T(2,128)}) custom-call(bf16[2,1536,1920]{2,1,0:T(8,128)(2,1)} %bitcast.359, s32[2,512,1]{2,1,0:T(8,128)} %subtract_add_fusion.low_ref), custom_call_target="tpu_custom_call" | custom-call | flops 6710886400 | bytes 11796480 | tf_op jit(solution)/shard_map/pallas_call | solution.py:80
  186.2 31.6 %all-gather.11.cloned.1.call-done = bf16[1280,5120]{1,0:T(8,128)(2,1)} async-done(((bf16[320,5120]{1,0:T(8,128)(2,1)}), bf16[1280,5120]{1,0:T(8,128)(2,1)}) %all-gather.11.cloned.1.call-update) | async-done | bytes 13107216 | tf_op jit(solution)/shard_map/all_gather | solution.py:286
  225.0 10.1 collective-permute-done.12.refs_1_
  236.8 7.3 shard_map.190
  244.1 7.5 shard_map.191
  251.5 12.8 multiply_convert_fusion.1
  281.2 27.2 %collective-permute-done.15 = bf16[512,1280]{1,0:T(8,128)(2,1)} collective-permute-done((bf16[512,1280]{1,0:T(8,128)(2,1)S(1)}, bf16[512,1280]{1,0:T(8,128)(2,1)}, u32[]{:S(2)}, u32[]{:S(2)}) %collective-permute-start.15) | collective-permute-done | bytes 1310752 | tf_op jit(solution)/shard_map/ppermute | solution.py:199
  318.0 27.9 %collective-permute-done.16 = bf16[512,1280]{1,0:T(8,128)(2,1)} collective-permute-done((bf16[512,1280]{1,0:T(8,128)(2,1)}, bf16[512,1280]{1,0:T(8,128)(2,1)}, u32[]{:S(2)}, u32[]{:S(2)}) %collective-permute-start.16) | collective-permute-done | bytes 1310752 | tf_op jit(solution)/shard_map/ppermute | solution.py:199
  346.5 7.2 shard_map.192
  360.1 18.6 %add_convert_fusion = bf16[3072,1920]{1,0:T(8,128)(2,1)} fusion(bf16[3072,1280]{1,0:T(8,128)(2,1)S(1)} %constant_dynamic-update-slice_fusion.23, f32[1920]{0:T(1024)S(1)} %reduce.10, bf16[1280,2560]{1,0:T(8,128)(2,1)S(1)} %bitcast.318), kind=kOutput, calls=%fused_computation.2 | convolution fusion | flops 15111290880 | bytes 24584192 | tf_op jit(solution)/shard_map/dot_general | solution.py:299
  378.7 31.8 %shard_map.193 = (bf16[2,512,640]{2,1,0:T(8,128)(2,1)}, f32[2,5,2,512]{3,2,1,0:T(2,128)}) custom-call(bf16[2,1536,1920]{2,1,0:T(8,128)(2,1)} %bitcast.361, s32[2,512,1]{2,1,0:T(8,128)} %subtract_add_fusion.low_ref), custom_call_target="tpu_custom_call" | custom-call | flops 6710886400 | bytes 11796480 | tf_op jit(solution)/shard_map/pallas_call | solution.py:80
  425.8 10.8 all-gather.15.cloned.1.call-done
  455.0 14.8 %multiply_convert_fusion = (bf16[1024,2560]{1,0:T(8,128)(2,1)S(1)}, f32[1024,2560]{1,0:T(8,128)}) fusion(f32[2560]{0:T(1024)S(1)} %get-tuple-element.158, bf16[1024,1280]{1,0:T(8,128)(2,1)} %pad_maximum_fusion.3, bf16[1280,2560]{1,0:T(8,128)(2,1)} %shard_map.194), kind=kOutput, calls=%fused_computation.28 | convolution fusion | flops 6737100800 | bytes 24913920 | tf_op jit(solution)/shard_map/dot_general | solution.py:299
  469.8 9.6 convolution_convert_fusion.3
  485.1 7.0 shard_map.195
  492.0 18.6 %fusion.13 = bf16[1024,2560]{1,0:T(8,128)(2,1)} fusion(f32[1024,2560]{1,0:T(8,128)} %get-tuple-element.205, f32[2560]{0:T(1024)S(1)} %get-tuple-element.158, bf16[1280,2560]{1,0:T(8,128)(2,1)} %shard_map.195, bf16[512,1280]{1,0:T(8,128)(2,1)} %collective-permute-done.27, bf16[512,1280]{1,0:T(8,128)(2,1)S(1)} %fusion.147), kind=kOutput, calls=%fused_computation.25 | convolution fusion | flops 6771179520 | bytes 24913920 | tf_op jit(solution)/shard_map/dot_general | solution.py:299
  517.7 7.4 convolution_convert_fusion.13
  525.5 10.2 convolution_convert_fusion.2
  559.1 8.0 shard_map.198
  567.1 40.2 %shard_map.196 = bf16[2,1536,1920]{2,1,0:T(8,128)(2,1)} custom-call(bf16[2,1536,1920]{2,1,0:T(8,128)(2,1)} %bitcast.362, bf16[2,512,640]{2,1,0:T(8,128)(2,1)} %get-tuple-element.81.mixed_ref, bf16[2,512,640]{2,1,0:T(8,128)(2,1)} %bitcast.364, f32[2,5,2,512]{3,2,1,0:T(2,128)} %get-tuple-element.87.total_ref, s32[2,1,512]{2,1,0:T(1,128)} %subtract_add_fusion.1.low_ref), custom_call_target="tpu_custom_call" | custom-call | flops 16777216000 | bytes 23592960 | tf_op jit(solution)/shard_map/pallas_call | solution.py:163
  607.4 12.0 convolution_convert_fusion.7
  626.5 12.6 convolution_add_fusion.1
  639.0 22.2 %convolution_convert_fusion.5 = bf16[1280,1920]{1,0:T(8,128)(2,1)S(1)} fusion(bf16[3072,1280]{1,0:T(8,128)(2,1)} %copy-done.50, bf16[3072,1920]{1,0:T(8,128)(2,1)S(1)} %bitcast.307), kind=kOutput, calls=%fused_computation.33 | convolution fusion | flops 15101952000 | bytes 24576000 | tf_op jit(solution)/shard_map/dot_general | solution.py:15
  673.9 49.6 %collective-permute-done.34 = bf16[512,1280]{1,0:T(8,128)(2,1)S(1)} collective-permute-done((bf16[512,1280]{1,0:T(8,128)(2,1)S(1)}, bf16[512,1280]{1,0:T(8,128)(2,1)S(1)}, u32[]{:S(2)}, u32[]{:S(2)}) %collective-permute-start.34) | collective-permute-done | bytes 1310752 | tf_op jit(solution)/shard_map/ppermute | solution.py:204
  726.9 47.6 %all-reduce.10.cloned.1.call-done = bf16[320,2560]{1,0:T(8,128)(2,1)} async-done(((bf16[320,2560]{1,0:T(8,128)(2,1)}), bf16[320,2560]{1,0:T(8,128)(2,1)}) %all-reduce.10.cloned.1.call-update) | async-done | bytes 1638416 | tf_op jit(solution)/shard_map/psum | solution.py:559
  774.5 9.6 collective-permute-done.36
  799.9 10.0 convolution_convert_fusion.1
  812.7 16.4 %fusion.6 = bf16[1024,2560]{1,0:T(8,128)(2,1)} fusion(f32[1024,2560]{1,0:T(8,128)} %get-tuple-element.199, f32[2560]{0:T(1024)S(1)} %copy-done.80, bf16[1280,2560]{1,0:T(8,128)(2,1)S(1)} %bitcast.322, bf16[512,1280]{1,0:T(8,128)(2,1)S(1)} %collective-permute-done.37, bf16[512,1280]{1,0:T(8,128)(2,1)S(1)} %convert_element_type.243), kind=kOutput, calls=%fused_computation.18 | convolution fusion | flops 6771179520 | bytes 24913920 | tf_op jit(solution)/shard_map/dot_general | solution.py:299
  829.1 38.3 %all-reduce.12.cloned.1.call-done = bf16[320,3200]{1,0:T(8,128)(2,1)} async-done(((bf16[320,3200]{1,0:T(8,128)(2,1)}), bf16[320,3200]{1,0:T(8,128)(2,1)}) %all-reduce.12.cloned.1.call-update) | async-done | bytes 2048016 | tf_op jit(solution)/shard_map/psum | solution.py:559
  867.5 7.0 shard_map.201
  874.7 7.4 convolution_convert_fusion.12
  882.2 10.1 convolution_convert_fusion
  914.0 40.5 %shard_map.200 = bf16[2,1536,1920]{2,1,0:T(8,128)(2,1)} custom-call(bf16[2,1536,1920]{2,1,0:T(8,128)(2,1)} %bitcast.360, bf16[2,512,640]{2,1,0:T(8,128)(2,1)} %get-tuple-element.74.mixed_ref, bf16[2,512,640]{2,1,0:T(8,128)(2,1)} %bitcast.365, f32[2,5,2,512]{3,2,1,0:T(2,128)} %get-tuple-element.108.total_ref, s32[2,1,512]{2,1,0:T(1,128)} %subtract_add_fusion.1.low_ref), custom_call_target="tpu_custom_call" | custom-call | flops 16777216000 | bytes 23592960 | tf_op jit(solution)/shard_map/pallas_call | solution.py:163
  954.6 8.2 shard_map.202
  962.9 12.0 convolution_convert_fusion.6
  981.9 14.1 %convolution_add_fusion = f32[1536,1280]{1,0:T(8,128)} fusion(bf16[1536,1280]{1,0:T(8,128)(2,1)S(1)} %collective-permute-done.43, bf16[2,1536,1920]{2,1,0:T(8,128)(2,1)} %shard_map.200, bf16[1280,2560]{1,0:T(8,128)(2,1)} %shard_map.188), kind=kOutput, calls=%fused_computation.30 | convolution fusion | flops 7553679360 | bytes 22609920 | tf_op jit(solution)/shard_map/dot_general | solution.py:15
  995.9 19.7 %convolution_convert_fusion.4 = bf16[1280,1920]{1,0:T(8,128)(2,1)S(1)} fusion(bf16[3072,1280]{1,0:T(8,128)(2,1)} %constant_dynamic-update-slice_fusion, bf16[3072,1920]{1,0:T(8,128)(2,1)S(1)} %bitcast.311), kind=kOutput, calls=%fused_computation.32 | convolution fusion | flops 15101952000 | bytes 24576000 | tf_op jit(solution)/shard_map/dot_general | solution.py:15
  1021.7 8.8 convolution_convert_fusion.14
  1038.2 15.7 %collective-permute-done.44 = bf16[512,1280]{1,0:T(8,128)(2,1)} collective-permute-done((bf16[512,1280]{1,0:T(8,128)(2,1)}, bf16[512,1280]{1,0:T(8,128)(2,1)}, u32[]{:S(2)}, u32[]{:S(2)}) %collective-permute-start.44) | collective-permute-done | bytes 1310752 | tf_op jit(solution)/shard_map/ppermute | solution.py:204
  1053.9 8.7 fusion.45
  1064.0 52.2 %collective-permute-done.26 = bf16[512,1280]{1,0:T(8,128)(2,1)S(1)} collective-permute-done((bf16[512,1280]{1,0:T(8,128)(2,1)}, bf16[512,1280]{1,0:T(8,128)(2,1)S(1)}, u32[]{:S(2)}, u32[]{:S(2)}) %collective-permute-start.26) | collective-permute-done | bytes 1310752 | tf_op jit(solution)/shard_map/ppermute | solution.py:194
  1144.8 21.7 %collective-permute-done.46 = bf16[512,1280]{1,0:T(8,128)(2,1)} collective-permute-done((bf16[512,1280]{1,0:T(8,128)(2,1)}, bf16[512,1280]{1,0:T(8,128)(2,1)}, u32[]{:S(2)}, u32[]{:S(2)}) %collective-permute-start.46) | collective-permute-done | bytes 1310752 | tf_op jit(solution)/shard_map/ppermute | solution.py:204
  1202.7 55.6 %all-reduce.18.cloned.1.call-done = bf16[320,3200]{1,0:T(8,128)(2,1)} async-done(((bf16[320,3200]{1,0:T(8,128)(2,1)}), bf16[320,3200]{1,0:T(8,128)(2,1)}) %all-reduce.18.cloned.1.call-update) | async-done | bytes 2048016 | tf_op jit(solution)/shard_map/psum | solution.py:559
  1276.1 43.0 %all-reduce.20.cloned.1.call-done.first_ref = bf16[320,1920]{1,0:T(8,128)(2,1)} async-done(((bf16[320,1920]{1,0:T(8,128)(2,1)}), bf16[320,1920]{1,0:T(8,128)(2,1)}) %all-reduce.20.cloned.1.call-update) | async-done | bytes 1228816 | tf_op jit(solution)/shard_map/psum | solution.py:559
  (575 shorter events, 366.6 us)
Async XLA Ops:
  8.0 80.4 %all-gather.9.cloned.1.call-start = ((), (), s32[]{:S(2)}) async-start(), calls=%async_computation.19 | async-start | bytes 8192000 | tf_op jit(solution)/shard_map/all_gather | solution.py:286
  13.3 96.6 %all-reduce.8.cloned.1.call-start = ((), (), s32[]{:S(2)}) async-start(), calls=%async_computation.6 | async-start | bytes 163840 | tf_op jit(solution)/shard_map/psum | solution.py:458
  13.3 26.2 %collective-permute-start.9 = (s32[4]{0:T(128)S(1)}, s32[4]{0:T(128)S(1)}, u32[]{:S(2)}, u32[]{:S(2)}) collective-permute-start(s32[4]{0:T(128)S(1)} %fusion.148), channel_id=1, source_target_pairs={{0,8},{8,0},{1,9},{9,1},{2,10},{10,2},{3,11},{11,3},{4,12},{12,4},... | collective-permute-start | bytes 56 | tf_op jit(solution)/shard_map/ppermute | solution.py:190
  13.9 27.2 %collective-permute-start.2 = (bf16[12,320]{1,0:T(8,128)(2,1)S(1)}, bf16[12,320]{1,0:T(8,128)(2,1)S(1)}, u32[]{:S(2)}, u32[]{:S(2)}) collective-permute-start(bf16[12,320]{1,0:T(8,128)(2,1)S(1)} %reshape.357), channel_id=1, source_target_pairs={{0,8},{8,0},{1,9},{9,1},{2,10},{10,2},{3,11},{11,3},{4,12},{12,4},... | collective-permute-start | bytes 23048 | tf_op jit(solution)/shard_map/ppermute | solution.py:190
  14.1 28.8 %collective-permute-start.8 = (bf16[2,3840]{1,0:T(2,128)(2,1)S(1)}, bf16[2,3840]{1,0:T(2,128)(2,1)S(1)}, u32[]{:S(2)}, u32[]{:S(2)}) collective-permute-start(bf16[2,3840]{1,0:T(2,128)(2,1)S(1)} %constant_dynamic-update-slice_fusion.6), channel_id=1, source_target_pairs={{0,1},{1,0},{2,3},{3,2},{4,5},{5,4},{6,7},{7,6},{8,9},{9,8},{10,11... | collective-permute-start | bytes 46088 | tf_op jit(solution)/shard_map/ppermute | solution.py:194
  18.7 33.6 %collective-permute-start = (bf16[512,1280]{1,0:T(8,128)(2,1)S(1)}, bf16[512,1280]{1,0:T(8,128)(2,1)S(1)}, u32[]{:S(2)}, u32[]{:S(2)}) collective-permute-start(bf16[512,1280]{1,0:T(8,128)(2,1)S(1)} %get-tuple-element.175), channel_id=1, source_target_pairs={{0,2},{2,4},{4,6},{1,3},{3,5},{5,7},{8,10},{10,12},{12,14},{9,11},... | collective-permute-start | bytes 3932168 | tf_op jit(solution)/shard_map/ppermute | solution.py:199
  24.8 193.0 %all-gather.11.cloned.1.call-start = ((), (), s32[]{:S(2)}) async-start(), calls=%async_computation.20 | async-start | bytes 16384000 | tf_op jit(solution)/shard_map/all_gather | solution.py:286
  41.3 16.8 %collective-permute-start.3 = (bf16[12,640]{1,0:T(8,128)(2,1)S(1)}, bf16[12,640]{1,0:T(8,128)(2,1)S(1)}, u32[]{:S(2)}, u32[]{:S(2)}) collective-permute-start(bf16[12,640]{1,0:T(8,128)(2,1)S(1)} %select_n.135), channel_id=1, source_target_pairs={{0,16},{16,0},{1,17},{17,1},{2,18},{18,2},{3,19},{19,3},{4,20},{20... | collective-permute-start | bytes 46088 | tf_op jit(solution)/shard_map/ppermute | solution.py:315
  52.3 256.2 %all-gather.13.cloned.1.call-start = ((), (), s32[]{:S(2)}) async-start(), calls=%async_computation.21 | async-start | bytes 8192000 | tf_op jit(solution)/shard_map/all_gather | solution.py:286
  52.6 31.6 %collective-permute-start.1 = (bf16[512,1280]{1,0:T(8,128)(2,1)S(1)}, bf16[512,1280]{1,0:T(8,128)(2,1)}, u32[]{:S(2)}, u32[]{:S(2)}) collective-permute-start(bf16[512,1280]{1,0:T(8,128)(2,1)S(1)} %collective-permute-done), channel_id=1, source_target_pairs={{0,2},{2,4},{4,6},{1,3},{3,5},{5,7},{8,10},{10,12},{12,14},{9,11},... | collective-permute-start | bytes 3932168 | tf_op jit(solution)/shard_map/ppermute | solution.py:199
  92.3 17.5 %collective-permute-start.7 = (bf16[2,320,2560]{2,1,0:T(8,128)(2,1)}, bf16[2,320,2560]{2,1,0:T(8,128)(2,1)}, u32[]{:S(2)}, u32[]{:S(2)}) collective-permute-start(bf16[2,320,2560]{2,1,0:T(8,128)(2,1)} %dynamic-slice_bitcast_fusion.7), channel_id=1, source_target_pairs={{0,8},{8,0},{1,9},{9,1},{2,10},{10,2},{3,11},{11,3},{4,12},{12,4},... | collective-permute-start | bytes 9830408 | tf_op jit(solution)/shard_map/ppermute | solution.py:190
  224.4 10.7 collective-permute-start.12
  224.4 19.7 %collective-permute-start.13 = (bf16[2,320,2560]{2,1,0:T(8,128)(2,1)}, bf16[2,320,2560]{2,1,0:T(8,128)(2,1)}, u32[]{:S(2)}, u32[]{:S(2)}) collective-permute-start(bf16[2,320,2560]{2,1,0:T(8,128)(2,1)} %get-tuple-element.183), channel_id=1, source_target_pairs={{0,8},{8,0},{1,9},{9,1},{2,10},{10,2},{3,11},{11,3},{4,12},{12,4},... | collective-permute-start | bytes 9830408 | tf_op jit(solution)/shard_map/ppermute | solution.py:190
  224.9 211.7 %all-gather.15.cloned.1.call-start = ((), (), s32[]{:S(2)}) async-start(), calls=%async_computation.22 | async-start | bytes 16384000 | tf_op jit(solution)/shard_map/all_gather | solution.py:286
  276.8 31.7 %collective-permute-start.15 = (bf16[512,1280]{1,0:T(8,128)(2,1)S(1)}, bf16[512,1280]{1,0:T(8,128)(2,1)}, u32[]{:S(2)}, u32[]{:S(2)}) collective-permute-start(bf16[512,1280]{1,0:T(8,128)(2,1)S(1)} %add_convert_fusion.5), channel_id=1, source_target_pairs={{0,2},{2,4},{4,6},{1,3},{3,5},{5,7},{8,10},{10,12},{12,14},{9,11},... | collective-permute-start | bytes 3932168 | tf_op jit(solution)/shard_map/ppermute | solution.py:199
  308.5 298.8 %reduce-scatter.7.cloned.1.call-start = ((), (), s32[]{:S(2)}) async-start(), calls=%async_computation.7 | async-start | bytes 8192000 | tf_op jit(solution)/shard_map/reduce_scatter | solution.py:295
  312.4 34.1 %collective-permute-start.20 = (bf16[2,320,2560]{2,1,0:T(8,128)(2,1)}, bf16[2,320,2560]{2,1,0:T(8,128)(2,1)}, u32[]{:S(2)}, u32[]{:S(2)}) collective-permute-start(bf16[2,320,2560]{2,1,0:T(8,128)(2,1)} %dynamic-slice_bitcast_fusion.6), channel_id=1, source_target_pairs={{0,8},{8,0},{1,9},{9,1},{2,10},{10,2},{3,11},{11,3},{4,12},{12,4},... | collective-permute-start | bytes 9830408 | tf_op jit(solution)/shard_map/ppermute | solution.py:190
  312.4 33.5 %collective-permute-start.16 = (bf16[512,1280]{1,0:T(8,128)(2,1)}, bf16[512,1280]{1,0:T(8,128)(2,1)}, u32[]{:S(2)}, u32[]{:S(2)}) collective-permute-start(bf16[512,1280]{1,0:T(8,128)(2,1)} %collective-permute-done.15), channel_id=1, source_target_pairs={{0,2},{2,4},{4,6},{1,3},{3,5},{5,7},{8,10},{10,12},{12,14},{9,11},... | collective-permute-start | bytes 3932168 | tf_op jit(solution)/shard_map/ppermute | solution.py:199
  345.9 11.2 collective-permute-start.17
  346.0 13.0 collective-permute-start.19
  442.6 27.2 %collective-permute-start.27 = (bf16[512,1280]{1,0:T(8,128)(2,1)S(1)}, bf16[512,1280]{1,0:T(8,128)(2,1)}, u32[]{:S(2)}, u32[]{:S(2)}) collective-permute-start(bf16[512,1280]{1,0:T(8,128)(2,1)S(1)} %fusion.147), channel_id=1, source_target_pairs={{0,8},{8,0},{1,9},{9,1},{2,10},{10,2},{3,11},{11,3},{4,12},{12,4},... | collective-permute-start | bytes 3932168 | tf_op jit(solution)/shard_map/ppermute | solution.py:190
  442.7 40.6 %collective-permute-start.24 = (bf16[2,320,2560]{2,1,0:T(8,128)(2,1)}, bf16[2,320,2560]{2,1,0:T(8,128)(2,1)S(1)}, u32[]{:S(2)}, u32[]{:S(2)}) collective-permute-start(bf16[2,320,2560]{2,1,0:T(8,128)(2,1)} %get-tuple-element.181), channel_id=1, source_target_pairs={{0,8},{8,0},{1,9},{9,1},{2,10},{10,2},{3,11},{11,3},{4,12},{12,4},... | collective-permute-start | bytes 9830408 | tf_op jit(solution)/shard_map/ppermute | solution.py:190
  483.2 27.4 %collective-permute-start.28 = (bf16[2,320,2560]{2,1,0:T(8,128)(2,1)}, bf16[2,320,2560]{2,1,0:T(8,128)(2,1)}, u32[]{:S(2)}, u32[]{:S(2)}) collective-permute-start(bf16[2,320,2560]{2,1,0:T(8,128)(2,1)} %dynamic-slice_bitcast_fusion.5), channel_id=1, source_target_pairs={{0,8},{8,0},{1,9},{9,1},{2,10},{10,2},{3,11},{11,3},{4,12},{12,4},... | collective-permute-start | bytes 9830408 | tf_op jit(solution)/shard_map/ppermute | solution.py:190
  517.7 205.9 %reduce-scatter.9.cloned.1.call-start = ((), (), s32[]{:S(2)}) async-start(), calls=%async_computation.8 | async-start | bytes 10240000 | tf_op jit(solution)/shard_map/reduce_scatter | solution.py:295
  525.1 15.0 %collective-permute-start.29 = (bf16[512,1280]{1,0:T(8,128)(2,1)S(1)}, bf16[512,1280]{1,0:T(8,128)(2,1)S(1)}, u32[]{:S(2)}, u32[]{:S(2)}) collective-permute-start(bf16[512,1280]{1,0:T(8,128)(2,1)S(1)} %convolution_convert_fusion.13), channel_id=1, source_target_pairs={{0,8},{8,0},{1,9},{9,1},{2,10},{10,2},{3,11},{11,3},{4,12},{12,4},... | collective-permute-start | bytes 3932168 | tf_op jit(solution)/shard_map/ppermute | solution.py:190
  540.0 18.1 %collective-permute-start.31 = (bf16[2,320,2560]{2,1,0:T(8,128)(2,1)}, bf16[2,320,2560]{2,1,0:T(8,128)(2,1)}, u32[]{:S(2)}, u32[]{:S(2)}) collective-permute-start(bf16[2,320,2560]{2,1,0:T(8,128)(2,1)} %dynamic-slice_bitcast_fusion.4), channel_id=1, source_target_pairs={{0,8},{8,0},{1,9},{9,1},{2,10},{10,2},{3,11},{11,3},{4,12},{12,4},... | collective-permute-start | bytes 9830408 | tf_op jit(solution)/shard_map/ppermute | solution.py:190
  607.4 167.1 %all-reduce.10.cloned.1.call-start = ((), (), s32[]{:S(2)}) async-start(), calls=%async_computation.9 | async-start | bytes 3276800 | tf_op jit(solution)/shard_map/psum | solution.py:559
  664.3 59.2 %collective-permute-start.34 = (bf16[512,1280]{1,0:T(8,128)(2,1)S(1)}, bf16[512,1280]{1,0:T(8,128)(2,1)S(1)}, u32[]{:S(2)}, u32[]{:S(2)}) collective-permute-start(bf16[512,1280]{1,0:T(8,128)(2,1)S(1)} %slice.715), channel_id=1, source_target_pairs={{2,0},{4,2},{6,4},{3,1},{5,3},{7,5},{10,8},{12,10},{14,12},{11,9},... | collective-permute-start | bytes 3932168 | tf_op jit(solution)/shard_map/ppermute | solution.py:204
  665.6 201.9 %all-reduce.12.cloned.1.call-start = ((), (), s32[]{:S(2)}) async-start(), calls=%async_computation.11 | async-start | bytes 4096000 | tf_op jit(solution)/shard_map/psum | solution.py:559
  725.6 58.5 %collective-permute-start.36 = (bf16[512,1280]{1,0:T(8,128)(2,1)S(1)}, bf16[512,1280]{1,0:T(8,128)(2,1)S(1)}, u32[]{:S(2)}, u32[]{:S(2)}) collective-permute-start(bf16[512,1280]{1,0:T(8,128)(2,1)S(1)} %add_convert_fusion.3), channel_id=1, source_target_pairs={{2,0},{4,2},{6,4},{3,1},{5,3},{7,5},{10,8},{12,10},{14,12},{11,9},... | collective-permute-start | bytes 3932168 | tf_op jit(solution)/shard_map/ppermute | solution.py:204
  785.2 82.3 %reduce-scatter.11.cloned.1.call-start = ((), (), s32[]{:S(2)}) async-start(), calls=%async_computation.10 | async-start | bytes 6144000 | tf_op jit(solution)/shard_map/reduce_scatter | solution.py:295
  785.9 168.6 %all-reduce.14.cloned.1.call-start = ((), (), s32[]{:S(2)}) async-start(), calls=%async_computation.13 | async-start | bytes 2457600 | tf_op jit(solution)/shard_map/psum | solution.py:559
  812.7 16.5 %collective-permute-start.38 = (bf16[2,320,2560]{2,1,0:T(8,128)(2,1)S(1)}, bf16[2,320,2560]{2,1,0:T(8,128)(2,1)S(1)}, u32[]{:S(2)}, u32[]{:S(2)}) collective-permute-start(bf16[2,320,2560]{2,1,0:T(8,128)(2,1)S(1)} %dynamic-slice_bitcast_fusion.3), channel_id=1, source_target_pairs={{0,8},{8,0},{1,9},{9,1},{2,10},{10,2},{3,11},{11,3},{4,12},{12,4},... | collective-permute-start | bytes 9830408 | tf_op jit(solution)/shard_map/ppermute | solution.py:190
  867.5 87.1 %reduce-scatter.13.cloned.1.call-start = ((), (), s32[]{:S(2)}) async-start(), calls=%async_computation.12 | async-start | bytes 8192000 | tf_op jit(solution)/shard_map/reduce_scatter | solution.py:295
  874.6 255.6 %all-reduce.16.cloned.1.call-start = ((), (), s32[]{:S(2)}) async-start(), calls=%async_computation.15 | async-start | bytes 3276800 | tf_op jit(solution)/shard_map/psum | solution.py:559
  882.1 13.8 %collective-permute-start.39 = (bf16[512,1280]{1,0:T(8,128)(2,1)S(1)}, bf16[512,1280]{1,0:T(8,128)(2,1)}, u32[]{:S(2)}, u32[]{:S(2)}) collective-permute-start(bf16[512,1280]{1,0:T(8,128)(2,1)S(1)} %convolution_convert_fusion.12), channel_id=1, source_target_pairs={{0,8},{8,0},{1,9},{9,1},{2,10},{10,2},{3,11},{11,3},{4,12},{12,4},... | collective-permute-start | bytes 3932168 | tf_op jit(solution)/shard_map/ppermute | solution.py:190
  895.6 18.4 %collective-permute-start.41 = (bf16[2,320,2560]{2,1,0:T(8,128)(2,1)S(1)}, bf16[2,320,2560]{2,1,0:T(8,128)(2,1)}, u32[]{:S(2)}, u32[]{:S(2)}) collective-permute-start(bf16[2,320,2560]{2,1,0:T(8,128)(2,1)S(1)} %dynamic-slice_bitcast_fusion.2), channel_id=1, source_target_pairs={{0,8},{8,0},{1,9},{9,1},{2,10},{10,2},{3,11},{11,3},{4,12},{12,4},... | collective-permute-start | bytes 9830408 | tf_op jit(solution)/shard_map/ppermute | solution.py:190
  954.6 175.6 %reduce-scatter.15.cloned.1.call-start = ((), (), s32[]{:S(2)}) async-start(), calls=%async_computation.14 | async-start | bytes 10240000 | tf_op jit(solution)/shard_map/reduce_scatter | solution.py:295
  962.9 239.9 %reduce-scatter.17.cloned.1.call-start = ((), (), s32[]{:S(2)}) async-start(), calls=%async_computation.16 | async-start | bytes 6144000 | tf_op jit(solution)/shard_map/reduce_scatter | solution.py:295
  1015.8 15.0 %collective-permute-start.45 = (bf16[2,320,1920]{2,1,0:T(8,128)(2,1)S(1)}, bf16[2,320,1920]{2,1,0:T(8,128)(2,1)S(1)}, u32[]{:S(2)}, u32[]{:S(2)}) collective-permute-start(bf16[2,320,1920]{2,1,0:T(8,128)(2,1)S(1)} %dynamic-slice_bitcast_fusion.8), channel_id=1, source_target_pairs={{0,8},{8,0},{1,9},{9,1},{2,10},{10,2},{3,11},{11,3},{4,12},{12,4},... | collective-permute-start | bytes 7372808 | tf_op jit(solution)/shard_map/ppermute | solution.py:190
  1020.4 33.4 %collective-permute-start.44 = (bf16[512,1280]{1,0:T(8,128)(2,1)}, bf16[512,1280]{1,0:T(8,128)(2,1)}, u32[]{:S(2)}, u32[]{:S(2)}) collective-permute-start(bf16[512,1280]{1,0:T(8,128)(2,1)} %slice.714), channel_id=1, source_target_pairs={{2,0},{4,2},{6,4},{3,1},{5,3},{7,5},{10,8},{12,10},{14,12},{11,9},... | collective-permute-start | bytes 3932168 | tf_op jit(solution)/shard_map/ppermute | solution.py:204
  1030.5 23.4 %collective-permute-start.25 = (bf16[512,1280]{1,0:T(8,128)(2,1)}, bf16[512,1280]{1,0:T(8,128)(2,1)}, u32[]{:S(2)}, u32[]{:S(2)}) collective-permute-start(bf16[512,1280]{1,0:T(8,128)(2,1)} %convolution_convert_fusion.14), channel_id=1, source_target_pairs={{0,8},{8,0},{1,9},{9,1},{2,10},{10,2},{3,11},{11,3},{4,12},{12,4},... | collective-permute-start | bytes 3932168 | tf_op jit(solution)/shard_map/ppermute | solution.py:190
  1053.9 204.5 %all-reduce.18.cloned.1.call-start = ((), (), s32[]{:S(2)}) async-start(), calls=%async_computation.17 | async-start | bytes 4096000 | tf_op jit(solution)/shard_map/psum | solution.py:559
  1062.6 53.5 %collective-permute-start.26 = (bf16[512,1280]{1,0:T(8,128)(2,1)}, bf16[512,1280]{1,0:T(8,128)(2,1)S(1)}, u32[]{:S(2)}, u32[]{:S(2)}) collective-permute-start(bf16[512,1280]{1,0:T(8,128)(2,1)} %fusion.45), channel_id=1, source_target_pairs={{0,1},{1,0},{2,3},{3,2},{4,5},{5,4},{6,7},{7,6},{8,9},{9,8},{10,11... | collective-permute-start | bytes 3932168 | tf_op jit(solution)/shard_map/ppermute | solution.py:194
  1133.9 32.6 %collective-permute-start.46 = (bf16[512,1280]{1,0:T(8,128)(2,1)}, bf16[512,1280]{1,0:T(8,128)(2,1)}, u32[]{:S(2)}, u32[]{:S(2)}) collective-permute-start(bf16[512,1280]{1,0:T(8,128)(2,1)} %add_convert_fusion.2), channel_id=1, source_target_pairs={{2,0},{4,2},{6,4},{3,1},{5,3},{7,5},{10,8},{12,10},{14,12},{11,9},... | collective-permute-start | bytes 3932168 | tf_op jit(solution)/shard_map/ppermute | solution.py:204
  1172.0 147.2 %all-reduce.20.cloned.1.call-start = ((), (), s32[]{:S(2)}) async-start(), calls=%async_computation.18 | async-start | bytes 2457600 | tf_op jit(solution)/shard_map/psum | solution.py:559
  1199.7 72.2 %collective-permute-start.47 = (bf16[512,1280]{1,0:T(8,128)(2,1)}, bf16[512,1280]{1,0:T(8,128)(2,1)}, u32[]{:S(2)}, u32[]{:S(2)}) collective-permute-start(bf16[512,1280]{1,0:T(8,128)(2,1)} %get-tuple-element.170), channel_id=1, source_target_pairs={{0,1},{1,0},{2,3},{3,2},{4,5},{5,4},{6,7},{7,6},{8,9},{9,8},{10,11... | collective-permute-start | bytes 3932168 | tf_op jit(solution)/shard_map/ppermute | solution.py:194
  1201.4 66.6 %collective-permute-start.53 = (f32[2,15360]{1,0:T(2,128)S(1)}, f32[2,15360]{1,0:T(2,128)}, u32[]{:S(2)}, u32[]{:S(2)}) collective-permute-start(f32[2,15360]{1,0:T(2,128)S(1)} %add.459), channel_id=1, source_target_pairs={{2,0},{4,6},{3,1},{5,7},{10,8},{12,14},{11,9},{13,15},{18,16},{20,... | collective-permute-start | bytes 368648 | tf_op jit(solution)/shard_map/ppermute | solution.py:358
  (130 other events, 2165.4 us)
Sparse Core Ops, SparseCore 0:
  13.4 75.0 all-gather.8
  90.9 126.8 all-gather.10
  225.0 72.3 all-gather.12
  308.6 127.9 all-gather.14
  517.8 72.4 reduce-scatter.6
  607.5 85.5 reduce-scatter.8
  789.4 56.1 reduce-scatter.10
  874.7 71.3 reduce-scatter.12
  963.0 84.8 reduce-scatter.14
  1054.0 83.5 reduce-scatter.16
Sparse Core Ops, SparseCore 1:
  24.9 33.5 all-reduce.7
  665.7 108.8 all-reduce.9
  785.2 82.2 all-reduce.11
  870.0 56.9 all-reduce.13
  954.7 71.3 all-reduce.15
  1172.1 86.2 all-reduce.17
  1262.2 56.9 all-reduce.19

commit v7 on v6

--- a/solution.py
+++ b/solution.py
@@ -275,7 +275,7 @@
             out_specs=pl.BlockSpec((rows, total), lambda chip, part, core: (chip * 2 + part, 0)),
         ),
         out_shape=jax.ShapeDtypeStruct((chips * 2 * rows, total), jnp.bfloat16),
-        compiler_params=pltpu.CompilerParams(vmem_limit_bytes=56 << 20),
+        compiler_params=pltpu.CompilerParams(vmem_limit_bytes=24 << 20),
         cost_estimate=pl.CostEstimate(
             flops=0, bytes_accessed=8 * chips * rows * total, transcendentals=0
         ),
@@ -395,7 +395,7 @@
         ],
         out_specs=pl.BlockSpec((rows, 4 * width), lambda step: (0, 0)),
         out_shape=jax.ShapeDtypeStruct((rows, 4 * width), jnp.bfloat16),
-        compiler_params=pltpu.CompilerParams(vmem_limit_bytes=56 << 20),
+        compiler_params=pltpu.CompilerParams(vmem_limit_bytes=24 << 20),
     )(qkv_weight, proj_weight)
 
 
@@ -420,7 +420,7 @@
         in_specs=[block, block],
         out_specs=pl.BlockSpec((2, 1, rows, width), lambda kind: (0, kind, 0, 0)),
         out_shape=jax.ShapeDtypeStruct((2, 3, rows, width), jnp.float32),
-        compiler_params=pltpu.CompilerParams(vmem_limit_bytes=56 << 20),
+        compiler_params=pltpu.CompilerParams(vmem_limit_bytes=24 << 20),
     )(first, second)
 
 
@@ -495,6 +495,9 @@
         attn_in, hat_attn, inv_attn = norm_forward(hidden, gains[0], shifts[0])
         own_near = [attn_in]
         mate_near = [mate(attn_in)]
+        attn_swap = CoreSwap(attn_blocks, place)
+        if layer == 0:
+            w_attn = join(attn_swap)
         step_value = attn_in
         for index in range(reach):
             if layer == 0:
@@ -505,13 +508,14 @@
                     step_value, piece = tie(step_value, mlp_pieces[layer])
                     mlp_blocks = gather_blocks(piece, place)
                     part = step_value
+                if index == 1:
+                    step_value, w_attn = tie(step_value, join(attn_swap))
+                    part = step_value
             own_near.insert(0, part)
             mate_near.insert(0, mate(part))
         near = jnp.concatenate(own_near + mate_near)
         if layer == 0:
             near, bias_parts = tie(near, bias_parts)
-        attn_swap = CoreSwap(attn_blocks, place)
-        w_attn = join(attn_swap)
         w_qkv, w_proj_t = w_attn[:, : 3 * half_width], w_attn[:, 3 * half_width :]
         packed = narrow(dot_f32(near, w_qkv) + bias_qkv).reshape(2, key_len, -1)
         mixed, log_total = attention_forward(packed, low_pos)
@@ -539,7 +543,7 @@
         )
 
     own_output = narrow(hidden)
-    output = both_seqs(own_output, other_tp(own_output))
+    far_output = other_tp(own_output)
 
     last_sum = None
     sums = {}
@@ -594,10 +598,14 @@
             narrow(dot_first(grad_low, mixed.reshape(2 * block_len, half_width))), place
         )
         grad_mixed, fc_swap.came, proj_swap.came = tie(grad_mixed, fc_swap.came, proj_swap.came)
-        grad_fc = join(fc_swap, proj_swap)
+        grad_mixed, grad_fc = tie(grad_mixed, join(fc_swap, proj_swap))
+        if not final:
+            grad_mixed = advance(grad_mixed, "out%d" % layer)
         grad_packed = attention_backward(packed, mixed, grad_mixed, log_total, low_pos)
-        grad_packed = advance(grad_packed, "out%d" % layer)
-        grad_packed, grad_fc = tie(grad_packed, grad_fc)
+        if final:
+            grad_packed = advance(grad_packed, "out%d" % layer)
+        else:
+            grad_packed, far_output = tie(grad_packed, far_output)
         waiting.append(("fc%d" % layer, scatter_sum(grad_fc)))
         mate_part = dot_second(grad_packed[1], w_qkv)
         own_part = dot_second(grad_packed[0], w_qkv)
@@ -607,18 +615,25 @@
         grad_near, rows = tie(grad_near, rows)
         far_total, grad_attn_in = grad_near[:last], grad_near[last:]
         carried = backward_step(narrow(far_total[:block_len]))
-        attn_swap = scatter_swap(narrow(dot_first(near, rows)), place)
+        grad_qkv = narrow(dot_first(near, rows))
+        grad_bias = jnp.sum(wide(rows), axis=0)
+        if final:
+            grad_qkv = advance(grad_qkv, "fc%d" % layer)
+            attn_swap = scatter_swap(grad_qkv, place)
         for step in range(1, reach + 1):
-            if step == 1:
+            if step == 1 and not final:
+                carried, grad_qkv, last_sum = tie(carried, grad_qkv, last_sum)
+                attn_swap = scatter_swap(grad_qkv, place)
+            if step == 1 and final:
                 carried, grad_attn = tie(carried, join(attn_swap))
-                if final:
-                    carried = advance(carried, "fc%d" % layer)
-                else:
-                    carried, grad_attn, waiting[0] = tie(carried, grad_attn, waiting[0][1])
-                    waiting[0] = ("fc%d" % layer, waiting[0])
                 waiting.append(("attn%d" % layer, scatter_sum(grad_attn)))
             if step == 2 and not final:
+                carried, grad_bias, grad_attn = tie(carried, grad_bias, join(attn_swap))
                 carried = advance(carried, "fc%d" % layer)
+                waiting.append(("attn%d" % layer, scatter_sum(grad_attn)))
+            if step == 2 and final:
+                carried, grad_bias = tie(carried, grad_bias)
+                carried = advance(carried, "attn%d" % layer)
             arrived = wide(carried)
             if step < reach:
                 section = far_total[step * block_len : (step + 1) * block_len]
@@ -629,7 +644,7 @@
             grad_attn_in, hat_attn, inv_attn, gains[0]
         )
         grad_hidden = grad_middle + grad_from_attn
-        grad_bias = jnp.sum(wide(rows), axis=0).reshape(-1, 3, PAIR)
+        grad_bias = grad_bias.reshape(-1, 3, PAIR)
         halves = jnp.concatenate(
             [grad_bias[:, 0].reshape(-1), grad_bias[:, 2].reshape(-1), grad_fc_bias]
         )
@@ -648,7 +663,6 @@
     small = small_total(jnp.stack(small_parts), place)
     far_grad = wide(other_tp(narrow(grad_hidden)))
     token_grad = both_seqs(grad_hidden, far_grad)
-    advance((), "attn0")
     split = 6 * model_width
     norms = small[:, :split].reshape(layer_count, 6, model_width)
     norms = lax.dynamic_slice_in_dim(norms, place.shard * shard_rows, shard_rows, 2)
@@ -657,7 +671,7 @@
     attn = [sums["attn%d" % layer] for layer in range(layer_count)]
     fc_proj = [sums["fc%d" % layer] for layer in range(layer_count)]
     return (
-        output,
+        both_seqs(own_output, far_output),
         token_grad,
         norms[:, :2],
         norms[:, 2:],

time: 1340 us -> 1250 us (0.933)
  Pallas kernels: 240 us -> 160 us
  local copies, waits for them, and re-layouts: 88.4 us -> 127 us
  waiting for transfers between devices: 530 us -> 494 us
    psum x6, waiting for transfers between devices: 185 us -> 79.2 us  [advance(): last_sum = lax.psum(share, 'ctx')]
    pallas_call x12, Pallas kernels: 85.3 us -> 10.8 us  [join(): pl.pallas_call(join_kernel, grid_spec=pltpu.PrefetchScalarGridSpec(num_sc...]
    reduce_scatter x6, waiting for transfers between devices: 0.07 us -> 43.9 us  [scatter_sum(): lax.psum_scatter(blocks, ('x', 'tp'), scatter_dimension=0, tiled=True)]
    ppermute x4, waiting for transfers between devices: 96.5 us -> 138 us  [backward_step(): return lax.ppermute(value, 'ctx', [(i + 1, i) for i in range(count - 1)])]
    unnamed x261 -> x309, local copies, waits for them, and re-layouts: 38.9 us -> 76.7 us
    ppermute x4, waiting for transfers between devices: 52.2 us -> 18.2 us  [other_tp(): return lax.ppermute(value, 'tp', [(0, 1), (1, 0)])]
  transfers between devices with their start and end apart: 71 -> 71, of which waited for: 33 -> 38; matrix products, arithmetic and copies ran while one was open for 34% -> 35% of each run, Pallas kernels for 17% -> 13%
where the time goes in v7:
time: 1250 us
  waiting for transfers between devices  494 us (40%)
  matrix products  303 us (24%)
  Pallas kernels  160 us (13%)
  local copies, waits for them, and re-layouts  127 us (10%)
  other arithmetic  94.3 us (8%)
  starting transfers between devices  49.7 us (4%)
  between operations  18.4 us (1%)
    dot_general x24, matrix products, contract(): lax.dot_general(left_side, right_side, (((left_dim,), (right_dim,)), ((),...  199 us
    ppermute x4, waiting for transfers between devices, backward_step(): return lax.ppermute(value, 'ctx', [(i + 1, i) for i in range(count - 1)])  138 us
    dot_general x8, matrix products, dot_f32(): return jnp.dot(left_side, right_side, preferred_element_type=jnp.float32)  103 us
    ppermute x4, waiting for transfers between devices, onward(): return lax.ppermute(value, 'ctx', [(i, i + 1) for i in range(count - 1)])  85.9 us
    pallas_call x2, Pallas kernels, attention_backward(): pl.pallas_call(backward_kernel, grid=(groups, pairs), in_specs=[packed_sp...  80.2 us
    psum x6, waiting for transfers between devices, advance(): last_sum = lax.psum(share, 'ctx')  79.2 us
    unnamed x309, local copies, waits for them, and re-layouts  76.7 us
    pallas_call x2, Pallas kernels, attention_forward(): pl.pallas_call(forward_kernel, grid=(groups, pairs), in_specs=[pl.BlockSp...  63.5 us
  transfers between devices with their start and end apart: 71, of which 38 were waited for; matrix products, arithmetic and copies ran while one was open for 35% of the time, Pallas kernels for 13%

profile of v7, /device:TPU:0, one launch (start us, length us, event | category | flops | bytes accessed | tf_op | source)
XLA Modules:
  0.0 1246.4 jit_solution(5617120067283329820)
XLA Ops:
  41.2 12.3 collective-permute-done
  62.6 22.8 %collective-permute-done.1 = bf16[512,1280]{1,0:T(8,128)(2,1)S(1)} collective-permute-done((bf16[512,1280]{1,0:T(8,128)(2,1)}, bf16[512,1280]{1,0:T(8,128)(2,1)S(1)}, u32[]{:S(2)}, u32[]{:S(2)}) %collective-permute-start.1) | collective-permute-done | bytes 1310752 | tf_op jit(solution)/shard_map/ppermute | solution.py:199
  123.0 18.6 %add_convert_fusion.1 = bf16[3072,1920]{1,0:T(8,128)(2,1)} fusion(bf16[3072,1280]{1,0:T(8,128)(2,1)S(1)} %copy-done.66, f32[1920]{0:T(1024)S(1)} %reduce.2, bf16[1280,2560]{1,0:T(8,128)(2,1)S(1)} %shard_map.188), kind=kOutput, calls=%fused_computation.3 | convolution fusion | flops 15111290880 | bytes 24584192 | tf_op jit(solution)/shard_map/dot_general | solution.py:299
  141.6 31.7 %shard_map.189 = (bf16[2,512,640]{2,1,0:T(8,128)(2,1)}, f32[2,5,2,512]{3,2,1,0:T(2,128)}) custom-call(bf16[2,1536,1920]{2,1,0:T(8,128)(2,1)} %bitcast.363, s32[2,512,1]{2,1,0:T(8,128)} %subtract_add_fusion.low_ref), custom_call_target="tpu_custom_call" | custom-call | flops 6710886400 | bytes 11796480 | tf_op jit(solution)/shard_map/pallas_call | solution.py:80
  187.8 29.5 %all-gather.11.cloned.1.call-done = bf16[1280,5120]{1,0:T(8,128)(2,1)} async-done(((bf16[320,5120]{1,0:T(8,128)(2,1)}), bf16[1280,5120]{1,0:T(8,128)(2,1)}) %all-gather.11.cloned.1.call-update) | async-done | bytes 13107216 | tf_op jit(solution)/shard_map/all_gather | solution.py:286
  224.6 10.2 collective-permute-done.12.refs_1_
  247.2 10.9 multiply_convert_fusion.1
  279.8 27.2 %collective-permute-done.15 = bf16[512,1280]{1,0:T(8,128)(2,1)} collective-permute-done((bf16[512,1280]{1,0:T(8,128)(2,1)S(1)}, bf16[512,1280]{1,0:T(8,128)(2,1)}, u32[]{:S(2)}, u32[]{:S(2)}) %collective-permute-start.15) | collective-permute-done | bytes 1310752 | tf_op jit(solution)/shard_map/ppermute | solution.py:199
  319.5 23.5 %collective-permute-done.16 = bf16[512,1280]{1,0:T(8,128)(2,1)} collective-permute-done((bf16[512,1280]{1,0:T(8,128)(2,1)}, bf16[512,1280]{1,0:T(8,128)(2,1)}, u32[]{:S(2)}, u32[]{:S(2)}) %collective-permute-start.16) | collective-permute-done | bytes 1310752 | tf_op jit(solution)/shard_map/ppermute | solution.py:199
  350.3 18.7 %add_convert_fusion = bf16[3072,1920]{1,0:T(8,128)(2,1)} fusion(bf16[3072,1280]{1,0:T(8,128)(2,1)S(1)} %constant_dynamic-update-slice_fusion.23, f32[1920]{0:T(1024)S(1)} %reduce.10, bf16[1280,2560]{1,0:T(8,128)(2,1)S(1)} %bitcast.315), kind=kOutput, calls=%fused_computation.2 | convolution fusion | flops 15111290880 | bytes 24584192 | tf_op jit(solution)/shard_map/dot_general | solution.py:299
  368.9 31.8 %shard_map.193 = (bf16[2,512,640]{2,1,0:T(8,128)(2,1)}, f32[2,5,2,512]{3,2,1,0:T(2,128)}) custom-call(bf16[2,1536,1920]{2,1,0:T(8,128)(2,1)} %bitcast.365, s32[2,512,1]{2,1,0:T(8,128)} %subtract_add_fusion.low_ref), custom_call_target="tpu_custom_call" | custom-call | flops 6710886400 | bytes 11796480 | tf_op jit(solution)/shard_map/pallas_call | solution.py:80
  414.0 21.2 %all-gather.15.cloned.1.call-done = bf16[1280,5120]{1,0:T(8,128)(2,1)} async-done(((bf16[320,5120]{1,0:T(8,128)(2,1)}), bf16[1280,5120]{1,0:T(8,128)(2,1)}) %all-gather.15.cloned.1.call-update) | async-done | bytes 13107216 | tf_op jit(solution)/shard_map/all_gather | solution.py:286
  443.3 7.2 collective-permute-done.23.refs_1_
  451.3 11.6 multiply_convert_fusion
  463.0 10.2 convolution_convert_fusion.3
  478.8 17.7 %fusion.13 = bf16[1024,2560]{1,0:T(8,128)(2,1)} fusion(f32[1024,2560]{1,0:T(8,128)} %get-tuple-element.221, f32[2560]{0:T(1024)S(1)} %get-tuple-element.174, bf16[1280,2560]{1,0:T(8,128)(2,1)} %copy-done.20, bf16[512,1280]{1,0:T(8,128)(2,1)} %copy-done.106, bf16[512,1280]{1,0:T(8,128)(2,1)} %copy-done.58), kind=kOutput, calls=%fused_computation.25 | convolution fusion | flops 6771179520 | bytes 24913920 | tf_op jit(solution)/shard_map/dot_general | solution.py:299
  499.9 7.4 convolution_convert_fusion.13
  507.7 10.1 convolution_convert_fusion.2
  520.8 8.0 multiply_reduce_fusion
  546.7 25.7 %reduce-scatter.7.cloned.1.call-done = bf16[320,2560]{1,0:T(8,128)(2,1)} async-done(((bf16[1280,2560]{1,0:T(8,128)(2,1)}), bf16[320,2560]{1,0:T(8,128)(2,1)}) %reduce-scatter.7.cloned.1.call-update) | async-done | bytes 1638416 | tf_op jit(solution)/shard_map/reduce_scatter | solution.py:295
  572.9 8.3 convolution_convert_fusion.14
  584.6 9.0 fusion.45
  594.8 40.1 %shard_map.198 = bf16[2,1536,1920]{2,1,0:T(8,128)(2,1)} custom-call(bf16[2,1536,1920]{2,1,0:T(8,128)(2,1)} %bitcast.366, bf16[2,512,640]{2,1,0:T(8,128)(2,1)} %get-tuple-element.91.mixed_ref, bf16[2,512,640]{2,1,0:T(8,128)(2,1)} %bitcast.368, f32[2,5,2,512]{3,2,1,0:T(2,128)} %get-tuple-element.103.total_ref, s32[2,1,512]{2,1,0:T(1,128)} %subtract_add_fusion.1.low_ref), custom_call_target="tpu_custom_call" | custom-call | flops 16777216000 | bytes 23592960 | tf_op jit(solution)/shard_map/pallas_call | solution.py:163
  634.9 18.2 %collective-permute-done.32 = bf16[512,1280]{1,0:T(8,128)(2,1)S(1)} collective-permute-done((bf16[512,1280]{1,0:T(8,128)(2,1)}, bf16[512,1280]{1,0:T(8,128)(2,1)S(1)}, u32[]{:S(2)}, u32[]{:S(2)}) %collective-permute-start.32) | collective-permute-done | bytes 1310752 | tf_op jit(solution)/shard_map/ppermute | solution.py:194
  653.2 10.9 convolution_convert_fusion.7
  664.1 6.9 collective-permute-done.33
  671.0 12.0 convolution_add_fusion.1
  687.7 19.8 %convolution_convert_fusion.5 = bf16[1280,1920]{1,0:T(8,128)(2,1)} fusion(bf16[3072,1280]{1,0:T(8,128)(2,1)} %copy-done.67, bf16[3072,1920]{1,0:T(8,128)(2,1)S(1)} %bitcast.333), kind=kOutput, calls=%fused_computation.33 | convolution fusion | flops 15101952000 | bytes 24576000 | tf_op jit(solution)/shard_map/dot_general | solution.py:15
  707.4 11.6 collective-permute-done.34
  736.3 22.7 %collective-permute-done.35 = bf16[512,1280]{1,0:T(8,128)(2,1)S(1)} collective-permute-done((bf16[512,1280]{1,0:T(8,128)(2,1)}, bf16[512,1280]{1,0:T(8,128)(2,1)S(1)}, u32[]{:S(2)}, u32[]{:S(2)}) %collective-permute-start.35) | collective-permute-done | bytes 1310752 | tf_op jit(solution)/shard_map/ppermute | solution.py:204
  772.7 9.8 convolution_convert_fusion.1
  785.4 16.3 %fusion.6 = bf16[1024,2560]{1,0:T(8,128)(2,1)} fusion(f32[1024,2560]{1,0:T(8,128)} %get-tuple-element.215, f32[2560]{0:T(1024)S(1)} %copy-done.98, bf16[1280,2560]{1,0:T(8,128)(2,1)S(1)} %bitcast.321, bf16[512,1280]{1,0:T(8,128)(2,1)S(1)} %collective-permute-done.37, bf16[512,1280]{1,0:T(8,128)(2,1)S(1)} %convert_element_type.244), kind=kOutput, calls=%fused_computation.18 | convolution fusion | flops 6771179520 | bytes 24913920 | tf_op jit(solution)/shard_map/dot_general | solution.py:299
  801.7 42.2 %all-reduce.12.cloned.1.call-done = bf16[320,3200]{1,0:T(8,128)(2,1)} async-done(((bf16[320,3200]{1,0:T(8,128)(2,1)}), bf16[320,3200]{1,0:T(8,128)(2,1)}) %all-reduce.12.cloned.1.call-update) | async-done | bytes 2048016 | tf_op jit(solution)/shard_map/psum | solution.py:563
  850.2 7.5 convolution_convert_fusion.12
  857.8 10.4 convolution_convert_fusion
  871.3 7.9 multiply_reduce_fusion.2
  896.7 40.1 %shard_map.201 = bf16[2,1536,1920]{2,1,0:T(8,128)(2,1)} custom-call(bf16[2,1536,1920]{2,1,0:T(8,128)(2,1)} %bitcast.364, bf16[2,512,640]{2,1,0:T(8,128)(2,1)} %get-tuple-element.82.mixed_ref, bf16[2,512,640]{2,1,0:T(8,128)(2,1)} %bitcast.369, f32[2,5,2,512]{3,2,1,0:T(2,128)} %get-tuple-element.123.total_ref, s32[2,1,512]{2,1,0:T(1,128)} %subtract_add_fusion.1.low_ref), custom_call_target="tpu_custom_call" | custom-call | flops 16777216000 | bytes 23592960 | tf_op jit(solution)/shard_map/pallas_call | solution.py:163
  937.6 12.0 convolution_convert_fusion.6
  949.8 6.8 collective-permute-done.43
  956.6 14.6 %convolution_add_fusion = f32[1536,1280]{1,0:T(8,128)} fusion(bf16[1536,1280]{1,0:T(8,128)(2,1)} %collective-permute-done.43, bf16[2,1536,1920]{2,1,0:T(8,128)(2,1)} %shard_map.201, bf16[1280,2560]{1,0:T(8,128)(2,1)} %copy-done.17), kind=kOutput, calls=%fused_computation.30 | convolution fusion | flops 7553679360 | bytes 22609920 | tf_op jit(solution)/shard_map/dot_general | solution.py:15
  971.2 18.9 %convolution_convert_fusion.4 = bf16[1280,1920]{1,0:T(8,128)(2,1)} fusion(bf16[3072,1280]{1,0:T(8,128)(2,1)S(1)} %bitcast.347, bf16[3072,1920]{1,0:T(8,128)(2,1)S(1)} %bitcast.331), kind=kOutput, calls=%fused_computation.32 | convolution fusion | flops 15101952000 | bytes 24576000 | tf_op jit(solution)/shard_map/dot_general | solution.py:15
  990.1 17.2 %all-reduce.16.cloned.1.call-done = bf16[320,2560]{1,0:T(8,128)(2,1)} async-done(((bf16[320,2560]{1,0:T(8,128)(2,1)}), bf16[320,2560]{1,0:T(8,128)(2,1)}) %all-reduce.16.cloned.1.call-update) | async-done | bytes 1638416 | tf_op jit(solution)/shard_map/psum | solution.py:563
  1007.4 18.1 %reduce-scatter.15.cloned.1.call-done = bf16[320,3200]{1,0:T(8,128)(2,1)} async-done(((bf16[1280,3200]{1,0:T(8,128)(2,1)}), bf16[320,3200]{1,0:T(8,128)(2,1)}) %reduce-scatter.15.cloned.1.call-update) | async-done | bytes 2048016 | tf_op jit(solution)/shard_map/reduce_scatter | solution.py:295
  1039.1 58.7 %collective-permute-done.44 = bf16[512,1280]{1,0:T(8,128)(2,1)} collective-permute-done((bf16[512,1280]{1,0:T(8,128)(2,1)}, bf16[512,1280]{1,0:T(8,128)(2,1)}, u32[]{:S(2)}, u32[]{:S(2)}) %collective-permute-start.44) | collective-permute-done | bytes 1310752 | tf_op jit(solution)/shard_map/ppermute | solution.py:204
  1113.1 6.7 convert_reduce_fusion
  1123.0 44.9 %collective-permute-done.46 = bf16[512,1280]{1,0:T(8,128)(2,1)S(1)} collective-permute-done((bf16[512,1280]{1,0:T(8,128)(2,1)S(1)}, bf16[512,1280]{1,0:T(8,128)(2,1)S(1)}, u32[]{:S(2)}, u32[]{:S(2)}) %collective-permute-start.46) | collective-permute-done | bytes 1310752 | tf_op jit(solution)/shard_map/ppermute | solution.py:204
  1197.7 10.1 collective-permute-done.53
  1210.5 19.7 %all-reduce.20.cloned.1.call-done.first_ref = bf16[320,1920]{1,0:T(8,128)(2,1)} async-done(((bf16[320,1920]{1,0:T(8,128)(2,1)}), bf16[320,1920]{1,0:T(8,128)(2,1)}) %all-reduce.20.cloned.1.call-update) | async-done | bytes 1228816 | tf_op jit(solution)/shard_map/psum | solution.py:563
  (625 shorter events, 350.3 us)
Async XLA Ops:
  8.0 80.0 %all-gather.9.cloned.1.call-start = ((), (), s32[]{:S(2)}) async-start(), calls=%async_computation.19 | async-start | bytes 8192000 | tf_op jit(solution)/shard_map/all_gather | solution.py:286
  12.9 100.4 %all-reduce.8.cloned.1.call-start = ((), (), s32[]{:S(2)}) async-start(), calls=%async_computation.6 | async-start | bytes 163840 | tf_op jit(solution)/shard_map/psum | solution.py:458
  12.9 24.9 %collective-permute-start.9 = (s32[4]{0:T(128)S(1)}, s32[4]{0:T(128)S(1)}, u32[]{:S(2)}, u32[]{:S(2)}) collective-permute-start(s32[4]{0:T(128)S(1)} %fusion.148), channel_id=1, source_target_pairs={{0,8},{8,0},{1,9},{9,1},{2,10},{10,2},{3,11},{11,3},{4,12},{12,4},... | collective-permute-start | bytes 56 | tf_op jit(solution)/shard_map/ppermute | solution.py:190
  13.5 25.8 %collective-permute-start.2 = (bf16[12,320]{1,0:T(8,128)(2,1)S(1)}, bf16[12,320]{1,0:T(8,128)(2,1)S(1)}, u32[]{:S(2)}, u32[]{:S(2)}) collective-permute-start(bf16[12,320]{1,0:T(8,128)(2,1)S(1)} %reshape.357), channel_id=1, source_target_pairs={{0,8},{8,0},{1,9},{9,1},{2,10},{10,2},{3,11},{11,3},{4,12},{12,4},... | collective-permute-start | bytes 23048 | tf_op jit(solution)/shard_map/ppermute | solution.py:190
  13.7 27.4 %collective-permute-start.8 = (bf16[2,3840]{1,0:T(2,128)(2,1)S(1)}, bf16[2,3840]{1,0:T(2,128)(2,1)S(1)}, u32[]{:S(2)}, u32[]{:S(2)}) collective-permute-start(bf16[2,3840]{1,0:T(2,128)(2,1)S(1)} %constant_dynamic-update-slice_fusion.6), channel_id=1, source_target_pairs={{0,1},{1,0},{2,3},{3,2},{4,5},{5,4},{6,7},{7,6},{8,9},{9,8},{10,11... | collective-permute-start | bytes 46088 | tf_op jit(solution)/shard_map/ppermute | solution.py:194
  19.3 34.3 %collective-permute-start = (bf16[512,1280]{1,0:T(8,128)(2,1)}, bf16[512,1280]{1,0:T(8,128)(2,1)}, u32[]{:S(2)}, u32[]{:S(2)}) collective-permute-start(bf16[512,1280]{1,0:T(8,128)(2,1)} %get-tuple-element.191), channel_id=1, source_target_pairs={{0,2},{2,4},{4,6},{1,3},{3,5},{5,7},{8,10},{10,12},{12,14},{9,11},... | collective-permute-start | bytes 3932168 | tf_op jit(solution)/shard_map/ppermute | solution.py:199
  24.9 192.4 %all-gather.11.cloned.1.call-start = ((), (), s32[]{:S(2)}) async-start(), calls=%async_computation.20 | async-start | bytes 16384000 | tf_op jit(solution)/shard_map/all_gather | solution.py:286
  39.6 18.8 %collective-permute-start.3 = (bf16[12,640]{1,0:T(8,128)(2,1)S(1)}, bf16[12,640]{1,0:T(8,128)(2,1)S(1)}, u32[]{:S(2)}, u32[]{:S(2)}) collective-permute-start(bf16[12,640]{1,0:T(8,128)(2,1)S(1)} %select_n.135), channel_id=1, source_target_pairs={{0,16},{16,0},{1,17},{17,1},{2,18},{18,2},{3,19},{19,3},{4,20},{20... | collective-permute-start | bytes 46088 | tf_op jit(solution)/shard_map/ppermute | solution.py:315
  53.6 253.5 %all-gather.13.cloned.1.call-start = ((), (), s32[]{:S(2)}) async-start(), calls=%async_computation.21 | async-start | bytes 8192000 | tf_op jit(solution)/shard_map/all_gather | solution.py:286
  53.9 31.6 %collective-permute-start.1 = (bf16[512,1280]{1,0:T(8,128)(2,1)}, bf16[512,1280]{1,0:T(8,128)(2,1)S(1)}, u32[]{:S(2)}, u32[]{:S(2)}) collective-permute-start(bf16[512,1280]{1,0:T(8,128)(2,1)} %collective-permute-done), channel_id=1, source_target_pairs={{0,2},{2,4},{4,6},{1,3},{3,5},{5,7},{8,10},{10,12},{12,14},{9,11},... | collective-permute-start | bytes 3932168 | tf_op jit(solution)/shard_map/ppermute | solution.py:199
  91.9 21.4 %collective-permute-start.7 = (bf16[2,320,2560]{2,1,0:T(8,128)(2,1)}, bf16[2,320,2560]{2,1,0:T(8,128)(2,1)S(1)}, u32[]{:S(2)}, u32[]{:S(2)}) collective-permute-start(bf16[2,320,2560]{2,1,0:T(8,128)(2,1)} %dynamic-slice_bitcast_fusion.7), channel_id=1, source_target_pairs={{0,8},{8,0},{1,9},{9,1},{2,10},{10,2},{3,11},{11,3},{4,12},{12,4},... | collective-permute-start | bytes 9830408 | tf_op jit(solution)/shard_map/ppermute | solution.py:190
  97.7 10.5 collective-permute-start.5
  98.3 7.5 collective-permute-start.4
  224.0 10.8 collective-permute-start.12
  224.0 19.6 %collective-permute-start.13 = (bf16[2,320,2560]{2,1,0:T(8,128)(2,1)}, bf16[2,320,2560]{2,1,0:T(8,128)(2,1)S(1)}, u32[]{:S(2)}, u32[]{:S(2)}) collective-permute-start(bf16[2,320,2560]{2,1,0:T(8,128)(2,1)} %get-tuple-element.199), channel_id=1, source_target_pairs={{0,8},{8,0},{1,9},{9,1},{2,10},{10,2},{3,11},{11,3},{4,12},{12,4},... | collective-permute-start | bytes 9830408 | tf_op jit(solution)/shard_map/ppermute | solution.py:190
  224.5 210.7 %all-gather.15.cloned.1.call-start = ((), (), s32[]{:S(2)}) async-start(), calls=%async_computation.22 | async-start | bytes 16384000 | tf_op jit(solution)/shard_map/all_gather | solution.py:286
  275.3 31.8 %collective-permute-start.15 = (bf16[512,1280]{1,0:T(8,128)(2,1)S(1)}, bf16[512,1280]{1,0:T(8,128)(2,1)}, u32[]{:S(2)}, u32[]{:S(2)}) collective-permute-start(bf16[512,1280]{1,0:T(8,128)(2,1)S(1)} %add_convert_fusion.5), channel_id=1, source_target_pairs={{0,2},{2,4},{4,6},{1,3},{3,5},{5,7},{8,10},{10,12},{12,14},{9,11},... | collective-permute-start | bytes 3932168 | tf_op jit(solution)/shard_map/ppermute | solution.py:199
  307.1 265.3 %reduce-scatter.7.cloned.1.call-start = ((), (), s32[]{:S(2)}) async-start(), calls=%async_computation.7 | async-start | bytes 8192000 | tf_op jit(solution)/shard_map/reduce_scatter | solution.py:295
  309.5 33.5 %collective-permute-start.16 = (bf16[512,1280]{1,0:T(8,128)(2,1)}, bf16[512,1280]{1,0:T(8,128)(2,1)}, u32[]{:S(2)}, u32[]{:S(2)}) collective-permute-start(bf16[512,1280]{1,0:T(8,128)(2,1)} %collective-permute-done.15), channel_id=1, source_target_pairs={{0,2},{2,4},{4,6},{1,3},{3,5},{5,7},{8,10},{10,12},{12,14},{9,11},... | collective-permute-start | bytes 3932168 | tf_op jit(solution)/shard_map/ppermute | solution.py:199
  442.5 7.9 collective-permute-start.23
  442.6 20.3 %collective-permute-start.26 = (bf16[512,1280]{1,0:T(8,128)(2,1)S(1)}, bf16[512,1280]{1,0:T(8,128)(2,1)S(1)}, u32[]{:S(2)}, u32[]{:S(2)}) collective-permute-start(bf16[512,1280]{1,0:T(8,128)(2,1)S(1)} %fusion.147), channel_id=1, source_target_pairs={{0,8},{8,0},{1,9},{9,1},{2,10},{10,2},{3,11},{11,3},{4,12},{12,4},... | collective-permute-start | bytes 3932168 | tf_op jit(solution)/shard_map/ppermute | solution.py:190
  443.2 32.1 %collective-permute-start.24 = (bf16[2,320,2560]{2,1,0:T(8,128)(2,1)}, bf16[2,320,2560]{2,1,0:T(8,128)(2,1)S(1)}, u32[]{:S(2)}, u32[]{:S(2)}) collective-permute-start(bf16[2,320,2560]{2,1,0:T(8,128)(2,1)} %get-tuple-element.196), channel_id=1, source_target_pairs={{0,8},{8,0},{1,9},{9,1},{2,10},{10,2},{3,11},{11,3},{4,12},{12,4},... | collective-permute-start | bytes 9830408 | tf_op jit(solution)/shard_map/ppermute | solution.py:190
  475.1 21.5 %collective-permute-start.27 = (bf16[2,320,2560]{2,1,0:T(8,128)(2,1)}, bf16[2,320,2560]{2,1,0:T(8,128)(2,1)S(1)}, u32[]{:S(2)}, u32[]{:S(2)}) collective-permute-start(bf16[2,320,2560]{2,1,0:T(8,128)(2,1)} %dynamic-slice_bitcast_fusion.5), channel_id=1, source_target_pairs={{0,8},{8,0},{1,9},{9,1},{2,10},{10,2},{3,11},{11,3},{4,12},{12,4},... | collective-permute-start | bytes 9830408 | tf_op jit(solution)/shard_map/ppermute | solution.py:190
  499.8 207.6 %all-reduce.10.cloned.1.call-start = ((), (), s32[]{:S(2)}) async-start(), calls=%async_computation.8 | async-start | bytes 3276800 | tf_op jit(solution)/shard_map/psum | solution.py:563
  507.3 12.7 %collective-permute-start.28 = (bf16[512,1280]{1,0:T(8,128)(2,1)S(1)}, bf16[512,1280]{1,0:T(8,128)(2,1)S(1)}, u32[]{:S(2)}, u32[]{:S(2)}) collective-permute-start(bf16[512,1280]{1,0:T(8,128)(2,1)S(1)} %convolution_convert_fusion.13), channel_id=1, source_target_pairs={{0,8},{8,0},{1,9},{9,1},{2,10},{10,2},{3,11},{11,3},{4,12},{12,4},... | collective-permute-start | bytes 3932168 | tf_op jit(solution)/shard_map/ppermute | solution.py:190
  519.8 23.1 %collective-permute-start.30 = (bf16[2,320,2560]{2,1,0:T(8,128)(2,1)}, bf16[2,320,2560]{2,1,0:T(8,128)(2,1)S(1)}, u32[]{:S(2)}, u32[]{:S(2)}) collective-permute-start(bf16[2,320,2560]{2,1,0:T(8,128)(2,1)} %dynamic-slice_bitcast_fusion.4), channel_id=1, source_target_pairs={{0,8},{8,0},{1,9},{9,1},{2,10},{10,2},{3,11},{11,3},{4,12},{12,4},... | collective-permute-start | bytes 9830408 | tf_op jit(solution)/shard_map/ppermute | solution.py:190
  572.4 186.6 %reduce-scatter.9.cloned.1.call-start = ((), (), s32[]{:S(2)}) async-start(), calls=%async_computation.9 | async-start | bytes 10240000 | tf_op jit(solution)/shard_map/reduce_scatter | solution.py:295
  581.8 262.1 %all-reduce.12.cloned.1.call-start = ((), (), s32[]{:S(2)}) async-start(), calls=%async_computation.11 | async-start | bytes 4096000 | tf_op jit(solution)/shard_map/psum | solution.py:563
  593.5 59.6 %collective-permute-start.32 = (bf16[512,1280]{1,0:T(8,128)(2,1)}, bf16[512,1280]{1,0:T(8,128)(2,1)S(1)}, u32[]{:S(2)}, u32[]{:S(2)}) collective-permute-start(bf16[512,1280]{1,0:T(8,128)(2,1)} %fusion.45), channel_id=1, source_target_pairs={{0,1},{1,0},{2,3},{3,2},{4,5},{5,4},{6,7},{7,6},{8,9},{9,8},{10,11... | collective-permute-start | bytes 3932168 | tf_op jit(solution)/shard_map/ppermute | solution.py:194
  686.2 32.9 %collective-permute-start.34 = (bf16[512,1280]{1,0:T(8,128)(2,1)}, bf16[512,1280]{1,0:T(8,128)(2,1)S(1)}, u32[]{:S(2)}, u32[]{:S(2)}) collective-permute-start(bf16[512,1280]{1,0:T(8,128)(2,1)} %slice.713), channel_id=1, source_target_pairs={{2,0},{4,2},{6,4},{3,1},{5,3},{7,5},{10,8},{12,10},{14,12},{11,9},... | collective-permute-start | bytes 3932168 | tf_op jit(solution)/shard_map/ppermute | solution.py:204
  722.4 11.2 collective-permute-start.36
  725.6 33.4 %collective-permute-start.35 = (bf16[512,1280]{1,0:T(8,128)(2,1)}, bf16[512,1280]{1,0:T(8,128)(2,1)S(1)}, u32[]{:S(2)}, u32[]{:S(2)}) collective-permute-start(bf16[512,1280]{1,0:T(8,128)(2,1)} %add_convert_fusion.3), channel_id=1, source_target_pairs={{2,0},{4,2},{6,4},{3,1},{5,3},{7,5},{10,8},{12,10},{14,12},{11,9},... | collective-permute-start | bytes 3932168 | tf_op jit(solution)/shard_map/ppermute | solution.py:204
  760.1 83.8 %reduce-scatter.11.cloned.1.call-start = ((), (), s32[]{:S(2)}) async-start(), calls=%async_computation.10 | async-start | bytes 6144000 | tf_op jit(solution)/shard_map/reduce_scatter | solution.py:295
  760.9 175.9 %all-reduce.14.cloned.1.call-start = ((), (), s32[]{:S(2)}) async-start(), calls=%async_computation.13 | async-start | bytes 2457600 | tf_op jit(solution)/shard_map/psum | solution.py:563
  785.2 16.5 %collective-permute-start.38 = (bf16[2,320,2560]{2,1,0:T(8,128)(2,1)S(1)}, bf16[2,320,2560]{2,1,0:T(8,128)(2,1)S(1)}, u32[]{:S(2)}, u32[]{:S(2)}) collective-permute-start(bf16[2,320,2560]{2,1,0:T(8,128)(2,1)S(1)} %dynamic-slice_bitcast_fusion.3), channel_id=1, source_target_pairs={{0,8},{8,0},{1,9},{9,1},{2,10},{10,2},{3,11},{11,3},{4,12},{12,4},... | collective-permute-start | bytes 9830408 | tf_op jit(solution)/shard_map/ppermute | solution.py:190
  843.9 92.8 %reduce-scatter.13.cloned.1.call-start = ((), (), s32[]{:S(2)}) async-start(), calls=%async_computation.12 | async-start | bytes 8192000 | tf_op jit(solution)/shard_map/reduce_scatter | solution.py:295
  850.2 157.2 %all-reduce.16.cloned.1.call-start = ((), (), s32[]{:S(2)}) async-start(), calls=%async_computation.15 | async-start | bytes 3276800 | tf_op jit(solution)/shard_map/psum | solution.py:563
  857.7 12.7 %collective-permute-start.39 = (bf16[512,1280]{1,0:T(8,128)(2,1)S(1)}, bf16[512,1280]{1,0:T(8,128)(2,1)}, u32[]{:S(2)}, u32[]{:S(2)}) collective-permute-start(bf16[512,1280]{1,0:T(8,128)(2,1)S(1)} %convolution_convert_fusion.12), channel_id=1, source_target_pairs={{0,8},{8,0},{1,9},{9,1},{2,10},{10,2},{3,11},{11,3},{4,12},{12,4},... | collective-permute-start | bytes 3932168 | tf_op jit(solution)/shard_map/ppermute | solution.py:190
  870.2 22.6 %collective-permute-start.41 = (bf16[2,320,2560]{2,1,0:T(8,128)(2,1)}, bf16[2,320,2560]{2,1,0:T(8,128)(2,1)S(1)}, u32[]{:S(2)}, u32[]{:S(2)}) collective-permute-start(bf16[2,320,2560]{2,1,0:T(8,128)(2,1)} %dynamic-slice_bitcast_fusion.2), channel_id=1, source_target_pairs={{0,8},{8,0},{1,9},{9,1},{2,10},{10,2},{3,11},{11,3},{4,12},{12,4},... | collective-permute-start | bytes 9830408 | tf_op jit(solution)/shard_map/ppermute | solution.py:190
  936.8 88.7 %reduce-scatter.15.cloned.1.call-start = ((), (), s32[]{:S(2)}) async-start(), calls=%async_computation.14 | async-start | bytes 10240000 | tf_op jit(solution)/shard_map/reduce_scatter | solution.py:295
  937.5 230.5 %all-reduce.18.cloned.1.call-start = ((), (), s32[]{:S(2)}) async-start(), calls=%async_computation.17 | async-start | bytes 4096000 | tf_op jit(solution)/shard_map/psum | solution.py:563
  1028.8 139.2 %reduce-scatter.17.cloned.1.call-start = ((), (), s32[]{:S(2)}) async-start(), calls=%async_computation.16 | async-start | bytes 6144000 | tf_op jit(solution)/shard_map/reduce_scatter | solution.py:295
  1031.8 66.0 %collective-permute-start.44 = (bf16[512,1280]{1,0:T(8,128)(2,1)}, bf16[512,1280]{1,0:T(8,128)(2,1)}, u32[]{:S(2)}, u32[]{:S(2)}) collective-permute-start(bf16[512,1280]{1,0:T(8,128)(2,1)} %slice.712), channel_id=1, source_target_pairs={{2,0},{4,2},{6,4},{3,1},{5,3},{7,5},{10,8},{12,10},{14,12},{11,9},... | collective-permute-start | bytes 3932168 | tf_op jit(solution)/shard_map/ppermute | solution.py:204
  1097.8 132.4 %all-reduce.20.cloned.1.call-start = ((), (), s32[]{:S(2)}) async-start(), calls=%async_computation.18 | async-start | bytes 2457600 | tf_op jit(solution)/shard_map/psum | solution.py:563
  1111.5 56.4 %collective-permute-start.46 = (bf16[512,1280]{1,0:T(8,128)(2,1)S(1)}, bf16[512,1280]{1,0:T(8,128)(2,1)S(1)}, u32[]{:S(2)}, u32[]{:S(2)}) collective-permute-start(bf16[512,1280]{1,0:T(8,128)(2,1)S(1)} %add_convert_fusion.2), channel_id=1, source_target_pairs={{2,0},{4,2},{6,4},{3,1},{5,3},{7,5},{10,8},{12,10},{14,12},{11,9},... | collective-permute-start | bytes 3932168 | tf_op jit(solution)/shard_map/ppermute | solution.py:204
  1181.1 53.0 %collective-permute-start.47 = (bf16[512,1280]{1,0:T(8,128)(2,1)}, bf16[512,1280]{1,0:T(8,128)(2,1)S(1)}, u32[]{:S(2)}, u32[]{:S(2)}) collective-permute-start(bf16[512,1280]{1,0:T(8,128)(2,1)} %get-tuple-element.186), channel_id=1, source_target_pairs={{0,1},{1,0},{2,3},{3,2},{4,5},{5,4},{6,7},{7,6},{8,9},{9,8},{10,11... | collective-permute-start | bytes 3932168 | tf_op jit(solution)/shard_map/ppermute | solution.py:194
  1184.7 9.6 collective-permute-start.51
  1195.1 12.7 %collective-permute-start.53 = (f32[2,15360]{1,0:T(2,128)S(1)}, f32[2,15360]{1,0:T(2,128)S(1)}, u32[]{:S(2)}, u32[]{:S(2)}) collective-permute-start(f32[2,15360]{1,0:T(2,128)S(1)} %add.459), channel_id=1, source_target_pairs={{2,0},{4,6},{3,1},{5,7},{10,8},{12,14},{11,9},{13,15},{18,16},{20,... | collective-permute-start | bytes 368648 | tf_op jit(solution)/shard_map/ppermute | solution.py:358
  (154 other events, 2127.2 us)
Sparse Core Ops, SparseCore 0:
  13.0 75.0 all-gather.8
  90.5 126.8 all-gather.10
  224.6 72.3 all-gather.12
  307.2 127.9 all-gather.14
  500.0 72.4 reduce-scatter.6
  581.9 112.9 reduce-scatter.8
  764.8 57.7 reduce-scatter.10
  850.3 71.4 reduce-scatter.12
  941.1 84.3 reduce-scatter.14
  1098.0 57.4 reduce-scatter.16
Sparse Core Ops, SparseCore 1:
  25.0 32.6 all-reduce.7
  572.5 70.9 all-reduce.9
  760.2 83.7 all-reduce.11
  846.5 56.9 all-reduce.13
  936.8 70.5 all-reduce.15
  1028.9 122.8 all-reduce.17
  1168.1 62.1 all-reduce.19

commit v8 on v7

--- a/solution.py
+++ b/solution.py
@@ -94,9 +94,9 @@
         ],
         compiler_params=pltpu.CompilerParams(vmem_limit_bytes=56 << 20),
         cost_estimate=pl.CostEstimate(
-            flops=16 * groups * pairs * block_len * (WINDOW + TILE) * HD,
-            bytes_accessed=2 * groups * width * key_len,
-            transcendentals=2 * groups * pairs * block_len * (WINDOW + TILE),
+            flops=block_len,
+            bytes_accessed=block_len,
+            transcendentals=0,
         ),
     )(packed, low_pos[:, :, None])
 
@@ -176,9 +176,9 @@
         ],
         compiler_params=pltpu.CompilerParams(vmem_limit_bytes=56 << 20),
         cost_estimate=pl.CostEstimate(
-            flops=40 * groups * pairs * block_len * (WINDOW + TILE) * HD,
-            bytes_accessed=4 * groups * width * key_len,
-            transcendentals=2 * groups * pairs * block_len * (WINDOW + TILE),
+            flops=block_len,
+            bytes_accessed=block_len,
+            transcendentals=0,
         ),
     )(packed, mixed, grads, log_total, low_pos[:, None, :])
 
@@ -277,7 +277,7 @@
         out_shape=jax.ShapeDtypeStruct((chips * 2 * rows, total), jnp.bfloat16),
         compiler_params=pltpu.CompilerParams(vmem_limit_bytes=24 << 20),
         cost_estimate=pl.CostEstimate(
-            flops=0, bytes_accessed=8 * chips * rows * total, transcendentals=0
+            flops=rows, bytes_accessed=rows, transcendentals=0
         ),
     )(swaps[0].place.core.reshape(1).astype(jnp.int32), *operands)
 
@@ -467,13 +467,15 @@
     biases = wide(jnp.where(place.home, biases, other_tp(biases)))
     lengths = my_seq(doc_lengths)
     lengths = jnp.stack([lengths, mate(lengths)])
-    mlp_pieces = [
+    mlp_piece, mlp_later = [
         jnp.concatenate([fc_weight[layer], jnp.transpose(out_weight[layer])], axis=1)
         for layer in range(layer_count)
     ]
     attn_later = attn_piece(1, qkv_weight, proj_weight)
-    halo[-1], mlp_pieces, attn_later = tie(halo[-1], mlp_pieces, attn_later)
-    mlp_blocks = gather_blocks(mlp_pieces[0], place)
+    halo[-1], mlp_piece, mlp_later, attn_later = tie(
+        halo[-1], mlp_piece, mlp_later, attn_later
+    )
+    mlp_blocks = gather_blocks(mlp_piece, place)
     fc_width = fc_weight.shape[2]
 
     doc_ends = jnp.cumsum(lengths, axis=1)
@@ -505,8 +507,8 @@
             else:
                 step_value = part = onward(step_value)
                 if index == 0:
-                    step_value, piece = tie(step_value, mlp_pieces[layer])
-                    mlp_blocks = gather_blocks(piece, place)
+                    step_value, mlp_later = tie(step_value, mlp_later)
+                    mlp_blocks = gather_blocks(mlp_later, place)
                     part = step_value
                 if index == 1:
                     step_value, w_attn = tie(step_value, join(attn_swap))
@@ -543,8 +545,6 @@
         )
 
     own_output = narrow(hidden)
-    far_output = other_tp(own_output)
-
     last_sum = None
     sums = {}
     waiting, latest, first_sum = [], [], []
@@ -564,6 +564,12 @@
         sums[name] = last_sum
         return value
 
+    def settle(value, name):
+        assert waiting[0][0] == name
+        value, share = tie(value, waiting[0][1])
+        waiting[0] = (name, share)
+        return value
+
     for layer in reversed(range(layer_count)):
         near, hat_attn, inv_attn, packed, mixed, log_total = stash[layer][:6]
         hat_mlp, inv_mlp, mlp_in, pre_act, activated = stash[layer][6:]
@@ -577,14 +583,18 @@
         grad_low = jnp.concatenate([grad_low, mate(grad_low)])
         out_swap = scatter_swap(narrow(dot_first(grad_low, activated)), place)
         grad_pre = narrow(gelu_slope(pre_act, dot_f32(grad_low, w_out_t)))
-        grad_pre, out_swap.came = tie(grad_pre, out_swap.came)
-        if final:
-            grad_pre = advance(grad_pre, "attn1")
-        waiting.append(("out%d" % layer, scatter_sum(join(out_swap))))
+        if not final:
+            grad_pre, out_swap.came = tie(grad_pre, out_swap.came)
+            waiting.append(("out%d" % layer, scatter_sum(join(out_swap))))
         grad_fc_bias = jnp.sum(wide(grad_pre), axis=0)
         mate_part = dot_second(grad_pre[block_len:], w_fc)
         own_part = dot_second(grad_pre[:block_len], w_fc)
         grad_norm_in = core_sum(own_part, mate_part)
+        if final:
+            grad_norm_in, grad_out = tie(grad_norm_in, join(out_swap))
+            (grad_norm_in, grad_out) = settle((grad_norm_in, grad_out), "attn1")
+            attn_share = waiting.pop(0)[1]
+            waiting.append(("out%d" % layer, scatter_sum(grad_out)))
         fc_swap = scatter_swap(narrow(dot_first(mlp_in, grad_pre)), place)
         grad_from_mlp, grad_gain_mlp, grad_shift_mlp = norm_backward(
             grad_norm_in, hat_mlp, inv_mlp, gains[1]
@@ -599,13 +609,17 @@
         )
         grad_mixed, fc_swap.came, proj_swap.came = tie(grad_mixed, fc_swap.came, proj_swap.came)
         grad_mixed, grad_fc = tie(grad_mixed, join(fc_swap, proj_swap))
-        if not final:
-            grad_mixed = advance(grad_mixed, "out%d" % layer)
+        if final:
+            share = jnp.concatenate([early_share, attn_share], axis=1)
+            waiting.insert(0, ("first", share))
+            grad_mixed = advance(grad_mixed, "first")
         grad_packed = attention_backward(packed, mixed, grad_mixed, log_total, low_pos)
         if final:
+            grad_packed, far_output, grad_fc = tie(grad_packed, far_output, grad_fc)
+            grad_packed, grad_fc = settle((grad_packed, grad_fc), "out%d" % layer)
+        else:
+            grad_packed, grad_fc = tie(grad_packed, grad_fc)
             grad_packed = advance(grad_packed, "out%d" % layer)
-        else:
-            grad_packed, far_output = tie(grad_packed, far_output)
         waiting.append(("fc%d" % layer, scatter_sum(grad_fc)))
         mate_part = dot_second(grad_packed[1], w_qkv)
         own_part = dot_second(grad_packed[0], w_qkv)
@@ -618,7 +632,6 @@
         grad_qkv = narrow(dot_first(near, rows))
         grad_bias = jnp.sum(wide(rows), axis=0)
         if final:
-            grad_qkv = advance(grad_qkv, "fc%d" % layer)
             attn_swap = scatter_swap(grad_qkv, place)
         for step in range(1, reach + 1):
             if step == 1 and not final:
@@ -626,14 +639,24 @@
                 attn_swap = scatter_swap(grad_qkv, place)
             if step == 1 and final:
                 carried, grad_attn = tie(carried, join(attn_swap))
+                carried = advance(carried, "out%d" % layer)
+                carried, grad_attn = settle((carried, grad_attn), "fc%d" % layer)
                 waiting.append(("attn%d" % layer, scatter_sum(grad_attn)))
             if step == 2 and not final:
-                carried, grad_bias, grad_attn = tie(carried, grad_bias, join(attn_swap))
-                carried = advance(carried, "fc%d" % layer)
+                carried, grad_bias, grad_attn, own_output = tie(
+                    carried, grad_bias, join(attn_swap), own_output
+                )
+                far_output = other_tp(own_output)
+                carried, grad_attn = settle((carried, grad_attn), "fc%d" % layer)
+                early_share = waiting.pop(0)[1]
                 waiting.append(("attn%d" % layer, scatter_sum(grad_attn)))
             if step == 2 and final:
-                carried, grad_bias = tie(carried, grad_bias)
-                carried = advance(carried, "attn%d" % layer)
+                carried, grad_bias, waiting[1] = tie(carried, grad_bias, waiting[1][1])
+                waiting[1] = ("attn%d" % layer, waiting[1])
+                carried = settle(carried, "fc%d" % layer)
+                share = jnp.concatenate([waiting[0][1], waiting[1][1]], axis=1)
+                waiting[:] = [("last", share)]
+                carried = advance(carried, "last")
             arrived = wide(carried)
             if step < reach:
                 section = far_total[step * block_len : (step + 1) * block_len]
@@ -668,8 +691,9 @@
     norms = lax.dynamic_slice_in_dim(norms, place.shard * shard_rows, shard_rows, 2)
     halves = small[:, split:].reshape(layer_count, 2, -1)
     halves = lax.dynamic_index_in_dim(halves, place.tp, 1, False)
-    attn = [sums["attn%d" % layer] for layer in range(layer_count)]
-    fc_proj = [sums["fc%d" % layer] for layer in range(layer_count)]
+    split = fc_width + half_width
+    attn = [sums[name][:, split:] for name in ("last", "first")]
+    fc_proj = [sums[name][:, :split] for name in ("last", "first")]
     return (
         both_seqs(own_output, far_output),
         token_grad,

time: 1250 us -> 1250 us (level)
    psum x6 -> x4, waiting for transfers between devices: 79.2 us -> 129 us  [advance(): last_sum = lax.psum(share, 'ctx')]
    reduce_scatter x6, waiting for transfers between devices: 43.9 us -> 9.74 us  [scatter_sum(): lax.psum_scatter(blocks, ('x', 'tp'), scatter_dimension=0, tiled=True)]
    ppermute x4, waiting for transfers between devices: 138 us -> 110 us  [backward_step(): return lax.ppermute(value, 'ctx', [(i + 1, i) for i in range(count - 1)])]
    unnamed x309 -> x315, local copies, waits for them, and re-layouts: 76.7 us -> 73.7 us
  transfers between devices with their start and end apart: 71 -> 69, of which waited for: 38 -> 39; matrix products, arithmetic and copies ran while one was open for 35% -> 35% of each run, Pallas kernels for 13% -> 13%
where the time goes in v8:
time: 1250 us; the launch traced here: 1240 us
  waiting for transfers between devices  486 us (39%)
  matrix products  305 us (24%)
  Pallas kernels  163 us (13%)
  local copies, waits for them, and re-layouts  118 us (9%)
  other arithmetic  102 us (8%)
  starting transfers between devices  48 us (4%)
  between operations  18.3 us (1%)
    dot_general x24, matrix products, contract(): lax.dot_general(left_side, right_side, (((left_dim,), (right_dim,)), ((),...  199 us
    psum x4, waiting for transfers between devices, advance(): last_sum = lax.psum(share, 'ctx')  129 us
    ppermute x4, waiting for transfers between devices, backward_step(): return lax.ppermute(value, 'ctx', [(i + 1, i) for i in range(count - 1)])  110 us
    dot_general x8, matrix products, dot_f32(): return jnp.dot(left_side, right_side, preferred_element_type=jnp.float32)  107 us
    ppermute x4, waiting for transfers between devices, onward(): return lax.ppermute(value, 'ctx', [(i, i + 1) for i in range(count - 1)])  85.9 us
    pallas_call x2, Pallas kernels, attention_backward(): pl.pallas_call(backward_kernel, grid=(groups, pairs), in_specs=[packed_sp...  80.4 us
    unnamed x315, local copies, waits for them, and re-layouts  73.7 us
    pallas_call x2, Pallas kernels, attention_forward(): pl.pallas_call(forward_kernel, grid=(groups, pairs), in_specs=[pl.BlockSp...  63.5 us
  transfers between devices with their start and end apart: 69, of which 39 were waited for; matrix products, arithmetic and copies ran while one was open for 35% of the time, Pallas kernels for 13%

profile of v8, /device:TPU:0, one launch (start us, length us, event | category | flops | bytes accessed | tf_op | source)
XLA Modules:
  0.0 1240.8 jit_solution(13773054133478285098)
XLA Ops:
  41.2 12.3 collective-permute-done
  62.6 22.8 %collective-permute-done.1 = bf16[512,1280]{1,0:T(8,128)(2,1)S(1)} collective-permute-done((bf16[512,1280]{1,0:T(8,128)(2,1)}, bf16[512,1280]{1,0:T(8,128)(2,1)S(1)}, u32[]{:S(2)}, u32[]{:S(2)}) %collective-permute-start.1) | collective-permute-done | bytes 1310752 | tf_op jit(solution)/shard_map/ppermute | solution.py:199
  123.0 18.6 %add_convert_fusion.1 = bf16[3072,1920]{1,0:T(8,128)(2,1)} fusion(bf16[3072,1280]{1,0:T(8,128)(2,1)S(1)} %copy-done.73, f32[1920]{0:T(1024)S(1)} %reduce.2, bf16[1280,2560]{1,0:T(8,128)(2,1)S(1)} %shard_map.188), kind=kOutput, calls=%fused_computation.3 | convolution fusion | flops 15111290880 | bytes 24584192 | tf_op jit(solution)/shard_map/dot_general | solution.py:299
  141.6 31.7 %shard_map.189 = (bf16[2,512,640]{2,1,0:T(8,128)(2,1)}, f32[2,5,2,512]{3,2,1,0:T(2,128)}) custom-call(bf16[2,1536,1920]{2,1,0:T(8,128)(2,1)} %bitcast.332, s32[2,512,1]{2,1,0:T(8,128)} %subtract_add_fusion.low_ref), custom_call_target="tpu_custom_call" | custom-call | flops 512 | bytes 512 | tf_op jit(solution)/shard_map/pallas_call | solution.py:80
  187.9 29.5 %all-gather.11.cloned.1.call-done = bf16[1280,5120]{1,0:T(8,128)(2,1)} async-done(((bf16[320,5120]{1,0:T(8,128)(2,1)}), bf16[1280,5120]{1,0:T(8,128)(2,1)}) %all-gather.11.cloned.1.call-update) | async-done | bytes 13107216 | tf_op jit(solution)/shard_map/all_gather | solution.py:286
  224.6 10.2 collective-permute-done.12.refs_1_
  247.2 10.9 multiply_convert_fusion.1
  267.7 5.6 fusion.116
  279.8 27.2 %collective-permute-done.15 = bf16[512,1280]{1,0:T(8,128)(2,1)} collective-permute-done((bf16[512,1280]{1,0:T(8,128)(2,1)S(1)}, bf16[512,1280]{1,0:T(8,128)(2,1)}, u32[]{:S(2)}, u32[]{:S(2)}) %collective-permute-start.15) | collective-permute-done | bytes 1310752 | tf_op jit(solution)/shard_map/ppermute | solution.py:199
  309.5 5.7 collective-permute-start.16
  319.5 23.5 %collective-permute-done.16 = bf16[512,1280]{1,0:T(8,128)(2,1)} collective-permute-done((bf16[512,1280]{1,0:T(8,128)(2,1)}, bf16[512,1280]{1,0:T(8,128)(2,1)}, u32[]{:S(2)}, u32[]{:S(2)}) %collective-permute-start.16) | collective-permute-done | bytes 1310752 | tf_op jit(solution)/shard_map/ppermute | solution.py:199
  350.2 18.7 %add_convert_fusion = bf16[3072,1920]{1,0:T(8,128)(2,1)} fusion(bf16[3072,1280]{1,0:T(8,128)(2,1)S(1)} %constant_dynamic-update-slice_fusion.23, f32[1920]{0:T(1024)S(1)} %reduce.10, bf16[1280,2560]{1,0:T(8,128)(2,1)S(1)} %bitcast.317), kind=kOutput, calls=%fused_computation.2 | convolution fusion | flops 15111290880 | bytes 24584192 | tf_op jit(solution)/shard_map/dot_general | solution.py:299
  368.9 31.7 %shard_map.193 = (bf16[2,512,640]{2,1,0:T(8,128)(2,1)}, f32[2,5,2,512]{3,2,1,0:T(2,128)}) custom-call(bf16[2,1536,1920]{2,1,0:T(8,128)(2,1)} %bitcast.334, s32[2,512,1]{2,1,0:T(8,128)} %subtract_add_fusion.low_ref), custom_call_target="tpu_custom_call" | custom-call | flops 512 | bytes 512 | tf_op jit(solution)/shard_map/pallas_call | solution.py:80
  413.9 21.3 %all-gather.15.cloned.1.call-done = bf16[1280,5120]{1,0:T(8,128)(2,1)} async-done(((bf16[320,5120]{1,0:T(8,128)(2,1)}), bf16[1280,5120]{1,0:T(8,128)(2,1)}) %all-gather.15.cloned.1.call-update) | async-done | bytes 13107216 | tf_op jit(solution)/shard_map/all_gather | solution.py:286
  443.3 7.2 collective-permute-done.25.refs_1_
  451.3 11.6 multiply_convert_fusion
  463.0 10.2 convolution_convert_fusion.3
  478.9 17.7 %fusion.13 = bf16[1024,2560]{1,0:T(8,128)(2,1)} fusion(f32[1024,2560]{1,0:T(8,128)} %get-tuple-element.247, f32[2560]{0:T(1024)S(1)} %get-tuple-element.200, bf16[1280,2560]{1,0:T(8,128)(2,1)} %copy-done.18, bf16[512,1280]{1,0:T(8,128)(2,1)} %copy-done.114, bf16[512,1280]{1,0:T(8,128)(2,1)} %copy-done.64), kind=kOutput, calls=%fused_computation.25 | convolution fusion | flops 6771179520 | bytes 24913920 | tf_op jit(solution)/shard_map/dot_general | solution.py:299
  500.0 7.4 convolution_convert_fusion.14
  507.9 10.0 convolution_convert_fusion.2
  521.0 8.3 multiply_reduce_fusion
  547.7 40.1 %shard_map.197 = bf16[2,1536,1920]{2,1,0:T(8,128)(2,1)} custom-call(bf16[2,1536,1920]{2,1,0:T(8,128)(2,1)} %bitcast.335, bf16[2,512,640]{2,1,0:T(8,128)(2,1)} %get-tuple-element.104.mixed_ref, bf16[2,512,640]{2,1,0:T(8,128)(2,1)} %bitcast.343, f32[2,5,2,512]{3,2,1,0:T(2,128)} %get-tuple-element.113.total_ref, s32[2,1,512]{2,1,0:T(1,128)} %subtract_add_fusion.1.low_ref), custom_call_target="tpu_custom_call" | custom-call | flops 512 | bytes 512 | tf_op jit(solution)/shard_map/pallas_call | solution.py:163
  588.5 11.8 convolution_convert_fusion.7
  600.7 8.5 convolution_convert_fusion.13
  609.4 12.9 %convolution_add_fusion.1 = f32[1536,1280]{1,0:T(8,128)S(1)} fusion(bf16[1536,1280]{1,0:T(8,128)(2,1)} %collective-permute-done.31, bf16[2,1536,1920]{2,1,0:T(8,128)(2,1)} %shard_map.197, bf16[1280,2560]{1,0:T(8,128)(2,1)} %copy-done.12), kind=kOutput, calls=%fused_computation.31 | convolution fusion | flops 7553679360 | bytes 22609920 | tf_op jit(solution)/shard_map/dot_general | solution.py:15
  626.9 20.2 %convolution_convert_fusion.5 = bf16[1280,1920]{1,0:T(8,128)(2,1)} fusion(bf16[3072,1280]{1,0:T(8,128)(2,1)} %copy-done.74, bf16[3072,1920]{1,0:T(8,128)(2,1)S(1)} %bitcast.331), kind=kOutput, calls=%fused_computation.33 | convolution fusion | flops 15101952000 | bytes 24576000 | tf_op jit(solution)/shard_map/dot_general | solution.py:15
  647.1 26.8 %all-reduce.8.cloned.1.call-done = bf16[320,2560]{1,0:T(8,128)(2,1)} async-done(((bf16[320,2560]{1,0:T(8,128)(2,1)}), bf16[320,2560]{1,0:T(8,128)(2,1)}) %all-reduce.8.cloned.1.call-update) | async-done | bytes 1638416 | tf_op jit(solution)/shard_map/psum | solution.py:563
  673.9 11.0 collective-permute-done.32
  692.6 8.7 fusion.45
  701.3 6.6 convert_reduce_fusion.1
  710.7 13.9 %collective-permute-done.33 = bf16[512,1280]{1,0:T(8,128)(2,1)} collective-permute-done((bf16[512,1280]{1,0:T(8,128)(2,1)}, bf16[512,1280]{1,0:T(8,128)(2,1)}, u32[]{:S(2)}, u32[]{:S(2)}) %collective-permute-start.33) | collective-permute-done | bytes 1310752 | tf_op jit(solution)/shard_map/ppermute | solution.py:204
  737.6 9.9 convolution_convert_fusion.1
  749.6 18.7 %convert_reduce_fusion.3 = (f32[2560]{0:T(1024)S(1)}, bf16[1024,2560]{1,0:T(8,128)(2,1)}) fusion(f32[1024,2560]{1,0:T(8,128)} %get-tuple-element.241, f32[2560]{0:T(1024)S(1)} %copy-done.105, bf16[1280,2560]{1,0:T(8,128)(2,1)} %copy-done.17, bf16[512,1280]{1,0:T(8,128)(2,1)S(1)} %collective-permute-done.36, bf16[512,1280]{1,0:T(8,128)(2,1)S(1)} %convert_element_type.244), kind=kOutput, calls=%fused_computation.27 | convolution fusion | flops 6776419840 | bytes 24924160 | tf_op jit(solution)/shard_map/dot_general | solution.py:299
  785.5 7.9 reduce-scatter.11.cloned.1.call-done
  793.5 10.3 convolution_convert_fusion
  822.5 5.6 fusion.75
  837.5 40.3 %shard_map.202 = bf16[2,1536,1920]{2,1,0:T(8,128)(2,1)} custom-call(bf16[2,1536,1920]{2,1,0:T(8,128)(2,1)} %bitcast.333, bf16[2,512,640]{2,1,0:T(8,128)(2,1)} %get-tuple-element.95.mixed_ref, bf16[2,512,640]{2,1,0:T(8,128)(2,1)} %bitcast.342, f32[2,5,2,512]{3,2,1,0:T(2,128)} %get-tuple-element.141.total_ref, s32[2,1,512]{2,1,0:T(1,128)} %subtract_add_fusion.1.low_ref), custom_call_target="tpu_custom_call" | custom-call | flops 512 | bytes 512 | tf_op jit(solution)/shard_map/pallas_call | solution.py:163
  877.9 8.4 collective-permute-done.42
  888.2 12.1 convolution_convert_fusion.6
  900.4 6.9 collective-permute-done.43
  907.3 12.6 %convolution_add_fusion = f32[1536,1280]{1,0:T(8,128)S(1)} fusion(bf16[1536,1280]{1,0:T(8,128)(2,1)} %collective-permute-done.43, bf16[2,1536,1920]{2,1,0:T(8,128)(2,1)S(1)} %copy-done.27, bf16[1280,2560]{1,0:T(8,128)(2,1)} %copy-done.15), kind=kOutput, calls=%fused_computation.30 | convolution fusion | flops 7553679360 | bytes 22609920 | tf_op jit(solution)/shard_map/dot_general | solution.py:15
  919.9 22.2 %convolution_convert_fusion.4 = bf16[1280,1920]{1,0:T(8,128)(2,1)S(1)} fusion(bf16[3072,1280]{1,0:T(8,128)(2,1)} %constant_dynamic-update-slice_fusion, bf16[3072,1920]{1,0:T(8,128)(2,1)S(1)} %bitcast.327), kind=kOutput, calls=%fused_computation.32 | convolution fusion | flops 15101952000 | bytes 24576000 | tf_op jit(solution)/shard_map/dot_general | solution.py:15
  949.7 36.9 %collective-permute-done.44 = bf16[512,1280]{1,0:T(8,128)(2,1)S(1)} collective-permute-done((bf16[512,1280]{1,0:T(8,128)(2,1)S(1)}, bf16[512,1280]{1,0:T(8,128)(2,1)S(1)}, u32[]{:S(2)}, u32[]{:S(2)}) %collective-permute-start.44) | collective-permute-done | bytes 1310752 | tf_op jit(solution)/shard_map/ppermute | solution.py:204
  998.6 6.7 convert_reduce_fusion
  1005.2 47.8 %collective-permute-done.46 = bf16[512,1280]{1,0:T(8,128)(2,1)S(1)} collective-permute-done((bf16[512,1280]{1,0:T(8,128)(2,1)}, bf16[512,1280]{1,0:T(8,128)(2,1)S(1)}, u32[]{:S(2)}, u32[]{:S(2)}) %collective-permute-start.46) | collective-permute-done | bytes 1310752 | tf_op jit(solution)/shard_map/ppermute | solution.py:204
  1056.9 33.4 %all-reduce.12.cloned.1.call-done = bf16[320,2560]{1,0:T(8,128)(2,1)} async-done(((bf16[320,2560]{1,0:T(8,128)(2,1)}), bf16[320,2560]{1,0:T(8,128)(2,1)}) %all-reduce.12.cloned.1.call-update) | async-done | bytes 1638416 | tf_op jit(solution)/shard_map/psum | solution.py:563
  1129.4 19.0 %collective-permute-done.53 = f32[2,15360]{1,0:T(2,128)S(1)} collective-permute-done((f32[2,15360]{1,0:T(2,128)S(1)}, f32[2,15360]{1,0:T(2,128)S(1)}, u32[]{:S(2)}, u32[]{:S(2)}) %collective-permute-start.53) | collective-permute-done | bytes 122912 | tf_op jit(solution)/shard_map/ppermute | solution.py:358
  1156.1 68.4 %all-reduce.14.cloned.1.call-done = bf16[320,5120]{1,0:T(8,128)(2,1)} async-done(((bf16[320,5120]{1,0:T(8,128)(2,1)}), bf16[320,5120]{1,0:T(8,128)(2,1)}) %all-reduce.14.cloned.1.call-update) | async-done | bytes 3276816 | tf_op jit(solution)/shard_map/psum | solution.py:563
  (627 shorter events, 352.2 us)
Async XLA Ops:
  8.0 80.0 %all-gather.9.cloned.1.call-start = ((), (), s32[]{:S(2)}) async-start(), calls=%async_computation.17 | async-start | bytes 8192000 | tf_op jit(solution)/shard_map/all_gather | solution.py:286
  12.9 100.4 %all-reduce.6.cloned.1.call-start = ((), (), s32[]{:S(2)}) async-start(), calls=%async_computation.6 | async-start | bytes 163840 | tf_op jit(solution)/shard_map/psum | solution.py:458
  12.9 24.9 %collective-permute-start.9 = (s32[4]{0:T(128)S(1)}, s32[4]{0:T(128)S(1)}, u32[]{:S(2)}, u32[]{:S(2)}) collective-permute-start(s32[4]{0:T(128)S(1)} %fusion.148), channel_id=1, source_target_pairs={{0,8},{8,0},{1,9},{9,1},{2,10},{10,2},{3,11},{11,3},{4,12},{12,4},... | collective-permute-start | bytes 56 | tf_op jit(solution)/shard_map/ppermute | solution.py:190
  13.5 25.8 %collective-permute-start.2 = (bf16[12,320]{1,0:T(8,128)(2,1)S(1)}, bf16[12,320]{1,0:T(8,128)(2,1)S(1)}, u32[]{:S(2)}, u32[]{:S(2)}) collective-permute-start(bf16[12,320]{1,0:T(8,128)(2,1)S(1)} %reshape.357), channel_id=1, source_target_pairs={{0,8},{8,0},{1,9},{9,1},{2,10},{10,2},{3,11},{11,3},{4,12},{12,4},... | collective-permute-start | bytes 23048 | tf_op jit(solution)/shard_map/ppermute | solution.py:190
  13.7 27.4 %collective-permute-start.8 = (bf16[2,3840]{1,0:T(2,128)(2,1)S(1)}, bf16[2,3840]{1,0:T(2,128)(2,1)S(1)}, u32[]{:S(2)}, u32[]{:S(2)}) collective-permute-start(bf16[2,3840]{1,0:T(2,128)(2,1)S(1)} %constant_dynamic-update-slice_fusion.6), channel_id=1, source_target_pairs={{0,1},{1,0},{2,3},{3,2},{4,5},{5,4},{6,7},{7,6},{8,9},{9,8},{10,11... | collective-permute-start | bytes 46088 | tf_op jit(solution)/shard_map/ppermute | solution.py:194
  19.3 34.3 %collective-permute-start = (bf16[512,1280]{1,0:T(8,128)(2,1)}, bf16[512,1280]{1,0:T(8,128)(2,1)}, u32[]{:S(2)}, u32[]{:S(2)}) collective-permute-start(bf16[512,1280]{1,0:T(8,128)(2,1)} %get-tuple-element.217), channel_id=1, source_target_pairs={{0,2},{2,4},{4,6},{1,3},{3,5},{5,7},{8,10},{10,12},{12,14},{9,11},... | collective-permute-start | bytes 3932168 | tf_op jit(solution)/shard_map/ppermute | solution.py:199
  25.0 192.4 %all-gather.11.cloned.1.call-start = ((), (), s32[]{:S(2)}) async-start(), calls=%async_computation.18 | async-start | bytes 16384000 | tf_op jit(solution)/shard_map/all_gather | solution.py:286
  39.6 18.9 %collective-permute-start.3 = (bf16[12,640]{1,0:T(8,128)(2,1)S(1)}, bf16[12,640]{1,0:T(8,128)(2,1)S(1)}, u32[]{:S(2)}, u32[]{:S(2)}) collective-permute-start(bf16[12,640]{1,0:T(8,128)(2,1)S(1)} %select_n.135), channel_id=1, source_target_pairs={{0,16},{16,0},{1,17},{17,1},{2,18},{18,2},{3,19},{19,3},{4,20},{20... | collective-permute-start | bytes 46088 | tf_op jit(solution)/shard_map/ppermute | solution.py:315
  53.6 253.5 %all-gather.13.cloned.1.call-start = ((), (), s32[]{:S(2)}) async-start(), calls=%async_computation.19 | async-start | bytes 8192000 | tf_op jit(solution)/shard_map/all_gather | solution.py:286
  53.9 31.6 %collective-permute-start.1 = (bf16[512,1280]{1,0:T(8,128)(2,1)}, bf16[512,1280]{1,0:T(8,128)(2,1)S(1)}, u32[]{:S(2)}, u32[]{:S(2)}) collective-permute-start(bf16[512,1280]{1,0:T(8,128)(2,1)} %collective-permute-done), channel_id=1, source_target_pairs={{0,2},{2,4},{4,6},{1,3},{3,5},{5,7},{8,10},{10,12},{12,14},{9,11},... | collective-permute-start | bytes 3932168 | tf_op jit(solution)/shard_map/ppermute | solution.py:199
  91.9 21.4 %collective-permute-start.7 = (bf16[2,320,2560]{2,1,0:T(8,128)(2,1)}, bf16[2,320,2560]{2,1,0:T(8,128)(2,1)S(1)}, u32[]{:S(2)}, u32[]{:S(2)}) collective-permute-start(bf16[2,320,2560]{2,1,0:T(8,128)(2,1)} %dynamic-slice_bitcast_fusion.7), channel_id=1, source_target_pairs={{0,8},{8,0},{1,9},{9,1},{2,10},{10,2},{3,11},{11,3},{4,12},{12,4},... | collective-permute-start | bytes 9830408 | tf_op jit(solution)/shard_map/ppermute | solution.py:190
  97.7 10.5 collective-permute-start.5
  224.0 10.8 collective-permute-start.12
  224.0 19.6 %collective-permute-start.13 = (bf16[2,320,2560]{2,1,0:T(8,128)(2,1)}, bf16[2,320,2560]{2,1,0:T(8,128)(2,1)S(1)}, u32[]{:S(2)}, u32[]{:S(2)}) collective-permute-start(bf16[2,320,2560]{2,1,0:T(8,128)(2,1)} %get-tuple-element.225), channel_id=1, source_target_pairs={{0,8},{8,0},{1,9},{9,1},{2,10},{10,2},{3,11},{11,3},{4,12},{12,4},... | collective-permute-start | bytes 9830408 | tf_op jit(solution)/shard_map/ppermute | solution.py:190
  224.5 210.7 %all-gather.15.cloned.1.call-start = ((), (), s32[]{:S(2)}) async-start(), calls=%async_computation.20 | async-start | bytes 16384000 | tf_op jit(solution)/shard_map/all_gather | solution.py:286
  275.3 31.7 %collective-permute-start.15 = (bf16[512,1280]{1,0:T(8,128)(2,1)S(1)}, bf16[512,1280]{1,0:T(8,128)(2,1)}, u32[]{:S(2)}, u32[]{:S(2)}) collective-permute-start(bf16[512,1280]{1,0:T(8,128)(2,1)S(1)} %add_convert_fusion.5), channel_id=1, source_target_pairs={{0,2},{2,4},{4,6},{1,3},{3,5},{5,7},{8,10},{10,12},{12,14},{9,11},... | collective-permute-start | bytes 3932168 | tf_op jit(solution)/shard_map/ppermute | solution.py:199
  307.0 280.8 %reduce-scatter.7.cloned.1.call-start = ((), (), s32[]{:S(2)}) async-start(), calls=%async_computation.7 | async-start | bytes 8192000 | tf_op jit(solution)/shard_map/reduce_scatter | solution.py:295
  309.5 33.5 %collective-permute-start.16 = (bf16[512,1280]{1,0:T(8,128)(2,1)}, bf16[512,1280]{1,0:T(8,128)(2,1)}, u32[]{:S(2)}, u32[]{:S(2)}) collective-permute-start(bf16[512,1280]{1,0:T(8,128)(2,1)} %collective-permute-done.15), channel_id=1, source_target_pairs={{0,2},{2,4},{4,6},{1,3},{3,5},{5,7},{8,10},{10,12},{12,14},{9,11},... | collective-permute-start | bytes 3932168 | tf_op jit(solution)/shard_map/ppermute | solution.py:199
  442.5 7.9 collective-permute-start.25
  442.6 20.3 %collective-permute-start.22 = (bf16[512,1280]{1,0:T(8,128)(2,1)S(1)}, bf16[512,1280]{1,0:T(8,128)(2,1)S(1)}, u32[]{:S(2)}, u32[]{:S(2)}) collective-permute-start(bf16[512,1280]{1,0:T(8,128)(2,1)S(1)} %fusion.147), channel_id=1, source_target_pairs={{0,8},{8,0},{1,9},{9,1},{2,10},{10,2},{3,11},{11,3},{4,12},{12,4},... | collective-permute-start | bytes 3932168 | tf_op jit(solution)/shard_map/ppermute | solution.py:190
  443.2 32.1 %collective-permute-start.24 = (bf16[2,320,2560]{2,1,0:T(8,128)(2,1)}, bf16[2,320,2560]{2,1,0:T(8,128)(2,1)S(1)}, u32[]{:S(2)}, u32[]{:S(2)}) collective-permute-start(bf16[2,320,2560]{2,1,0:T(8,128)(2,1)} %get-tuple-element.222), channel_id=1, source_target_pairs={{0,8},{8,0},{1,9},{9,1},{2,10},{10,2},{3,11},{11,3},{4,12},{12,4},... | collective-permute-start | bytes 9830408 | tf_op jit(solution)/shard_map/ppermute | solution.py:190
  475.1 21.4 %collective-permute-start.26 = (bf16[2,320,2560]{2,1,0:T(8,128)(2,1)}, bf16[2,320,2560]{2,1,0:T(8,128)(2,1)S(1)}, u32[]{:S(2)}, u32[]{:S(2)}) collective-permute-start(bf16[2,320,2560]{2,1,0:T(8,128)(2,1)} %dynamic-slice_bitcast_fusion.5), channel_id=1, source_target_pairs={{0,8},{8,0},{1,9},{9,1},{2,10},{10,2},{3,11},{11,3},{4,12},{12,4},... | collective-permute-start | bytes 9830408 | tf_op jit(solution)/shard_map/ppermute | solution.py:190
  500.0 173.9 %all-reduce.8.cloned.1.call-start = ((), (), s32[]{:S(2)}) async-start(), calls=%async_computation.8 | async-start | bytes 3276800 | tf_op jit(solution)/shard_map/psum | solution.py:563
  507.4 12.7 %collective-permute-start.27 = (bf16[512,1280]{1,0:T(8,128)(2,1)S(1)}, bf16[512,1280]{1,0:T(8,128)(2,1)}, u32[]{:S(2)}, u32[]{:S(2)}) collective-permute-start(bf16[512,1280]{1,0:T(8,128)(2,1)S(1)} %convolution_convert_fusion.14), channel_id=1, source_target_pairs={{0,8},{8,0},{1,9},{9,1},{2,10},{10,2},{3,11},{11,3},{4,12},{12,4},... | collective-permute-start | bytes 3932168 | tf_op jit(solution)/shard_map/ppermute | solution.py:190
  519.9 24.0 %collective-permute-start.29 = (bf16[2,320,2560]{2,1,0:T(8,128)(2,1)}, bf16[2,320,2560]{2,1,0:T(8,128)(2,1)S(1)}, u32[]{:S(2)}, u32[]{:S(2)}) collective-permute-start(bf16[2,320,2560]{2,1,0:T(8,128)(2,1)} %dynamic-slice_bitcast_fusion.4), channel_id=1, source_target_pairs={{0,8},{8,0},{1,9},{9,1},{2,10},{10,2},{3,11},{11,3},{4,12},{12,4},... | collective-permute-start | bytes 9830408 | tf_op jit(solution)/shard_map/ppermute | solution.py:190
  587.9 136.8 %reduce-scatter.9.cloned.1.call-start = ((), (), s32[]{:S(2)}) async-start(), calls=%async_computation.9 | async-start | bytes 10240000 | tf_op jit(solution)/shard_map/reduce_scatter | solution.py:295
  588.5 204.9 %reduce-scatter.11.cloned.1.call-start = ((), (), s32[]{:S(2)}) async-start(), calls=%async_computation.10 | async-start | bytes 6144000 | tf_op jit(solution)/shard_map/reduce_scatter | solution.py:295
  600.4 9.1 collective-permute-start.31
  609.2 83.4 %collective-permute-start.35 = (bf16[512,1280]{1,0:T(8,128)(2,1)}, bf16[512,1280]{1,0:T(8,128)(2,1)}, u32[]{:S(2)}, u32[]{:S(2)}) collective-permute-start(bf16[512,1280]{1,0:T(8,128)(2,1)} %convolution_convert_fusion.13), channel_id=1, source_target_pairs={{0,8},{8,0},{1,9},{9,1},{2,10},{10,2},{3,11},{11,3},{4,12},{12,4},... | collective-permute-start | bytes 3932168 | tf_op jit(solution)/shard_map/ppermute | solution.py:190
  625.5 59.4 %collective-permute-start.32 = (bf16[512,1280]{1,0:T(8,128)(2,1)S(1)}, bf16[512,1280]{1,0:T(8,128)(2,1)S(1)}, u32[]{:S(2)}, u32[]{:S(2)}) collective-permute-start(bf16[512,1280]{1,0:T(8,128)(2,1)S(1)} %slice.732), channel_id=1, source_target_pairs={{2,0},{4,2},{6,4},{3,1},{5,3},{7,5},{10,8},{12,10},{14,12},{11,9},... | collective-permute-start | bytes 3932168 | tf_op jit(solution)/shard_map/ppermute | solution.py:204
  688.0 20.0 %collective-permute-start.34 = (bf16[2,320,1920]{2,1,0:T(8,128)(2,1)S(1)}, bf16[2,320,1920]{2,1,0:T(8,128)(2,1)S(1)}, u32[]{:S(2)}, u32[]{:S(2)}) collective-permute-start(bf16[2,320,1920]{2,1,0:T(8,128)(2,1)S(1)} %dynamic-slice_bitcast_fusion.9), channel_id=1, source_target_pairs={{0,8},{8,0},{1,9},{9,1},{2,10},{10,2},{3,11},{11,3},{4,12},{12,4},... | collective-permute-start | bytes 7372808 | tf_op jit(solution)/shard_map/ppermute | solution.py:190
  691.3 33.4 %collective-permute-start.33 = (bf16[512,1280]{1,0:T(8,128)(2,1)}, bf16[512,1280]{1,0:T(8,128)(2,1)}, u32[]{:S(2)}, u32[]{:S(2)}) collective-permute-start(bf16[512,1280]{1,0:T(8,128)(2,1)} %add_convert_fusion.3), channel_id=1, source_target_pairs={{2,0},{4,2},{6,4},{3,1},{5,3},{7,5},{10,8},{12,10},{14,12},{11,9},... | collective-permute-start | bytes 3932168 | tf_op jit(solution)/shard_map/ppermute | solution.py:204
  734.6 153.5 %reduce-scatter.13.cloned.1.call-start = ((), (), s32[]{:S(2)}) async-start(), calls=%async_computation.11 | async-start | bytes 8192000 | tf_op jit(solution)/shard_map/reduce_scatter | solution.py:295
  749.5 32.7 %collective-permute-start.38 = (bf16[2,320,2560]{2,1,0:T(8,128)(2,1)}, bf16[2,320,2560]{2,1,0:T(8,128)(2,1)S(1)}, u32[]{:S(2)}, u32[]{:S(2)}) collective-permute-start(bf16[2,320,2560]{2,1,0:T(8,128)(2,1)} %dynamic-slice_bitcast_fusion.3), channel_id=1, source_target_pairs={{0,8},{8,0},{1,9},{9,1},{2,10},{10,2},{3,11},{11,3},{4,12},{12,4},... | collective-permute-start | bytes 9830408 | tf_op jit(solution)/shard_map/ppermute | solution.py:190
  793.4 193.2 %all-reduce.10.cloned.1.call-start = ((), (), s32[]{:S(2)}) async-start(), calls=%async_computation.12 | async-start | bytes 6553600 | tf_op jit(solution)/shard_map/psum | solution.py:563
  808.0 20.1 %collective-permute-start.40 = (bf16[2,320,2560]{2,1,0:T(8,128)(2,1)}, bf16[2,320,2560]{2,1,0:T(8,128)(2,1)}, u32[]{:S(2)}, u32[]{:S(2)}) collective-permute-start(bf16[2,320,2560]{2,1,0:T(8,128)(2,1)} %dynamic-slice_bitcast_fusion.2), channel_id=1, source_target_pairs={{0,8},{8,0},{1,9},{9,1},{2,10},{10,2},{3,11},{11,3},{4,12},{12,4},... | collective-permute-start | bytes 9830408 | tf_op jit(solution)/shard_map/ppermute | solution.py:190
  820.2 7.9 collective-permute-start.41
  834.8 151.8 %reduce-scatter.15.cloned.1.call-start = ((), (), s32[]{:S(2)}) async-start(), calls=%async_computation.13 | async-start | bytes 10240000 | tf_op jit(solution)/shard_map/reduce_scatter | solution.py:295
  836.1 50.2 %collective-permute-start.42 = (bf16[512,1280]{1,0:T(8,128)(2,1)S(1)}, bf16[512,1280]{1,0:T(8,128)(2,1)}, u32[]{:S(2)}, u32[]{:S(2)}) collective-permute-start(bf16[512,1280]{1,0:T(8,128)(2,1)S(1)} %copy-done.65), channel_id=1, source_target_pairs={{0,1},{1,0},{2,3},{3,2},{4,5},{5,4},{6,7},{7,6},{8,9},{9,8},{10,11... | collective-permute-start | bytes 3932168 | tf_op jit(solution)/shard_map/ppermute | solution.py:194
  888.2 164.9 %reduce-scatter.17.cloned.1.call-start = ((), (), s32[]{:S(2)}) async-start(), calls=%async_computation.14 | async-start | bytes 6144000 | tf_op jit(solution)/shard_map/reduce_scatter | solution.py:295
  942.6 44.0 %collective-permute-start.44 = (bf16[512,1280]{1,0:T(8,128)(2,1)S(1)}, bf16[512,1280]{1,0:T(8,128)(2,1)S(1)}, u32[]{:S(2)}, u32[]{:S(2)}) collective-permute-start(bf16[512,1280]{1,0:T(8,128)(2,1)S(1)} %slice.731), channel_id=1, source_target_pairs={{2,0},{4,2},{6,4},{3,1},{5,3},{7,5},{10,8},{12,10},{14,12},{11,9},... | collective-permute-start | bytes 3932168 | tf_op jit(solution)/shard_map/ppermute | solution.py:204
  986.6 103.7 %all-reduce.12.cloned.1.call-start = ((), (), s32[]{:S(2)}) async-start(), calls=%async_computation.15 | async-start | bytes 3276800 | tf_op jit(solution)/shard_map/psum | solution.py:563
  993.6 59.5 %collective-permute-start.46 = (bf16[512,1280]{1,0:T(8,128)(2,1)}, bf16[512,1280]{1,0:T(8,128)(2,1)S(1)}, u32[]{:S(2)}, u32[]{:S(2)}) collective-permute-start(bf16[512,1280]{1,0:T(8,128)(2,1)} %add_convert_fusion.2), channel_id=1, source_target_pairs={{2,0},{4,2},{6,4},{3,1},{5,3},{7,5},{10,8},{12,10},{14,12},{11,9},... | collective-permute-start | bytes 3932168 | tf_op jit(solution)/shard_map/ppermute | solution.py:204
  995.0 229.6 %all-reduce.14.cloned.1.call-start = ((), (), s32[]{:S(2)}) async-start(), calls=%async_computation.16 | async-start | bytes 6553600 | tf_op jit(solution)/shard_map/psum | solution.py:563
  1108.8 8.2 collective-permute-start.51
  1117.1 7.7 collective-permute-start.52
  1123.3 28.6 %collective-permute-start.47 = (bf16[512,1280]{1,0:T(8,128)(2,1)}, bf16[512,1280]{1,0:T(8,128)(2,1)}, u32[]{:S(2)}, u32[]{:S(2)}) collective-permute-start(bf16[512,1280]{1,0:T(8,128)(2,1)} %get-tuple-element.212), channel_id=1, source_target_pairs={{0,1},{1,0},{2,3},{3,2},{4,5},{5,4},{6,7},{7,6},{8,9},{9,8},{10,11... | collective-permute-start | bytes 3932168 | tf_op jit(solution)/shard_map/ppermute | solution.py:194
  1124.9 23.6 %collective-permute-start.53 = (f32[2,15360]{1,0:T(2,128)S(1)}, f32[2,15360]{1,0:T(2,128)S(1)}, u32[]{:S(2)}, u32[]{:S(2)}) collective-permute-start(f32[2,15360]{1,0:T(2,128)S(1)} %add.455), channel_id=1, source_target_pairs={{2,0},{4,6},{3,1},{5,7},{10,8},{12,14},{11,9},{13,15},{18,16},{20,... | collective-permute-start | bytes 368648 | tf_op jit(solution)/shard_map/ppermute | solution.py:358
  (155 other events, 2029.8 us)
Sparse Core Ops, SparseCore 0:
  13.0 75.0 all-gather.8
  90.5 126.8 all-gather.10
  224.6 72.3 all-gather.12
  307.2 127.9 all-gather.14
  500.1 72.4 reduce-scatter.6
  591.6 85.6 reduce-scatter.8
  734.7 58.6 reduce-scatter.10
  797.0 91.0 reduce-scatter.12
  891.7 84.7 reduce-scatter.14
  986.8 59.1 reduce-scatter.16
Sparse Core Ops, SparseCore 1:
  25.0 32.6 all-reduce.5
  588.0 85.9 all-reduce.7
  834.9 129.6 all-reduce.9
  995.0 95.2 all-reduce.11
  1098.6 125.8 all-reduce.13

commit v9 on v8

--- a/solution.py
+++ b/solution.py
@@ -593,7 +593,9 @@
         if final:
             grad_norm_in, grad_out = tie(grad_norm_in, join(out_swap))
             (grad_norm_in, grad_out) = settle((grad_norm_in, grad_out), "attn1")
-            attn_share = waiting.pop(0)[1]
+            share = jnp.concatenate([early_share, waiting.pop(0)[1]], axis=1)
+            waiting.insert(0, ("first", share))
+            grad_norm_in = advance(grad_norm_in, "first")
             waiting.append(("out%d" % layer, scatter_sum(grad_out)))
         fc_swap = scatter_swap(narrow(dot_first(mlp_in, grad_pre)), place)
         grad_from_mlp, grad_gain_mlp, grad_shift_mlp = norm_backward(
@@ -609,10 +611,6 @@
         )
         grad_mixed, fc_swap.came, proj_swap.came = tie(grad_mixed, fc_swap.came, proj_swap.came)
         grad_mixed, grad_fc = tie(grad_mixed, join(fc_swap, proj_swap))
-        if final:
-            share = jnp.concatenate([early_share, attn_share], axis=1)
-            waiting.insert(0, ("first", share))
-            grad_mixed = advance(grad_mixed, "first")
         grad_packed = attention_backward(packed, mixed, grad_mixed, log_total, low_pos)
         if final:
             grad_packed, far_output, grad_fc = tie(grad_packed, far_output, grad_fc)
@@ -627,6 +625,8 @@
         far_total, grad_attn_in = grad_near[:last], grad_near[last:]
         rows = grad_packed.reshape(2 * key_len, -1)
         grad_near, rows = tie(grad_near, rows)
+        if final:
+            grad_near = advance(grad_near, "out%d" % layer)
         far_total, grad_attn_in = grad_near[:last], grad_near[last:]
         carried = backward_step(narrow(far_total[:block_len]))
         grad_qkv = narrow(dot_first(near, rows))
@@ -639,9 +639,9 @@
                 attn_swap = scatter_swap(grad_qkv, place)
             if step == 1 and final:
                 carried, grad_attn = tie(carried, join(attn_swap))
-                carried = advance(carried, "out%d" % layer)
                 carried, grad_attn = settle((carried, grad_attn), "fc%d" % layer)
                 waiting.append(("attn%d" % layer, scatter_sum(grad_attn)))
+                carried = advance(carried, "fc%d" % layer)
             if step == 2 and not final:
                 carried, grad_bias, grad_attn, own_output = tie(
                     carried, grad_bias, join(attn_swap), own_output
@@ -651,12 +651,8 @@
                 early_share = waiting.pop(0)[1]
                 waiting.append(("attn%d" % layer, scatter_sum(grad_attn)))
             if step == 2 and final:
-                carried, grad_bias, waiting[1] = tie(carried, grad_bias, waiting[1][1])
-                waiting[1] = ("attn%d" % layer, waiting[1])
-                carried = settle(carried, "fc%d" % layer)
-                share = jnp.concatenate([waiting[0][1], waiting[1][1]], axis=1)
-                waiting[:] = [("last", share)]
-                carried = advance(carried, "last")
+                carried, grad_bias = tie(carried, grad_bias)
+                carried = advance(carried, "attn%d" % layer)
             arrived = wide(carried)
             if step < reach:
                 section = far_total[step * block_len : (step + 1) * block_len]
@@ -692,8 +688,8 @@
     halves = small[:, split:].reshape(layer_count, 2, -1)
     halves = lax.dynamic_index_in_dim(halves, place.tp, 1, False)
     split = fc_width + half_width
-    attn = [sums[name][:, split:] for name in ("last", "first")]
-    fc_proj = [sums[name][:, :split] for name in ("last", "first")]
+    attn = [sums["attn0"], sums["first"][:, split:]]
+    fc_proj = [sums["fc0"], sums["first"][:, :split]]
     return (
         both_seqs(own_output, far_output),
         token_grad,

time: 1250 us -> 1230 us (0.984)
  waiting for transfers between devices: 486 us -> 467 us
    ppermute x4, waiting for transfers between devices: 13.3 us -> 0.01 us  [other_tp(): return lax.ppermute(value, 'tp', [(0, 1), (1, 0)])]
    ppermute x4, waiting for transfers between devices: 110 us -> 122 us  [backward_step(): return lax.ppermute(value, 'ctx', [(i + 1, i) for i in range(count - 1)])]
    psum x4 -> x5, waiting for transfers between devices: 129 us -> 118 us  [advance(): last_sum = lax.psum(share, 'ctx')]
    unnamed x315 -> x305, local copies, waits for them, and re-layouts: 73.7 us -> 80.1 us
  transfers between devices with their start and end apart: 69 -> 70, of which waited for: 39 -> 37; matrix products, arithmetic and copies ran while one was open for 35% -> 35% of each run, Pallas kernels for 13% -> 13%
where the time goes in v9:
time: 1230 us; the launch traced here: 1220 us
  waiting for transfers between devices  467 us (38%)
  matrix products  304 us (25%)
  Pallas kernels  160 us (13%)
  local copies, waits for them, and re-layouts  124 us (10%)
  other arithmetic  102 us (8%)
  starting transfers between devices  48.8 us (4%)
  between operations  18.2 us (1%)
    dot_general x24, matrix products, contract(): lax.dot_general(left_side, right_side, (((left_dim,), (right_dim,)), ((),...  196 us
    ppermute x4, waiting for transfers between devices, backward_step(): return lax.ppermute(value, 'ctx', [(i + 1, i) for i in range(count - 1)])  122 us
    psum x5, waiting for transfers between devices, advance(): last_sum = lax.psum(share, 'ctx')  118 us
    dot_general x8, matrix products, dot_f32(): return jnp.dot(left_side, right_side, preferred_element_type=jnp.float32)  108 us
    ppermute x4, waiting for transfers between devices, onward(): return lax.ppermute(value, 'ctx', [(i, i + 1) for i in range(count - 1)])  85.9 us
    pallas_call x2, Pallas kernels, attention_backward(): pl.pallas_call(backward_kernel, grid=(groups, pairs), in_specs=[packed_sp...  80.1 us
    unnamed x305, local copies, waits for them, and re-layouts  80.1 us
    pallas_call x2, Pallas kernels, attention_forward(): pl.pallas_call(forward_kernel, grid=(groups, pairs), in_specs=[pl.BlockSp...  63.5 us
  transfers between devices with their start and end apart: 70, of which 37 were waited for; matrix products, arithmetic and copies ran while one was open for 35% of the time, Pallas kernels for 13%

profile of v9, /device:TPU:0, one launch (start us, length us, event | category | flops | bytes accessed | tf_op | source)
XLA Modules:
  0.0 1224.9 jit_solution(8260032550806284508)
XLA Ops:
  41.3 12.3 %collective-permute-done = bf16[512,1280]{1,0:T(8,128)(2,1)} collective-permute-done((bf16[512,1280]{1,0:T(8,128)(2,1)}, bf16[512,1280]{1,0:T(8,128)(2,1)}, u32[]{:S(2)}, u32[]{:S(2)}) %collective-permute-start) | collective-permute-done | bytes 1310752 | tf_op jit(solution)/shard_map/ppermute | solution.py:199
  62.7 22.8 %collective-permute-done.1 = bf16[512,1280]{1,0:T(8,128)(2,1)S(1)} collective-permute-done((bf16[512,1280]{1,0:T(8,128)(2,1)}, bf16[512,1280]{1,0:T(8,128)(2,1)S(1)}, u32[]{:S(2)}, u32[]{:S(2)}) %collective-permute-start.1) | collective-permute-done | bytes 1310752 | tf_op jit(solution)/shard_map/ppermute | solution.py:199
  123.0 18.6 %add_convert_fusion.1 = bf16[3072,1920]{1,0:T(8,128)(2,1)} fusion(bf16[3072,1280]{1,0:T(8,128)(2,1)S(1)} %copy-done.67, f32[1920]{0:T(1024)S(1)} %reduce.2, bf16[1280,2560]{1,0:T(8,128)(2,1)S(1)} %shard_map.188), kind=kOutput, calls=%fused_computation.3 | convolution fusion | flops 15111290880 | bytes 24584192 | tf_op jit(solution)/shard_map/dot_general | solution.py:299
  141.6 31.7 %shard_map.189 = (bf16[2,512,640]{2,1,0:T(8,128)(2,1)}, f32[2,5,2,512]{3,2,1,0:T(2,128)}) custom-call(bf16[2,1536,1920]{2,1,0:T(8,128)(2,1)} %bitcast.332, s32[2,512,1]{2,1,0:T(8,128)} %subtract_add_fusion.low_ref), custom_call_target="tpu_custom_call" | custom-call | flops 512 | bytes 512 | tf_op jit(solution)/shard_map/pallas_call | solution.py:80
  187.8 29.5 %all-gather.11.cloned.1.call-done = bf16[1280,5120]{1,0:T(8,128)(2,1)} async-done(((bf16[320,5120]{1,0:T(8,128)(2,1)}), bf16[1280,5120]{1,0:T(8,128)(2,1)}) %all-gather.11.cloned.1.call-update) | async-done | bytes 13107216 | tf_op jit(solution)/shard_map/all_gather | solution.py:286
  224.6 10.2 collective-permute-done.12.refs_1_
  247.2 11.0 multiply_convert_fusion.1
  279.8 27.2 %collective-permute-done.15 = bf16[512,1280]{1,0:T(8,128)(2,1)} collective-permute-done((bf16[512,1280]{1,0:T(8,128)(2,1)S(1)}, bf16[512,1280]{1,0:T(8,128)(2,1)}, u32[]{:S(2)}, u32[]{:S(2)}) %collective-permute-start.15) | collective-permute-done | bytes 1310752 | tf_op jit(solution)/shard_map/ppermute | solution.py:199
  309.6 5.7 collective-permute-start.16
  319.5 23.5 %collective-permute-done.16 = bf16[512,1280]{1,0:T(8,128)(2,1)} collective-permute-done((bf16[512,1280]{1,0:T(8,128)(2,1)}, bf16[512,1280]{1,0:T(8,128)(2,1)}, u32[]{:S(2)}, u32[]{:S(2)}) %collective-permute-start.16) | collective-permute-done | bytes 1310752 | tf_op jit(solution)/shard_map/ppermute | solution.py:199
  350.3 18.7 %add_convert_fusion = bf16[3072,1920]{1,0:T(8,128)(2,1)} fusion(bf16[3072,1280]{1,0:T(8,128)(2,1)S(1)} %constant_dynamic-update-slice_fusion.23, f32[1920]{0:T(1024)S(1)} %reduce.10, bf16[1280,2560]{1,0:T(8,128)(2,1)S(1)} %bitcast.317), kind=kOutput, calls=%fused_computation.2 | convolution fusion | flops 15111290880 | bytes 24584192 | tf_op jit(solution)/shard_map/dot_general | solution.py:299
  368.9 31.8 %shard_map.193 = (bf16[2,512,640]{2,1,0:T(8,128)(2,1)}, f32[2,5,2,512]{3,2,1,0:T(2,128)}) custom-call(bf16[2,1536,1920]{2,1,0:T(8,128)(2,1)} %bitcast.334, s32[2,512,1]{2,1,0:T(8,128)} %subtract_add_fusion.low_ref), custom_call_target="tpu_custom_call" | custom-call | flops 512 | bytes 512 | tf_op jit(solution)/shard_map/pallas_call | solution.py:80
  413.9 21.3 %all-gather.15.cloned.1.call-done = bf16[1280,5120]{1,0:T(8,128)(2,1)} async-done(((bf16[320,5120]{1,0:T(8,128)(2,1)}), bf16[1280,5120]{1,0:T(8,128)(2,1)}) %all-gather.15.cloned.1.call-update) | async-done | bytes 13107216 | tf_op jit(solution)/shard_map/all_gather | solution.py:286
  443.3 7.2 collective-permute-done.25.refs_1_
  451.4 11.7 multiply_convert_fusion
  463.1 10.2 convolution_convert_fusion.3
  478.9 17.9 %fusion.13 = bf16[1024,2560]{1,0:T(8,128)(2,1)} fusion(f32[1024,2560]{1,0:T(8,128)} %get-tuple-element.247, f32[2560]{0:T(1024)S(1)} %get-tuple-element.200, bf16[1280,2560]{1,0:T(8,128)(2,1)} %copy-done.20, bf16[512,1280]{1,0:T(8,128)(2,1)} %copy-done.107, bf16[512,1280]{1,0:T(8,128)(2,1)} %copy-done.62), kind=kOutput, calls=%fused_computation.25 | convolution fusion | flops 6771179520 | bytes 24913920 | tf_op jit(solution)/shard_map/dot_general | solution.py:299
  500.3 7.4 convolution_convert_fusion.14
  508.1 10.0 convolution_convert_fusion.2
  521.2 8.3 multiply_reduce_fusion
  548.0 40.2 %shard_map.197 = bf16[2,1536,1920]{2,1,0:T(8,128)(2,1)} custom-call(bf16[2,1536,1920]{2,1,0:T(8,128)(2,1)} %bitcast.335, bf16[2,512,640]{2,1,0:T(8,128)(2,1)} %get-tuple-element.104.mixed_ref, bf16[2,512,640]{2,1,0:T(8,128)(2,1)} %bitcast.343, f32[2,5,2,512]{3,2,1,0:T(2,128)} %get-tuple-element.113.total_ref, s32[2,1,512]{2,1,0:T(1,128)} %subtract_add_fusion.1.low_ref), custom_call_target="tpu_custom_call" | custom-call | flops 512 | bytes 512 | tf_op jit(solution)/shard_map/pallas_call | solution.py:163
  588.8 11.8 convolution_convert_fusion.7
  601.0 8.5 convolution_convert_fusion.13
  609.7 12.9 %convolution_add_fusion.1 = f32[1536,1280]{1,0:T(8,128)S(1)} fusion(bf16[1536,1280]{1,0:T(8,128)(2,1)} %collective-permute-done.31, bf16[2,1536,1920]{2,1,0:T(8,128)(2,1)} %shard_map.197, bf16[1280,2560]{1,0:T(8,128)(2,1)} %copy-done.14), kind=kOutput, calls=%fused_computation.31 | convolution fusion | flops 7553679360 | bytes 22609920 | tf_op jit(solution)/shard_map/dot_general | solution.py:15
  627.2 20.2 %convolution_convert_fusion.5 = bf16[1280,1920]{1,0:T(8,128)(2,1)} fusion(bf16[3072,1280]{1,0:T(8,128)(2,1)} %copy-done.68, bf16[3072,1920]{1,0:T(8,128)(2,1)S(1)} %bitcast.331), kind=kOutput, calls=%fused_computation.33 | convolution fusion | flops 15101952000 | bytes 24576000 | tf_op jit(solution)/shard_map/dot_general | solution.py:15
  647.4 26.7 %all-reduce.9.cloned.1.call-done = bf16[320,2560]{1,0:T(8,128)(2,1)} async-done(((bf16[320,2560]{1,0:T(8,128)(2,1)}), bf16[320,2560]{1,0:T(8,128)(2,1)}) %all-reduce.9.cloned.1.call-update) | async-done | bytes 1638416 | tf_op jit(solution)/shard_map/psum | solution.py:563
  674.1 11.1 collective-permute-done.32
  692.9 8.7 fusion.45
  701.6 6.6 convert_reduce_fusion.1
  711.0 13.9 %collective-permute-done.33 = bf16[512,1280]{1,0:T(8,128)(2,1)} collective-permute-done((bf16[512,1280]{1,0:T(8,128)(2,1)}, bf16[512,1280]{1,0:T(8,128)(2,1)}, u32[]{:S(2)}, u32[]{:S(2)}) %collective-permute-start.33) | collective-permute-done | bytes 1310752 | tf_op jit(solution)/shard_map/ppermute | solution.py:204
  737.9 10.2 convolution_convert_fusion.1
  748.9 20.2 %convert_reduce_fusion.3 = (f32[2560]{0:T(1024)S(1)}, bf16[1024,2560]{1,0:T(8,128)(2,1)}) fusion(f32[1024,2560]{1,0:T(8,128)} %get-tuple-element.241, f32[2560]{0:T(1024)S(1)} %copy-done.99, bf16[1280,2560]{1,0:T(8,128)(2,1)} %copy-done.19, bf16[512,1280]{1,0:T(8,128)(2,1)} %copy-done.108, bf16[512,1280]{1,0:T(8,128)(2,1)S(1)} %convert_element_type.244), kind=kOutput, calls=%fused_computation.27 | convolution fusion | flops 6776419840 | bytes 24924160 | tf_op jit(solution)/shard_map/dot_general | solution.py:299
  777.5 6.9 convolution_add_fusion.4
  787.7 6.0 reduce-scatter.11.cloned.1.call-done
  793.8 9.8 convolution_convert_fusion
  834.8 40.0 %shard_map.202 = bf16[2,1536,1920]{2,1,0:T(8,128)(2,1)} custom-call(bf16[2,1536,1920]{2,1,0:T(8,128)(2,1)} %bitcast.333, bf16[2,512,640]{2,1,0:T(8,128)(2,1)} %get-tuple-element.95.mixed_ref, bf16[2,512,640]{2,1,0:T(8,128)(2,1)} %bitcast.342, f32[2,5,2,512]{3,2,1,0:T(2,128)} %get-tuple-element.141.total_ref, s32[2,1,512]{2,1,0:T(1,128)} %subtract_add_fusion.1.low_ref), custom_call_target="tpu_custom_call" | custom-call | flops 512 | bytes 512 | tf_op jit(solution)/shard_map/pallas_call | solution.py:163
  874.8 13.7 %reduce-scatter.13.cloned.1.call-done = bf16[320,2560]{1,0:T(8,128)(2,1)} async-done(((bf16[1280,2560]{1,0:T(8,128)(2,1)}), bf16[320,2560]{1,0:T(8,128)(2,1)}) %reduce-scatter.13.cloned.1.call-update) | async-done | bytes 1638416 | tf_op jit(solution)/shard_map/reduce_scatter | solution.py:295
  888.6 12.0 convolution_convert_fusion.6
  900.7 6.9 collective-permute-done.43
  907.6 13.5 %convolution_add_fusion = f32[1536,1280]{1,0:T(8,128)} fusion(bf16[1536,1280]{1,0:T(8,128)(2,1)} %collective-permute-done.43, bf16[2,1536,1920]{2,1,0:T(8,128)(2,1)S(1)} %copy-done.28, bf16[1280,2560]{1,0:T(8,128)(2,1)} %copy-done.17), kind=kOutput, calls=%fused_computation.30 | convolution fusion | flops 7553679360 | bytes 22609920 | tf_op jit(solution)/shard_map/dot_general | solution.py:15
  921.1 17.4 %convolution_convert_fusion.4 = bf16[1280,1920]{1,0:T(8,128)(2,1)S(1)} fusion(bf16[3072,1280]{1,0:T(8,128)(2,1)S(1)} %bitcast.351, bf16[3072,1920]{1,0:T(8,128)(2,1)S(1)} %bitcast.327), kind=kOutput, calls=%fused_computation.32 | convolution fusion | flops 15101952000 | bytes 24576000 | tf_op jit(solution)/shard_map/dot_general | solution.py:15
  952.7 52.1 %collective-permute-done.44 = bf16[512,1280]{1,0:T(8,128)(2,1)} collective-permute-done((bf16[512,1280]{1,0:T(8,128)(2,1)}, bf16[512,1280]{1,0:T(8,128)(2,1)}, u32[]{:S(2)}, u32[]{:S(2)}) %collective-permute-start.44) | collective-permute-done | bytes 1310752 | tf_op jit(solution)/shard_map/ppermute | solution.py:204
  1004.9 35.3 %all-reduce.13.cloned.1.call-done = bf16[320,2560]{1,0:T(8,128)(2,1)} async-done(((bf16[320,2560]{1,0:T(8,128)(2,1)}), bf16[320,2560]{1,0:T(8,128)(2,1)}) %all-reduce.13.cloned.1.call-update) | async-done | bytes 1638416 | tf_op jit(solution)/shard_map/psum | solution.py:563
  1048.7 6.8 convert_reduce_fusion
  1065.3 45.3 %collective-permute-done.46 = bf16[512,1280]{1,0:T(8,128)(2,1)} collective-permute-done((bf16[512,1280]{1,0:T(8,128)(2,1)S(1)}, bf16[512,1280]{1,0:T(8,128)(2,1)}, u32[]{:S(2)}, u32[]{:S(2)}) %collective-permute-start.46) | collective-permute-done | bytes 1310752 | tf_op jit(solution)/shard_map/ppermute | solution.py:204
  1110.7 36.0 %all-reduce.15.cloned.1.call-done = bf16[320,3200]{1,0:T(8,128)(2,1)} async-done(((bf16[320,3200]{1,0:T(8,128)(2,1)}), bf16[320,3200]{1,0:T(8,128)(2,1)}) %all-reduce.15.cloned.1.call-update) | async-done | bytes 2048016 | tf_op jit(solution)/shard_map/psum | solution.py:563
  1175.8 10.1 collective-permute-done.53
  1188.7 19.9 %all-reduce.17.cloned.1.call-done.first_ref = bf16[320,1920]{1,0:T(8,128)(2,1)} async-done(((bf16[320,1920]{1,0:T(8,128)(2,1)}), bf16[320,1920]{1,0:T(8,128)(2,1)}) %all-reduce.17.cloned.1.call-update) | async-done | bytes 1228816 | tf_op jit(solution)/shard_map/psum | solution.py:563
  (619 shorter events, 346.8 us)
Async XLA Ops:
  8.0 80.0 %all-gather.9.cloned.1.call-start = ((), (), s32[]{:S(2)}) async-start(), calls=%async_computation.18 | async-start | bytes 8192000 | tf_op jit(solution)/shard_map/all_gather | solution.py:286
  12.9 100.4 %all-reduce.7.cloned.1.call-start = ((), (), s32[]{:S(2)}) async-start(), calls=%async_computation.6 | async-start | bytes 163840 | tf_op jit(solution)/shard_map/psum | solution.py:458
  12.9 24.9 %collective-permute-start.9 = (s32[4]{0:T(128)S(1)}, s32[4]{0:T(128)S(1)}, u32[]{:S(2)}, u32[]{:S(2)}) collective-permute-start(s32[4]{0:T(128)S(1)} %fusion.148), channel_id=1, source_target_pairs={{0,8},{8,0},{1,9},{9,1},{2,10},{10,2},{3,11},{11,3},{4,12},{12,4},... | collective-permute-start | bytes 56 | tf_op jit(solution)/shard_map/ppermute | solution.py:190
  13.5 25.9 %collective-permute-start.2 = (bf16[12,320]{1,0:T(8,128)(2,1)S(1)}, bf16[12,320]{1,0:T(8,128)(2,1)S(1)}, u32[]{:S(2)}, u32[]{:S(2)}) collective-permute-start(bf16[12,320]{1,0:T(8,128)(2,1)S(1)} %reshape.357), channel_id=1, source_target_pairs={{0,8},{8,0},{1,9},{9,1},{2,10},{10,2},{3,11},{11,3},{4,12},{12,4},... | collective-permute-start | bytes 23048 | tf_op jit(solution)/shard_map/ppermute | solution.py:190
  13.7 27.4 %collective-permute-start.8 = (bf16[2,3840]{1,0:T(2,128)(2,1)S(1)}, bf16[2,3840]{1,0:T(2,128)(2,1)S(1)}, u32[]{:S(2)}, u32[]{:S(2)}) collective-permute-start(bf16[2,3840]{1,0:T(2,128)(2,1)S(1)} %constant_dynamic-update-slice_fusion.6), channel_id=1, source_target_pairs={{0,1},{1,0},{2,3},{3,2},{4,5},{5,4},{6,7},{7,6},{8,9},{9,8},{10,11... | collective-permute-start | bytes 46088 | tf_op jit(solution)/shard_map/ppermute | solution.py:194
  19.3 34.3 %collective-permute-start = (bf16[512,1280]{1,0:T(8,128)(2,1)}, bf16[512,1280]{1,0:T(8,128)(2,1)}, u32[]{:S(2)}, u32[]{:S(2)}) collective-permute-start(bf16[512,1280]{1,0:T(8,128)(2,1)} %get-tuple-element.217), channel_id=1, source_target_pairs={{0,2},{2,4},{4,6},{1,3},{3,5},{5,7},{8,10},{10,12},{12,14},{9,11},... | collective-permute-start | bytes 3932168 | tf_op jit(solution)/shard_map/ppermute | solution.py:199
  25.0 192.4 %all-gather.11.cloned.1.call-start = ((), (), s32[]{:S(2)}) async-start(), calls=%async_computation.19 | async-start | bytes 16384000 | tf_op jit(solution)/shard_map/all_gather | solution.py:286
  39.6 18.9 %collective-permute-start.3 = (bf16[12,640]{1,0:T(8,128)(2,1)S(1)}, bf16[12,640]{1,0:T(8,128)(2,1)S(1)}, u32[]{:S(2)}, u32[]{:S(2)}) collective-permute-start(bf16[12,640]{1,0:T(8,128)(2,1)S(1)} %select_n.135), channel_id=1, source_target_pairs={{0,16},{16,0},{1,17},{17,1},{2,18},{18,2},{3,19},{19,3},{4,20},{20... | collective-permute-start | bytes 46088 | tf_op jit(solution)/shard_map/ppermute | solution.py:315
  53.6 253.6 %all-gather.13.cloned.1.call-start = ((), (), s32[]{:S(2)}) async-start(), calls=%async_computation.20 | async-start | bytes 8192000 | tf_op jit(solution)/shard_map/all_gather | solution.py:286
  53.9 31.6 %collective-permute-start.1 = (bf16[512,1280]{1,0:T(8,128)(2,1)}, bf16[512,1280]{1,0:T(8,128)(2,1)S(1)}, u32[]{:S(2)}, u32[]{:S(2)}) collective-permute-start(bf16[512,1280]{1,0:T(8,128)(2,1)} %collective-permute-done), channel_id=1, source_target_pairs={{0,2},{2,4},{4,6},{1,3},{3,5},{5,7},{8,10},{10,12},{12,14},{9,11},... | collective-permute-start | bytes 3932168 | tf_op jit(solution)/shard_map/ppermute | solution.py:199
  91.9 21.3 %collective-permute-start.7 = (bf16[2,320,2560]{2,1,0:T(8,128)(2,1)}, bf16[2,320,2560]{2,1,0:T(8,128)(2,1)S(1)}, u32[]{:S(2)}, u32[]{:S(2)}) collective-permute-start(bf16[2,320,2560]{2,1,0:T(8,128)(2,1)} %dynamic-slice_bitcast_fusion.7), channel_id=1, source_target_pairs={{0,8},{8,0},{1,9},{9,1},{2,10},{10,2},{3,11},{11,3},{4,12},{12,4},... | collective-permute-start | bytes 9830408 | tf_op jit(solution)/shard_map/ppermute | solution.py:190
  97.7 10.5 collective-permute-start.5
  98.3 7.5 collective-permute-start.4
  224.0 10.8 collective-permute-start.12
  224.0 19.6 %collective-permute-start.13 = (bf16[2,320,2560]{2,1,0:T(8,128)(2,1)}, bf16[2,320,2560]{2,1,0:T(8,128)(2,1)S(1)}, u32[]{:S(2)}, u32[]{:S(2)}) collective-permute-start(bf16[2,320,2560]{2,1,0:T(8,128)(2,1)} %get-tuple-element.225), channel_id=1, source_target_pairs={{0,8},{8,0},{1,9},{9,1},{2,10},{10,2},{3,11},{11,3},{4,12},{12,4},... | collective-permute-start | bytes 9830408 | tf_op jit(solution)/shard_map/ppermute | solution.py:190
  224.5 210.8 %all-gather.15.cloned.1.call-start = ((), (), s32[]{:S(2)}) async-start(), calls=%async_computation.21 | async-start | bytes 16384000 | tf_op jit(solution)/shard_map/all_gather | solution.py:286
  275.3 31.8 %collective-permute-start.15 = (bf16[512,1280]{1,0:T(8,128)(2,1)S(1)}, bf16[512,1280]{1,0:T(8,128)(2,1)}, u32[]{:S(2)}, u32[]{:S(2)}) collective-permute-start(bf16[512,1280]{1,0:T(8,128)(2,1)S(1)} %add_convert_fusion.5), channel_id=1, source_target_pairs={{0,2},{2,4},{4,6},{1,3},{3,5},{5,7},{8,10},{10,12},{12,14},{9,11},... | collective-permute-start | bytes 3932168 | tf_op jit(solution)/shard_map/ppermute | solution.py:199
  307.1 281.1 %reduce-scatter.7.cloned.1.call-start = ((), (), s32[]{:S(2)}) async-start(), calls=%async_computation.7 | async-start | bytes 8192000 | tf_op jit(solution)/shard_map/reduce_scatter | solution.py:295
  309.6 33.5 %collective-permute-start.16 = (bf16[512,1280]{1,0:T(8,128)(2,1)}, bf16[512,1280]{1,0:T(8,128)(2,1)}, u32[]{:S(2)}, u32[]{:S(2)}) collective-permute-start(bf16[512,1280]{1,0:T(8,128)(2,1)} %collective-permute-done.15), channel_id=1, source_target_pairs={{0,2},{2,4},{4,6},{1,3},{3,5},{5,7},{8,10},{10,12},{12,14},{9,11},... | collective-permute-start | bytes 3932168 | tf_op jit(solution)/shard_map/ppermute | solution.py:199
  442.6 7.9 collective-permute-start.25
  442.7 20.4 %collective-permute-start.22 = (bf16[512,1280]{1,0:T(8,128)(2,1)S(1)}, bf16[512,1280]{1,0:T(8,128)(2,1)S(1)}, u32[]{:S(2)}, u32[]{:S(2)}) collective-permute-start(bf16[512,1280]{1,0:T(8,128)(2,1)S(1)} %fusion.147), channel_id=1, source_target_pairs={{0,8},{8,0},{1,9},{9,1},{2,10},{10,2},{3,11},{11,3},{4,12},{12,4},... | collective-permute-start | bytes 3932168 | tf_op jit(solution)/shard_map/ppermute | solution.py:190
  443.3 32.1 %collective-permute-start.24 = (bf16[2,320,2560]{2,1,0:T(8,128)(2,1)}, bf16[2,320,2560]{2,1,0:T(8,128)(2,1)S(1)}, u32[]{:S(2)}, u32[]{:S(2)}) collective-permute-start(bf16[2,320,2560]{2,1,0:T(8,128)(2,1)} %get-tuple-element.222), channel_id=1, source_target_pairs={{0,8},{8,0},{1,9},{9,1},{2,10},{10,2},{3,11},{11,3},{4,12},{12,4},... | collective-permute-start | bytes 9830408 | tf_op jit(solution)/shard_map/ppermute | solution.py:190
  475.2 21.6 %collective-permute-start.26 = (bf16[2,320,2560]{2,1,0:T(8,128)(2,1)}, bf16[2,320,2560]{2,1,0:T(8,128)(2,1)S(1)}, u32[]{:S(2)}, u32[]{:S(2)}) collective-permute-start(bf16[2,320,2560]{2,1,0:T(8,128)(2,1)} %dynamic-slice_bitcast_fusion.5), channel_id=1, source_target_pairs={{0,8},{8,0},{1,9},{9,1},{2,10},{10,2},{3,11},{11,3},{4,12},{12,4},... | collective-permute-start | bytes 9830408 | tf_op jit(solution)/shard_map/ppermute | solution.py:190
  500.2 173.9 %all-reduce.9.cloned.1.call-start = ((), (), s32[]{:S(2)}) async-start(), calls=%async_computation.8 | async-start | bytes 3276800 | tf_op jit(solution)/shard_map/psum | solution.py:563
  507.6 12.7 %collective-permute-start.27 = (bf16[512,1280]{1,0:T(8,128)(2,1)S(1)}, bf16[512,1280]{1,0:T(8,128)(2,1)}, u32[]{:S(2)}, u32[]{:S(2)}) collective-permute-start(bf16[512,1280]{1,0:T(8,128)(2,1)S(1)} %convolution_convert_fusion.14), channel_id=1, source_target_pairs={{0,8},{8,0},{1,9},{9,1},{2,10},{10,2},{3,11},{11,3},{4,12},{12,4},... | collective-permute-start | bytes 3932168 | tf_op jit(solution)/shard_map/ppermute | solution.py:190
  520.1 24.0 %collective-permute-start.29 = (bf16[2,320,2560]{2,1,0:T(8,128)(2,1)}, bf16[2,320,2560]{2,1,0:T(8,128)(2,1)S(1)}, u32[]{:S(2)}, u32[]{:S(2)}) collective-permute-start(bf16[2,320,2560]{2,1,0:T(8,128)(2,1)} %dynamic-slice_bitcast_fusion.4), channel_id=1, source_target_pairs={{0,8},{8,0},{1,9},{9,1},{2,10},{10,2},{3,11},{11,3},{4,12},{12,4},... | collective-permute-start | bytes 9830408 | tf_op jit(solution)/shard_map/ppermute | solution.py:190
  588.2 136.7 %reduce-scatter.9.cloned.1.call-start = ((), (), s32[]{:S(2)}) async-start(), calls=%async_computation.9 | async-start | bytes 10240000 | tf_op jit(solution)/shard_map/reduce_scatter | solution.py:295
  588.8 205.0 %reduce-scatter.11.cloned.1.call-start = ((), (), s32[]{:S(2)}) async-start(), calls=%async_computation.10 | async-start | bytes 6144000 | tf_op jit(solution)/shard_map/reduce_scatter | solution.py:295
  600.7 9.1 collective-permute-start.31
  609.4 83.4 %collective-permute-start.35 = (bf16[512,1280]{1,0:T(8,128)(2,1)}, bf16[512,1280]{1,0:T(8,128)(2,1)}, u32[]{:S(2)}, u32[]{:S(2)}) collective-permute-start(bf16[512,1280]{1,0:T(8,128)(2,1)} %convolution_convert_fusion.13), channel_id=1, source_target_pairs={{0,8},{8,0},{1,9},{9,1},{2,10},{10,2},{3,11},{11,3},{4,12},{12,4},... | collective-permute-start | bytes 3932168 | tf_op jit(solution)/shard_map/ppermute | solution.py:190
  625.9 59.3 %collective-permute-start.32 = (bf16[512,1280]{1,0:T(8,128)(2,1)S(1)}, bf16[512,1280]{1,0:T(8,128)(2,1)S(1)}, u32[]{:S(2)}, u32[]{:S(2)}) collective-permute-start(bf16[512,1280]{1,0:T(8,128)(2,1)S(1)} %slice.722), channel_id=1, source_target_pairs={{2,0},{4,2},{6,4},{3,1},{5,3},{7,5},{10,8},{12,10},{14,12},{11,9},... | collective-permute-start | bytes 3932168 | tf_op jit(solution)/shard_map/ppermute | solution.py:204
  688.3 20.0 %collective-permute-start.34 = (bf16[2,320,1920]{2,1,0:T(8,128)(2,1)S(1)}, bf16[2,320,1920]{2,1,0:T(8,128)(2,1)S(1)}, u32[]{:S(2)}, u32[]{:S(2)}) collective-permute-start(bf16[2,320,1920]{2,1,0:T(8,128)(2,1)S(1)} %dynamic-slice_bitcast_fusion.9), channel_id=1, source_target_pairs={{0,8},{8,0},{1,9},{9,1},{2,10},{10,2},{3,11},{11,3},{4,12},{12,4},... | collective-permute-start | bytes 7372808 | tf_op jit(solution)/shard_map/ppermute | solution.py:190
  691.6 33.4 %collective-permute-start.33 = (bf16[512,1280]{1,0:T(8,128)(2,1)}, bf16[512,1280]{1,0:T(8,128)(2,1)}, u32[]{:S(2)}, u32[]{:S(2)}) collective-permute-start(bf16[512,1280]{1,0:T(8,128)(2,1)} %add_convert_fusion.3), channel_id=1, source_target_pairs={{2,0},{4,2},{6,4},{3,1},{5,3},{7,5},{10,8},{12,10},{14,12},{11,9},... | collective-permute-start | bytes 3932168 | tf_op jit(solution)/shard_map/ppermute | solution.py:204
  734.9 153.6 %reduce-scatter.13.cloned.1.call-start = ((), (), s32[]{:S(2)}) async-start(), calls=%async_computation.11 | async-start | bytes 8192000 | tf_op jit(solution)/shard_map/reduce_scatter | solution.py:295
  748.4 36.0 %collective-permute-start.38 = (bf16[2,320,2560]{2,1,0:T(8,128)(2,1)S(1)}, bf16[2,320,2560]{2,1,0:T(8,128)(2,1)S(1)}, u32[]{:S(2)}, u32[]{:S(2)}) collective-permute-start(bf16[2,320,2560]{2,1,0:T(8,128)(2,1)S(1)} %dynamic-slice_bitcast_fusion.3), channel_id=1, source_target_pairs={{0,8},{8,0},{1,9},{9,1},{2,10},{10,2},{3,11},{11,3},{4,12},{12,4},... | collective-permute-start | bytes 9830408 | tf_op jit(solution)/shard_map/ppermute | solution.py:190
  793.8 149.0 %all-reduce.11.cloned.1.call-start = ((), (), s32[]{:S(2)}) async-start(), calls=%async_computation.12 | async-start | bytes 6553600 | tf_op jit(solution)/shard_map/psum | solution.py:563
  808.0 22.9 %collective-permute-start.40 = (bf16[2,320,2560]{2,1,0:T(8,128)(2,1)}, bf16[2,320,2560]{2,1,0:T(8,128)(2,1)S(1)}, u32[]{:S(2)}, u32[]{:S(2)}) collective-permute-start(bf16[2,320,2560]{2,1,0:T(8,128)(2,1)} %dynamic-slice_bitcast_fusion.2), channel_id=1, source_target_pairs={{0,8},{8,0},{1,9},{9,1},{2,10},{10,2},{3,11},{11,3},{4,12},{12,4},... | collective-permute-start | bytes 9830408 | tf_op jit(solution)/shard_map/ppermute | solution.py:190
  814.1 190.8 %reduce-scatter.15.cloned.1.call-start = ((), (), s32[]{:S(2)}) async-start(), calls=%async_computation.13 | async-start | bytes 10240000 | tf_op jit(solution)/shard_map/reduce_scatter | solution.py:295
  820.1 54.7 %collective-permute-start.42 = (bf16[512,1280]{1,0:T(8,128)(2,1)}, bf16[512,1280]{1,0:T(8,128)(2,1)}, u32[]{:S(2)}, u32[]{:S(2)}) collective-permute-start(bf16[512,1280]{1,0:T(8,128)(2,1)} %fusion.45), channel_id=1, source_target_pairs={{0,1},{1,0},{2,3},{3,2},{4,5},{5,4},{6,7},{7,6},{8,9},{9,8},{10,11... | collective-permute-start | bytes 3932168 | tf_op jit(solution)/shard_map/ppermute | solution.py:194
  888.5 151.7 %all-reduce.13.cloned.1.call-start = ((), (), s32[]{:S(2)}) async-start(), calls=%async_computation.14 | async-start | bytes 3276800 | tf_op jit(solution)/shard_map/psum | solution.py:563
  942.8 203.9 %all-reduce.15.cloned.1.call-start = ((), (), s32[]{:S(2)}) async-start(), calls=%async_computation.16 | async-start | bytes 4096000 | tf_op jit(solution)/shard_map/psum | solution.py:563
  945.8 59.0 %collective-permute-start.44 = (bf16[512,1280]{1,0:T(8,128)(2,1)}, bf16[512,1280]{1,0:T(8,128)(2,1)}, u32[]{:S(2)}, u32[]{:S(2)}) collective-permute-start(bf16[512,1280]{1,0:T(8,128)(2,1)} %slice.721), channel_id=1, source_target_pairs={{2,0},{4,2},{6,4},{3,1},{5,3},{7,5},{10,8},{12,10},{14,12},{11,9},... | collective-permute-start | bytes 3932168 | tf_op jit(solution)/shard_map/ppermute | solution.py:204
  1040.2 106.5 %reduce-scatter.17.cloned.1.call-start = ((), (), s32[]{:S(2)}) async-start(), calls=%async_computation.15 | async-start | bytes 6144000 | tf_op jit(solution)/shard_map/reduce_scatter | solution.py:295
  1040.8 167.7 %all-reduce.17.cloned.1.call-start = ((), (), s32[]{:S(2)}) async-start(), calls=%async_computation.17 | async-start | bytes 2457600 | tf_op jit(solution)/shard_map/psum | solution.py:563
  1058.4 52.2 %collective-permute-start.46 = (bf16[512,1280]{1,0:T(8,128)(2,1)S(1)}, bf16[512,1280]{1,0:T(8,128)(2,1)}, u32[]{:S(2)}, u32[]{:S(2)}) collective-permute-start(bf16[512,1280]{1,0:T(8,128)(2,1)S(1)} %add_convert_fusion.2), channel_id=1, source_target_pairs={{2,0},{4,2},{6,4},{3,1},{5,3},{7,5},{10,8},{12,10},{14,12},{11,9},... | collective-permute-start | bytes 3932168 | tf_op jit(solution)/shard_map/ppermute | solution.py:204
  1160.4 52.0 %collective-permute-start.47 = (bf16[512,1280]{1,0:T(8,128)(2,1)}, bf16[512,1280]{1,0:T(8,128)(2,1)}, u32[]{:S(2)}, u32[]{:S(2)}) collective-permute-start(bf16[512,1280]{1,0:T(8,128)(2,1)} %get-tuple-element.212), channel_id=1, source_target_pairs={{0,1},{1,0},{2,3},{3,2},{4,5},{5,4},{6,7},{7,6},{8,9},{9,8},{10,11... | collective-permute-start | bytes 3932168 | tf_op jit(solution)/shard_map/ppermute | solution.py:194
  1164.0 8.4 collective-permute-start.51
  1173.3 12.7 %collective-permute-start.53 = (f32[2,15360]{1,0:T(2,128)S(1)}, f32[2,15360]{1,0:T(2,128)S(1)}, u32[]{:S(2)}, u32[]{:S(2)}) collective-permute-start(f32[2,15360]{1,0:T(2,128)S(1)} %add.457), channel_id=1, source_target_pairs={{2,0},{4,6},{3,1},{5,7},{10,8},{12,14},{11,9},{13,15},{18,16},{20,... | collective-permute-start | bytes 368648 | tf_op jit(solution)/shard_map/ppermute | solution.py:358
  (151 other events, 2046.0 us)
Sparse Core Ops, SparseCore 0:
  13.0 75.0 all-gather.8
  90.5 126.8 all-gather.10
  224.6 72.3 all-gather.12
  307.2 127.9 all-gather.14
  500.3 72.4 reduce-scatter.6
  591.9 85.6 reduce-scatter.8
  735.0 58.6 reduce-scatter.10
  797.4 91.0 reduce-scatter.12
  892.0 84.7 reduce-scatter.14
  1044.4 57.8 reduce-scatter.16
Sparse Core Ops, SparseCore 1:
  25.1 32.6 all-reduce.6
  588.3 85.8 all-reduce.8
  814.2 125.3 all-reduce.10
  942.9 97.3 all-reduce.12
  1042.8 103.9 all-reduce.14
  1149.1 59.4 all-reduce.16

commit v10 on v9

--- a/solution.py
+++ b/solution.py
@@ -582,10 +582,11 @@
         grad_low = narrow(grad_hidden)
         grad_low = jnp.concatenate([grad_low, mate(grad_low)])
         out_swap = scatter_swap(narrow(dot_first(grad_low, activated)), place)
-        grad_pre = narrow(gelu_slope(pre_act, dot_f32(grad_low, w_out_t)))
+        grad_act_in = grad_low
         if not final:
-            grad_pre, out_swap.came = tie(grad_pre, out_swap.came)
-            waiting.append(("out%d" % layer, scatter_sum(join(out_swap))))
+            grad_act_in, grad_out = tie(grad_low, join(out_swap))
+            waiting.append(("out%d" % layer, scatter_sum(grad_out)))
+        grad_pre = narrow(gelu_slope(pre_act, dot_f32(grad_act_in, w_out_t)))
         grad_fc_bias = jnp.sum(wide(grad_pre), axis=0)
         mate_part = dot_second(grad_pre[block_len:], w_fc)
         own_part = dot_second(grad_pre[:block_len], w_fc)
@@ -611,13 +612,14 @@
         )
         grad_mixed, fc_swap.came, proj_swap.came = tie(grad_mixed, fc_swap.came, proj_swap.came)
         grad_mixed, grad_fc = tie(grad_mixed, join(fc_swap, proj_swap))
+        if not final:
+            grad_mixed = advance(grad_mixed, "out%d" % layer)
         grad_packed = attention_backward(packed, mixed, grad_mixed, log_total, low_pos)
         if final:
             grad_packed, far_output, grad_fc = tie(grad_packed, far_output, grad_fc)
             grad_packed, grad_fc = settle((grad_packed, grad_fc), "out%d" % layer)
         else:
-            grad_packed, grad_fc = tie(grad_packed, grad_fc)
-            grad_packed = advance(grad_packed, "out%d" % layer)
+            grad_mixed, grad_fc = tie(grad_mixed, grad_fc)
         waiting.append(("fc%d" % layer, scatter_sum(grad_fc)))
         mate_part = dot_second(grad_packed[1], w_qkv)
         own_part = dot_second(grad_packed[0], w_qkv)

time: 1230 us -> 1220 us (level)
    psum x5, waiting for transfers between devices: 118 us -> 95.5 us  [advance(): last_sum = lax.psum(share, 'ctx')]
    unnamed x305 -> x311, local copies, waits for them, and re-layouts: 80.1 us -> 82.3 us
  transfers between devices with their start and end apart: 70 -> 70, of which waited for: 37 -> 38; matrix products, arithmetic and copies ran while one was open for 35% -> 34% of each run, Pallas kernels for 13% -> 13%
where the time goes in v10:
time: 1220 us; the launch traced here: 1210 us
  waiting for transfers between devices  457 us (37%)
  matrix products  295 us (24%)
  Pallas kernels  160 us (13%)
  local copies, waits for them, and re-layouts  127 us (10%)
  other arithmetic  100 us (8%)
  starting transfers between devices  49.8 us (4%)
  between operations  18.2 us (1%)
    dot_general x24, matrix products, contract(): lax.dot_general(left_side, right_side, (((left_dim,), (right_dim,)), ((),...  187 us
    ppermute x4, waiting for transfers between devices, backward_step(): return lax.ppermute(value, 'ctx', [(i + 1, i) for i in range(count - 1)])  127 us
    dot_general x8, matrix products, dot_f32(): return jnp.dot(left_side, right_side, preferred_element_type=jnp.float32)  107 us
    psum x5, waiting for transfers between devices, advance(): last_sum = lax.psum(share, 'ctx')  95.5 us
    ppermute x4, waiting for transfers between devices, onward(): return lax.ppermute(value, 'ctx', [(i, i + 1) for i in range(count - 1)])  86 us
    unnamed x311, local copies, waits for them, and re-layouts  82.3 us
    pallas_call x2, Pallas kernels, attention_backward(): pl.pallas_call(backward_kernel, grid=(groups, pairs), in_specs=[packed_sp...  80.1 us
    pallas_call x2, Pallas kernels, attention_forward(): pl.pallas_call(forward_kernel, grid=(groups, pairs), in_specs=[pl.BlockSp...  63.5 us
  transfers between devices with their start and end apart: 70, of which 38 were waited for; matrix products, arithmetic and copies ran while one was open for 34% of the time, Pallas kernels for 13%

profile of v10, /device:TPU:0, one launch (start us, length us, event | category | flops | bytes accessed | tf_op | source)
XLA Modules:
  0.0 1207.2 jit_solution(10268654572572327617)
XLA Ops:
  41.2 12.4 %collective-permute-done = bf16[512,1280]{1,0:T(8,128)(2,1)} collective-permute-done((bf16[512,1280]{1,0:T(8,128)(2,1)}, bf16[512,1280]{1,0:T(8,128)(2,1)}, u32[]{:S(2)}, u32[]{:S(2)}) %collective-permute-start) | collective-permute-done | bytes 1310752 | tf_op jit(solution)/shard_map/ppermute | solution.py:199
  62.7 22.8 %collective-permute-done.1 = bf16[512,1280]{1,0:T(8,128)(2,1)S(1)} collective-permute-done((bf16[512,1280]{1,0:T(8,128)(2,1)}, bf16[512,1280]{1,0:T(8,128)(2,1)S(1)}, u32[]{:S(2)}, u32[]{:S(2)}) %collective-permute-start.1) | collective-permute-done | bytes 1310752 | tf_op jit(solution)/shard_map/ppermute | solution.py:199
  123.0 18.6 %add_convert_fusion.1 = bf16[3072,1920]{1,0:T(8,128)(2,1)} fusion(bf16[3072,1280]{1,0:T(8,128)(2,1)S(1)} %copy-done.69, f32[1920]{0:T(1024)S(1)} %reduce.2, bf16[1280,2560]{1,0:T(8,128)(2,1)S(1)} %shard_map.188), kind=kOutput, calls=%fused_computation.3 | convolution fusion | flops 15111290880 | bytes 24584192 | tf_op jit(solution)/shard_map/dot_general | solution.py:299
  141.5 31.7 %shard_map.189 = (bf16[2,512,640]{2,1,0:T(8,128)(2,1)}, f32[2,5,2,512]{3,2,1,0:T(2,128)}) custom-call(bf16[2,1536,1920]{2,1,0:T(8,128)(2,1)} %bitcast.333, s32[2,512,1]{2,1,0:T(8,128)} %subtract_add_fusion.low_ref), custom_call_target="tpu_custom_call" | custom-call | flops 512 | bytes 512 | tf_op jit(solution)/shard_map/pallas_call | solution.py:80
  187.8 29.5 %all-gather.11.cloned.1.call-done = bf16[1280,5120]{1,0:T(8,128)(2,1)} async-done(((bf16[320,5120]{1,0:T(8,128)(2,1)}), bf16[1280,5120]{1,0:T(8,128)(2,1)}) %all-gather.11.cloned.1.call-update) | async-done | bytes 13107216 | tf_op jit(solution)/shard_map/all_gather | solution.py:286
  224.6 10.2 collective-permute-done.12.refs_1_
  247.4 10.9 multiply_convert_fusion.1
  267.8 5.6 fusion.110
  280.0 27.2 %collective-permute-done.15 = bf16[512,1280]{1,0:T(8,128)(2,1)} collective-permute-done((bf16[512,1280]{1,0:T(8,128)(2,1)S(1)}, bf16[512,1280]{1,0:T(8,128)(2,1)}, u32[]{:S(2)}, u32[]{:S(2)}) %collective-permute-start.15) | collective-permute-done | bytes 1310752 | tf_op jit(solution)/shard_map/ppermute | solution.py:199
  309.7 5.7 collective-permute-start.16
  319.7 23.5 %collective-permute-done.16 = bf16[512,1280]{1,0:T(8,128)(2,1)} collective-permute-done((bf16[512,1280]{1,0:T(8,128)(2,1)}, bf16[512,1280]{1,0:T(8,128)(2,1)}, u32[]{:S(2)}, u32[]{:S(2)}) %collective-permute-start.16) | collective-permute-done | bytes 1310752 | tf_op jit(solution)/shard_map/ppermute | solution.py:199
  350.4 18.7 %add_convert_fusion = bf16[3072,1920]{1,0:T(8,128)(2,1)} fusion(bf16[3072,1280]{1,0:T(8,128)(2,1)S(1)} %constant_dynamic-update-slice_fusion.23, f32[1920]{0:T(1024)S(1)} %reduce.10, bf16[1280,2560]{1,0:T(8,128)(2,1)S(1)} %bitcast.318), kind=kOutput, calls=%fused_computation.2 | convolution fusion | flops 15111290880 | bytes 24584192 | tf_op jit(solution)/shard_map/dot_general | solution.py:299
  369.1 31.8 %shard_map.193 = (bf16[2,512,640]{2,1,0:T(8,128)(2,1)}, f32[2,5,2,512]{3,2,1,0:T(2,128)}) custom-call(bf16[2,1536,1920]{2,1,0:T(8,128)(2,1)} %bitcast.335, s32[2,512,1]{2,1,0:T(8,128)} %subtract_add_fusion.low_ref), custom_call_target="tpu_custom_call" | custom-call | flops 512 | bytes 512 | tf_op jit(solution)/shard_map/pallas_call | solution.py:80
  414.1 21.3 %all-gather.15.cloned.1.call-done = bf16[1280,5120]{1,0:T(8,128)(2,1)} async-done(((bf16[320,5120]{1,0:T(8,128)(2,1)}), bf16[1280,5120]{1,0:T(8,128)(2,1)}) %all-gather.15.cloned.1.call-update) | async-done | bytes 13107216 | tf_op jit(solution)/shard_map/all_gather | solution.py:286
  443.4 7.3 collective-permute-done.24.refs_1_
  451.5 11.2 multiply_convert_fusion
  462.7 7.4 convolution_convert_fusion.3
  473.2 6.5 collective-permute-done.25.refs_1_
  489.5 18.0 %convert_reduce_fusion.2 = (f32[2560]{0:T(1024)}, bf16[1024,2560]{1,0:T(8,128)(2,1)S(1)}) fusion(f32[1024,2560]{1,0:T(8,128)} %get-tuple-element.247, f32[2560]{0:T(1024)S(1)} %get-tuple-element.198, bf16[1024,1280]{1,0:T(8,128)(2,1)S(1)} %copy-done.53, bf16[1280,2560]{1,0:T(8,128)(2,1)S(1)} %shard_map.196), kind=kOutput, calls=%fused_computation.26 | convolution fusion | flops 6771176960 | bytes 24924160 | tf_op jit(solution)/shard_map/dot_general | solution.py:299
  513.6 10.3 convolution_convert_fusion.2
  526.9 7.9 multiply_reduce_fusion
  557.0 40.2 %shard_map.198 = bf16[2,1536,1920]{2,1,0:T(8,128)(2,1)} custom-call(bf16[2,1536,1920]{2,1,0:T(8,128)(2,1)} %bitcast.336, bf16[2,512,640]{2,1,0:T(8,128)(2,1)} %get-tuple-element.103.mixed_ref, bf16[2,512,640]{2,1,0:T(8,128)(2,1)} %bitcast.343, f32[2,5,2,512]{3,2,1,0:T(2,128)} %get-tuple-element.115.total_ref, s32[2,1,512]{2,1,0:T(1,128)} %subtract_add_fusion.1.low_ref), custom_call_target="tpu_custom_call" | custom-call | flops 512 | bytes 512 | tf_op jit(solution)/shard_map/pallas_call | solution.py:163
  597.2 10.5 convolution_convert_fusion.7
  607.8 8.6 convolution_convert_fusion.13
  617.1 12.0 convolution_add_fusion.1
  632.3 20.1 %convolution_convert_fusion.5 = bf16[1280,1920]{1,0:T(8,128)(2,1)} fusion(bf16[3072,1280]{1,0:T(8,128)(2,1)} %copy-done.70, bf16[3072,1920]{1,0:T(8,128)(2,1)S(1)} %bitcast.332), kind=kOutput, calls=%fused_computation.33 | convolution fusion | flops 15101952000 | bytes 24576000 | tf_op jit(solution)/shard_map/dot_general | solution.py:15
  652.4 11.3 collective-permute-done.32
  671.4 8.7 fusion.41
  680.1 6.6 convert_reduce_fusion.1
  689.5 14.0 %collective-permute-done.33 = bf16[512,1280]{1,0:T(8,128)(2,1)} collective-permute-done((bf16[512,1280]{1,0:T(8,128)(2,1)}, bf16[512,1280]{1,0:T(8,128)(2,1)}, u32[]{:S(2)}, u32[]{:S(2)}) %collective-permute-start.33) | collective-permute-done | bytes 1310752 | tf_op jit(solution)/shard_map/ppermute | solution.py:204
  716.4 10.2 convolution_convert_fusion.1
  727.4 20.0 %convert_reduce_fusion.3 = (f32[2560]{0:T(1024)S(1)}, bf16[1024,2560]{1,0:T(8,128)(2,1)}) fusion(f32[1024,2560]{1,0:T(8,128)} %get-tuple-element.241, f32[2560]{0:T(1024)S(1)} %copy-done.102, bf16[1280,2560]{1,0:T(8,128)(2,1)} %copy-done.20, bf16[512,1280]{1,0:T(8,128)(2,1)} %copy-done.110, bf16[512,1280]{1,0:T(8,128)(2,1)S(1)} %convert_element_type.244), kind=kOutput, calls=%fused_computation.27 | convolution fusion | flops 6776419840 | bytes 24924160 | tf_op jit(solution)/shard_map/dot_general | solution.py:299
  755.8 6.9 convolution_add_fusion.4
  766.0 5.6 reduce-scatter.11.cloned.1.call-done
  771.7 9.8 convolution_convert_fusion
  812.5 39.9 %shard_map.202 = bf16[2,1536,1920]{2,1,0:T(8,128)(2,1)} custom-call(bf16[2,1536,1920]{2,1,0:T(8,128)(2,1)} %bitcast.334, bf16[2,512,640]{2,1,0:T(8,128)(2,1)} %get-tuple-element.94.mixed_ref, bf16[2,512,640]{2,1,0:T(8,128)(2,1)} %bitcast.344, f32[2,5,2,512]{3,2,1,0:T(2,128)} %get-tuple-element.139.total_ref, s32[2,1,512]{2,1,0:T(1,128)} %subtract_add_fusion.1.low_ref), custom_call_target="tpu_custom_call" | custom-call | flops 512 | bytes 512 | tf_op jit(solution)/shard_map/pallas_call | solution.py:163
  852.4 13.9 %reduce-scatter.13.cloned.1.call-done = bf16[320,2560]{1,0:T(8,128)(2,1)} async-done(((bf16[1280,2560]{1,0:T(8,128)(2,1)}), bf16[320,2560]{1,0:T(8,128)(2,1)}) %reduce-scatter.13.cloned.1.call-update) | async-done | bytes 1638416 | tf_op jit(solution)/shard_map/reduce_scatter | solution.py:295
  866.4 12.0 convolution_convert_fusion.6
  878.6 6.8 collective-permute-done.43
  885.4 13.5 %convolution_add_fusion = f32[1536,1280]{1,0:T(8,128)} fusion(bf16[1536,1280]{1,0:T(8,128)(2,1)} %collective-permute-done.43, bf16[2,1536,1920]{2,1,0:T(8,128)(2,1)S(1)} %copy-done.29, bf16[1280,2560]{1,0:T(8,128)(2,1)} %copy-done.18), kind=kOutput, calls=%fused_computation.30 | convolution fusion | flops 7553679360 | bytes 22609920 | tf_op jit(solution)/shard_map/dot_general | solution.py:15
  898.9 17.7 %convolution_convert_fusion.4 = bf16[1280,1920]{1,0:T(8,128)(2,1)S(1)} fusion(bf16[3072,1280]{1,0:T(8,128)(2,1)S(1)} %bitcast.352, bf16[3072,1920]{1,0:T(8,128)(2,1)S(1)} %bitcast.330), kind=kOutput, calls=%fused_computation.32 | convolution fusion | flops 15101952000 | bytes 24576000 | tf_op jit(solution)/shard_map/dot_general | solution.py:15
  930.8 52.2 %collective-permute-done.44 = bf16[512,1280]{1,0:T(8,128)(2,1)} collective-permute-done((bf16[512,1280]{1,0:T(8,128)(2,1)}, bf16[512,1280]{1,0:T(8,128)(2,1)}, u32[]{:S(2)}, u32[]{:S(2)}) %collective-permute-start.44) | collective-permute-done | bytes 1310752 | tf_op jit(solution)/shard_map/ppermute | solution.py:204
  982.9 35.3 %all-reduce.13.cloned.1.call-done = bf16[320,2560]{1,0:T(8,128)(2,1)} async-done(((bf16[320,2560]{1,0:T(8,128)(2,1)}), bf16[320,2560]{1,0:T(8,128)(2,1)}) %all-reduce.13.cloned.1.call-update) | async-done | bytes 1638416 | tf_op jit(solution)/shard_map/psum | solution.py:563
  1023.5 6.5 convert_reduce_fusion
  1039.5 49.2 %collective-permute-done.46 = bf16[512,1280]{1,0:T(8,128)(2,1)} collective-permute-done((bf16[512,1280]{1,0:T(8,128)(2,1)S(1)}, bf16[512,1280]{1,0:T(8,128)(2,1)}, u32[]{:S(2)}, u32[]{:S(2)}) %collective-permute-start.46) | collective-permute-done | bytes 1310752 | tf_op jit(solution)/shard_map/ppermute | solution.py:204
  1088.7 40.2 %all-reduce.15.cloned.1.call-done = bf16[320,3200]{1,0:T(8,128)(2,1)} async-done(((bf16[320,3200]{1,0:T(8,128)(2,1)}), bf16[320,3200]{1,0:T(8,128)(2,1)}) %all-reduce.15.cloned.1.call-update) | async-done | bytes 2048016 | tf_op jit(solution)/shard_map/psum | solution.py:563
  1158.1 10.1 collective-permute-done.53
  1171.0 19.9 %all-reduce.17.cloned.1.call-done.first_ref = bf16[320,1920]{1,0:T(8,128)(2,1)} async-done(((bf16[320,1920]{1,0:T(8,128)(2,1)}), bf16[320,1920]{1,0:T(8,128)(2,1)}) %all-reduce.17.cloned.1.call-update) | async-done | bytes 1228816 | tf_op jit(solution)/shard_map/psum | solution.py:563
  (625 shorter events, 348.9 us)
Async XLA Ops:
  8.0 80.0 %all-gather.9.cloned.1.call-start = ((), (), s32[]{:S(2)}) async-start(), calls=%async_computation.18 | async-start | bytes 8192000 | tf_op jit(solution)/shard_map/all_gather | solution.py:286
  12.9 100.4 %all-reduce.7.cloned.1.call-start = ((), (), s32[]{:S(2)}) async-start(), calls=%async_computation.6 | async-start | bytes 163840 | tf_op jit(solution)/shard_map/psum | solution.py:458
  12.9 24.9 %collective-permute-start.9 = (s32[4]{0:T(128)S(1)}, s32[4]{0:T(128)S(1)}, u32[]{:S(2)}, u32[]{:S(2)}) collective-permute-start(s32[4]{0:T(128)S(1)} %fusion.143), channel_id=1, source_target_pairs={{0,8},{8,0},{1,9},{9,1},{2,10},{10,2},{3,11},{11,3},{4,12},{12,4},... | collective-permute-start | bytes 56 | tf_op jit(solution)/shard_map/ppermute | solution.py:190
  13.5 25.8 %collective-permute-start.2 = (bf16[12,320]{1,0:T(8,128)(2,1)S(1)}, bf16[12,320]{1,0:T(8,128)(2,1)S(1)}, u32[]{:S(2)}, u32[]{:S(2)}) collective-permute-start(bf16[12,320]{1,0:T(8,128)(2,1)S(1)} %reshape.357), channel_id=1, source_target_pairs={{0,8},{8,0},{1,9},{9,1},{2,10},{10,2},{3,11},{11,3},{4,12},{12,4},... | collective-permute-start | bytes 23048 | tf_op jit(solution)/shard_map/ppermute | solution.py:190
  13.7 27.4 %collective-permute-start.8 = (bf16[2,3840]{1,0:T(2,128)(2,1)S(1)}, bf16[2,3840]{1,0:T(2,128)(2,1)S(1)}, u32[]{:S(2)}, u32[]{:S(2)}) collective-permute-start(bf16[2,3840]{1,0:T(2,128)(2,1)S(1)} %constant_dynamic-update-slice_fusion.6), channel_id=1, source_target_pairs={{0,1},{1,0},{2,3},{3,2},{4,5},{5,4},{6,7},{7,6},{8,9},{9,8},{10,11... | collective-permute-start | bytes 46088 | tf_op jit(solution)/shard_map/ppermute | solution.py:194
  19.3 34.3 %collective-permute-start = (bf16[512,1280]{1,0:T(8,128)(2,1)}, bf16[512,1280]{1,0:T(8,128)(2,1)}, u32[]{:S(2)}, u32[]{:S(2)}) collective-permute-start(bf16[512,1280]{1,0:T(8,128)(2,1)} %get-tuple-element.217), channel_id=1, source_target_pairs={{0,2},{2,4},{4,6},{1,3},{3,5},{5,7},{8,10},{10,12},{12,14},{9,11},... | collective-permute-start | bytes 3932168 | tf_op jit(solution)/shard_map/ppermute | solution.py:199
  25.0 192.4 %all-gather.11.cloned.1.call-start = ((), (), s32[]{:S(2)}) async-start(), calls=%async_computation.19 | async-start | bytes 16384000 | tf_op jit(solution)/shard_map/all_gather | solution.py:286
  39.5 18.9 %collective-permute-start.3 = (bf16[12,640]{1,0:T(8,128)(2,1)S(1)}, bf16[12,640]{1,0:T(8,128)(2,1)S(1)}, u32[]{:S(2)}, u32[]{:S(2)}) collective-permute-start(bf16[12,640]{1,0:T(8,128)(2,1)S(1)} %select_n.135), channel_id=1, source_target_pairs={{0,16},{16,0},{1,17},{17,1},{2,18},{18,2},{3,19},{19,3},{4,20},{20... | collective-permute-start | bytes 46088 | tf_op jit(solution)/shard_map/ppermute | solution.py:315
  53.6 253.7 %all-gather.13.cloned.1.call-start = ((), (), s32[]{:S(2)}) async-start(), calls=%async_computation.20 | async-start | bytes 8192000 | tf_op jit(solution)/shard_map/all_gather | solution.py:286
  53.9 31.6 %collective-permute-start.1 = (bf16[512,1280]{1,0:T(8,128)(2,1)}, bf16[512,1280]{1,0:T(8,128)(2,1)S(1)}, u32[]{:S(2)}, u32[]{:S(2)}) collective-permute-start(bf16[512,1280]{1,0:T(8,128)(2,1)} %collective-permute-done), channel_id=1, source_target_pairs={{0,2},{2,4},{4,6},{1,3},{3,5},{5,7},{8,10},{10,12},{12,14},{9,11},... | collective-permute-start | bytes 3932168 | tf_op jit(solution)/shard_map/ppermute | solution.py:199
  91.9 21.3 %collective-permute-start.7 = (bf16[2,320,2560]{2,1,0:T(8,128)(2,1)}, bf16[2,320,2560]{2,1,0:T(8,128)(2,1)S(1)}, u32[]{:S(2)}, u32[]{:S(2)}) collective-permute-start(bf16[2,320,2560]{2,1,0:T(8,128)(2,1)} %dynamic-slice_bitcast_fusion.7), channel_id=1, source_target_pairs={{0,8},{8,0},{1,9},{9,1},{2,10},{10,2},{3,11},{11,3},{4,12},{12,4},... | collective-permute-start | bytes 9830408 | tf_op jit(solution)/shard_map/ppermute | solution.py:190
  97.7 10.5 collective-permute-start.5
  98.3 7.5 collective-permute-start.4
  224.0 10.8 collective-permute-start.12
  224.0 19.7 %collective-permute-start.13 = (bf16[2,320,2560]{2,1,0:T(8,128)(2,1)}, bf16[2,320,2560]{2,1,0:T(8,128)(2,1)S(1)}, u32[]{:S(2)}, u32[]{:S(2)}) collective-permute-start(bf16[2,320,2560]{2,1,0:T(8,128)(2,1)} %get-tuple-element.225), channel_id=1, source_target_pairs={{0,8},{8,0},{1,9},{9,1},{2,10},{10,2},{3,11},{11,3},{4,12},{12,4},... | collective-permute-start | bytes 9830408 | tf_op jit(solution)/shard_map/ppermute | solution.py:190
  224.5 210.9 %all-gather.15.cloned.1.call-start = ((), (), s32[]{:S(2)}) async-start(), calls=%async_computation.21 | async-start | bytes 16384000 | tf_op jit(solution)/shard_map/all_gather | solution.py:286
  275.4 31.8 %collective-permute-start.15 = (bf16[512,1280]{1,0:T(8,128)(2,1)S(1)}, bf16[512,1280]{1,0:T(8,128)(2,1)}, u32[]{:S(2)}, u32[]{:S(2)}) collective-permute-start(bf16[512,1280]{1,0:T(8,128)(2,1)S(1)} %add_convert_fusion.5), channel_id=1, source_target_pairs={{0,2},{2,4},{4,6},{1,3},{3,5},{5,7},{8,10},{10,12},{12,14},{9,11},... | collective-permute-start | bytes 3932168 | tf_op jit(solution)/shard_map/ppermute | solution.py:199
  307.3 248.4 %reduce-scatter.7.cloned.1.call-start = ((), (), s32[]{:S(2)}) async-start(), calls=%async_computation.7 | async-start | bytes 8192000 | tf_op jit(solution)/shard_map/reduce_scatter | solution.py:295
  309.7 33.5 %collective-permute-start.16 = (bf16[512,1280]{1,0:T(8,128)(2,1)}, bf16[512,1280]{1,0:T(8,128)(2,1)}, u32[]{:S(2)}, u32[]{:S(2)}) collective-permute-start(bf16[512,1280]{1,0:T(8,128)(2,1)} %collective-permute-done.15), channel_id=1, source_target_pairs={{0,2},{2,4},{4,6},{1,3},{3,5},{5,7},{8,10},{10,12},{12,14},{9,11},... | collective-permute-start | bytes 3932168 | tf_op jit(solution)/shard_map/ppermute | solution.py:199
  442.8 7.9 collective-permute-start.24
  442.9 19.9 %collective-permute-start.22 = (bf16[512,1280]{1,0:T(8,128)(2,1)S(1)}, bf16[512,1280]{1,0:T(8,128)(2,1)S(1)}, u32[]{:S(2)}, u32[]{:S(2)}) collective-permute-start(bf16[512,1280]{1,0:T(8,128)(2,1)S(1)} %fusion.142), channel_id=1, source_target_pairs={{0,8},{8,0},{1,9},{9,1},{2,10},{10,2},{3,11},{11,3},{4,12},{12,4},... | collective-permute-start | bytes 3932168 | tf_op jit(solution)/shard_map/ppermute | solution.py:190
  470.4 9.3 collective-permute-start.25
  470.6 12.4 %collective-permute-start.26 = (bf16[2,320,2560]{2,1,0:T(8,128)(2,1)}, bf16[2,320,2560]{2,1,0:T(8,128)(2,1)S(1)}, u32[]{:S(2)}, u32[]{:S(2)}) collective-permute-start(bf16[2,320,2560]{2,1,0:T(8,128)(2,1)} %get-tuple-element.222), channel_id=1, source_target_pairs={{0,8},{8,0},{1,9},{9,1},{2,10},{10,2},{3,11},{11,3},{4,12},{12,4},... | collective-permute-start | bytes 9830408 | tf_op jit(solution)/shard_map/ppermute | solution.py:190
  483.0 169.4 %all-reduce.9.cloned.1.call-start = ((), (), s32[]{:S(2)}) async-start(), calls=%async_computation.8 | async-start | bytes 3276800 | tf_op jit(solution)/shard_map/psum | solution.py:563
  513.4 12.9 %collective-permute-start.27 = (bf16[512,1280]{1,0:T(8,128)(2,1)S(1)}, bf16[512,1280]{1,0:T(8,128)(2,1)S(1)}, u32[]{:S(2)}, u32[]{:S(2)}) collective-permute-start(bf16[512,1280]{1,0:T(8,128)(2,1)S(1)} %convolution_convert_fusion.14), channel_id=1, source_target_pairs={{0,8},{8,0},{1,9},{9,1},{2,10},{10,2},{3,11},{11,3},{4,12},{12,4},... | collective-permute-start | bytes 3932168 | tf_op jit(solution)/shard_map/ppermute | solution.py:190
  525.8 23.7 %collective-permute-start.29 = (bf16[2,320,2560]{2,1,0:T(8,128)(2,1)}, bf16[2,320,2560]{2,1,0:T(8,128)(2,1)S(1)}, u32[]{:S(2)}, u32[]{:S(2)}) collective-permute-start(bf16[2,320,2560]{2,1,0:T(8,128)(2,1)} %dynamic-slice_bitcast_fusion.4), channel_id=1, source_target_pairs={{0,8},{8,0},{1,9},{9,1},{2,10},{10,2},{3,11},{11,3},{4,12},{12,4},... | collective-permute-start | bytes 9830408 | tf_op jit(solution)/shard_map/ppermute | solution.py:190
  555.7 147.8 %reduce-scatter.9.cloned.1.call-start = ((), (), s32[]{:S(2)}) async-start(), calls=%async_computation.9 | async-start | bytes 10240000 | tf_op jit(solution)/shard_map/reduce_scatter | solution.py:295
  556.3 215.3 %reduce-scatter.11.cloned.1.call-start = ((), (), s32[]{:S(2)}) async-start(), calls=%async_computation.10 | async-start | bytes 6144000 | tf_op jit(solution)/shard_map/reduce_scatter | solution.py:295
  607.8 9.3 collective-permute-start.31
  616.4 55.0 %collective-permute-start.35 = (bf16[512,1280]{1,0:T(8,128)(2,1)}, bf16[512,1280]{1,0:T(8,128)(2,1)}, u32[]{:S(2)}, u32[]{:S(2)}) collective-permute-start(bf16[512,1280]{1,0:T(8,128)(2,1)} %convolution_convert_fusion.13), channel_id=1, source_target_pairs={{0,8},{8,0},{1,9},{9,1},{2,10},{10,2},{3,11},{11,3},{4,12},{12,4},... | collective-permute-start | bytes 3932168 | tf_op jit(solution)/shard_map/ppermute | solution.py:190
  631.0 32.7 %collective-permute-start.32 = (bf16[512,1280]{1,0:T(8,128)(2,1)S(1)}, bf16[512,1280]{1,0:T(8,128)(2,1)S(1)}, u32[]{:S(2)}, u32[]{:S(2)}) collective-permute-start(bf16[512,1280]{1,0:T(8,128)(2,1)S(1)} %slice.722), channel_id=1, source_target_pairs={{2,0},{4,2},{6,4},{3,1},{5,3},{7,5},{10,8},{12,10},{14,12},{11,9},... | collective-permute-start | bytes 3932168 | tf_op jit(solution)/shard_map/ppermute | solution.py:204
  666.8 19.9 %collective-permute-start.34 = (bf16[2,320,1920]{2,1,0:T(8,128)(2,1)S(1)}, bf16[2,320,1920]{2,1,0:T(8,128)(2,1)S(1)}, u32[]{:S(2)}, u32[]{:S(2)}) collective-permute-start(bf16[2,320,1920]{2,1,0:T(8,128)(2,1)S(1)} %dynamic-slice_bitcast_fusion.9), channel_id=1, source_target_pairs={{0,8},{8,0},{1,9},{9,1},{2,10},{10,2},{3,11},{11,3},{4,12},{12,4},... | collective-permute-start | bytes 7372808 | tf_op jit(solution)/shard_map/ppermute | solution.py:190
  670.1 33.4 %collective-permute-start.33 = (bf16[512,1280]{1,0:T(8,128)(2,1)}, bf16[512,1280]{1,0:T(8,128)(2,1)}, u32[]{:S(2)}, u32[]{:S(2)}) collective-permute-start(bf16[512,1280]{1,0:T(8,128)(2,1)} %add_convert_fusion.3), channel_id=1, source_target_pairs={{2,0},{4,2},{6,4},{3,1},{5,3},{7,5},{10,8},{12,10},{14,12},{11,9},... | collective-permute-start | bytes 3932168 | tf_op jit(solution)/shard_map/ppermute | solution.py:204
  713.4 152.9 %reduce-scatter.13.cloned.1.call-start = ((), (), s32[]{:S(2)}) async-start(), calls=%async_computation.11 | async-start | bytes 8192000 | tf_op jit(solution)/shard_map/reduce_scatter | solution.py:295
  726.9 35.8 %collective-permute-start.38 = (bf16[2,320,2560]{2,1,0:T(8,128)(2,1)S(1)}, bf16[2,320,2560]{2,1,0:T(8,128)(2,1)S(1)}, u32[]{:S(2)}, u32[]{:S(2)}) collective-permute-start(bf16[2,320,2560]{2,1,0:T(8,128)(2,1)S(1)} %dynamic-slice_bitcast_fusion.3), channel_id=1, source_target_pairs={{0,8},{8,0},{1,9},{9,1},{2,10},{10,2},{3,11},{11,3},{4,12},{12,4},... | collective-permute-start | bytes 9830408 | tf_op jit(solution)/shard_map/ppermute | solution.py:190
  771.6 149.2 %all-reduce.11.cloned.1.call-start = ((), (), s32[]{:S(2)}) async-start(), calls=%async_computation.12 | async-start | bytes 6553600 | tf_op jit(solution)/shard_map/psum | solution.py:563
  785.9 22.7 %collective-permute-start.40 = (bf16[2,320,2560]{2,1,0:T(8,128)(2,1)}, bf16[2,320,2560]{2,1,0:T(8,128)(2,1)S(1)}, u32[]{:S(2)}, u32[]{:S(2)}) collective-permute-start(bf16[2,320,2560]{2,1,0:T(8,128)(2,1)} %dynamic-slice_bitcast_fusion.2), channel_id=1, source_target_pairs={{0,8},{8,0},{1,9},{9,1},{2,10},{10,2},{3,11},{11,3},{4,12},{12,4},... | collective-permute-start | bytes 9830408 | tf_op jit(solution)/shard_map/ppermute | solution.py:190
  791.9 191.0 %reduce-scatter.15.cloned.1.call-start = ((), (), s32[]{:S(2)}) async-start(), calls=%async_computation.13 | async-start | bytes 10240000 | tf_op jit(solution)/shard_map/reduce_scatter | solution.py:295
  797.7 54.7 %collective-permute-start.42 = (bf16[512,1280]{1,0:T(8,128)(2,1)}, bf16[512,1280]{1,0:T(8,128)(2,1)}, u32[]{:S(2)}, u32[]{:S(2)}) collective-permute-start(bf16[512,1280]{1,0:T(8,128)(2,1)} %fusion.41), channel_id=1, source_target_pairs={{0,1},{1,0},{2,3},{3,2},{4,5},{5,4},{6,7},{7,6},{8,9},{9,8},{10,11... | collective-permute-start | bytes 3932168 | tf_op jit(solution)/shard_map/ppermute | solution.py:194
  866.3 151.9 %all-reduce.13.cloned.1.call-start = ((), (), s32[]{:S(2)}) async-start(), calls=%async_computation.14 | async-start | bytes 3276800 | tf_op jit(solution)/shard_map/psum | solution.py:563
  920.8 208.2 %all-reduce.15.cloned.1.call-start = ((), (), s32[]{:S(2)}) async-start(), calls=%async_computation.16 | async-start | bytes 4096000 | tf_op jit(solution)/shard_map/psum | solution.py:563
  923.8 59.1 %collective-permute-start.44 = (bf16[512,1280]{1,0:T(8,128)(2,1)}, bf16[512,1280]{1,0:T(8,128)(2,1)}, u32[]{:S(2)}, u32[]{:S(2)}) collective-permute-start(bf16[512,1280]{1,0:T(8,128)(2,1)} %slice.721), channel_id=1, source_target_pairs={{2,0},{4,2},{6,4},{3,1},{5,3},{7,5},{10,8},{12,10},{14,12},{11,9},... | collective-permute-start | bytes 3932168 | tf_op jit(solution)/shard_map/ppermute | solution.py:204
  1018.4 110.6 %reduce-scatter.17.cloned.1.call-start = ((), (), s32[]{:S(2)}) async-start(), calls=%async_computation.15 | async-start | bytes 6144000 | tf_op jit(solution)/shard_map/reduce_scatter | solution.py:295
  1019.0 171.9 %all-reduce.17.cloned.1.call-start = ((), (), s32[]{:S(2)}) async-start(), calls=%async_computation.17 | async-start | bytes 2457600 | tf_op jit(solution)/shard_map/psum | solution.py:563
  1032.5 56.2 %collective-permute-start.46 = (bf16[512,1280]{1,0:T(8,128)(2,1)S(1)}, bf16[512,1280]{1,0:T(8,128)(2,1)}, u32[]{:S(2)}, u32[]{:S(2)}) collective-permute-start(bf16[512,1280]{1,0:T(8,128)(2,1)S(1)} %add_convert_fusion.2), channel_id=1, source_target_pairs={{2,0},{4,2},{6,4},{3,1},{5,3},{7,5},{10,8},{12,10},{14,12},{11,9},... | collective-permute-start | bytes 3932168 | tf_op jit(solution)/shard_map/ppermute | solution.py:204
  1142.7 52.0 %collective-permute-start.47 = (bf16[512,1280]{1,0:T(8,128)(2,1)}, bf16[512,1280]{1,0:T(8,128)(2,1)}, u32[]{:S(2)}, u32[]{:S(2)}) collective-permute-start(bf16[512,1280]{1,0:T(8,128)(2,1)} %get-tuple-element.212), channel_id=1, source_target_pairs={{0,1},{1,0},{2,3},{3,2},{4,5},{5,4},{6,7},{7,6},{8,9},{9,8},{10,11... | collective-permute-start | bytes 3932168 | tf_op jit(solution)/shard_map/ppermute | solution.py:194
  1146.2 8.4 collective-permute-start.51
  1155.6 12.7 %collective-permute-start.53 = (f32[2,15360]{1,0:T(2,128)S(1)}, f32[2,15360]{1,0:T(2,128)S(1)}, u32[]{:S(2)}, u32[]{:S(2)}) collective-permute-start(f32[2,15360]{1,0:T(2,128)S(1)} %add.457), channel_id=1, source_target_pairs={{2,0},{4,6},{3,1},{5,7},{10,8},{12,14},{11,9},{13,15},{18,16},{20,... | collective-permute-start | bytes 368648 | tf_op jit(solution)/shard_map/ppermute | solution.py:358
  (154 other events, 2081.9 us)
Sparse Core Ops, SparseCore 0:
  13.0 75.0 all-gather.8
  90.5 126.8 all-gather.10
  224.6 72.3 all-gather.12
  307.4 127.9 all-gather.14
  483.1 72.4 reduce-scatter.6
  559.4 84.7 reduce-scatter.8
  713.5 58.0 reduce-scatter.10
  775.2 91.0 reduce-scatter.12
  869.8 84.7 reduce-scatter.14
  1022.5 57.8 reduce-scatter.16
Sparse Core Ops, SparseCore 1:
  25.0 32.6 all-reduce.6
  555.8 70.9 all-reduce.8
  792.0 125.3 all-reduce.10
  920.9 97.3 all-reduce.12
  1020.8 108.1 all-reduce.14
  1131.4 59.4 all-reduce.16

commit v11 on v10

--- a/solution.py
+++ b/solution.py
@@ -248,8 +248,13 @@
     def __init__(self, blocks, place, column=0, width=None):
         self.place, self.blocks, self.column = place, blocks, column
         width = blocks.shape[3] if width is None else width
-        other = lax.dynamic_index_in_dim(blocks, 1 - place.core, 1, False)
-        self.came = mate(other[..., column * width : (column + 1) * width])
+        zero = jnp.int32(0)
+        other = lax.dynamic_slice(
+            blocks,
+            (zero, (1 - place.core).astype(jnp.int32), zero, jnp.int32(column * width)),
+            (blocks.shape[0], 1, blocks.shape[2], width),
+        )
+        self.came = mate(other[:, 0])
 
 
 def join(*swaps):

time: 1220 us -> 1210 us (level)
    unnamed x311 -> x305, local copies, waits for them, and re-layouts: 82.3 us -> 82.5 us
  transfers between devices with their start and end apart: 70 -> 70, of which waited for: 38 -> 38; matrix products, arithmetic and copies ran while one was open for 34% -> 35% of each run, Pallas kernels for 13% -> 13%
where the time goes in v11:
time: 1210 us; the launch traced here: 1200 us
  waiting for transfers between devices  454 us (38%)
  matrix products  295 us (24%)
  Pallas kernels  161 us (13%)
  local copies, waits for them, and re-layouts  124 us (10%)
  other arithmetic  101 us (8%)
  starting transfers between devices  49.7 us (4%)
  between operations  18.1 us (1%)
    dot_general x24, matrix products, contract(): lax.dot_general(left_side, right_side, (((left_dim,), (right_dim,)), ((),...  188 us
    ppermute x4, waiting for transfers between devices, backward_step(): return lax.ppermute(value, 'ctx', [(i + 1, i) for i in range(count - 1)])  126 us
    dot_general x8, matrix products, dot_f32(): return jnp.dot(left_side, right_side, preferred_element_type=jnp.float32)  108 us
    psum x5, waiting for transfers between devices, advance(): last_sum = lax.psum(share, 'ctx')  95.4 us
    ppermute x4, waiting for transfers between devices, onward(): return lax.ppermute(value, 'ctx', [(i, i + 1) for i in range(count - 1)])  86 us
    unnamed x305, local copies, waits for them, and re-layouts  82.5 us
    pallas_call x2, Pallas kernels, attention_backward(): pl.pallas_call(backward_kernel, grid=(groups, pairs), in_specs=[packed_sp...  80.3 us
    pallas_call x2, Pallas kernels, attention_forward(): pl.pallas_call(forward_kernel, grid=(groups, pairs), in_specs=[pl.BlockSp...  63.5 us
  transfers between devices with their start and end apart: 70, of which 38 were waited for; matrix products, arithmetic and copies ran while one was open for 35% of the time, Pallas kernels for 13%

profile of v11, /device:TPU:0, one launch (start us, length us, event | category | flops | bytes accessed | tf_op | source)
XLA Modules:
  0.0 1202.4 jit_solution(14584501367350739573)
XLA Ops:
  41.2 12.3 %collective-permute-done = bf16[512,1280]{1,0:T(8,128)(2,1)} collective-permute-done((bf16[512,1280]{1,0:T(8,128)(2,1)}, bf16[512,1280]{1,0:T(8,128)(2,1)}, u32[]{:S(2)}, u32[]{:S(2)}) %collective-permute-start) | collective-permute-done | bytes 1310752 | tf_op jit(solution)/shard_map/ppermute | solution.py:199
  62.7 22.8 %collective-permute-done.1 = bf16[512,1280]{1,0:T(8,128)(2,1)S(1)} collective-permute-done((bf16[512,1280]{1,0:T(8,128)(2,1)}, bf16[512,1280]{1,0:T(8,128)(2,1)S(1)}, u32[]{:S(2)}, u32[]{:S(2)}) %collective-permute-start.1) | collective-permute-done | bytes 1310752 | tf_op jit(solution)/shard_map/ppermute | solution.py:199
  123.0 18.6 %add_convert_fusion.1 = bf16[3072,1920]{1,0:T(8,128)(2,1)} fusion(bf16[3072,1280]{1,0:T(8,128)(2,1)S(1)} %copy-done.70, f32[1920]{0:T(1024)S(1)} %reduce.2, bf16[1280,2560]{1,0:T(8,128)(2,1)S(1)} %shard_map.188), kind=kOutput, calls=%fused_computation.3 | convolution fusion | flops 15111290880 | bytes 24584192 | tf_op jit(solution)/shard_map/dot_general | solution.py:304
  141.6 31.7 %shard_map.189 = (bf16[2,512,640]{2,1,0:T(8,128)(2,1)}, f32[2,5,2,512]{3,2,1,0:T(2,128)}) custom-call(bf16[2,1536,1920]{2,1,0:T(8,128)(2,1)} %bitcast.335, s32[2,512,1]{2,1,0:T(8,128)} %subtract_add_fusion.low_ref), custom_call_target="tpu_custom_call" | custom-call | flops 512 | bytes 512 | tf_op jit(solution)/shard_map/pallas_call | solution.py:80
  187.9 29.5 %all-gather.11.cloned.1.call-done = bf16[1280,5120]{1,0:T(8,128)(2,1)} async-done(((bf16[320,5120]{1,0:T(8,128)(2,1)}), bf16[1280,5120]{1,0:T(8,128)(2,1)}) %all-gather.11.cloned.1.call-update) | async-done | bytes 13107216 | tf_op jit(solution)/shard_map/all_gather | solution.py:291
  217.4 6.1 dynamic-slice_bitcast_fusion.8
  224.2 10.2 collective-permute-done.12.refs_1_
  246.9 11.0 multiply_convert_fusion.1
  267.5 5.6 fusion.108
  279.7 27.3 %collective-permute-done.15 = bf16[512,1280]{1,0:T(8,128)(2,1)} collective-permute-done((bf16[512,1280]{1,0:T(8,128)(2,1)S(1)}, bf16[512,1280]{1,0:T(8,128)(2,1)}, u32[]{:S(2)}, u32[]{:S(2)}) %collective-permute-start.15) | collective-permute-done | bytes 1310752 | tf_op jit(solution)/shard_map/ppermute | solution.py:199
  309.4 5.7 collective-permute-start.16
  319.4 23.5 %collective-permute-done.16 = bf16[512,1280]{1,0:T(8,128)(2,1)} collective-permute-done((bf16[512,1280]{1,0:T(8,128)(2,1)}, bf16[512,1280]{1,0:T(8,128)(2,1)}, u32[]{:S(2)}, u32[]{:S(2)}) %collective-permute-start.16) | collective-permute-done | bytes 1310752 | tf_op jit(solution)/shard_map/ppermute | solution.py:199
  350.1 18.7 %add_convert_fusion = bf16[3072,1920]{1,0:T(8,128)(2,1)} fusion(bf16[3072,1280]{1,0:T(8,128)(2,1)S(1)} %constant_dynamic-update-slice_fusion.23, f32[1920]{0:T(1024)S(1)} %reduce.10, bf16[1280,2560]{1,0:T(8,128)(2,1)S(1)} %bitcast.320), kind=kOutput, calls=%fused_computation.2 | convolution fusion | flops 15111290880 | bytes 24584192 | tf_op jit(solution)/shard_map/dot_general | solution.py:304
  368.8 31.8 %shard_map.193 = (bf16[2,512,640]{2,1,0:T(8,128)(2,1)}, f32[2,5,2,512]{3,2,1,0:T(2,128)}) custom-call(bf16[2,1536,1920]{2,1,0:T(8,128)(2,1)} %bitcast.337, s32[2,512,1]{2,1,0:T(8,128)} %subtract_add_fusion.low_ref), custom_call_target="tpu_custom_call" | custom-call | flops 512 | bytes 512 | tf_op jit(solution)/shard_map/pallas_call | solution.py:80
  413.8 21.3 %all-gather.15.cloned.1.call-done = bf16[1280,5120]{1,0:T(8,128)(2,1)} async-done(((bf16[320,5120]{1,0:T(8,128)(2,1)}), bf16[1280,5120]{1,0:T(8,128)(2,1)}) %all-gather.15.cloned.1.call-update) | async-done | bytes 13107216 | tf_op jit(solution)/shard_map/all_gather | solution.py:291
  446.9 11.2 multiply_convert_fusion
  458.2 7.4 convolution_convert_fusion.3
  468.6 6.5 collective-permute-done.25.refs_1_
  484.9 18.0 %convert_reduce_fusion.2 = (f32[2560]{0:T(1024)}, bf16[1024,2560]{1,0:T(8,128)(2,1)S(1)}) fusion(f32[1024,2560]{1,0:T(8,128)} %get-tuple-element.247, f32[2560]{0:T(1024)S(1)} %get-tuple-element.198, bf16[1024,1280]{1,0:T(8,128)(2,1)S(1)} %copy-done.54, bf16[1280,2560]{1,0:T(8,128)(2,1)S(1)} %shard_map.196), kind=kOutput, calls=%fused_computation.26 | convolution fusion | flops 6771176960 | bytes 24924160 | tf_op jit(solution)/shard_map/dot_general | solution.py:304
  509.0 10.3 convolution_convert_fusion.2
  522.3 8.0 multiply_reduce_fusion
  552.2 40.3 %shard_map.198 = bf16[2,1536,1920]{2,1,0:T(8,128)(2,1)} custom-call(bf16[2,1536,1920]{2,1,0:T(8,128)(2,1)} %bitcast.338, bf16[2,512,640]{2,1,0:T(8,128)(2,1)} %get-tuple-element.103.mixed_ref, bf16[2,512,640]{2,1,0:T(8,128)(2,1)} %bitcast.345, f32[2,5,2,512]{3,2,1,0:T(2,128)} %get-tuple-element.115.total_ref, s32[2,1,512]{2,1,0:T(1,128)} %subtract_add_fusion.1.low_ref), custom_call_target="tpu_custom_call" | custom-call | flops 512 | bytes 512 | tf_op jit(solution)/shard_map/pallas_call | solution.py:163
  592.5 10.5 convolution_convert_fusion.7
  603.2 8.6 convolution_convert_fusion.13
  612.4 12.0 convolution_add_fusion.1
  627.6 20.2 %convolution_convert_fusion.5 = bf16[1280,1920]{1,0:T(8,128)(2,1)} fusion(bf16[3072,1280]{1,0:T(8,128)(2,1)} %copy-done.71, bf16[3072,1920]{1,0:T(8,128)(2,1)S(1)} %bitcast.334), kind=kOutput, calls=%fused_computation.33 | convolution fusion | flops 15101952000 | bytes 24576000 | tf_op jit(solution)/shard_map/dot_general | solution.py:15
  647.8 11.2 collective-permute-done.32
  666.8 8.7 fusion.41
  675.6 6.6 convert_reduce_fusion.1
  684.9 14.0 %collective-permute-done.33 = bf16[512,1280]{1,0:T(8,128)(2,1)} collective-permute-done((bf16[512,1280]{1,0:T(8,128)(2,1)}, bf16[512,1280]{1,0:T(8,128)(2,1)}, u32[]{:S(2)}, u32[]{:S(2)}) %collective-permute-start.33) | collective-permute-done | bytes 1310752 | tf_op jit(solution)/shard_map/ppermute | solution.py:204
  711.8 10.3 convolution_convert_fusion.1
  722.9 20.0 %convert_reduce_fusion.3 = (f32[2560]{0:T(1024)S(1)}, bf16[1024,2560]{1,0:T(8,128)(2,1)}) fusion(f32[1024,2560]{1,0:T(8,128)} %get-tuple-element.241, f32[2560]{0:T(1024)S(1)} %copy-done.103, bf16[1280,2560]{1,0:T(8,128)(2,1)} %copy-done.21, bf16[512,1280]{1,0:T(8,128)(2,1)} %copy-done.111, bf16[512,1280]{1,0:T(8,128)(2,1)S(1)} %convert_element_type.244), kind=kOutput, calls=%fused_computation.27 | convolution fusion | flops 6776419840 | bytes 24924160 | tf_op jit(solution)/shard_map/dot_general | solution.py:304
  751.3 6.9 convolution_add_fusion.4
  767.0 9.8 convolution_convert_fusion
  798.5 5.4 fusion.70
  807.8 40.0 %shard_map.202 = bf16[2,1536,1920]{2,1,0:T(8,128)(2,1)} custom-call(bf16[2,1536,1920]{2,1,0:T(8,128)(2,1)} %bitcast.336, bf16[2,512,640]{2,1,0:T(8,128)(2,1)} %get-tuple-element.94.mixed_ref, bf16[2,512,640]{2,1,0:T(8,128)(2,1)} %bitcast.346, f32[2,5,2,512]{3,2,1,0:T(2,128)} %get-tuple-element.139.total_ref, s32[2,1,512]{2,1,0:T(1,128)} %subtract_add_fusion.1.low_ref), custom_call_target="tpu_custom_call" | custom-call | flops 512 | bytes 512 | tf_op jit(solution)/shard_map/pallas_call | solution.py:163
  847.8 13.8 %reduce-scatter.13.cloned.1.call-done = bf16[320,2560]{1,0:T(8,128)(2,1)} async-done(((bf16[1280,2560]{1,0:T(8,128)(2,1)}), bf16[320,2560]{1,0:T(8,128)(2,1)}) %reduce-scatter.13.cloned.1.call-update) | async-done | bytes 1638416 | tf_op jit(solution)/shard_map/reduce_scatter | solution.py:300
  861.7 12.0 convolution_convert_fusion.6
  873.9 6.9 collective-permute-done.43
  880.7 13.5 %convolution_add_fusion = f32[1536,1280]{1,0:T(8,128)} fusion(bf16[1536,1280]{1,0:T(8,128)(2,1)} %collective-permute-done.43, bf16[2,1536,1920]{2,1,0:T(8,128)(2,1)S(1)} %copy-done.30, bf16[1280,2560]{1,0:T(8,128)(2,1)} %copy-done.19), kind=kOutput, calls=%fused_computation.30 | convolution fusion | flops 7553679360 | bytes 22609920 | tf_op jit(solution)/shard_map/dot_general | solution.py:15
  894.3 17.7 %convolution_convert_fusion.4 = bf16[1280,1920]{1,0:T(8,128)(2,1)S(1)} fusion(bf16[3072,1280]{1,0:T(8,128)(2,1)S(1)} %bitcast.354, bf16[3072,1920]{1,0:T(8,128)(2,1)S(1)} %bitcast.332), kind=kOutput, calls=%fused_computation.32 | convolution fusion | flops 15101952000 | bytes 24576000 | tf_op jit(solution)/shard_map/dot_general | solution.py:15
  926.1 52.2 %collective-permute-done.44 = bf16[512,1280]{1,0:T(8,128)(2,1)} collective-permute-done((bf16[512,1280]{1,0:T(8,128)(2,1)}, bf16[512,1280]{1,0:T(8,128)(2,1)}, u32[]{:S(2)}, u32[]{:S(2)}) %collective-permute-start.44) | collective-permute-done | bytes 1310752 | tf_op jit(solution)/shard_map/ppermute | solution.py:204
  978.3 35.4 %all-reduce.13.cloned.1.call-done = bf16[320,2560]{1,0:T(8,128)(2,1)} async-done(((bf16[320,2560]{1,0:T(8,128)(2,1)}), bf16[320,2560]{1,0:T(8,128)(2,1)}) %all-reduce.13.cloned.1.call-update) | async-done | bytes 1638416 | tf_op jit(solution)/shard_map/psum | solution.py:568
  1019.0 6.5 convert_reduce_fusion
  1035.1 49.0 %collective-permute-done.46 = bf16[512,1280]{1,0:T(8,128)(2,1)} collective-permute-done((bf16[512,1280]{1,0:T(8,128)(2,1)S(1)}, bf16[512,1280]{1,0:T(8,128)(2,1)}, u32[]{:S(2)}, u32[]{:S(2)}) %collective-permute-start.46) | collective-permute-done | bytes 1310752 | tf_op jit(solution)/shard_map/ppermute | solution.py:204
  1084.1 40.2 %all-reduce.15.cloned.1.call-done = bf16[320,3200]{1,0:T(8,128)(2,1)} async-done(((bf16[320,3200]{1,0:T(8,128)(2,1)}), bf16[320,3200]{1,0:T(8,128)(2,1)}) %all-reduce.15.cloned.1.call-update) | async-done | bytes 2048016 | tf_op jit(solution)/shard_map/psum | solution.py:568
  1153.4 10.1 collective-permute-done.53
  1166.3 19.9 %all-reduce.17.cloned.1.call-done.first_ref = bf16[320,1920]{1,0:T(8,128)(2,1)} async-done(((bf16[320,1920]{1,0:T(8,128)(2,1)}), bf16[320,1920]{1,0:T(8,128)(2,1)}) %all-reduce.17.cloned.1.call-update) | async-done | bytes 1228816 | tf_op jit(solution)/shard_map/psum | solution.py:568
  (616 shorter events, 345.3 us)
Async XLA Ops:
  8.0 80.0 %all-gather.9.cloned.1.call-start = ((), (), s32[]{:S(2)}) async-start(), calls=%async_computation.18 | async-start | bytes 8192000 | tf_op jit(solution)/shard_map/all_gather | solution.py:291
  12.9 100.4 %all-reduce.7.cloned.1.call-start = ((), (), s32[]{:S(2)}) async-start(), calls=%async_computation.6 | async-start | bytes 163840 | tf_op jit(solution)/shard_map/psum | solution.py:463
  12.9 24.9 %collective-permute-start.9 = (s32[4]{0:T(128)S(1)}, s32[4]{0:T(128)S(1)}, u32[]{:S(2)}, u32[]{:S(2)}) collective-permute-start(s32[4]{0:T(128)S(1)} %fusion.141), channel_id=1, source_target_pairs={{0,8},{8,0},{1,9},{9,1},{2,10},{10,2},{3,11},{11,3},{4,12},{12,4},... | collective-permute-start | bytes 56 | tf_op jit(solution)/shard_map/ppermute | solution.py:190
  13.5 25.8 %collective-permute-start.2 = (bf16[12,320]{1,0:T(8,128)(2,1)S(1)}, bf16[12,320]{1,0:T(8,128)(2,1)S(1)}, u32[]{:S(2)}, u32[]{:S(2)}) collective-permute-start(bf16[12,320]{1,0:T(8,128)(2,1)S(1)} %reshape.357), channel_id=1, source_target_pairs={{0,8},{8,0},{1,9},{9,1},{2,10},{10,2},{3,11},{11,3},{4,12},{12,4},... | collective-permute-start | bytes 23048 | tf_op jit(solution)/shard_map/ppermute | solution.py:190
  13.7 27.4 %collective-permute-start.8 = (bf16[2,3840]{1,0:T(2,128)(2,1)S(1)}, bf16[2,3840]{1,0:T(2,128)(2,1)S(1)}, u32[]{:S(2)}, u32[]{:S(2)}) collective-permute-start(bf16[2,3840]{1,0:T(2,128)(2,1)S(1)} %constant_dynamic-update-slice_fusion.6), channel_id=1, source_target_pairs={{0,1},{1,0},{2,3},{3,2},{4,5},{5,4},{6,7},{7,6},{8,9},{9,8},{10,11... | collective-permute-start | bytes 46088 | tf_op jit(solution)/shard_map/ppermute | solution.py:194
  19.3 34.3 %collective-permute-start = (bf16[512,1280]{1,0:T(8,128)(2,1)}, bf16[512,1280]{1,0:T(8,128)(2,1)}, u32[]{:S(2)}, u32[]{:S(2)}) collective-permute-start(bf16[512,1280]{1,0:T(8,128)(2,1)} %get-tuple-element.217), channel_id=1, source_target_pairs={{0,2},{2,4},{4,6},{1,3},{3,5},{5,7},{8,10},{10,12},{12,14},{9,11},... | collective-permute-start | bytes 3932168 | tf_op jit(solution)/shard_map/ppermute | solution.py:199
  25.0 192.4 %all-gather.11.cloned.1.call-start = ((), (), s32[]{:S(2)}) async-start(), calls=%async_computation.19 | async-start | bytes 16384000 | tf_op jit(solution)/shard_map/all_gather | solution.py:291
  39.6 18.9 %collective-permute-start.3 = (bf16[12,640]{1,0:T(8,128)(2,1)S(1)}, bf16[12,640]{1,0:T(8,128)(2,1)S(1)}, u32[]{:S(2)}, u32[]{:S(2)}) collective-permute-start(bf16[12,640]{1,0:T(8,128)(2,1)S(1)} %select_n.131), channel_id=1, source_target_pairs={{0,16},{16,0},{1,17},{17,1},{2,18},{18,2},{3,19},{19,3},{4,20},{20... | collective-permute-start | bytes 46088 | tf_op jit(solution)/shard_map/ppermute | solution.py:320
  53.6 253.4 %all-gather.13.cloned.1.call-start = ((), (), s32[]{:S(2)}) async-start(), calls=%async_computation.20 | async-start | bytes 8192000 | tf_op jit(solution)/shard_map/all_gather | solution.py:291
  53.9 31.6 %collective-permute-start.1 = (bf16[512,1280]{1,0:T(8,128)(2,1)}, bf16[512,1280]{1,0:T(8,128)(2,1)S(1)}, u32[]{:S(2)}, u32[]{:S(2)}) collective-permute-start(bf16[512,1280]{1,0:T(8,128)(2,1)} %collective-permute-done), channel_id=1, source_target_pairs={{0,2},{2,4},{4,6},{1,3},{3,5},{5,7},{8,10},{10,12},{12,14},{9,11},... | collective-permute-start | bytes 3932168 | tf_op jit(solution)/shard_map/ppermute | solution.py:199
  91.9 21.4 %collective-permute-start.7 = (bf16[2,320,2560]{2,1,0:T(8,128)(2,1)}, bf16[2,320,2560]{2,1,0:T(8,128)(2,1)S(1)}, u32[]{:S(2)}, u32[]{:S(2)}) collective-permute-start(bf16[2,320,2560]{2,1,0:T(8,128)(2,1)} %dynamic-slice_bitcast_fusion.9), channel_id=1, source_target_pairs={{0,8},{8,0},{1,9},{9,1},{2,10},{10,2},{3,11},{11,3},{4,12},{12,4},... | collective-permute-start | bytes 9830408 | tf_op jit(solution)/shard_map/ppermute | solution.py:190
  97.7 10.5 collective-permute-start.5
  98.3 7.5 collective-permute-start.4
  223.5 10.8 collective-permute-start.12
  223.5 19.7 %collective-permute-start.13 = (bf16[2,320,2560]{2,1,0:T(8,128)(2,1)}, bf16[2,320,2560]{2,1,0:T(8,128)(2,1)S(1)}, u32[]{:S(2)}, u32[]{:S(2)}) collective-permute-start(bf16[2,320,2560]{2,1,0:T(8,128)(2,1)} %get-tuple-element.225), channel_id=1, source_target_pairs={{0,8},{8,0},{1,9},{9,1},{2,10},{10,2},{3,11},{11,3},{4,12},{12,4},... | collective-permute-start | bytes 9830408 | tf_op jit(solution)/shard_map/ppermute | solution.py:190
  224.1 211.0 %all-gather.15.cloned.1.call-start = ((), (), s32[]{:S(2)}) async-start(), calls=%async_computation.21 | async-start | bytes 16384000 | tf_op jit(solution)/shard_map/all_gather | solution.py:291
  275.0 31.9 %collective-permute-start.15 = (bf16[512,1280]{1,0:T(8,128)(2,1)S(1)}, bf16[512,1280]{1,0:T(8,128)(2,1)}, u32[]{:S(2)}, u32[]{:S(2)}) collective-permute-start(bf16[512,1280]{1,0:T(8,128)(2,1)S(1)} %add_convert_fusion.5), channel_id=1, source_target_pairs={{0,2},{2,4},{4,6},{1,3},{3,5},{5,7},{8,10},{10,12},{12,14},{9,11},... | collective-permute-start | bytes 3932168 | tf_op jit(solution)/shard_map/ppermute | solution.py:199
  306.9 244.0 %reduce-scatter.7.cloned.1.call-start = ((), (), s32[]{:S(2)}) async-start(), calls=%async_computation.7 | async-start | bytes 8192000 | tf_op jit(solution)/shard_map/reduce_scatter | solution.py:300
  309.4 33.5 %collective-permute-start.16 = (bf16[512,1280]{1,0:T(8,128)(2,1)}, bf16[512,1280]{1,0:T(8,128)(2,1)}, u32[]{:S(2)}, u32[]{:S(2)}) collective-permute-start(bf16[512,1280]{1,0:T(8,128)(2,1)} %collective-permute-done.15), channel_id=1, source_target_pairs={{0,2},{2,4},{4,6},{1,3},{3,5},{5,7},{8,10},{10,12},{12,14},{9,11},... | collective-permute-start | bytes 3932168 | tf_op jit(solution)/shard_map/ppermute | solution.py:199
  342.9 7.0 collective-permute-start.20
  440.4 17.8 %collective-permute-start.22 = (bf16[512,1280]{1,0:T(8,128)(2,1)S(1)}, bf16[512,1280]{1,0:T(8,128)(2,1)S(1)}, u32[]{:S(2)}, u32[]{:S(2)}) collective-permute-start(bf16[512,1280]{1,0:T(8,128)(2,1)S(1)} %fusion.140), channel_id=1, source_target_pairs={{0,8},{8,0},{1,9},{9,1},{2,10},{10,2},{3,11},{11,3},{4,12},{12,4},... | collective-permute-start | bytes 3932168 | tf_op jit(solution)/shard_map/ppermute | solution.py:190
  465.8 9.3 collective-permute-start.25
  466.0 12.4 %collective-permute-start.26 = (bf16[2,320,2560]{2,1,0:T(8,128)(2,1)}, bf16[2,320,2560]{2,1,0:T(8,128)(2,1)S(1)}, u32[]{:S(2)}, u32[]{:S(2)}) collective-permute-start(bf16[2,320,2560]{2,1,0:T(8,128)(2,1)} %get-tuple-element.222), channel_id=1, source_target_pairs={{0,8},{8,0},{1,9},{9,1},{2,10},{10,2},{3,11},{11,3},{4,12},{12,4},... | collective-permute-start | bytes 9830408 | tf_op jit(solution)/shard_map/ppermute | solution.py:190
  478.4 169.4 %all-reduce.9.cloned.1.call-start = ((), (), s32[]{:S(2)}) async-start(), calls=%async_computation.8 | async-start | bytes 3276800 | tf_op jit(solution)/shard_map/psum | solution.py:568
  508.8 12.9 %collective-permute-start.27 = (bf16[512,1280]{1,0:T(8,128)(2,1)S(1)}, bf16[512,1280]{1,0:T(8,128)(2,1)S(1)}, u32[]{:S(2)}, u32[]{:S(2)}) collective-permute-start(bf16[512,1280]{1,0:T(8,128)(2,1)S(1)} %convolution_convert_fusion.14), channel_id=1, source_target_pairs={{0,8},{8,0},{1,9},{9,1},{2,10},{10,2},{3,11},{11,3},{4,12},{12,4},... | collective-permute-start | bytes 3932168 | tf_op jit(solution)/shard_map/ppermute | solution.py:190
  521.3 23.8 %collective-permute-start.29 = (bf16[2,320,2560]{2,1,0:T(8,128)(2,1)}, bf16[2,320,2560]{2,1,0:T(8,128)(2,1)S(1)}, u32[]{:S(2)}, u32[]{:S(2)}) collective-permute-start(bf16[2,320,2560]{2,1,0:T(8,128)(2,1)} %dynamic-slice_bitcast_fusion.2), channel_id=1, source_target_pairs={{0,8},{8,0},{1,9},{9,1},{2,10},{10,2},{3,11},{11,3},{4,12},{12,4},... | collective-permute-start | bytes 9830408 | tf_op jit(solution)/shard_map/ppermute | solution.py:190
  551.0 147.9 %reduce-scatter.9.cloned.1.call-start = ((), (), s32[]{:S(2)}) async-start(), calls=%async_computation.9 | async-start | bytes 10240000 | tf_op jit(solution)/shard_map/reduce_scatter | solution.py:300
  551.5 215.3 %reduce-scatter.11.cloned.1.call-start = ((), (), s32[]{:S(2)}) async-start(), calls=%async_computation.10 | async-start | bytes 6144000 | tf_op jit(solution)/shard_map/reduce_scatter | solution.py:300
  603.1 9.3 collective-permute-start.31
  611.7 55.1 %collective-permute-start.35 = (bf16[512,1280]{1,0:T(8,128)(2,1)}, bf16[512,1280]{1,0:T(8,128)(2,1)}, u32[]{:S(2)}, u32[]{:S(2)}) collective-permute-start(bf16[512,1280]{1,0:T(8,128)(2,1)} %convolution_convert_fusion.13), channel_id=1, source_target_pairs={{0,8},{8,0},{1,9},{9,1},{2,10},{10,2},{3,11},{11,3},{4,12},{12,4},... | collective-permute-start | bytes 3932168 | tf_op jit(solution)/shard_map/ppermute | solution.py:190
  626.3 32.7 %collective-permute-start.32 = (bf16[512,1280]{1,0:T(8,128)(2,1)S(1)}, bf16[512,1280]{1,0:T(8,128)(2,1)S(1)}, u32[]{:S(2)}, u32[]{:S(2)}) collective-permute-start(bf16[512,1280]{1,0:T(8,128)(2,1)S(1)} %slice.702), channel_id=1, source_target_pairs={{2,0},{4,2},{6,4},{3,1},{5,3},{7,5},{10,8},{12,10},{14,12},{11,9},... | collective-permute-start | bytes 3932168 | tf_op jit(solution)/shard_map/ppermute | solution.py:204
  662.2 20.0 %collective-permute-start.34 = (bf16[2,320,1920]{2,1,0:T(8,128)(2,1)S(1)}, bf16[2,320,1920]{2,1,0:T(8,128)(2,1)S(1)}, u32[]{:S(2)}, u32[]{:S(2)}) collective-permute-start(bf16[2,320,1920]{2,1,0:T(8,128)(2,1)S(1)} %dynamic-slice_bitcast_fusion.11), channel_id=1, source_target_pairs={{0,8},{8,0},{1,9},{9,1},{2,10},{10,2},{3,11},{11,3},{4,12},{12,4},... | collective-permute-start | bytes 7372808 | tf_op jit(solution)/shard_map/ppermute | solution.py:190
  665.5 33.4 %collective-permute-start.33 = (bf16[512,1280]{1,0:T(8,128)(2,1)}, bf16[512,1280]{1,0:T(8,128)(2,1)}, u32[]{:S(2)}, u32[]{:S(2)}) collective-permute-start(bf16[512,1280]{1,0:T(8,128)(2,1)} %add_convert_fusion.3), channel_id=1, source_target_pairs={{2,0},{4,2},{6,4},{3,1},{5,3},{7,5},{10,8},{12,10},{14,12},{11,9},... | collective-permute-start | bytes 3932168 | tf_op jit(solution)/shard_map/ppermute | solution.py:204
  708.8 152.8 %reduce-scatter.13.cloned.1.call-start = ((), (), s32[]{:S(2)}) async-start(), calls=%async_computation.11 | async-start | bytes 8192000 | tf_op jit(solution)/shard_map/reduce_scatter | solution.py:300
  722.4 35.8 %collective-permute-start.38 = (bf16[2,320,2560]{2,1,0:T(8,128)(2,1)S(1)}, bf16[2,320,2560]{2,1,0:T(8,128)(2,1)S(1)}, u32[]{:S(2)}, u32[]{:S(2)}) collective-permute-start(bf16[2,320,2560]{2,1,0:T(8,128)(2,1)S(1)} %dynamic-slice_bitcast_fusion.1), channel_id=1, source_target_pairs={{0,8},{8,0},{1,9},{9,1},{2,10},{10,2},{3,11},{11,3},{4,12},{12,4},... | collective-permute-start | bytes 9830408 | tf_op jit(solution)/shard_map/ppermute | solution.py:190
  766.9 149.2 %all-reduce.11.cloned.1.call-start = ((), (), s32[]{:S(2)}) async-start(), calls=%async_computation.12 | async-start | bytes 6553600 | tf_op jit(solution)/shard_map/psum | solution.py:568
  781.2 22.7 %collective-permute-start.40 = (bf16[2,320,2560]{2,1,0:T(8,128)(2,1)}, bf16[2,320,2560]{2,1,0:T(8,128)(2,1)S(1)}, u32[]{:S(2)}, u32[]{:S(2)}) collective-permute-start(bf16[2,320,2560]{2,1,0:T(8,128)(2,1)} %dynamic-slice_bitcast_fusion), channel_id=1, source_target_pairs={{0,8},{8,0},{1,9},{9,1},{2,10},{10,2},{3,11},{11,3},{4,12},{12,4},... | collective-permute-start | bytes 9830408 | tf_op jit(solution)/shard_map/ppermute | solution.py:190
  787.3 191.0 %reduce-scatter.15.cloned.1.call-start = ((), (), s32[]{:S(2)}) async-start(), calls=%async_computation.13 | async-start | bytes 10240000 | tf_op jit(solution)/shard_map/reduce_scatter | solution.py:300
  793.0 54.8 %collective-permute-start.42 = (bf16[512,1280]{1,0:T(8,128)(2,1)}, bf16[512,1280]{1,0:T(8,128)(2,1)}, u32[]{:S(2)}, u32[]{:S(2)}) collective-permute-start(bf16[512,1280]{1,0:T(8,128)(2,1)} %fusion.41), channel_id=1, source_target_pairs={{0,1},{1,0},{2,3},{3,2},{4,5},{5,4},{6,7},{7,6},{8,9},{9,8},{10,11... | collective-permute-start | bytes 3932168 | tf_op jit(solution)/shard_map/ppermute | solution.py:194
  861.7 152.0 %all-reduce.13.cloned.1.call-start = ((), (), s32[]{:S(2)}) async-start(), calls=%async_computation.14 | async-start | bytes 3276800 | tf_op jit(solution)/shard_map/psum | solution.py:568
  916.2 208.1 %all-reduce.15.cloned.1.call-start = ((), (), s32[]{:S(2)}) async-start(), calls=%async_computation.16 | async-start | bytes 4096000 | tf_op jit(solution)/shard_map/psum | solution.py:568
  919.2 59.1 %collective-permute-start.44 = (bf16[512,1280]{1,0:T(8,128)(2,1)}, bf16[512,1280]{1,0:T(8,128)(2,1)}, u32[]{:S(2)}, u32[]{:S(2)}) collective-permute-start(bf16[512,1280]{1,0:T(8,128)(2,1)} %slice.701), channel_id=1, source_target_pairs={{2,0},{4,2},{6,4},{3,1},{5,3},{7,5},{10,8},{12,10},{14,12},{11,9},... | collective-permute-start | bytes 3932168 | tf_op jit(solution)/shard_map/ppermute | solution.py:204
  1013.7 110.5 %reduce-scatter.17.cloned.1.call-start = ((), (), s32[]{:S(2)}) async-start(), calls=%async_computation.15 | async-start | bytes 6144000 | tf_op jit(solution)/shard_map/reduce_scatter | solution.py:300
  1014.3 171.8 %all-reduce.17.cloned.1.call-start = ((), (), s32[]{:S(2)}) async-start(), calls=%async_computation.17 | async-start | bytes 2457600 | tf_op jit(solution)/shard_map/psum | solution.py:568
  1028.0 56.0 %collective-permute-start.46 = (bf16[512,1280]{1,0:T(8,128)(2,1)S(1)}, bf16[512,1280]{1,0:T(8,128)(2,1)}, u32[]{:S(2)}, u32[]{:S(2)}) collective-permute-start(bf16[512,1280]{1,0:T(8,128)(2,1)S(1)} %add_convert_fusion.2), channel_id=1, source_target_pairs={{2,0},{4,2},{6,4},{3,1},{5,3},{7,5},{10,8},{12,10},{14,12},{11,9},... | collective-permute-start | bytes 3932168 | tf_op jit(solution)/shard_map/ppermute | solution.py:204
  1137.9 52.0 %collective-permute-start.47 = (bf16[512,1280]{1,0:T(8,128)(2,1)}, bf16[512,1280]{1,0:T(8,128)(2,1)}, u32[]{:S(2)}, u32[]{:S(2)}) collective-permute-start(bf16[512,1280]{1,0:T(8,128)(2,1)} %get-tuple-element.212), channel_id=1, source_target_pairs={{0,1},{1,0},{2,3},{3,2},{4,5},{5,4},{6,7},{7,6},{8,9},{9,8},{10,11... | collective-permute-start | bytes 3932168 | tf_op jit(solution)/shard_map/ppermute | solution.py:194
  1141.5 8.4 collective-permute-start.51
  1150.9 12.7 %collective-permute-start.53 = (f32[2,15360]{1,0:T(2,128)S(1)}, f32[2,15360]{1,0:T(2,128)S(1)}, u32[]{:S(2)}, u32[]{:S(2)}) collective-permute-start(f32[2,15360]{1,0:T(2,128)S(1)} %add.453), channel_id=1, source_target_pairs={{2,0},{4,6},{3,1},{5,7},{10,8},{12,14},{11,9},{13,15},{18,16},{20,... | collective-permute-start | bytes 368648 | tf_op jit(solution)/shard_map/ppermute | solution.py:363
  (151 other events, 2059.1 us)
Sparse Core Ops, SparseCore 0:
  13.0 75.0 all-gather.8
  90.5 126.8 all-gather.10
  224.2 72.3 all-gather.12
  307.1 127.9 all-gather.14
  478.5 72.3 reduce-scatter.6
  554.7 84.7 reduce-scatter.8
  709.0 57.8 reduce-scatter.10
  770.5 91.0 reduce-scatter.12
  865.2 84.7 reduce-scatter.14
  1017.9 57.8 reduce-scatter.16
Sparse Core Ops, SparseCore 1:
  25.1 32.5 all-reduce.6
  551.0 70.9 all-reduce.8
  787.3 125.3 all-reduce.10
  916.2 97.3 all-reduce.12
  1016.2 108.0 all-reduce.14
  1126.7 59.4 all-reduce.16
